TPU v7x, 32 devices: a whole 2x2x4 slice. The times are simulated.
32 devices in a mesh: dp: 16 (over z, y, x), tensor: 2 (over core).
Axes of the slice: x: 2, y: 2, z: 4, core: 2. Of those that a mesh axis runs over, the one named last changes fastest.
Arguments:
- inputs: bfloat16 [16384, 768], P(('dp', 'tensor')), may hold values from -9 to 9, as said below
- row_lengths: int32 [128], P('dp'), may hold values from 0 to 512, as said below
- project_weight: bfloat16 [768, 3, 768], P(None, None, 'tensor'), may hold values from -0.21875 to 0.21875
- merge_weight: bfloat16 [768, 768], P('tensor'), may hold values from -1.75 to 1.75
- up_weight: bfloat16 [768, 3072], P(None, 'tensor'), may hold values from -0.21875 to 0.21875
- down_weight: bfloat16 [3072, 768], P('tensor'), may hold values from -0.109375 to 0.109375
- query_value_bias: float32 [2, 768], P(None, 'tensor'), may hold values from -1.5 to 1.5
- merge_bias: float32 [768], replicated, may hold values from -1.5 to 1.5
- up_bias: float32 [3072], P('tensor'), may hold values from -1.5 to 1.5
- down_bias: float32 [768], replicated, may hold values from -1.5 to 1.5
- norm_gains: float32 [2, 768], replicated, may hold values from 0.5 to 1.5
- norm_shifts: float32 [2, 768], replicated, may hold values from -1 to 1
- clip_scales: float32 [3], replicated, may hold values from 2 to 5
- cotangent: bfloat16 [16384, 768], P(('dp', 'tensor')), may hold values from -6 to 6
Outputs:
- output: bfloat16 [16384, 768], P(('dp', 'tensor'))
- input_grad: float32 [16384, 768], P(('dp', 'tensor'))
- project_grad: float32 [768, 3, 768], P(None, None, 'tensor')
- merge_grad: float32 [768, 768], P('tensor')
- up_grad: float32 [768, 3072], P(None, 'tensor')
- down_grad: float32 [3072, 768], P('tensor')
- query_value_bias_grad: float32 [2, 768], P(None, 'tensor')
- merge_bias_grad: float32 [768], replicated
- up_bias_grad: float32 [3072], P('tensor')
- down_bias_grad: float32 [768], replicated
- gain_grad: float32 [2, 768], replicated
- shift_grad: float32 [2, 768], replicated
- new_scales: float32 [3], replicated
Inputs may be any that keep to these rules, and one draw needn't show every extreme that they name: `row_lengths`: each aligned block of 512 entries-worth of slots (4 entries) holds either one row, whose length (more than 128) is in its first entry with zeros in the others, or 4 rows whose lengths (at least 1) are in their entries. Some row has 512 tokens. `inputs`: activations of order one.
All inputs are finite; a program needn't handle non-finite values.
Results may differ from a plain program's by a relative error of at most 0.014.
The roundings to bfloat16 on the way count: a program that leaves them out, or rounds other values in their place, can miss the bound.
Values may be sent and summed in bfloat16 or wider, within the bound.
No kernel may reach another device: no remote copies, remote signals or barrier semaphores. Data moves between devices by JAX's collectives and lax.ppermute only.
A program may use at most 128 MiB of HBM per device.

v0:
```python
from functools import partial

import jax
import jax.numpy as jnp
from jax import lax
from jax.sharding import PartitionSpec as P

HEAD = 64
LONG = 512
SHORT = 128


EPSILON = 1e-12
DECAY = 0.9


def softclip(value, scale):
    return scale * jnp.tanh(value / scale)


def clip_slope(value, scale):
    bent = jnp.tanh(value / scale)
    return 1.0 - bent * bent


def norm_parts(value, gain, shift):
    mean = jnp.mean(value, axis=-1, keepdims=True)
    centred = value - mean
    inverse = lax.rsqrt(jnp.mean(centred * centred, axis=-1, keepdims=True) + EPSILON)
    unit = centred * inverse
    return (unit * gain + shift, unit, inverse)


def norm_back(grad, unit, inverse, gain):
    scaled = grad * gain
    return inverse * (
        scaled
        - jnp.mean(scaled, axis=-1, keepdims=True)
        - unit * jnp.mean(scaled * unit, axis=-1, keepdims=True)
    )


def block_mask(lengths):
    places = jnp.arange(LONG, dtype=jnp.int32)
    single = lengths[0] > SHORT
    per_slot = jnp.repeat(lengths, SHORT, total_repeat_length=LONG)
    member = jnp.where(single, 0, places // SHORT)
    inner = jnp.where(single, places, places % SHORT)
    limit = jnp.where(single, lengths[0], per_slot)
    usable = inner < limit
    return (member[:, None] == member[None, :]) & usable[None, :]


def masked_scores(queries, key_rows, lengths):
    scores = (
        jnp.einsum("qhd,khd->hqk", queries, key_rows, preferred_element_type=jnp.float32) * 0.125
    )
    return jnp.where(block_mask(lengths)[None], scores, -1e30)


def attend_forward(parts):
    queries, key_rows, values, lengths = parts
    masked = masked_scores(queries, key_rows, lengths)
    top = jnp.max(masked, axis=-1, keepdims=True)
    log_total = top + jnp.log(jnp.sum(jnp.exp(masked - top), axis=-1, keepdims=True))
    weights = jnp.exp(masked - log_total).astype(jnp.bfloat16)
    return (
        jnp.einsum("hqk,khd->qhd", weights, values, preferred_element_type=jnp.float32),
        log_total,
    )


def attend_backward(parts):
    queries, key_rows, values, grad_context, log_total, lengths = parts
    weights = jnp.exp(masked_scores(queries, key_rows, lengths) - log_total)
    grad_weights = jnp.einsum(
        "qhd,khd->hqk", grad_context, values, preferred_element_type=jnp.float32
    )
    inner = jnp.sum(weights * grad_weights, axis=-1, keepdims=True)
    grad_scores = (weights * (grad_weights - inner)).astype(jnp.bfloat16)
    grad_values = jnp.einsum(
        "hqk,qhd->khd",
        weights.astype(jnp.bfloat16),
        grad_context,
        preferred_element_type=jnp.float32,
    )
    grad_queries = (
        jnp.einsum("hqk,khd->qhd", grad_scores, key_rows, preferred_element_type=jnp.float32)
        * 0.125
    )
    grad_keys = (
        jnp.einsum("hqk,qhd->khd", grad_scores, queries, preferred_element_type=jnp.float32) * 0.125
    )
    return (grad_queries, grad_keys, grad_values)


def local(
    inputs,
    row_lengths,
    project_weight,
    merge_weight,
    up_weight,
    down_weight,
    query_value_bias,
    merge_bias,
    up_bias,
    down_bias,
    norm_gains,
    norm_shifts,
    clip_scales,
    cotangent,
):
    share = inputs.shape[0]
    member = lax.axis_index("tensor")
    rows = lax.all_gather(inputs, "tensor", axis=0, tiled=True)
    total = rows.shape[0]
    local_peaks = jnp.stack(
        [
            jnp.max(jnp.abs(project_weight[:, 0])),
            jnp.max(jnp.abs(project_weight[:, 1])),
            jnp.max(jnp.abs(project_weight[:, 2])),
            jnp.max(jnp.abs(merge_weight)),
            jnp.max(jnp.abs(up_weight)),
            jnp.max(jnp.abs(down_weight)),
        ]
    ).astype(jnp.float32)
    weight_scales = 0.5 * lax.pmax(local_peaks, "tensor")
    project_scale = weight_scales[0:3][None, :, None]
    project_q = softclip(project_weight.astype(jnp.float32), project_scale).astype(jnp.bfloat16)
    merge_q = softclip(merge_weight.astype(jnp.float32), weight_scales[3]).astype(jnp.bfloat16)
    up_q = softclip(up_weight.astype(jnp.float32), weight_scales[4]).astype(jnp.bfloat16)
    down_q = softclip(down_weight.astype(jnp.float32), weight_scales[5]).astype(jnp.bfloat16)
    own_inputs = inputs.astype(jnp.float32)
    quantized = softclip(rows.astype(jnp.float32), clip_scales[0]).astype(jnp.bfloat16)
    projected = jnp.einsum("td,dcf->tcf", quantized, project_q, preferred_element_type=jnp.float32)
    queries = (projected[:, 0] + query_value_bias[0]).astype(jnp.bfloat16)
    key_rows = projected[:, 1].astype(jnp.bfloat16)
    values = (projected[:, 2] + query_value_bias[1]).astype(jnp.bfloat16)
    local_heads = projected.shape[2] // HEAD
    blocks = total // LONG
    block_shape = (blocks, LONG, local_heads, HEAD)
    lengths = row_lengths.reshape(blocks, LONG // SHORT)
    query_blocks = queries.reshape(block_shape)
    key_blocks = key_rows.reshape(block_shape)
    value_blocks = values.reshape(block_shape)
    context_blocks, log_totals = lax.map(
        attend_forward, (query_blocks, key_blocks, value_blocks, lengths)
    )
    context = context_blocks.reshape(total, -1).astype(jnp.bfloat16)
    branch_all = lax.psum(jnp.dot(context, merge_q, preferred_element_type=jnp.float32), "tensor")
    normed_all, unit_all, inverse_all = norm_parts(
        rows.astype(jnp.float32) + branch_all + merge_bias, norm_gains[0], norm_shifts[0]
    )
    normed_q = softclip(normed_all, clip_scales[1]).astype(jnp.bfloat16)
    normed = lax.dynamic_slice_in_dim(normed_all, member * share, share, 0)
    unit_first = lax.dynamic_slice_in_dim(unit_all, member * share, share, 0)
    inverse_first = lax.dynamic_slice_in_dim(inverse_all, member * share, share, 0)
    hidden = jnp.dot(normed_q, up_q, preferred_element_type=jnp.float32) + up_bias
    active, gelu_back = jax.vjp(partial(jax.nn.gelu, approximate=False), hidden)
    active_q = softclip(active, clip_scales[2]).astype(jnp.bfloat16)
    feed = lax.psum_scatter(
        jnp.dot(
            lax.slice_in_dim(active_q, 0, share * lax.axis_size("tensor"), axis=0),
            down_q,
            preferred_element_type=jnp.float32,
        ),
        "tensor",
        scatter_dimension=0,
        tiled=True,
    )
    result, unit_second, inverse_second = norm_parts(
        normed + feed + down_bias, norm_gains[1], norm_shifts[1]
    )
    output = result.astype(jnp.bfloat16)
    upstream = cotangent.astype(jnp.float32)
    gain_second = jnp.sum(upstream * unit_second, axis=0)
    shift_second = jnp.sum(upstream, axis=0)
    grad_sum_second = norm_back(upstream, unit_second, inverse_second, norm_gains[1])
    down_bias_part = jnp.sum(grad_sum_second, axis=0)
    grad_feed = lax.all_gather(grad_sum_second.astype(jnp.bfloat16), "tensor", axis=0, tiled=True)
    down_part = jnp.einsum("tf,td->fd", active_q, grad_feed, preferred_element_type=jnp.float32)
    grad_active = jnp.einsum("td,fd->tf", grad_feed, down_q, preferred_element_type=jnp.float32)
    grad_hidden = gelu_back(grad_active * clip_slope(active, clip_scales[2]))[0].astype(
        jnp.bfloat16
    )
    up_bias_part = jnp.sum(grad_hidden.astype(jnp.float32), axis=0)
    up_part = jnp.einsum("td,tf->df", normed_q, grad_hidden, preferred_element_type=jnp.float32)
    grad_normed = (
        lax.psum_scatter(
            jnp.einsum(
                "tf,df->td",
                lax.slice_in_dim(grad_hidden, 0, share * lax.axis_size("tensor"), axis=0),
                up_q,
                preferred_element_type=jnp.float32,
            ),
            "tensor",
            scatter_dimension=0,
            tiled=True,
        )
        * clip_slope(normed, clip_scales[1])
        + grad_sum_second
    )
    gain_first = jnp.sum(grad_normed * unit_first, axis=0)
    shift_first = jnp.sum(grad_normed, axis=0)
    grad_sum_first = norm_back(grad_normed, unit_first, inverse_first, norm_gains[0])
    merge_bias_part = jnp.sum(grad_sum_first, axis=0)
    grad_branch = lax.all_gather(grad_sum_first.astype(jnp.bfloat16), "tensor", axis=0, tiled=True)
    merge_part = jnp.einsum("th,td->hd", context, grad_branch, preferred_element_type=jnp.float32)
    grad_context = jnp.einsum(
        "td,hd->th", grad_branch, merge_q, preferred_element_type=jnp.float32
    ).astype(jnp.bfloat16)
    grad_queries, grad_keys, grad_values = lax.map(
        attend_backward,
        (
            query_blocks,
            key_blocks,
            value_blocks,
            grad_context.reshape(block_shape),
            log_totals,
            lengths,
        ),
    )
    grad_projected = jnp.stack(
        [
            grad_queries.reshape(total, -1),
            grad_keys.reshape(total, -1),
            grad_values.reshape(total, -1),
        ],
        axis=1,
    ).astype(jnp.bfloat16)
    bias_part = jnp.stack(
        [
            jnp.sum(grad_projected[:, 0].astype(jnp.float32), axis=0),
            jnp.sum(grad_projected[:, 2].astype(jnp.float32), axis=0),
        ]
    )
    project_part = jnp.einsum(
        "td,tcf->dcf", quantized, grad_projected, preferred_element_type=jnp.float32
    )
    input_grad = (
        lax.psum_scatter(
            jnp.einsum(
                "tcf,dcf->td",
                lax.slice_in_dim(grad_projected, 0, lax.axis_size("tensor") * share, axis=0),
                project_q,
                preferred_element_type=jnp.float32,
            ).astype(jnp.bfloat16),
            "tensor",
            scatter_dimension=0,
            tiled=True,
        ).astype(jnp.float32)
        * clip_slope(own_inputs, clip_scales[0])
        + grad_sum_first
    )
    down_part, up_part, up_bias_part, merge_part, project_part, bias_part = lax.psum(
        (down_part, up_part, up_bias_part, merge_part, project_part, bias_part), "dp"
    )
    project_grad = project_part * clip_slope(project_weight.astype(jnp.float32), project_scale)
    merge_grad = merge_part * clip_slope(merge_weight.astype(jnp.float32), weight_scales[3])
    up_grad = up_part * clip_slope(up_weight.astype(jnp.float32), weight_scales[4])
    down_grad = down_part * clip_slope(down_weight.astype(jnp.float32), weight_scales[5])
    gain_grad, shift_grad, merge_bias_grad, down_bias_grad = lax.psum(
        (
            jnp.stack([gain_first, gain_second]),
            jnp.stack([shift_first, shift_second]),
            merge_bias_part,
            down_bias_part,
        ),
        ("dp", "tensor"),
    )
    peaks = lax.pmax(
        (jnp.max(jnp.abs(own_inputs)), jnp.max(jnp.abs(normed)), jnp.max(jnp.abs(active))),
        ("dp", "tensor"),
    )
    new_scales = DECAY * clip_scales + (1.0 - DECAY) * jnp.stack(peaks)
    return (
        output,
        input_grad,
        project_grad,
        merge_grad,
        up_grad,
        down_grad,
        bias_part,
        merge_bias_grad,
        up_bias_part,
        down_bias_grad,
        gain_grad,
        shift_grad,
        new_scales,
    )


def solution(mesh):
    return jax.shard_map(
        local,
        mesh=mesh,
        in_specs=(
            P(("dp", "tensor"), None),
            P("dp"),
            P(None, None, "tensor"),
            P("tensor", None),
            P(None, "tensor"),
            P("tensor", None),
            P(None, "tensor"),
            P(),
            P("tensor"),
            P(),
            P(),
            P(),
            P(),
            P(("dp", "tensor"), None),
        ),
        out_specs=(
            P(("dp", "tensor"), None),
            P(("dp", "tensor"), None),
            P(None, None, "tensor"),
            P("tensor", None),
            P(None, "tensor"),
            P("tensor", None),
            P(None, "tensor"),
            P(),
            P("tensor"),
            P(),
            P(),
            P(),
            P(),
        ),
        check_vma=False,
    )
```

profile of v0, /device:TPU:1, one launch (start us, length us, event | category | flops | bytes accessed | tf_op | source)
XLA Modules:
  0.0 710.5 jit_solution(12613855432812613204)
XLA Ops:
  9.9 2.3 abs_reduce_fusion.5
  12.2 2.6 abs_reduce_fusion.1
  15.7 4.0 stack.70
  19.7 2.5 pmax.28
  23.8 4.6 fusion.99
  39.3 2.6 squeeze.142
  43.8 17.7 %while.36 = (s32[]{:T(128)}, bf16[2,512,6,64]{1,3,2,0:T(8,128)(2,1)S(1)}, f32[2,6,512,1]{2,1,3,0:T(8,128)S(1)}, bf16[2,512,6,64]{1,3,2,0:T(8,128)(2,1)}, s32[2,4...) while((s32[]{:T(128)}, ...), condition=%wide.region_10.12_spmd, body=%wide.region_7.11_spmd.sunk | while | flops 420492800 | bytes 22015216 | solution.py:146
  44.5 2.6 fusion.163
  49.9 2.8 fusion.165
  53.3 2.6 fusion.163
  58.7 2.8 fusion.165
  63.4 3.4 fusion.105
  67.5 25.1 %all-reduce.7.cloned.1.call-done = f32[1024,768]{1,0:T(8,128)} async-done(((f32[1024,768]{1,0:T(8,128)}), f32[1024,768]{1,0:T(8,128)}) %all-reduce.7.cloned.1.call-update) | async-done | bytes 3145744 | tf_op jit(solution)/shard_map/psum | solution.py:150
  92.6 2.5 fusion.101
  96.3 2.5 multiply_add_fusion
  98.8 18.1 %abs_reduce_fusion = (f32[]{:T(128)}, f32[1024,1536]{1,0:T(8,128)S(1)}, f32[1024,1536]{1,0:T(8,128)S(1)}) fusion(f32[1536]{0:T(1024)S(1)} %copy-done.40, bf16[768,1536]{1,0:T(8,128)(2,1)S(1)} %copy-done.9, f32[]{:T(128)} %bitcast.42, f32[1024,768]{1,0:T(8,128)S(1)} %get-tuple-element.578, f32[]{:T(128)} %bitcast.41), kind=kOutput, calls=%fused_computation.97 | convolution fusion | flops 2528378880 | bytes 18094092 | tf_op jit(solution)/shard_map/dot_general | solution.py:158
  116.9 2.6 multiply_convert_fusion.1
  123.4 5.0 fusion.108
  128.5 12.1 %reduce-scatter.4.cloned.1.call-done = f32[512,768]{1,0:T(8,128)} async-done(((f32[1024,768]{1,0:T(8,128)}), f32[512,768]{1,0:T(8,128)}) %reduce-scatter.4.cloned.1.call-update) | async-done | bytes 1572880 | tf_op jit(solution)/shard_map/reduce_scatter | solution.py:161
  140.7 2.1 fusion.114
  147.8 10.9 %all-gather.6.cloned.1.call-done = bf16[1024,768]{1,0:T(8,128)(2,1)} async-done(((bf16[512,768]{1,0:T(8,128)(2,1)}), bf16[1024,768]{1,0:T(8,128)(2,1)}) %all-gather.6.cloned.1.call-update) | async-done | bytes 1572880 | tf_op jit(solution)/shard_map/all_gather | solution.py:180
  158.7 12.1 %convert_reduce_fusion = (f32[1536]{0:T(1024)S(1)}, bf16[1024,1536]{1,0:T(8,128)(2,1)S(1)}) fusion(f32[1024,1536]{1,0:T(8,128)} %copy-done.16, f32[]{:T(128)} %bitcast.40, bf16[1024,768]{1,0:T(8,128)(2,1)} %all-gather.6.cloned.1.call-done, bf16[1536,768]{1,0:T(8,128)(2,1)} %param.29, f32[]{:T(128)} %bitcast.43, f32[1024,1536]{1,0:T(8,128)} %copy-done.17, ...), kind=kOutput, calls=%fused_computation.98 | convolution fusion | flops 2455239168 | bytes 19673096 | tf_op jit(solution)/shard_map/td,fd->tf/dot_general | solution.py:182
  172.6 4.9 fusion.106
  177.6 12.1 %reduce-scatter.6.cloned.1.call-done = f32[512,768]{1,0:T(8,128)} async-done(((f32[1024,768]{1,0:T(8,128)}), f32[512,768]{1,0:T(8,128)}) %reduce-scatter.6.cloned.1.call-update) | async-done | bytes 1572880 | tf_op jit(solution)/shard_map/reduce_scatter | solution.py:189
  189.7 5.0 multiply_reduce_fusion.2
  197.3 11.1 %all-gather.8.cloned.1.call-done = bf16[1024,768]{1,0:T(8,128)(2,1)} async-done(((bf16[512,768]{1,0:T(8,128)(2,1)}), bf16[1024,768]{1,0:T(8,128)(2,1)}) %all-gather.8.cloned.1.call-update) | async-done | bytes 1572880 | tf_op jit(solution)/shard_map/all_gather | solution.py:207
  208.4 3.1 convolution_convert_fusion
  216.2 33.9 %while.37 = (s32[]{:T(128)}, bf16[2,512,6,64]{1,3,2,0:T(8,128)(2,1)}, bf16[2,512,6,64]{1,3,2,0:T(8,128)(2,1)}, bf16[2,512,6,64]{1,3,2,0:T(8,128)(2,1)}, bf16[2,5...) while((s32[]{:T(128)}, ...), condition=%wide.region_24.26_spmd, body=%wide.region_22.25_spmd.sunk | while | flops 1031157248 | bytes 59734336 | solution.py:212
  217.1 2.6 fusion.178
  221.0 3.5 fusion.181
  224.6 3.3 multiply_reduce_fusion.7
  234.0 2.6 fusion.178
  237.9 3.5 fusion.181
  241.4 3.3 multiply_reduce_fusion.7
  255.5 2.9 stack_reshape.12
  261.4 5.7 bitcast_convert_fusion
  267.2 7.4 %fusion.121 = f32[1536,768]{1,0:T(8,128)} fusion(bf16[1024,1536]{1,0:T(8,128)(2,1)} %copy-done.23, bf16[1024,768]{1,0:T(8,128)(2,1)} %all-gather.6.cloned.1.call-done), kind=kOutput, calls=%fused_computation.220 | convolution fusion | flops 2415919104 | bytes 9437184 | tf_op jit(solution)/shard_map/tf,td->fd/dot_general | solution.py:181
  274.6 5.1 fusion.109
  282.2 4.7 fusion.97
  287.7 46.3 %all-reduce = (f32[768]{0:T(1024)}, f32[768]{0:T(1024)}, f32[2,768]{1,0:T(2,128)}, f32[2,768]{1,0:T(2,128)}) all-reduce(f32[768]{0:T(1024)S(1)} %get-tuple-element.573, f32[768]{0:T(1024)S(1)} %copy-done.39, f32[2,768]{1,0:T(2,128)S(1)} %pad_maximum_fusion.3, ...), channel_id=1, replica_groups=mesh['dp'=16,'tensor'=2] {'dp','tensor'}, use_global_device_ids=true, to_apply=%region_34.36 | all-reduce | flops 4608 | bytes 36864 | tf_op jit(solution)/shard_map/psum | solution.py:262
  334.4 63.4 %all-reduce.2 = (f32[2,384]{1,0:T(2,128)}, f32[1536]{0:T(1024)}) all-reduce(f32[2,384]{1,0:T(2,128)S(1)} %pad_maximum_fusion.5, f32[1536]{0:T(1024)S(1)} %get-tuple-element.605), channel_id=1, replica_groups=mesh['dp'=16,'tensor'=2] {'dp'}, use_global_device_ids=true, to_apply=%region_32.34 | all-reduce | flops 2304 | bytes 18432 | tf_op jit(solution)/shard_map/psum | solution.py:255
  397.8 4.3 fusion.91
  402.1 55.5 %all-reduce.1 = (f32[1]{0:T(128)}, f32[1]{0:T(128)}, f32[1]{0:T(128)}) all-reduce(f32[1]{0:T(128)} %bitcast.48, f32[1]{0:T(128)} %bitcast.47, f32[1]{0:T(128)} %bitcast.46), channel_id=1, replica_groups=mesh['dp'=16,'tensor'=2] {'dp','tensor'}, use_global_device_ids=true, to_apply=%region_50.52 | all-reduce | flops 3 | bytes 24 | tf_op jit(solution)/shard_map/pmax | solution.py:271
  457.6 2.5 fusion.102
  460.0 229.0 %all-reduce.9.cloned.1.call-done = (f32[768,3,384]{2,0,1:T(8,128)}, f32[384,768]{1,0:T(8,128)}, f32[768,1536]{1,0:T(8,128)}, f32[1536,768]{1,0:T(8,128)}) async-done(((f32[768,3,384]{2,0,1:T(8,128)}, f32[384,768]{1,0:T(8,128)}, f32[768,1536]{1,0:T(8,128)}, f32[1536,768]{1,0:T(8,128)}), (f32[768,3,384]{2,0,1:T(8,128)}, f32[384,768]{1,0:T(8,128)}, f32[768,1536]{1,0:T(8,128)}, ...) | async-done | bytes 14155792 | tf_op jit(solution)/shard_map/psum | solution.py:255
  689.0 4.7 subtract_multiply_fusion.2
  695.8 3.8 subtract_multiply_fusion.1
  699.7 3.8 subtract_multiply_fusion
  (243 shorter events, 75.1 us)
Async XLA Ops:
  7.2 16.6 %all-gather.4.cloned.1.call-start = ((), (), s32[]{:S(2)}) async-start(), calls=%async_computation.3 | async-start | bytes 2359296 | tf_op jit(solution)/shard_map/all_gather | solution.py:115
  7.9 84.7 %all-reduce.7.cloned.1.call-start = ((), (), s32[]{:S(2)}) async-start(), calls=%async_computation.4 | async-start | bytes 6291456 | tf_op jit(solution)/shard_map/psum | solution.py:150
  8.0 6.8 copy-start.8
  9.9 12.3 %copy-start.50 = (s32[8]{0:T(128)S(1)}, s32[8]{0:T(128)}, u32[]{:S(2)}) copy-start(s32[8]{0:T(128)} %param.25) | copy-start | bytes 100
  9.9 12.4 %copy-start.48 = (f32[2,384]{1,0:T(2,128)S(1)}, f32[2,384]{1,0:T(2,128)}, u32[]{:S(2)}) copy-start(f32[2,384]{1,0:T(2,128)} %param.30) | copy-start | bytes 9220
  9.9 12.5 %copy-start.43 = (f32[3]{0:T(128)S(1)}, f32[3]{0:T(128)}, u32[]{:S(2)}) copy-start(f32[3]{0:T(128)} %param.36) | copy-start | bytes 40
  9.9 13.9 %copy-start.14 = (bf16[768,3,384]{2,0,1:T(8,128)(2,1)S(1)}, bf16[768,3,384]{2,0,1:T(8,128)(2,1)}, u32[]{:S(2)}) copy-start(bf16[768,3,384]{2,0,1:T(8,128)(2,1)} %param.26) | copy-start | bytes 5308420
  23.1 5.3 copy-start.41
  33.4 4.3 copy-start.18
  66.8 25.9 %copy-start.1 = (bf16[1024,768]{1,0:T(8,128)(2,1)S(1)}, bf16[1024,768]{1,0:T(8,128)(2,1)}, u32[]{:S(2)}) copy-start(bf16[1024,768]{1,0:T(8,128)(2,1)} %all-gather.4.cloned.1.call-done) | copy-start | bytes 4718596
  66.8 25.9 %copy-start.36 = (f32[768]{0:T(1024)S(1)}, f32[768]{0:T(1024)}, u32[]{:S(2)}) copy-start(f32[768]{0:T(1024)} %param.31) | copy-start | bytes 9220
  66.8 73.9 %reduce-scatter.4.cloned.1.call-start = ((), (), s32[]{:S(2)}) async-start(), calls=%async_computation.5 | async-start | bytes 4718592 | tf_op jit(solution)/shard_map/reduce_scatter | solution.py:161
  92.6 2.8 copy-start
  96.3 2.5 copy-start.9
  96.3 2.5 copy-start.40
  98.8 18.1 %copy-start.5 = (f32[1024,768]{1,0:T(8,128)}, f32[1024,768]{1,0:T(8,128)S(1)}, u32[]{:S(2)}) copy-start(f32[1024,768]{1,0:T(8,128)S(1)} %get-tuple-element.578) | copy-start | bytes 9437188
  116.9 3.0 copy-start.16
  116.9 4.9 copy-start.17
  116.9 6.5 copy-start.12
  128.4 12.2 %copy-start.47 = (f32[768]{0:T(1024)S(1)}, f32[768]{0:T(1024)}, u32[]{:S(2)}) copy-start(f32[768]{0:T(1024)} %param.33) | copy-start | bytes 9220
  128.5 30.2 %all-gather.6.cloned.1.call-start = ((), (), s32[]{:S(2)}) async-start(), calls=%async_computation.6 | async-start | bytes 2359296 | tf_op jit(solution)/shard_map/all_gather | solution.py:180
  128.5 14.6 %copy-start.24 = (bf16[512,768]{1,0:T(8,128)(2,1)S(1)}, bf16[512,768]{1,0:T(8,128)(2,1)}, u32[]{:S(2)}) copy-start(bf16[512,768]{1,0:T(8,128)(2,1)} %param.37) | copy-start | bytes 2359300
  147.6 42.1 %reduce-scatter.6.cloned.1.call-start = ((), (), s32[]{:S(2)}) async-start(), calls=%async_computation.7 | async-start | bytes 4718592 | tf_op jit(solution)/shard_map/reduce_scatter | solution.py:189
  158.7 13.9 %copy-start.10 = (bf16[768,1536]{1,0:T(8,128)(2,1)S(1)}, bf16[768,1536]{1,0:T(8,128)(2,1)}, u32[]{:S(2)}) copy-start(bf16[768,1536]{1,0:T(8,128)(2,1)} %param.28) | copy-start | bytes 7077892
  177.5 30.9 %all-gather.8.cloned.1.call-start = ((), (), s32[]{:S(2)}) async-start(), calls=%async_computation.8 | async-start | bytes 2359296 | tf_op jit(solution)/shard_map/all_gather | solution.py:207
  189.7 5.0 copy-start.7
  194.7 13.7 %copy-start.27 = (bf16[384,768]{1,0:T(8,128)(2,1)S(1)}, bf16[384,768]{1,0:T(8,128)(2,1)}, u32[]{:S(2)}) copy-start(bf16[384,768]{1,0:T(8,128)(2,1)} %param.27) | copy-start | bytes 1769476
  197.2 200.6 %reduce-scatter.8.cloned.1.call-start = ((), (), s32[]{:S(2)}) async-start(), calls=%async_computation.9 | async-start | bytes 2359296 | tf_op jit(solution)/shard_map/reduce_scatter | solution.py:241
  250.1 3.8 copy-start.22
  252.7 7.0 copy-start.19
  258.5 2.9 copy-start.42
  261.4 5.7 copy-start.34
  267.2 421.8 %all-reduce.9.cloned.1.call-start = ((), (), s32[]{:S(2)}) async-start(), calls=%async_computation.10 | async-start | bytes 28311552 | tf_op jit(solution)/shard_map/psum | solution.py:255
  267.2 7.4 %copy-start.6 = (f32[1024,768]{1,0:T(8,128)S(1)}, f32[1024,768]{1,0:T(8,128)}, u32[]{:S(2)}) copy-start(f32[1024,768]{1,0:T(8,128)} %copy-done.5) | copy-start | bytes 9437188
  267.2 7.4 %copy-start.52 = (bf16[1024,1536]{1,0:T(8,128)(2,1)S(1)}, bf16[1024,1536]{1,0:T(8,128)(2,1)}, u32[]{:S(2)}) copy-start(bf16[1024,1536]{1,0:T(8,128)(2,1)} %copy-done.51) | copy-start | bytes 9437188
  274.6 5.1 copy-start.31
  274.6 5.1 copy-start.49
  279.8 2.5 copy-start.35
  287.0 110.8 %copy-start.4 = (f32[512,768]{1,0:T(8,128)S(1)}, f32[512,768]{1,0:T(8,128)}, u32[]{:S(2)}) copy-start(f32[512,768]{1,0:T(8,128)} %copy-done.3) | copy-start | bytes 4718596
  334.0 123.5 %copy-start.44 = (f32[3]{0:T(128)S(1)}, f32[3]{0:T(128)}, u32[]{:S(2)}) copy-start(f32[3]{0:T(128)} %param.36) | copy-start | bytes 40
  334.4 354.6 %copy-start.15 = (bf16[768,3,384]{2,0,1:T(8,128)(2,1)S(1)}, bf16[768,3,384]{2,0,1:T(8,128)(2,1)}, u32[]{:S(2)}) copy-start(bf16[768,3,384]{2,0,1:T(8,128)(2,1)} %param.26) | copy-start | bytes 5308420
  689.0 6.8 slice-start.2
  689.0 4.7 copy-start.28
  689.0 4.7 copy-start.29
  689.0 6.8 slice-start.3
  695.8 3.9 slice-start
  695.8 3.9 copy-start.13
  695.8 3.9 slice-start.1
  (19 other events, 25.8 us)
Sparse Core Ops, SparseCore 0:
  9.6 12.2 all-gather.3
  66.9 25.6 all-reduce.6
  128.6 12.0 reduce-scatter.3
  147.7 10.9 all-gather.5
  177.6 12.0 reduce-scatter.5
  197.3 10.9 all-gather.7
  267.3 10.2 reduce-scatter.7
  287.1 401.8 all-reduce.8
where the time goes:
time: 717 us; the launch traced here: 711 us
  waiting for transfers between devices  301 us (42%)
  blocking collectives  168 us (23%)
  matrix products  104 us (15%)
  other arithmetic  70.5 us (10%)
  local copies, waits for them, and re-layouts  50.6 us (7%)
  between operations  14.9 us (2%)
    psum x1, waiting for transfers between devices, local(): lax.psum((down_part, up_part, up_bias_part, merge_part, project_part, bia...  229 us
    psum x1, blocking collectives, local(): lax.psum((down_part, up_part, up_bias_part, merge_part, project_part, bia...  63.4 us
    pmax x1, blocking collectives, local(): lax.pmax((jnp.max(jnp.abs(own_inputs)), jnp.max(jnp.abs(normed)), jnp.max...  55.5 us
    psum x1, blocking collectives, local(): lax.psum((jnp.stack([gain_first, gain_second]), jnp.stack([shift_first, s...  46.3 us
    psum x1, waiting for transfers between devices, local(): lax.psum(jnp.dot(context, merge_q, preferred_element_type=jnp.float32), '...  25.1 us
    dot_general x1, matrix products, local(): jnp.dot(normed_q, up_q, preferred_element_type=jnp.float32) + up_bias  18.1 us
  transfers between devices with their start and end apart: 8, of which 6 were waited for; matrix products, arithmetic and copies ran while one was open for 6% of the time, Pallas kernels for 0%

commit v1 on v0

v1 whole, which is shorter than its diff:
```python
from functools import partial

import jax
import jax.numpy as jnp
from jax import lax
from jax.experimental import pallas as pl
from jax.experimental.pallas import tpu as pltpu
from jax.sharding import PartitionSpec as P

HEAD = 64
LONG = 512
SHORT = 128
EPSILON = 1e-12
DECAY = 0.9
F32 = jnp.float32
BF16 = jnp.bfloat16
VMEM = pl.BlockSpec(memory_space=pltpu.VMEM)
SMEM = pl.BlockSpec(memory_space=pltpu.SMEM)
LANES = 384
TILE = 64


def dot(a, b, ca, cb):
    return lax.dot_general(a, b, (((ca,), (cb,)), ((), ())), preferred_element_type=F32)


def shaped(shape, dtype):
    return jax.ShapeDtypeStruct(shape, dtype)


def call(body, out_shape, ins, flops, scratch=(), grid_spec=None, in_specs=None, out_specs=None):
    nbytes = sum(a.size * a.dtype.itemsize for a in ins)
    nbytes += sum(o.size * o.dtype.itemsize for o in jax.tree.leaves(out_shape))
    params = dict(
        out_shape=out_shape,
        compiler_params=pltpu.CompilerParams(vmem_limit_bytes=56 << 20),
        cost_estimate=pl.CostEstimate(flops=int(flops), bytes_accessed=nbytes, transcendentals=0),
    )
    if grid_spec is not None:
        return pl.pallas_call(body, grid_spec=grid_spec, **params)(*ins)
    return pl.pallas_call(
        body, in_specs=in_specs, out_specs=out_specs, scratch_shapes=list(scratch), **params
    )(*ins)


def peaks_body(project, merge, up, down, qv_bias, up_bias, pack):
    step = pl.program_id(0)

    @pl.when(step == 0)
    def _():
        pack[...] = jnp.zeros_like(pack)
        pack[0:1, :] = up_bias[...]
        pack[1:3, 0:LANES] = qv_bias[...]

    def peak(value):
        top = jnp.max(jnp.abs(value.astype(F32)), axis=0, keepdims=True)
        return jnp.max(top, axis=1, keepdims=True)

    parts = [peak(project[0]), peak(project[1]), peak(project[2])]
    parts += [peak(merge[...]), peak(up[...]), peak(down[...])]
    for row, part in enumerate(parts):
        at = slice(8 + row, 9 + row)
        pack[at, :] = jnp.maximum(pack[at, :], part)


def scale_row(own, other, row, width):
    at = slice(8 + row, 9 + row)
    return 0.5 * jnp.maximum(own[at, 0:width], other[at, 0:width])


def clip_tile(value, scale):
    return (scale * jnp.tanh(value.astype(F32) / scale)).astype(BF16)


def clip_project_body(own, other, project, out):
    for part in range(3):
        scale = scale_row(own, other, part, LANES)
        out[part] = clip_tile(project[part], scale)


def clip_rest_body(own, other, merge, up, down, merge_q, up_q, down_q):
    for row, (src, dst) in enumerate(((merge, merge_q), (up, up_q), (down, down_q))):
        dst[...] = clip_tile(src[...], scale_row(own, other, 3 + row, src.shape[1]))


def key_bias(lengths, first):
    key = lax.broadcasted_iota(jnp.int32, (LONG, 1), 0)
    query = lax.broadcasted_iota(jnp.int32, (1, LONG), 1)
    single = lengths[first] > SHORT
    limit = jnp.full((LONG, 1), lengths[first], jnp.int32)
    for slot in range(1, LONG // SHORT):
        own = jnp.where(single, lengths[first], slot * SHORT + lengths[first + slot])
        limit = jnp.where(key >= slot * SHORT, own, limit)
    key_row = jnp.where(single, 0, key // SHORT)
    query_row = jnp.where(single, 0, query // SHORT)
    key_row = jnp.where(key < limit, key_row, -1)
    return jnp.where(key_row == query_row, 0.0, -1e30).astype(F32)


def qkv_into(xq, weight, bias_pack, q_ref, k_ref, v_ref):
    for part, ref in enumerate((q_ref, k_ref, v_ref)):
        value = dot(xq, weight[part], 1, 0)
        if part == 0:
            value = value + bias_pack[1:2, 0:LANES]
        if part == 2:
            value = value + bias_pack[2:3, 0:LANES]
        value = value.astype(BF16)
        if part == 0:
            value = value * jnp.asarray(0.125, BF16)
        ref[...] = value.T


def attend(lengths, first, q_ref, k_ref, v_ref, c_ref, lse_ref, bias_ref):
    bias_ref[...] = key_bias(lengths, first)

    def head(index, carry):
        at = pl.ds(pl.multiple_of(index * HEAD, HEAD), HEAD)
        scores = dot(k_ref[at, :], q_ref[at, :], 0, 0) + bias_ref[...]
        top = jnp.max(scores, axis=0, keepdims=True)
        prob = jnp.exp(scores - top)
        total = jnp.sum(prob, axis=0, keepdims=True)
        mixed = dot(v_ref[at, :], prob.astype(BF16), 1, 0)
        c_ref[at, :] = (mixed * (1.0 / total)).astype(BF16)
        lse_ref[pl.ds(index, 1), :] = top + jnp.log(total)
        return carry

    lax.fori_loop(0, q_ref.shape[0] // HEAD, head, 0)


def forward_first_body(
    ids, lengths, clips, inputs, weight, pack, xq, q_ref, k_ref, v_ref, c_ref, lse_ref, bias_ref
):
    scale = clips[0]
    xq[...] = (scale * jnp.tanh(inputs[...].astype(F32) / scale)).astype(BF16)
    qkv_into(xq[...], weight, pack, q_ref, k_ref, v_ref)
    attend(lengths, ids[2], q_ref, k_ref, v_ref, c_ref, lse_ref, bias_ref)


def forward_second_body(
    ids, lengths, xq, weight, pack, q_ref, k_ref, v_ref, c_ref, lse_ref, bias_ref
):
    qkv_into(xq[...], weight, pack, q_ref, k_ref, v_ref)
    attend(lengths, ids[2], q_ref, k_ref, v_ref, c_ref, lse_ref, bias_ref)


def backward_heads_body(
    ids,
    lengths,
    which,
    xq,
    q_ref,
    k_ref,
    v_ref,
    c_ref,
    lse_ref,
    merge_q,
    grad_branch,
    chunk,
    d_ref,
    qv_row,
    bias_ref,
    g_ref,
    x_t,
):
    rel = ids[which[0]]
    blocks = chunk.shape[0]
    bias_ref[...] = key_bias(lengths, ids[2])
    x_t[...] = xq[...].T
    g_ref[...] = dot(merge_q[...], grad_branch[...], 1, 1).astype(BF16)
    width = q_ref.shape[0]

    def head(index, carry):
        at = pl.ds(pl.multiple_of(index * HEAD, HEAD), HEAD)
        q, k, v, g = q_ref[at, :], k_ref[at, :], v_ref[at, :], g_ref[at, :]
        scores = dot(k, q, 0, 0) + bias_ref[...]
        prob = jnp.exp(scores - lse_ref[pl.ds(index, 1), :])
        grad_prob = dot(v, g, 0, 0)
        inner = jnp.sum(g.astype(F32) * c_ref[at, :].astype(F32), axis=0, keepdims=True)
        grad_score = (prob * (grad_prob - inner)).astype(BF16)
        d_ref[2, at, :] = dot(g, prob.astype(BF16), 1, 1).astype(BF16)
        d_ref[0, at, :] = (dot(k, grad_score, 1, 0) * 0.125).astype(BF16)
        d_ref[1, at, :] = dot(q, grad_score, 1, 1).astype(BF16)
        return carry

    lax.fori_loop(0, width // HEAD, head, 0)
    rows = x_t.shape[0] // blocks
    base = 3 * rows
    for part in range(3):
        grad = dot(x_t[...], d_ref[part], 1, 1)
        for block in range(blocks):
            piece = grad[block * rows : (block + 1) * rows, :]
            chunk[block ^ rel, part * rows : (part + 1) * rows, :] = piece.astype(BF16)
    ones = jnp.ones((8, xq.shape[0]), BF16)
    qv_row[:, 0:LANES] = dot(ones, d_ref[0], 1, 1)
    qv_row[:, LANES : 2 * LANES] = dot(ones, d_ref[2], 1, 1)
    grad = dot(c_ref[...], grad_branch[...], 1, 0)
    step = width // blocks
    for block in range(blocks):
        piece = grad[block * step : (block + 1) * step, :]
        piece = jnp.concatenate([piece[:, :LANES], piece[:, LANES:]], axis=0)
        chunk[block ^ rel, base : base + 2 * step, :] = piece.astype(BF16)


ERF_P = 0.3275911 * 0.7071067811865476
ERF_A = (0.254829592, -0.284496736, 1.421413741, -1.453152027, 1.061405429)


def gelu_parts(hidden, scale):
    bell = jnp.exp(-0.5 * hidden * hidden)
    t = 1.0 / (1.0 + ERF_P * jnp.abs(hidden))
    poly = ERF_A[4]
    for coefficient in (ERF_A[3], ERF_A[2], ERF_A[1], ERF_A[0]):
        poly = poly * t + coefficient
    tail = 0.5 * poly * t * bell
    area = jnp.where(hidden >= 0.0, 1.0 - tail, tail)
    active = hidden * area
    slope = area + hidden * bell * 0.3989422804014327
    bent = jnp.tanh(active / scale)
    return (scale * bent).astype(BF16), ((1.0 - bent * bent) * slope).astype(BF16), active


def fold(value, op):
    rows, lanes = value.shape
    return op(value.reshape(rows // 8, 8, lanes), axis=0)


def middle_body(
    clips,
    c_own,
    c_other,
    merge_own,
    merge_other,
    inputs,
    up_own,
    up_other,
    down_own,
    down_other,
    pack_own,
    pack_other,
    vectors,
    cotangent,
    unit_out,
    inverse_out,
    normed_q,
    active_own,
    active_other,
    factor_own,
    factor_other,
    output,
    grad_sum,
    grad_feed,
    sums,
    work,
    hidden_ref,
    tops,
    sum_ref,
):
    total = inputs.shape[0]
    work[...] = dot(c_own[...], merge_own[...], 0, 0) + dot(c_other[...], merge_other[...], 0, 0)
    tops[...] = jnp.zeros_like(tops)
    sum_ref[...] = jnp.zeros_like(sum_ref)
    clip_first, clip_second = clips[1], clips[2]

    def first_norm(index, carry):
        at = pl.ds(pl.multiple_of(index * TILE, TILE), TILE)
        rows = inputs[at, :].astype(F32)
        value = rows + work[at, :] + vectors[0:1, :]
        mean = jnp.mean(value, axis=-1, keepdims=True)
        centred = value - mean
        inverse = lax.rsqrt(jnp.mean(centred * centred, axis=-1, keepdims=True) + EPSILON)
        unit = centred * inverse
        normed = unit * vectors[2:3, :] + vectors[4:5, :]
        unit_out[at, :] = unit
        inverse_out[at, :] = jnp.broadcast_to(inverse, (TILE, 128))
        normed_q[at, :] = (clip_first * jnp.tanh(normed / clip_first)).astype(BF16)
        tops[0] = jnp.maximum(tops[0], fold(jnp.abs(rows), jnp.max))
        tops[1] = jnp.maximum(tops[1], fold(jnp.abs(normed), jnp.max))
        work[at, :] = normed
        return carry

    lax.fori_loop(0, total // TILE, first_norm, 0)
    span = hidden_ref.shape[1]
    for weight, pack, active_ref, factor_ref in (
        (up_own, pack_own, active_own, factor_own),
        (up_other, pack_other, active_other, factor_other),
    ):

        def columns(index, carry):
            cols = pl.ds(pl.multiple_of(index * span, span), span)
            hidden_ref[...] = dot(normed_q[...], weight[:, cols], 1, 0)
            bias = pack[0:1, cols]

            def rows(row, carry):
                at = pl.ds(pl.multiple_of(row * TILE, TILE), TILE)
                clipped, factor, active = gelu_parts(hidden_ref[at, :] + bias, clip_second)
                active_ref[at, cols] = clipped
                factor_ref[at, cols] = factor
                tops[2, :, 0:span] = jnp.maximum(tops[2, :, 0:span], fold(jnp.abs(active), jnp.max))
                return carry

            lax.fori_loop(0, total // TILE, rows, 0)
            return carry

        lax.fori_loop(0, weight.shape[1] // span, columns, 0)
    work[...] += dot(active_own[...], down_own[...], 1, 0) + dot(
        active_other[...], down_other[...], 1, 0
    )

    def second_norm(index, carry):
        at = pl.ds(pl.multiple_of(index * TILE, TILE), TILE)
        value = work[at, :] + vectors[1:2, :]
        mean = jnp.mean(value, axis=-1, keepdims=True)
        centred = value - mean
        inverse = lax.rsqrt(jnp.mean(centred * centred, axis=-1, keepdims=True) + EPSILON)
        unit = centred * inverse
        output[at, :] = (unit * vectors[3:4, :] + vectors[5:6, :]).astype(BF16)
        upstream = cotangent[at, :].astype(F32)
        scaled = upstream * vectors[3:4, :]
        grad = inverse * (
            scaled
            - jnp.mean(scaled, axis=-1, keepdims=True)
            - unit * jnp.mean(scaled * unit, axis=-1, keepdims=True)
        )
        grad_sum[at, :] = grad
        grad_feed[at, :] = grad.astype(BF16)
        sum_ref[0] += fold(upstream * unit, jnp.sum)
        sum_ref[1] += fold(upstream, jnp.sum)
        sum_ref[2] += fold(grad, jnp.sum)
        return carry

    lax.fori_loop(0, total // TILE, second_norm, 0)
    for row in range(3):
        sums[row : row + 1, :] = jnp.sum(sum_ref[row], axis=0, keepdims=True)
    for row in range(3):
        top = jnp.max(jnp.max(tops[row], axis=0, keepdims=True), axis=1, keepdims=True)
        sums[3 + row : 4 + row, :] = jnp.broadcast_to(top, (1, sums.shape[1]))
    sums[6:8, :] = jnp.zeros((2, sums.shape[1]), F32)


def down_grad_body(ids, which, active, grad_feed, chunk):
    rel = ids[which[0]]
    blocks = chunk.shape[0]
    rows = active.shape[1] // blocks
    per = blocks // 4

    def tile(index, carry):
        cols = pl.ds(pl.multiple_of(index * per * rows, per * rows), per * rows)
        grad = dot(active[:, cols], grad_feed[...], 0, 0)
        for block in range(per):
            piece = grad[block * rows : (block + 1) * rows, :].astype(BF16)
            to = (index * per + block) ^ rel
            chunk[to, 0:rows, :] = piece[:, :LANES]
            chunk[to, rows : 2 * rows, :] = piece[:, LANES:]
        return carry

    lax.fori_loop(0, 4, tile, 0)


def up_grad_body(
    ids, which, grad_feed, down, up, factor, normed_q, before, chunk, bias_row, grad_normed, g_ref
):
    rel = ids[which[0]]
    blocks = chunk.shape[0]
    span = 512

    def columns(index, carry):
        cols = pl.ds(pl.multiple_of(index * span, span), span)
        grad = dot(grad_feed[...], down[cols, :], 1, 1) * factor[:, cols].astype(F32)
        grad = grad.astype(BF16)
        g_ref[:, cols] = grad
        bias_row[0:1, cols] = jnp.sum(grad.astype(F32), axis=0, keepdims=True)
        return carry

    lax.fori_loop(0, g_ref.shape[1] // span, columns, 0)
    rows = normed_q.shape[1] // blocks
    per = 8

    def tile(index, carry):
        cols = pl.ds(pl.multiple_of(index * per * rows, per * rows), per * rows)
        grad = dot(normed_q[:, cols], g_ref[...], 0, 0)
        for block in range(per):
            to = (index * per + block) ^ rel
            for part in range(grad.shape[1] // LANES):
                piece = grad[block * rows : (block + 1) * rows, part * LANES : (part + 1) * LANES]
                chunk[to, part * rows : (part + 1) * rows, :] = piece.astype(BF16)
        return carry

    lax.fori_loop(0, blocks // per, tile, 0)
    result = dot(g_ref[...], up[...], 1, 1)
    if before is not None:
        result = result + before[...]
    grad_normed[...] = result


def up_grad_first_body(
    ids, which, grad_feed, down, up, factor, normed_q, chunk, bias_row, grad_normed, g_ref
):
    up_grad_body(
        ids, which, grad_feed, down, up, factor, normed_q, None, chunk, bias_row, grad_normed, g_ref
    )


def first_norm_back_body(
    clips,
    grad_normed,
    grad_sum,
    unit_ref,
    inverse_ref,
    vectors,
    sums,
    bias_other,
    bias_own,
    grad_first,
    grad_branch,
    pack_other,
    pack_own,
    sum_ref,
):
    clip_first = clips[1]
    sum_ref[...] = jnp.zeros_like(sum_ref)

    def rows(index, carry):
        at = pl.ds(pl.multiple_of(index * TILE, TILE), TILE)
        unit = unit_ref[at, :]
        bent = jnp.tanh((unit * vectors[2:3, :] + vectors[4:5, :]) / clip_first)
        grad = grad_normed[at, :] * (1.0 - bent * bent) + grad_sum[at, :]
        scaled = grad * vectors[2:3, :]
        back = inverse_ref[at, 0:1] * (
            scaled
            - jnp.mean(scaled, axis=-1, keepdims=True)
            - unit * jnp.mean(scaled * unit, axis=-1, keepdims=True)
        )
        grad_first[at, :] = back
        grad_branch[at, :] = back.astype(BF16)
        sum_ref[0] += fold(grad * unit, jnp.sum)
        sum_ref[1] += fold(grad, jnp.sum)
        sum_ref[2] += fold(back, jnp.sum)
        return carry

    lax.fori_loop(0, unit_ref.shape[0] // TILE, rows, 0)
    width = unit_ref.shape[1]
    for pack, bias in ((pack_other, bias_other), (pack_own, bias_own)):
        pack[...] = jnp.zeros_like(pack)
        for row, source in ((0, 0), (2, 1), (4, 2)):
            pack[row : row + 1, :] = jnp.sum(sum_ref[source], axis=0, keepdims=True)
        pack[1:2, :] = sums[0:1, :]
        pack[3:4, :] = sums[1:2, :]
        pack[5:6, :] = sums[2:3, :]
        pack[6:7, :] = bias[0:1, 0:width]
        pack[7:8, :] = bias[0:1, width : 2 * width]
        pack[12:15, :] = sums[3:6, :]


def input_grad_body(clips, inputs, d_own, d_other, w_own, w_other, grad_first, out):
    total = None
    for d_ref, weight in ((d_own, w_own), (d_other, w_other)):
        for part in range(3):
            term = dot(d_ref[part], weight[part], 0, 1)
            total = term if total is None else total + term
    bent = jnp.tanh(inputs[...].astype(F32) / clips[0])
    out[...] = total * (1.0 - bent * bent) + grad_first[...]


def slope_of(weight, scale):
    bent = jnp.tanh(weight.astype(F32) / scale)
    return 1.0 - bent * bent


def down_final_body(ids, own, other, chunk, weight, out):
    rows = weight.shape[0]
    value = chunk[0].astype(F32)
    slope = slope_of(weight[...], scale_row(own, other, 5, weight.shape[1]))
    out[:, :LANES] = value[:rows] * slope[:, :LANES]
    out[:, LANES:] = value[rows:] * slope[:, LANES:]


def up_final_body(ids, own, other, chunk, weight, out):
    rows = weight.shape[0]
    value = chunk[0].astype(F32)
    slope = slope_of(weight[...], scale_row(own, other, 4, weight.shape[1]))
    for part in range(weight.shape[1] // LANES):
        cols = slice(part * LANES, (part + 1) * LANES)
        out[:, cols] = value[part * rows : (part + 1) * rows] * slope[:, cols]


def rest_final_body(ids, own, other, chunk, project, merge, project_out, merge_out):
    rows = project.shape[1]
    step = merge.shape[1]
    value = chunk[0].astype(F32)
    for part in range(3):
        slope = slope_of(project[part], scale_row(own, other, part, LANES))
        project_out[part] = value[part * rows : (part + 1) * rows] * slope
    slope = slope_of(merge[0], scale_row(own, other, 3, merge.shape[2]))
    base = 3 * rows
    merge_out[0, :, :LANES] = value[base : base + step] * slope[:, :LANES]
    merge_out[0, :, LANES:] = value[base + step : base + 2 * step] * slope[:, LANES:]


class Exchange:
    def __init__(self, size):
        self.bits = size.bit_length() - 1
        assert 1 << self.bits == size
        self.size = size
        order = list(range(self.bits))
        turned = order[:]
        if self.bits > 1:
            turned[0], turned[1] = 1, 0
        self.orders = (order, turned)
        self.halvings = min(self.bits, 4)
        self.blocks = 1 << self.halvings

    def relative(self, position, core):
        total = 0
        for stage in range(self.halvings):
            bit = (position >> self.orders[core][stage]) & 1
            total = total + (bit << (self.halvings - 1 - stage))
        return total

    def swap(self, value, stage, same=False):
        pairs = []
        for index in range(self.size):
            for core in range(2):
                to = index ^ (1 << self.orders[0 if same else core][stage])
                pairs.append((2 * index + core, 2 * to + core))
        return lax.ppermute(value, ("dp", "tensor"), pairs)

    def core_swap(self, value):
        return lax.ppermute(value, "tensor", [(0, 1), (1, 0)])

    def reduce(self, mine, received):
        terms = [mine, received]
        count = self.blocks

        def add(lo, hi):
            total = terms[0][lo:hi].astype(F32)
            for term in terms[1:]:
                total = total + term[lo:hi].astype(F32)
            return total.astype(BF16)

        for stage in range(self.halvings):
            count //= 2
            terms.append(self.swap(add(count, 2 * count), stage))
        value = add(0, 1)
        for stage in range(self.halvings, self.bits):
            value = (value.astype(F32) + self.swap(value, stage).astype(F32)).astype(BF16)
        for stage in reversed(range(self.halvings)):
            value = jnp.concatenate([value, self.swap(value, stage)], axis=0)
        return value


def local(
    inputs,
    row_lengths,
    project_weight,
    merge_weight,
    up_weight,
    down_weight,
    query_value_bias,
    merge_bias,
    up_bias,
    down_bias,
    norm_gains,
    norm_shifts,
    clip_scales,
    cotangent,
):
    exchange = Exchange(lax.axis_size("dp"))
    blocks = exchange.blocks
    member = lax.axis_index("tensor")
    place = lax.axis_index("dp")
    rel0, rel1 = exchange.relative(place, 0), exchange.relative(place, 1)
    own_rel = jnp.where(member == 0, rel0, rel1)
    other_rel = jnp.where(member == 0, rel1, rel0)
    ids = jnp.stack([own_rel, other_rel, member * (LONG // SHORT)]).astype(jnp.int32)
    own_id = jnp.zeros((1,), jnp.int32)
    other_id = jnp.ones((1,), jnp.int32)
    total, width = inputs.shape
    hidden = up_weight.shape[1]
    project = jnp.transpose(project_weight, (1, 0, 2))

    steps = 4
    own_pack = pl.pallas_call(
        peaks_body,
        grid=(steps,),
        in_specs=[
            pl.BlockSpec((3, width // steps, LANES), lambda i: (0, i, 0)),
            pl.BlockSpec((LANES // steps, width), lambda i: (i, 0)),
            pl.BlockSpec((width // steps, hidden), lambda i: (i, 0)),
            pl.BlockSpec((hidden // steps, width), lambda i: (i, 0)),
            pl.BlockSpec((2, LANES), lambda i: (0, 0)),
            pl.BlockSpec((1, hidden), lambda i: (0, 0)),
        ],
        out_specs=pl.BlockSpec((16, hidden), lambda i: (0, 0)),
        out_shape=shaped((16, hidden), F32),
    )(project, merge_weight, up_weight, down_weight, query_value_bias, up_bias[None])
    other_pack = exchange.core_swap(own_pack)
    pack_spec = pl.BlockSpec((16, hidden), lambda i: (0, 0))
    project_block = pl.BlockSpec((3, width // steps, LANES), lambda i: (0, i, 0))
    project_own = pl.pallas_call(
        clip_project_body,
        grid=(steps,),
        in_specs=[pack_spec, pack_spec, project_block],
        out_specs=project_block,
        out_shape=shaped(project.shape, BF16),
    )(own_pack, other_pack, project)
    project_other = exchange.core_swap(project_own)
    rest_blocks = [
        pl.BlockSpec((LANES // steps, width), lambda i: (i, 0)),
        pl.BlockSpec((width // steps, hidden), lambda i: (i, 0)),
        pl.BlockSpec((hidden // steps, width), lambda i: (i, 0)),
    ]
    merge_own, up_own, down_own = pl.pallas_call(
        clip_rest_body,
        grid=(steps,),
        in_specs=[pack_spec, pack_spec] + rest_blocks,
        out_specs=rest_blocks,
        out_shape=[shaped(a.shape, BF16) for a in (merge_weight, up_weight, down_weight)],
    )(own_pack, other_pack, merge_weight, up_weight, down_weight)
    merge_other = exchange.core_swap(merge_own)
    up_other = exchange.core_swap(up_own)
    down_other = exchange.core_swap(down_own)

    head_shape = shaped((LANES, total), BF16)
    heads_out = [head_shape] * 4 + [shaped((8, total), F32)]
    mask_scratch = pltpu.VMEM((LONG, LONG), F32)
    heads_flops = 2 * total * width * 3 * LANES * 4
    xq, *own_heads = call(
        forward_first_body,
        [shaped((total, width), BF16)] + heads_out,
        (ids, row_lengths, clip_scales, inputs, project_own, own_pack),
        heads_flops,
        [mask_scratch],
        in_specs=[SMEM] * 3 + [VMEM] * 3,
        out_specs=[VMEM] * 6,
    )
    other_heads = call(
        forward_second_body,
        heads_out,
        (ids, row_lengths, xq, project_other, other_pack),
        heads_flops,
        [mask_scratch],
        in_specs=[SMEM] * 2 + [VMEM] * 3,
        out_specs=[VMEM] * 5,
    )

    vectors = jnp.concatenate([merge_bias[None], down_bias[None], norm_gains, norm_shifts], axis=0)
    rows_f32 = shaped((total, width), F32)
    rows_bf16 = shaped((total, width), BF16)
    wide = shaped((total, hidden), BF16)
    (
        unit,
        inverse,
        normed_q,
        active_own,
        active_other,
        factor_own,
        factor_other,
        output,
        grad_sum,
        grad_feed,
        sums,
    ) = call(
        middle_body,
        [
            rows_f32,
            shaped((total, 128), F32),
            rows_bf16,
            wide,
            wide,
            wide,
            wide,
            rows_bf16,
            rows_f32,
            rows_bf16,
            shaped((8, width), F32),
        ],
        (
            clip_scales,
            own_heads[3],
            other_heads[3],
            merge_own,
            merge_other,
            inputs,
            up_own,
            up_other,
            down_own,
            down_other,
            own_pack,
            other_pack,
            vectors,
            cotangent,
        ),
        2 * total * width * 4 * hidden * 3,
        [
            pltpu.VMEM((total, width), F32),
            pltpu.VMEM((total, 256), F32),
            pltpu.VMEM((3, 8, width), F32),
            pltpu.VMEM((3, 8, width), F32),
        ],
        in_specs=[SMEM] + [VMEM] * 13,
        out_specs=[VMEM] * 11,
    )

    chunk_shape = shaped((blocks, 2 * hidden // blocks, LANES), BF16)

    def down_half(which, active):
        return call(
            down_grad_body,
            chunk_shape,
            (ids, which, active, grad_feed),
            2 * total * width * hidden,
            in_specs=[SMEM] * 2 + [VMEM] * 2,
            out_specs=VMEM,
        )

    down_got = exchange.core_swap(down_half(other_id, active_other))
    down_rel = exchange.reduce(down_half(own_id, active_own), down_got)

    def up_half(body, which, down, up, factor, *before):
        return call(
            body,
            [chunk_shape, shaped((1, hidden), F32), rows_f32],
            (ids, which, grad_feed, down, up, factor, normed_q) + before,
            2 * total * width * hidden * 3,
            [pltpu.VMEM((total, hidden), BF16)],
            in_specs=[SMEM] * 2 + [VMEM] * (5 + len(before)),
            out_specs=[VMEM] * 3,
        )

    up_theirs, bias_other, partial_normed = up_half(
        up_grad_first_body, other_id, down_other, up_other, factor_other
    )
    up_got = exchange.core_swap(up_theirs)
    up_mine, bias_own, grad_normed = up_half(
        up_grad_body, own_id, down_own, up_own, factor_own, partial_normed
    )
    up_rel = exchange.reduce(up_mine, up_got)

    small = shaped((16, width), F32)
    grad_first, grad_branch, small_theirs, small_mine = call(
        first_norm_back_body,
        [rows_f32, rows_bf16, small, small],
        (clip_scales, grad_normed, grad_sum, unit, inverse, vectors, sums, bias_other, bias_own),
        2 * total * width * 1000,
        [pltpu.VMEM((3, 8, width), F32)],
        in_specs=[SMEM] + [VMEM] * 8,
        out_specs=[VMEM] * 4,
    )

    def heads_half(which, heads, merge_q):
        return call(
            backward_heads_body,
            [
                chunk_shape,
                shaped((3, LANES, total), BF16),
                shaped((8, 2 * LANES), F32),
            ],
            (ids, row_lengths, which, xq) + tuple(heads) + (merge_q, grad_branch),
            heads_flops * 2,
            [
                mask_scratch,
                pltpu.VMEM((LANES, total), BF16),
                pltpu.VMEM((width, total), BF16),
            ],
            in_specs=[SMEM] * 3 + [VMEM] * 8,
            out_specs=[VMEM] * 3,
        )

    rest_theirs, d_other, qv_other = heads_half(other_id, other_heads, merge_other)
    rest_got = exchange.core_swap(rest_theirs)
    rest_mine, d_own, qv_own = heads_half(own_id, own_heads, merge_own)
    rest_rel = exchange.reduce(rest_mine, rest_got)
    input_grad = call(
        input_grad_body,
        rows_f32,
        (clip_scales, inputs, d_own, d_other, project_own, project_other, grad_first),
        2 * total * width * 6 * LANES,
        in_specs=[SMEM] + [VMEM] * 6,
        out_specs=VMEM,
    )

    def joined(sums_part, qv_row):
        return jnp.concatenate([sums_part[:8], qv_row[:1], sums_part[12:15]], axis=0)

    row = lax.broadcasted_iota(jnp.int32, (12, width), 0)

    def merge_small(a, b):
        return jnp.where(row < 9, a + b, jnp.maximum(a, b))

    small_all = joined(small_mine, qv_own)
    small_all = merge_small(small_all, exchange.core_swap(joined(small_theirs, qv_other)))
    for stage in range(exchange.bits):
        small_all = merge_small(small_all, exchange.swap(small_all, stage, same=True))

    def final(body, rel, weights, weight_specs, out_shapes, out_specs):
        spec = pltpu.PrefetchScalarGridSpec(
            num_scalar_prefetch=1,
            grid=(blocks,),
            in_specs=[
                pl.BlockSpec((16, hidden), lambda i, s: (0, 0)),
                pl.BlockSpec((16, hidden), lambda i, s: (0, 0)),
                pl.BlockSpec((1,) + rel.shape[1:], lambda i, s: (i ^ s[0], 0, 0)),
            ]
            + weight_specs,
            out_specs=out_specs,
        )
        return call(
            body,
            out_shapes,
            (ids, own_pack, other_pack, rel) + weights,
            1,
            grid_spec=spec,
        )

    down_spec = pl.BlockSpec((hidden // blocks, width), lambda i, s: (i, 0))
    down_grad = final(
        down_final_body,
        down_rel,
        (down_weight,),
        [down_spec],
        shaped(down_weight.shape, F32),
        down_spec,
    )
    up_spec = pl.BlockSpec((width // blocks, hidden), lambda i, s: (i, 0))
    up_grad = final(
        up_final_body, up_rel, (up_weight,), [up_spec], shaped(up_weight.shape, F32), up_spec
    )
    project_spec = pl.BlockSpec((3, width // blocks, LANES), lambda i, s: (0, i, 0))
    merge_spec = pl.BlockSpec((1, LANES // blocks, width), lambda i, s: (i, 0, 0))
    merge_parts = merge_weight.reshape(blocks, LANES // blocks, width)
    project_grad, merge_grad = final(
        rest_final_body,
        rest_rel,
        (project, merge_parts),
        [project_spec, merge_spec],
        [shaped(project.shape, F32), shaped(merge_parts.shape, F32)],
        [project_spec, merge_spec],
    )
    peaks = small_all[9:12, 0]
    return (
        output,
        input_grad,
        jnp.transpose(project_grad, (1, 0, 2)),
        merge_grad.reshape(merge_weight.shape),
        up_grad,
        down_grad,
        small_all[8].reshape(2, LANES),
        small_all[4],
        small_all[6:8].reshape(hidden),
        small_all[5],
        small_all[0:2],
        small_all[2:4],
        DECAY * clip_scales + (1.0 - DECAY) * peaks,
    )


def solution(mesh):
    return jax.shard_map(
        local,
        mesh=mesh,
        in_specs=(
            P(("dp", "tensor"), None),
            P("dp"),
            P(None, None, "tensor"),
            P("tensor", None),
            P(None, "tensor"),
            P("tensor", None),
            P(None, "tensor"),
            P(),
            P("tensor"),
            P(),
            P(),
            P(),
            P(),
            P(("dp", "tensor"), None),
        ),
        out_specs=(
            P(("dp", "tensor"), None),
            P(("dp", "tensor"), None),
            P(None, None, "tensor"),
            P("tensor", None),
            P(None, "tensor"),
            P("tensor", None),
            P(None, "tensor"),
            P(),
            P("tensor"),
            P(),
            P(),
            P(),
            P(),
        ),
        check_vma=False,
    )
```

time: 717 us -> 343 us (0.48)
  waiting for transfers between devices: 301 us -> 83.7 us
  blocking collectives: 168 us -> 0 us
  Pallas kernels: 0 us -> 160 us
  matrix products: 104 us -> 0 us
  starting transfers between devices: 0.71 us -> 50.3 us
  other arithmetic: 70.5 us -> 32 us
  local copies, waits for them, and re-layouts: 50.6 us -> 13.4 us
  between operations: 14.9 us -> 1 us
    psum x2 -> x0, waiting for transfers between devices: 254 us -> none  [the longest x1 229 us: local(): lax.psum((down_part, up_part, up_bias_part, merge_part, project_part, bia...]
    pallas_call x0 -> x17, Pallas kernels: none -> 160 us  [the longest x11 111 us: call(): pl.pallas_call(body, in_specs=in_specs, out_specs=out_specs, scratch_shap...]
    psum x2 -> x0, blocking collectives: 110 us -> none  [the longest x1 63.4 us: local(): lax.psum((down_part, up_part, up_bias_part, merge_part, project_part, bia...]
    dot_general x26 -> x0, matrix products: 104 us -> none  [the longest x1 18.1 us: local(): jnp.dot(normed_q, up_q, preferred_element_type=jnp.float32) + up_bias]
    ppermute x0 -> x37, waiting for transfers between devices: none -> 83.7 us  [the longest x28 82.2 us: swap(): return lax.ppermute(value, ('dp', 'tensor'), pairs)]
    pmax x2 -> x0, blocking collectives: 57.9 us -> none  [the longest x1 55.5 us: local(): lax.pmax((jnp.max(jnp.abs(own_inputs)), jnp.max(jnp.abs(normed)), jnp.max...]
    ppermute x0 -> x37, starting transfers between devices: none -> 50.3 us  [the longest x28 48.1 us: swap(): return lax.ppermute(value, ('dp', 'tensor'), pairs)]
    reduce_scatter x3 -> x0, waiting for transfers between devices: 24.2 us -> none  [the longest x1 12.1 us: local(): lax.psum_scatter(jnp.dot(lax.slice_in_dim(active_q, 0, share * lax.axis_s...]
  transfers between devices with their start and end apart: 8 -> 37, of which waited for: 6 -> 13; matrix products, arithmetic and copies ran while one was open for 6% -> 11% of each run, Pallas kernels for 0% -> 21%
where the time goes in v1:
time: 343 us; the launch traced here: 341 us
  Pallas kernels  160 us (47%)
  waiting for transfers between devices  83.7 us (24%)
  starting transfers between devices  50.3 us (15%)
  other arithmetic  32 us (9%)
  local copies, waits for them, and re-layouts  13.4 us (4%)
    pallas_call x11, Pallas kernels, call(): pl.pallas_call(body, in_specs=in_specs, out_specs=out_specs, scratch_shap...  111 us
    ppermute x28, waiting for transfers between devices, swap(): return lax.ppermute(value, ('dp', 'tensor'), pairs)  82.2 us
    ppermute x28, starting transfers between devices, swap(): return lax.ppermute(value, ('dp', 'tensor'), pairs)  48.1 us
    pallas_call x3, Pallas kernels, call(): return pl.pallas_call(body, grid_spec=grid_spec, **params)(*ins)  35.2 us
    convert_element_type x12, other arithmetic, add(): return total.astype(BF16)  16.9 us
    concatenate x9, other arithmetic, reduce(): value = jnp.concatenate([value, self.swap(value, stage)], axis=0)  6.86 us
  transfers between devices with their start and end apart: 37, of which 13 were waited for; matrix products, arithmetic and copies ran while one was open for 11% of the time, Pallas kernels for 21%

profile of v1, /device:TPU:1, one launch (start us, length us, event | category | flops | bytes accessed | tf_op | source)
XLA Modules:
  0.0 340.8 jit_solution(17212521725286336775)
XLA Ops:
  1.9 4.8 %shard_map.237.own.pack.pack_own = f32[16,1536]{1,0:T(8,128)} custom-call(bf16[3,768,384]{2,1,0:T(8,128)(2,1)} %bitcast.7, bf16[384,768]{1,0:T(8,128)(2,1)} %merge.3, bf16[768,1536]{1,0:T(8,128)(2,1)} %weight.2, bf16[1536,768]{1,0:T(8,128)(2,1)} %weight.3, f32[2,384]{1,0:T(2,128)} %qv_bias.1, f32[1,1536]{1,0:T(1,128)} %broadcast_in_dim.9.up_bias), custom_call_target="tpu_custom_call" | custom-call | tf_op jit(solution)/shard_map/pallas_call | solution.py:582
  8.9 5.6 %shard_map.241 = (bf16[384,768]{1,0:T(8,128)(2,1)}, bf16[768,1536]{1,0:T(8,128)(2,1)}, bf16[1536,768]{1,0:T(8,128)(2,1)}) custom-call(f32[16,1536]{1,0:T(8,128)} %shard_map.237.own.pack.pack_own, f32[16,1536]{1,0:T(8,128)} %copy-done.6, bf16[384,768]{1,0:T(8,128)(2,1)} %merge.3, bf16[768,1536]{1,0:T(8,128)(2,1)} %weight.2, bf16[1536,768]{1,0:T(8,128)(2,1)} %weight.3), custom_call_target="tpu_custom_call" | custom-call | tf_op jit(solution)/shard_map/pallas_call | solution.py:612
  15.1 4.0 %shard_map.238.weight.w_own = bf16[3,768,384]{2,1,0:T(8,128)(2,1)} custom-call(f32[16,1536]{1,0:T(8,128)} %shard_map.237.own.pack.pack_own, f32[16,1536]{1,0:T(8,128)} %copy-done.6, bf16[3,768,384]{2,1,0:T(8,128)(2,1)} %bitcast.8), custom_call_target="tpu_custom_call" | custom-call | tf_op jit(solution)/shard_map/pallas_call | solution.py:599
  20.8 8.0 %shard_map.239 = (bf16[512,768]{1,0:T(8,128)(2,1)}, bf16[384,512]{1,0:T(8,128)(2,1)}, bf16[384,512]{1,0:T(8,128)(2,1)}, bf16[384,512]{1,0:T(8,128)(2,1)}, bf16[384,512]{1,0:T(8,128)(2,1)}, /*index=5*/f32[8,512]{1,0:T(8,128)}) custom-call(s32[3]{0:T(128)} %pad_add_fusion.ids, s32[8]{0:T(128)} %lengths.7, f32[3]{0:T(128)} %clips.7, bf16[512,768]{1,0:T(8,128)(2,1)} %inputs.5, ...), custom_call_target="tpu_custom_call" | custom-call | flops 3623878656 | bytes 5029944 | tf_op jit(solution)/shard_map/pallas_call | solution.py:41
  30.1 8.0 %shard_map.240 = (bf16[384,512]{1,0:T(8,128)(2,1)}, bf16[384,512]{1,0:T(8,128)(2,1)}, bf16[384,512]{1,0:T(8,128)(2,1)}, bf16[384,512]{1,0:T(8,128)(2,1)}, f32[8,512]{1,0:T(8,128)}) custom-call(s32[3]{0:T(128)} %pad_add_fusion.ids, s32[8]{0:T(128)} %lengths.7, bf16[512,768]{1,0:T(8,128)(2,1)} %get-tuple-element.57.xq, bf16[3,768,384]{2,1,0:T(8,128)(2,1)} %copy-done.11, ...), custom_call_target="tpu_custom_call" | custom-call | flops 3623878656 | bytes 4243500 | tf_op jit(solution)/shard_map/pallas_call | solution.py:41
  38.9 29.4 %shard_map.242 = (f32[512,768]{1,0:T(8,128)}, f32[512,128]{1,0:T(8,128)}, bf16[512,768]{1,0:T(8,128)(2,1)}, bf16[512,1536]{1,0:T(8,128)(2,1)}, bf16[512,1536]{1,...) custom-call(f32[3]{0:T(128)} %clips.7, ...), custom_call_target="tpu_custom_call" | custom-call | flops 14495514624 | bytes 25274380 | tf_op jit(solution)/shard_map/pallas_call | solution.py:41
  68.3 9.4 %shard_map.243 = (bf16[16,192,384]{2,1,0:T(8,128)(2,1)}, f32[1,1536]{1,0:T(1,128)}, f32[512,768]{1,0:T(8,128)}) custom-call(s32[3]{0:T(128)} %pad_add_fusion.ids, s32[1]{0:T(128)} %constant.10.clone.1.which, bf16[512,768]{1,0:T(8,128)(2,1)} %get-tuple-element.67.grad_feed, bf16[1536,768]{1,0:T(8,128)(2,1)} %collective-permute-done.4.down_other.down, ...), custom_call_target="tpu_custom_call" | custom-call | flops 3623878656 | bytes 11802640 | tf_op jit(solution)/shard_map/pallas_call | solution.py:41
  77.7 9.9 %shard_map.244 = (bf16[16,192,384]{2,1,0:T(8,128)(2,1)}, f32[1,1536]{1,0:T(1,128)}, f32[512,768]{1,0:T(8,128)}) custom-call(s32[3]{0:T(128)} %pad_add_fusion.ids, s32[1]{0:T(128)} %constant.9.clone.1.which, bf16[512,768]{1,0:T(8,128)(2,1)} %get-tuple-element.67.grad_feed, bf16[1536,768]{1,0:T(8,128)(2,1)} %get-tuple-element.61.down_own.down, ...), custom_call_target="tpu_custom_call" | custom-call | flops 3623878656 | bytes 13375504 | tf_op jit(solution)/shard_map/pallas_call | solution.py:41
  87.6 5.6 %shard_map.245 = (f32[512,768]{1,0:T(8,128)}, bf16[512,768]{1,0:T(8,128)(2,1)}, f32[16,768]{1,0:T(8,128)}, f32[16,768]{1,0:T(8,128)}) custom-call(f32[3]{0:T(128)} %clips.7, f32[512,768]{1,0:T(8,128)} %get-tuple-element.72.grad_normed, f32[512,768]{1,0:T(8,128)} %get-tuple-element.73.grad_sum, f32[512,768]{1,0:T(8,128)} %get-tuple-element.74.unit_ref, ...), custom_call_target="tpu_custom_call" | custom-call | flops 786432000 | bytes 7493644 | tf_op jit(solution)/shard_map/pallas_call | solution.py:41
  93.3 11.2 %shard_map.247 = (bf16[16,192,384]{2,1,0:T(8,128)(2,1)}, bf16[3,384,512]{2,1,0:T(8,128)(2,1)}, f32[8,768]{1,0:T(8,128)}) custom-call(s32[3]{0:T(128)} %pad_add_fusion.ids, s32[8]{0:T(128)} %lengths.7, s32[1]{0:T(128)} %constant.10.clone.1.which, bf16[512,768]{1,0:T(8,128)(2,1)} %get-tuple-element.57.xq, bf16[384,512]{1,0:T(8,128)(2,1)} %get-tuple-element.81.q_ref, ...), custom_call_target="tpu_custom_call" | custom-call | flops 7247757312 | bytes 7315504 | tf_op jit(solution)/shard_map/pallas_call | solution.py:41
  105.0 5.2 %shard_map.252 = bf16[16,192,384]{2,1,0:T(8,128)(2,1)} custom-call(s32[3]{0:T(128)} %pad_add_fusion.ids, s32[1]{0:T(128)} %constant.10.clone.1.which, bf16[512,1536]{1,0:T(8,128)(2,1)} %get-tuple-element.94.active, bf16[512,768]{1,0:T(8,128)(2,1)} %get-tuple-element.67.grad_feed), custom_call_target="tpu_custom_call" | custom-call | flops 1207959552 | bytes 4718608 | tf_op jit(solution)/shard_map/pallas_call | solution.py:41
  111.6 11.2 %shard_map.246 = (bf16[16,192,384]{2,1,0:T(8,128)(2,1)}, bf16[3,384,512]{2,1,0:T(8,128)(2,1)}, f32[8,768]{1,0:T(8,128)}) custom-call(s32[3]{0:T(128)} %pad_add_fusion.ids, s32[8]{0:T(128)} %lengths.7, s32[1]{0:T(128)} %constant.9.clone.1.which, bf16[512,768]{1,0:T(8,128)(2,1)} %get-tuple-element.57.xq, bf16[384,512]{1,0:T(8,128)(2,1)} %get-tuple-element.63.q_ref, ...), custom_call_target="tpu_custom_call" | custom-call | flops 7247757312 | bytes 7315504 | tf_op jit(solution)/shard_map/pallas_call | solution.py:41
  123.6 2.4 collective-permute-start.33
  126.0 1.5 collective-permute-done.33
  127.6 1.5 collective-permute-start.34
  129.1 5.5 %shard_map.251 = bf16[16,192,384]{2,1,0:T(8,128)(2,1)} custom-call(s32[3]{0:T(128)} %pad_add_fusion.ids, s32[1]{0:T(128)} %constant.9.clone.1.which, bf16[512,1536]{1,0:T(8,128)(2,1)} %get-tuple-element.93.active, bf16[512,768]{1,0:T(8,128)(2,1)} %get-tuple-element.67.grad_feed), custom_call_target="tpu_custom_call" | custom-call | flops 1207959552 | bytes 4718608 | tf_op jit(solution)/shard_map/pallas_call | solution.py:41
  136.5 2.7 add_convert_fusion.1
  140.4 2.6 add_convert_fusion
  143.4 2.3 collective-permute-start.36
  145.7 7.3 %shard_map.248 = f32[512,768]{1,0:T(8,128)} custom-call(f32[3]{0:T(128)} %clips.7, bf16[512,768]{1,0:T(8,128)(2,1)} %inputs.5, bf16[3,384,512]{2,1,0:T(8,128)(2,1)} %get-tuple-element.80.d_own, bf16[3,384,512]{2,1,0:T(8,128)(2,1)} %get-tuple-element.85.d_other, bf16[3,768,384]{2,1,0:T(8,128)(2,1)} %shard_map.238.weight.w_own, ...), custom_call_target="tpu_custom_call" | custom-call | flops 1811939328 | bytes 9830412 | tf_op jit(solution)/shard_map/pallas_call | solution.py:41
  153.9 1.5 add_convert_fusion.5
  156.7 9.3 %collective-permute-done.15 = bf16[8,192,384]{2,1,0:T(8,128)(2,1)} collective-permute-done((bf16[8,192,384]{2,1,0:T(8,128)(2,1)}, bf16[8,192,384]{2,1,0:T(8,128)(2,1)}, u32[]{:S(2)}, u32[]{:S(2)}) %collective-permute-start.15) | collective-permute-done | bytes 1179680 | tf_op jit(solution)/shard_map/ppermute | solution.py:525
  167.5 2.1 collective-permute-start.16
  169.6 16.3 %collective-permute-done.24 = bf16[8,192,384]{2,1,0:T(8,128)(2,1)} collective-permute-done((bf16[8,192,384]{2,1,0:T(8,128)(2,1)}, bf16[8,192,384]{2,1,0:T(8,128)(2,1)}, u32[]{:S(2)}, u32[]{:S(2)}) %collective-permute-start.24) | collective-permute-done | bytes 1179680 | tf_op jit(solution)/shard_map/ppermute | solution.py:525
  187.4 1.6 collective-permute-start.25
  193.5 4.6 %collective-permute-done.25 = bf16[4,192,384]{2,1,0:T(8,128)(2,1)S(1)} collective-permute-done((bf16[4,192,384]{2,1,0:T(8,128)(2,1)S(1)}, bf16[4,192,384]{2,1,0:T(8,128)(2,1)S(1)}, u32[]{:S(2)}, u32[]{:S(2)}) %collective-permute-start.25) | collective-permute-done | bytes 589856 | tf_op jit(solution)/shard_map/ppermute | solution.py:525
  200.7 2.9 collective-permute-start.9
  204.6 2.7 collective-permute-start.18
  207.3 4.2 %collective-permute-done.26 = bf16[2,192,384]{2,1,0:T(8,128)(2,1)S(1)} collective-permute-done((bf16[2,192,384]{2,1,0:T(8,128)(2,1)S(1)}, bf16[2,192,384]{2,1,0:T(8,128)(2,1)S(1)}, u32[]{:S(2)}, u32[]{:S(2)}) %collective-permute-start.26) | collective-permute-done | bytes 294944 | tf_op jit(solution)/shard_map/ppermute | solution.py:525
  212.7 2.9 collective-permute-start.27
  215.6 1.8 constant_dynamic-update-slice_fusion.9
  217.4 1.7 collective-permute-done.27
  219.1 1.8 constant_dynamic-update-slice_fusion.14
  224.4 6.5 %collective-permute-done.19 = bf16[1,192,384]{2,1,0:T(8,128)(2,1)S(1)} collective-permute-done((bf16[1,192,384]{2,1,0:T(8,128)(2,1)S(1)}, bf16[1,192,384]{2,1,0:T(8,128)(2,1)S(1)}, u32[]{:S(2)}, u32[]{:S(2)}) %collective-permute-start.19) | collective-permute-done | bytes 147488 | tf_op jit(solution)/shard_map/ppermute | solution.py:525
  231.6 4.9 %collective-permute-start.20 = (bf16[2,192,384]{2,1,0:T(8,128)(2,1)}, bf16[2,192,384]{2,1,0:T(8,128)(2,1)S(1)}, u32[]{:S(2)}, u32[]{:S(2)}) collective-permute-start(bf16[2,192,384]{2,1,0:T(8,128)(2,1)} %pad_maximum_fusion.7), channel_id=1, source_target_pairs={{0,8},{1,9},{2,10},{3,11},{4,12},{5,13},{6,14},{7,15},{8,0},{9,1},... | collective-permute-start | bytes 884744 | tf_op jit(solution)/shard_map/ppermute | solution.py:525
  237.9 1.5 collective-permute-start.29
  242.2 2.0 collective-permute-start.11
  244.9 5.0 %collective-permute-done.29 = bf16[2,192,384]{2,1,0:T(8,128)(2,1)S(1)} collective-permute-done((bf16[2,192,384]{2,1,0:T(8,128)(2,1)}, bf16[2,192,384]{2,1,0:T(8,128)(2,1)S(1)}, u32[]{:S(2)}, u32[]{:S(2)}) %collective-permute-start.29) | collective-permute-done | bytes 294944 | tf_op jit(solution)/shard_map/ppermute | solution.py:525
  252.9 3.3 collective-permute-done.11
  259.1 4.6 %collective-permute-start.22 = (bf16[8,192,384]{2,1,0:T(8,128)(2,1)S(1)}, bf16[8,192,384]{2,1,0:T(8,128)(2,1)S(1)}, u32[]{:S(2)}, u32[]{:S(2)}) collective-permute-start(bf16[8,192,384]{2,1,0:T(8,128)(2,1)S(1)} %pad_maximum_fusion.1), channel_id=1, source_target_pairs={{0,2},{1,5},{2,0},{3,7},{4,6},{5,1},{6,4},{7,3},{8,10},{9,13},{10,... | collective-permute-start | bytes 3538952 | tf_op jit(solution)/shard_map/ppermute | solution.py:525
  266.3 2.1 pad_maximum_fusion
  268.4 4.4 %collective-permute-start.13 = (bf16[8,192,384]{2,1,0:T(8,128)(2,1)}, bf16[8,192,384]{2,1,0:T(8,128)(2,1)}, u32[]{:S(2)}, u32[]{:S(2)}) collective-permute-start(bf16[8,192,384]{2,1,0:T(8,128)(2,1)} %pad_maximum_fusion), channel_id=1, source_target_pairs={{0,2},{1,5},{2,0},{3,7},{4,6},{5,1},{6,4},{7,3},{8,10},{9,13},{10,... | collective-permute-start | bytes 3538952 | tf_op jit(solution)/shard_map/ppermute | solution.py:525
  273.3 16.2 %collective-permute-done.22 = bf16[8,192,384]{2,1,0:T(8,128)(2,1)S(1)} collective-permute-done((bf16[8,192,384]{2,1,0:T(8,128)(2,1)S(1)}, bf16[8,192,384]{2,1,0:T(8,128)(2,1)S(1)}, u32[]{:S(2)}, u32[]{:S(2)}) %collective-permute-start.22) | collective-permute-done | bytes 1179680 | tf_op jit(solution)/shard_map/ppermute | solution.py:525
  289.8 12.5 %collective-permute-done.31 = bf16[8,192,384]{2,1,0:T(8,128)(2,1)S(1)} collective-permute-done((bf16[8,192,384]{2,1,0:T(8,128)(2,1)S(1)}, bf16[8,192,384]{2,1,0:T(8,128)(2,1)S(1)}, u32[]{:S(2)}, u32[]{:S(2)}) %collective-permute-start.31) | collective-permute-done | bytes 1179680 | tf_op jit(solution)/shard_map/ppermute | solution.py:525
  302.7 11.8 %shard_map.250 = f32[768,1536]{1,0:T(8,128)} custom-call(s32[3]{0:T(128)} %pad_add_fusion.ids, f32[16,1536]{1,0:T(8,128)} %shard_map.237.own.pack.pack_own, f32[16,1536]{1,0:T(8,128)} %copy-done.6, bf16[16,192,384]{2,1,0:T(8,128)(2,1)} %copy-done.3, bf16[768,1536]{1,0:T(8,128)(2,1)} %weight.2), custom_call_target="tpu_custom_call" | custom-call | flops 1 | bytes 9633804 | tf_op jit(solution)/shard_map/pallas_call | solution.py:40
  314.4 11.8 %shard_map.253 = f32[1536,768]{1,0:T(8,128)} custom-call(s32[3]{0:T(128)} %pad_add_fusion.ids, f32[16,1536]{1,0:T(8,128)} %shard_map.237.own.pack.pack_own, f32[16,1536]{1,0:T(8,128)} %copy-done.6, bf16[16,192,384]{2,1,0:T(8,128)(2,1)} %copy-done.5, bf16[1536,768]{1,0:T(8,128)(2,1)} %weight.3), custom_call_target="tpu_custom_call" | custom-call | flops 1 | bytes 9633804 | tf_op jit(solution)/shard_map/pallas_call | solution.py:40
  326.2 1.5 constant_dynamic-update-slice_fusion.chunk
  329.1 11.7 %shard_map.249 = (f32[3,768,384]{2,1,0:T(8,128)}, f32[16,24,768]{2,1,0:T(8,128)}) custom-call(s32[3]{0:T(128)} %pad_add_fusion.ids, f32[16,1536]{1,0:T(8,128)} %shard_map.237.own.pack.pack_own, f32[16,1536]{1,0:T(8,128)} %copy-done.6, bf16[16,192,384]{2,1,0:T(8,128)(2,1)} %copy-done.1, bf16[3,768,384]{2,1,0:T(8,128)(2,1)} %bitcast.9, ...), custom_call_target="tpu_custom_call" | custom-call | flops 1 | bytes 9633804 | tf_op jit(solution)/shard_map/pallas_call | solution.py:40
  (147 shorter events, 48.4 us)
Async XLA Ops:
  6.7 1.5 collective-permute-start
  14.5 5.9 %copy-start.20 = (bf16[384,768]{1,0:T(8,128)(2,1)S(1)}, bf16[384,768]{1,0:T(8,128)(2,1)}, u32[]{:S(2)}) copy-start(bf16[384,768]{1,0:T(8,128)(2,1)} %get-tuple-element.59.merge_own.merge_q) | copy-start | bytes 1769476
  14.6 23.5 %collective-permute-start.3 = (bf16[768,1536]{1,0:T(8,128)(2,1)}, bf16[768,1536]{1,0:T(8,128)(2,1)}, u32[]{:S(2)}, u32[]{:S(2)}) collective-permute-start(bf16[768,1536]{1,0:T(8,128)(2,1)} %get-tuple-element.60.up_own.up), channel_id=1, source_target_pairs={{0,1},{1,0},{2,3},{3,2},{4,5},{5,4},{6,7},{7,6},{8,9},{9,8},{10,11... | collective-permute-start | bytes 7077896 | tf_op jit(solution)/shard_map/ppermute | solution.py:528
  14.8 23.3 %collective-permute-start.4 = (bf16[1536,768]{1,0:T(8,128)(2,1)}, bf16[1536,768]{1,0:T(8,128)(2,1)}, u32[]{:S(2)}, u32[]{:S(2)}) collective-permute-start(bf16[1536,768]{1,0:T(8,128)(2,1)} %get-tuple-element.61.down_own.down), channel_id=1, source_target_pairs={{0,1},{1,0},{2,3},{3,2},{4,5},{5,4},{6,7},{7,6},{8,9},{9,8},{10,11... | collective-permute-start | bytes 7077896 | tf_op jit(solution)/shard_map/ppermute | solution.py:528
  19.1 9.7 %collective-permute-start.1 = (bf16[3,768,384]{2,1,0:T(8,128)(2,1)}, bf16[3,768,384]{2,1,0:T(8,128)(2,1)S(1)}, u32[]{:S(2)}, u32[]{:S(2)}) collective-permute-start(bf16[3,768,384]{2,1,0:T(8,128)(2,1)} %shard_map.238.weight.w_own), channel_id=1, source_target_pairs={{0,1},{1,0},{2,3},{3,2},{4,5},{5,4},{6,7},{7,6},{8,9},{9,8},{10,11... | collective-permute-start | bytes 5308424 | tf_op jit(solution)/shard_map/ppermute | solution.py:528
  20.5 17.5 %collective-permute-start.2 = (bf16[384,768]{1,0:T(8,128)(2,1)S(1)}, bf16[384,768]{1,0:T(8,128)(2,1)S(1)}, u32[]{:S(2)}, u32[]{:S(2)}) collective-permute-start(bf16[384,768]{1,0:T(8,128)(2,1)S(1)} %copy-done.20), channel_id=1, source_target_pairs={{0,1},{1,0},{2,3},{3,2},{4,5},{5,4},{6,7},{7,6},{8,9},{9,8},{10,11... | collective-permute-start | bytes 1769480 | tf_op jit(solution)/shard_map/ppermute | solution.py:528
  104.5 31.4 %collective-permute-start.5 = (bf16[16,192,384]{2,1,0:T(8,128)(2,1)}, bf16[16,192,384]{2,1,0:T(8,128)(2,1)S(1)}, u32[]{:S(2)}, u32[]{:S(2)}) collective-permute-start(bf16[16,192,384]{2,1,0:T(8,128)(2,1)} %get-tuple-element.88), channel_id=1, source_target_pairs={{0,1},{1,0},{2,3},{3,2},{4,5},{5,4},{6,7},{7,6},{8,9},{9,8},{10,11... | collective-permute-start | bytes 7077896 | tf_op jit(solution)/shard_map/ppermute | solution.py:528
  104.6 31.9 %collective-permute-start.14 = (bf16[16,192,384]{2,1,0:T(8,128)(2,1)}, bf16[16,192,384]{2,1,0:T(8,128)(2,1)}, u32[]{:S(2)}, u32[]{:S(2)}) collective-permute-start(bf16[16,192,384]{2,1,0:T(8,128)(2,1)} %get-tuple-element.92), channel_id=1, source_target_pairs={{0,1},{1,0},{2,3},{3,2},{4,5},{5,4},{6,7},{7,6},{8,9},{9,8},{10,11... | collective-permute-start | bytes 7077896 | tf_op jit(solution)/shard_map/ppermute | solution.py:528
  105.0 5.4 %copy-start.14 = (f32[16,768]{1,0:T(8,128)S(1)}, f32[16,768]{1,0:T(8,128)}, u32[]{:S(2)}) copy-start(f32[16,768]{1,0:T(8,128)} %get-tuple-element.97) | copy-start | bytes 147460
  110.2 30.1 %collective-permute-start.23 = (bf16[16,192,384]{2,1,0:T(8,128)(2,1)}, bf16[16,192,384]{2,1,0:T(8,128)(2,1)}, u32[]{:S(2)}, u32[]{:S(2)}) collective-permute-start(bf16[16,192,384]{2,1,0:T(8,128)(2,1)} %shard_map.252), channel_id=1, source_target_pairs={{0,1},{1,0},{2,3},{3,2},{4,5},{5,4},{6,7},{7,6},{8,9},{9,8},{10,11... | collective-permute-start | bytes 7077896 | tf_op jit(solution)/shard_map/ppermute | solution.py:528
  111.1 12.4 %collective-permute-start.32 = (f32[12,768]{1,0:T(8,128)S(1)}, f32[12,768]{1,0:T(8,128)S(1)}, u32[]{:S(2)}, u32[]{:S(2)}) collective-permute-start(f32[12,768]{1,0:T(8,128)S(1)} %pad_maximum_fusion.10), channel_id=1, source_target_pairs={{0,1},{1,0},{2,3},{3,2},{4,5},{5,4},{6,7},{7,6},{8,9},{9,8},{10,11... | collective-permute-start | bytes 110600 | tf_op jit(solution)/shard_map/ppermute | solution.py:528
  111.6 11.2 %copy-start.13 = (f32[16,768]{1,0:T(8,128)S(1)}, f32[16,768]{1,0:T(8,128)}, u32[]{:S(2)}) copy-start(f32[16,768]{1,0:T(8,128)} %get-tuple-element.95) | copy-start | bytes 147460
  123.6 3.8 %collective-permute-start.33 = (f32[12,768]{1,0:T(8,128)S(1)}, f32[12,768]{1,0:T(8,128)S(1)}, u32[]{:S(2)}, u32[]{:S(2)}) collective-permute-start(f32[12,768]{1,0:T(8,128)S(1)} %maximum_select_fusion.4), channel_id=1, source_target_pairs={{0,2},{1,3},{2,0},{3,1},{4,6},{5,7},{6,4},{7,5},{8,10},{9,11},{10,... | collective-permute-start | bytes 110600 | tf_op jit(solution)/shard_map/ppermute | solution.py:525
  127.6 7.0 %collective-permute-start.34 = (f32[12,768]{1,0:T(8,128)S(1)}, f32[12,768]{1,0:T(8,128)S(1)}, u32[]{:S(2)}, u32[]{:S(2)}) collective-permute-start(f32[12,768]{1,0:T(8,128)S(1)} %maximum_select_fusion.3), channel_id=1, source_target_pairs={{0,4},{1,5},{2,6},{3,7},{4,0},{5,1},{6,2},{7,3},{8,12},{9,13},{10,... | collective-permute-start | bytes 110600 | tf_op jit(solution)/shard_map/ppermute | solution.py:525
  129.1 6.9 %copy-start.10 = (bf16[16,192,384]{2,1,0:T(8,128)(2,1)S(1)}, bf16[16,192,384]{2,1,0:T(8,128)(2,1)}, u32[]{:S(2)}) copy-start(bf16[16,192,384]{2,1,0:T(8,128)(2,1)} %get-tuple-element.87) | copy-start | bytes 7077892
  134.6 8.7 %collective-permute-start.35 = (f32[12,768]{1,0:T(8,128)S(1)}, f32[12,768]{1,0:T(8,128)S(1)}, u32[]{:S(2)}, u32[]{:S(2)}) collective-permute-start(f32[12,768]{1,0:T(8,128)S(1)} %maximum_select_fusion.2), channel_id=1, source_target_pairs={{0,8},{1,9},{2,10},{3,11},{4,12},{5,13},{6,14},{7,15},{8,0},{9,1},... | collective-permute-start | bytes 110600 | tf_op jit(solution)/shard_map/ppermute | solution.py:525
  136.2 17.6 %collective-permute-start.6 = (bf16[8,192,384]{2,1,0:T(8,128)(2,1)S(1)}, bf16[8,192,384]{2,1,0:T(8,128)(2,1)}, u32[]{:S(2)}, u32[]{:S(2)}) collective-permute-start(bf16[8,192,384]{2,1,0:T(8,128)(2,1)S(1)} %add_convert_fusion.2), channel_id=1, source_target_pairs={{0,2},{1,5},{2,0},{3,7},{4,6},{5,1},{6,4},{7,3},{8,10},{9,13},{10,... | collective-permute-start | bytes 3538952 | tf_op jit(solution)/shard_map/ppermute | solution.py:525
  139.3 26.7 %collective-permute-start.15 = (bf16[8,192,384]{2,1,0:T(8,128)(2,1)}, bf16[8,192,384]{2,1,0:T(8,128)(2,1)}, u32[]{:S(2)}, u32[]{:S(2)}) collective-permute-start(bf16[8,192,384]{2,1,0:T(8,128)(2,1)} %add_convert_fusion.1), channel_id=1, source_target_pairs={{0,2},{1,5},{2,0},{3,7},{4,6},{5,1},{6,4},{7,3},{8,10},{9,13},{10,... | collective-permute-start | bytes 3538952 | tf_op jit(solution)/shard_map/ppermute | solution.py:525
  142.9 43.0 %collective-permute-start.24 = (bf16[8,192,384]{2,1,0:T(8,128)(2,1)}, bf16[8,192,384]{2,1,0:T(8,128)(2,1)}, u32[]{:S(2)}, u32[]{:S(2)}) collective-permute-start(bf16[8,192,384]{2,1,0:T(8,128)(2,1)} %add_convert_fusion), channel_id=1, source_target_pairs={{0,2},{1,5},{2,0},{3,7},{4,6},{5,1},{6,4},{7,3},{8,10},{9,13},{10,... | collective-permute-start | bytes 3538952 | tf_op jit(solution)/shard_map/ppermute | solution.py:525
  143.4 9.6 %collective-permute-start.36 = (f32[12,768]{1,0:T(8,128)S(1)}, f32[12,768]{1,0:T(8,128)}, u32[]{:S(2)}, u32[]{:S(2)}) collective-permute-start(f32[12,768]{1,0:T(8,128)S(1)} %maximum_select_fusion.1), channel_id=1, source_target_pairs={{0,16},{1,17},{2,18},{3,19},{4,20},{5,21},{6,22},{7,23},{8,24},{9,... | collective-permute-start | bytes 110600 | tf_op jit(solution)/shard_map/ppermute | solution.py:525
  153.9 85.6 %copy-start.12 = (f32[12,768]{1,0:T(8,128)}, f32[12,768]{1,0:T(8,128)S(1)}, u32[]{:S(2)}) copy-start(f32[12,768]{1,0:T(8,128)S(1)} %maximum_select_fusion) | copy-start | bytes 110596
  155.4 34.2 %collective-permute-start.7 = (bf16[4,192,384]{2,1,0:T(8,128)(2,1)S(1)}, bf16[4,192,384]{2,1,0:T(8,128)(2,1)S(1)}, u32[]{:S(2)}, u32[]{:S(2)}) collective-permute-start(bf16[4,192,384]{2,1,0:T(8,128)(2,1)S(1)} %add_convert_fusion.5), channel_id=1, source_target_pairs={{0,4},{1,3},{2,6},{3,1},{4,0},{5,7},{6,2},{7,5},{8,12},{9,11},{10,... | collective-permute-start | bytes 1769480 | tf_op jit(solution)/shard_map/ppermute | solution.py:525
  167.5 23.9 %collective-permute-start.16 = (bf16[4,192,384]{2,1,0:T(8,128)(2,1)S(1)}, bf16[4,192,384]{2,1,0:T(8,128)(2,1)S(1)}, u32[]{:S(2)}, u32[]{:S(2)}) collective-permute-start(bf16[4,192,384]{2,1,0:T(8,128)(2,1)S(1)} %add_convert_fusion.4), channel_id=1, source_target_pairs={{0,4},{1,3},{2,6},{3,1},{4,0},{5,7},{6,2},{7,5},{8,12},{9,11},{10,... | collective-permute-start | bytes 1769480 | tf_op jit(solution)/shard_map/ppermute | solution.py:525
  187.4 10.8 %collective-permute-start.25 = (bf16[4,192,384]{2,1,0:T(8,128)(2,1)S(1)}, bf16[4,192,384]{2,1,0:T(8,128)(2,1)S(1)}, u32[]{:S(2)}, u32[]{:S(2)}) collective-permute-start(bf16[4,192,384]{2,1,0:T(8,128)(2,1)S(1)} %add_convert_fusion.3), channel_id=1, source_target_pairs={{0,4},{1,3},{2,6},{3,1},{4,0},{5,7},{6,2},{7,5},{8,12},{9,11},{10,... | collective-permute-start | bytes 1769480 | tf_op jit(solution)/shard_map/ppermute | solution.py:525
  190.7 8.8 %collective-permute-start.8 = (bf16[2,192,384]{2,1,0:T(8,128)(2,1)S(1)}, bf16[2,192,384]{2,1,0:T(8,128)(2,1)S(1)}, u32[]{:S(2)}, u32[]{:S(2)}) collective-permute-start(bf16[2,192,384]{2,1,0:T(8,128)(2,1)S(1)} %add_convert_fusion.8), channel_id=1, source_target_pairs={{0,8},{1,9},{2,10},{3,11},{4,12},{5,13},{6,14},{7,15},{8,0},{9,1},... | collective-permute-start | bytes 884744 | tf_op jit(solution)/shard_map/ppermute | solution.py:525
  192.5 11.0 %collective-permute-start.17 = (bf16[2,192,384]{2,1,0:T(8,128)(2,1)S(1)}, bf16[2,192,384]{2,1,0:T(8,128)(2,1)S(1)}, u32[]{:S(2)}, u32[]{:S(2)}) collective-permute-start(bf16[2,192,384]{2,1,0:T(8,128)(2,1)S(1)} %add_convert_fusion.7), channel_id=1, source_target_pairs={{0,8},{1,9},{2,10},{3,11},{4,12},{5,13},{6,14},{7,15},{8,0},{9,1},... | collective-permute-start | bytes 884744 | tf_op jit(solution)/shard_map/ppermute | solution.py:525
  199.3 12.3 %collective-permute-start.26 = (bf16[2,192,384]{2,1,0:T(8,128)(2,1)S(1)}, bf16[2,192,384]{2,1,0:T(8,128)(2,1)S(1)}, u32[]{:S(2)}, u32[]{:S(2)}) collective-permute-start(bf16[2,192,384]{2,1,0:T(8,128)(2,1)S(1)} %add_convert_fusion.6), channel_id=1, source_target_pairs={{0,8},{1,9},{2,10},{3,11},{4,12},{5,13},{6,14},{7,15},{8,0},{9,1},... | collective-permute-start | bytes 884744 | tf_op jit(solution)/shard_map/ppermute | solution.py:525
  200.7 21.6 %collective-permute-start.9 = (bf16[1,192,384]{2,1,0:T(8,128)(2,1)S(1)}, bf16[1,192,384]{2,1,0:T(8,128)(2,1)S(1)}, u32[]{:S(2)}, u32[]{:S(2)}) collective-permute-start(bf16[1,192,384]{2,1,0:T(8,128)(2,1)S(1)} %add_convert_fusion.14), channel_id=1, source_target_pairs={{0,16},{1,17},{2,18},{3,19},{4,20},{5,21},{6,22},{7,23},{8,24},{9,... | collective-permute-start | bytes 442376 | tf_op jit(solution)/shard_map/ppermute | solution.py:525
  204.6 11.0 %collective-permute-start.18 = (bf16[1,192,384]{2,1,0:T(8,128)(2,1)S(1)}, bf16[1,192,384]{2,1,0:T(8,128)(2,1)S(1)}, u32[]{:S(2)}, u32[]{:S(2)}) collective-permute-start(bf16[1,192,384]{2,1,0:T(8,128)(2,1)S(1)} %add_convert_fusion.12), channel_id=1, source_target_pairs={{0,16},{1,17},{2,18},{3,19},{4,20},{5,21},{6,22},{7,23},{8,24},{9,... | collective-permute-start | bytes 442376 | tf_op jit(solution)/shard_map/ppermute | solution.py:525
  212.7 6.4 %collective-permute-start.27 = (bf16[1,192,384]{2,1,0:T(8,128)(2,1)S(1)}, bf16[1,192,384]{2,1,0:T(8,128)(2,1)S(1)}, u32[]{:S(2)}, u32[]{:S(2)}) collective-permute-start(bf16[1,192,384]{2,1,0:T(8,128)(2,1)S(1)} %add_convert_fusion.10), channel_id=1, source_target_pairs={{0,16},{1,17},{2,18},{3,19},{4,20},{5,21},{6,22},{7,23},{8,24},{9,... | collective-permute-start | bytes 442376 | tf_op jit(solution)/shard_map/ppermute | solution.py:525
  217.3 13.5 %collective-permute-start.19 = (bf16[1,192,384]{2,1,0:T(8,128)(2,1)S(1)}, bf16[1,192,384]{2,1,0:T(8,128)(2,1)S(1)}, u32[]{:S(2)}, u32[]{:S(2)}) collective-permute-start(bf16[1,192,384]{2,1,0:T(8,128)(2,1)S(1)} %get-tuple-element.105), channel_id=1, source_target_pairs={{0,16},{1,17},{2,18},{3,19},{4,20},{5,21},{6,22},{7,23},{8,24},{9,... | collective-permute-start | bytes 442376 | tf_op jit(solution)/shard_map/ppermute | solution.py:525
  220.9 15.7 %collective-permute-start.28 = (bf16[1,192,384]{2,1,0:T(8,128)(2,1)S(1)}, bf16[1,192,384]{2,1,0:T(8,128)(2,1)S(1)}, u32[]{:S(2)}, u32[]{:S(2)}) collective-permute-start(bf16[1,192,384]{2,1,0:T(8,128)(2,1)S(1)} %get-tuple-element.103), channel_id=1, source_target_pairs={{0,16},{1,17},{2,18},{3,19},{4,20},{5,21},{6,22},{7,23},{8,24},{9,... | collective-permute-start | bytes 442376 | tf_op jit(solution)/shard_map/ppermute | solution.py:525
  223.3 17.9 %collective-permute-start.10 = (bf16[1,192,384]{2,1,0:T(8,128)(2,1)S(1)}, bf16[1,192,384]{2,1,0:T(8,128)(2,1)}, u32[]{:S(2)}, u32[]{:S(2)}) collective-permute-start(bf16[1,192,384]{2,1,0:T(8,128)(2,1)S(1)} %get-tuple-element.107), channel_id=1, source_target_pairs={{0,16},{1,17},{2,18},{3,19},{4,20},{5,21},{6,22},{7,23},{8,24},{9,... | collective-permute-start | bytes 442376 | tf_op jit(solution)/shard_map/ppermute | solution.py:525
  231.6 26.8 %copy-start.19 = (f32[3]{0:T(128)S(1)}, f32[3]{0:T(128)}, u32[]{:S(2)}) copy-start(f32[3]{0:T(128)} %clips.7) | copy-start | bytes 40
  231.6 12.6 %collective-permute-start.20 = (bf16[2,192,384]{2,1,0:T(8,128)(2,1)}, bf16[2,192,384]{2,1,0:T(8,128)(2,1)S(1)}, u32[]{:S(2)}, u32[]{:S(2)}) collective-permute-start(bf16[2,192,384]{2,1,0:T(8,128)(2,1)} %pad_maximum_fusion.7), channel_id=1, source_target_pairs={{0,8},{1,9},{2,10},{3,11},{4,12},{5,13},{6,14},{7,15},{8,0},{9,1},... | collective-permute-start | bytes 884744 | tf_op jit(solution)/shard_map/ppermute | solution.py:525
  237.9 12.0 %collective-permute-start.29 = (bf16[2,192,384]{2,1,0:T(8,128)(2,1)}, bf16[2,192,384]{2,1,0:T(8,128)(2,1)S(1)}, u32[]{:S(2)}, u32[]{:S(2)}) collective-permute-start(bf16[2,192,384]{2,1,0:T(8,128)(2,1)} %pad_maximum_fusion.8), channel_id=1, source_target_pairs={{0,8},{1,9},{2,10},{3,11},{4,12},{5,13},{6,14},{7,15},{8,0},{9,1},... | collective-permute-start | bytes 884744 | tf_op jit(solution)/shard_map/ppermute | solution.py:525
  242.2 14.0 %collective-permute-start.11 = (bf16[2,192,384]{2,1,0:T(8,128)(2,1)S(1)}, bf16[2,192,384]{2,1,0:T(8,128)(2,1)S(1)}, u32[]{:S(2)}, u32[]{:S(2)}) collective-permute-start(bf16[2,192,384]{2,1,0:T(8,128)(2,1)S(1)} %pad_maximum_fusion.6), channel_id=1, source_target_pairs={{0,8},{1,9},{2,10},{3,11},{4,12},{5,13},{6,14},{7,15},{8,0},{9,1},... | collective-permute-start | bytes 884744 | tf_op jit(solution)/shard_map/ppermute | solution.py:525
  244.3 19.5 %copy-start.8 = (bf16[1,192,384]{2,1,0:T(8,128)(2,1)S(1)}, bf16[1,192,384]{2,1,0:T(8,128)(2,1)}, u32[]{:S(2)}) copy-start(bf16[1,192,384]{2,1,0:T(8,128)(2,1)} %copy-done.7) | copy-start | bytes 442372
  244.3 14.7 %collective-permute-start.21 = (bf16[4,192,384]{2,1,0:T(8,128)(2,1)S(1)}, bf16[4,192,384]{2,1,0:T(8,128)(2,1)S(1)}, u32[]{:S(2)}, u32[]{:S(2)}) collective-permute-start(bf16[4,192,384]{2,1,0:T(8,128)(2,1)S(1)} %pad_maximum_fusion.4), channel_id=1, source_target_pairs={{0,4},{1,3},{2,6},{3,1},{4,0},{5,7},{6,2},{7,5},{8,12},{9,11},{10,... | collective-permute-start | bytes 1769480 | tf_op jit(solution)/shard_map/ppermute | solution.py:525
  250.9 12.8 %collective-permute-start.30 = (bf16[4,192,384]{2,1,0:T(8,128)(2,1)S(1)}, bf16[4,192,384]{2,1,0:T(8,128)(2,1)S(1)}, u32[]{:S(2)}, u32[]{:S(2)}) collective-permute-start(bf16[4,192,384]{2,1,0:T(8,128)(2,1)S(1)} %pad_maximum_fusion.5), channel_id=1, source_target_pairs={{0,4},{1,3},{2,6},{3,1},{4,0},{5,7},{6,2},{7,5},{8,12},{9,11},{10,... | collective-permute-start | bytes 1769480 | tf_op jit(solution)/shard_map/ppermute | solution.py:525
  257.2 9.1 %collective-permute-start.12 = (bf16[4,192,384]{2,1,0:T(8,128)(2,1)S(1)}, bf16[4,192,384]{2,1,0:T(8,128)(2,1)S(1)}, u32[]{:S(2)}, u32[]{:S(2)}) collective-permute-start(bf16[4,192,384]{2,1,0:T(8,128)(2,1)S(1)} %pad_maximum_fusion.3), channel_id=1, source_target_pairs={{0,4},{1,3},{2,6},{3,1},{4,0},{5,7},{6,2},{7,5},{8,12},{9,11},{10,... | collective-permute-start | bytes 1769480 | tf_op jit(solution)/shard_map/ppermute | solution.py:525
  259.1 13.7 %copy-start.2 = (bf16[16,192,384]{2,1,0:T(8,128)(2,1)S(1)}, bf16[16,192,384]{2,1,0:T(8,128)(2,1)}, u32[]{:S(2)}) copy-start(bf16[16,192,384]{2,1,0:T(8,128)(2,1)} %get-tuple-element.104) | copy-start | bytes 7077892
  259.1 13.8 %copy-start.4 = (bf16[16,192,384]{2,1,0:T(8,128)(2,1)S(1)}, bf16[16,192,384]{2,1,0:T(8,128)(2,1)}, u32[]{:S(2)}) copy-start(bf16[16,192,384]{2,1,0:T(8,128)(2,1)} %get-tuple-element.102) | copy-start | bytes 7077892
  259.1 30.4 %collective-permute-start.22 = (bf16[8,192,384]{2,1,0:T(8,128)(2,1)S(1)}, bf16[8,192,384]{2,1,0:T(8,128)(2,1)S(1)}, u32[]{:S(2)}, u32[]{:S(2)}) collective-permute-start(bf16[8,192,384]{2,1,0:T(8,128)(2,1)S(1)} %pad_maximum_fusion.1), channel_id=1, source_target_pairs={{0,2},{1,5},{2,0},{3,7},{4,6},{5,1},{6,4},{7,3},{8,10},{9,13},{10,... | collective-permute-start | bytes 3538952 | tf_op jit(solution)/shard_map/ppermute | solution.py:525
  263.9 38.4 %collective-permute-start.31 = (bf16[8,192,384]{2,1,0:T(8,128)(2,1)S(1)}, bf16[8,192,384]{2,1,0:T(8,128)(2,1)S(1)}, u32[]{:S(2)}, u32[]{:S(2)}) collective-permute-start(bf16[8,192,384]{2,1,0:T(8,128)(2,1)S(1)} %pad_maximum_fusion.2), channel_id=1, source_target_pairs={{0,2},{1,5},{2,0},{3,7},{4,6},{5,1},{6,4},{7,3},{8,10},{9,13},{10,... | collective-permute-start | bytes 3538952 | tf_op jit(solution)/shard_map/ppermute | solution.py:525
  268.4 57.8 %collective-permute-start.13 = (bf16[8,192,384]{2,1,0:T(8,128)(2,1)}, bf16[8,192,384]{2,1,0:T(8,128)(2,1)}, u32[]{:S(2)}, u32[]{:S(2)}) collective-permute-start(bf16[8,192,384]{2,1,0:T(8,128)(2,1)} %pad_maximum_fusion), channel_id=1, source_target_pairs={{0,2},{1,5},{2,0},{3,7},{4,6},{5,1},{6,4},{7,3},{8,10},{9,13},{10,... | collective-permute-start | bytes 3538952 | tf_op jit(solution)/shard_map/ppermute | solution.py:525
  289.8 12.9 %copy-start.3 = (bf16[16,192,384]{2,1,0:T(8,128)(2,1)}, bf16[16,192,384]{2,1,0:T(8,128)(2,1)S(1)}, u32[]{:S(2)}) copy-start(bf16[16,192,384]{2,1,0:T(8,128)(2,1)S(1)} %constant_dynamic-update-slice_fusion.5.chunk) | copy-start | bytes 7077892
  302.5 11.9 %copy-start.5 = (bf16[16,192,384]{2,1,0:T(8,128)(2,1)}, bf16[16,192,384]{2,1,0:T(8,128)(2,1)S(1)}, u32[]{:S(2)}) copy-start(bf16[16,192,384]{2,1,0:T(8,128)(2,1)S(1)} %constant_dynamic-update-slice_fusion.10.chunk) | copy-start | bytes 7077892
  (11 other events, 31.1 us)

commit v2 on v1

--- a/solution.py
+++ b/solution.py
@@ -16,6 +16,58 @@
 BF16 = jnp.bfloat16
 VMEM = pl.BlockSpec(memory_space=pltpu.VMEM)
 SMEM = pl.BlockSpec(memory_space=pltpu.SMEM)
+SPANS = ((0, 4), (4, 2))
+ORDER = (
+    "down.theirs",
+    "down.mine",
+    "down.add0",
+    "up.theirs",
+    "up.mine",
+    "down.add1",
+    "up.add0",
+    "norm",
+    "heads0",
+    "down.add2",
+    "heads1",
+    "up.add1",
+    "down.add3",
+    "rest1.add0",
+    "rest0.add0",
+    "up.add2",
+    "down.sum",
+    "input",
+    "up.add3",
+    "down.join3",
+    "rest0.add1",
+    "rest1.add1",
+    "small.theirs",
+    "up.sum",
+    "rest0.add2",
+    "down.join2",
+    "rest1.add2",
+    "small.mine",
+    "up.join3",
+    "rest0.add3",
+    "down.join1",
+    "small.sum0",
+    "rest1.add3",
+    "rest0.sum",
+    "up.join2",
+    "rest1.sum",
+    "small.sum1",
+    "rest0.join3",
+    "small.sum2",
+    "rest1.join3",
+    "rest0.join2",
+    "small.sum3",
+    "up.join1",
+    "rest1.join2",
+    "rest0.join1",
+    "down.final",
+    "rest1.join1",
+    "up.final",
+    "rest.final",
+)
 LANES = 384
 TILE = 64
 
@@ -28,12 +80,14 @@
     return jax.ShapeDtypeStruct(shape, dtype)
 
 
-def call(body, out_shape, ins, flops, scratch=(), grid_spec=None, in_specs=None, out_specs=None):
+def call(
+    body, out_shape, ins, flops, scratch=(), grid_spec=None, in_specs=None, out_specs=None, limit=None
+):
     nbytes = sum(a.size * a.dtype.itemsize for a in ins)
     nbytes += sum(o.size * o.dtype.itemsize for o in jax.tree.leaves(out_shape))
     params = dict(
         out_shape=out_shape,
-        compiler_params=pltpu.CompilerParams(vmem_limit_bytes=56 << 20),
+        compiler_params=pltpu.CompilerParams(vmem_limit_bytes=limit or (nbytes + (6 << 20))),
         cost_estimate=pl.CostEstimate(flops=int(flops), bytes_accessed=nbytes, transcendentals=0),
     )
     if grid_spec is not None:
@@ -144,61 +198,73 @@
 
 
 def backward_heads_body(
+    heads,
+    which,
     ids,
     lengths,
-    which,
     xq,
-    q_ref,
-    k_ref,
-    v_ref,
-    c_ref,
-    lse_ref,
-    merge_q,
     grad_branch,
-    chunk,
-    d_ref,
-    qv_row,
+    other_half,
+    own_half,
+    theirs,
+    mine,
+    d_other,
+    d_own,
+    qv_other,
+    qv_own,
     bias_ref,
     g_ref,
     x_t,
 ):
-    rel = ids[which[0]]
-    blocks = chunk.shape[0]
     bias_ref[...] = key_bias(lengths, ids[2])
     x_t[...] = xq[...].T
-    g_ref[...] = dot(merge_q[...], grad_branch[...], 1, 1).astype(BF16)
-    width = q_ref.shape[0]
-
-    def head(index, carry):
-        at = pl.ds(pl.multiple_of(index * HEAD, HEAD), HEAD)
-        q, k, v, g = q_ref[at, :], k_ref[at, :], v_ref[at, :], g_ref[at, :]
-        scores = dot(k, q, 0, 0) + bias_ref[...]
-        prob = jnp.exp(scores - lse_ref[pl.ds(index, 1), :])
-        grad_prob = dot(v, g, 0, 0)
-        inner = jnp.sum(g.astype(F32) * c_ref[at, :].astype(F32), axis=0, keepdims=True)
-        grad_score = (prob * (grad_prob - inner)).astype(BF16)
-        d_ref[2, at, :] = dot(g, prob.astype(BF16), 1, 1).astype(BF16)
-        d_ref[0, at, :] = (dot(k, grad_score, 1, 0) * 0.125).astype(BF16)
-        d_ref[1, at, :] = dot(q, grad_score, 1, 1).astype(BF16)
-        return carry
-
-    lax.fori_loop(0, width // HEAD, head, 0)
-    rows = x_t.shape[0] // blocks
-    base = 3 * rows
-    for part in range(3):
-        grad = dot(x_t[...], d_ref[part], 1, 1)
+    ones = jnp.ones((8, xq.shape[0]), BF16)
+    start, count = heads
+    width = count * HEAD
+    for half, rel, chunk, d_ref, qv_row in (
+        (other_half, ids[which[1]], theirs, d_other, qv_other),
+        (own_half, ids[which[0]], mine, d_own, qv_own),
+    ):
+        q_ref, k_ref, v_ref, c_ref, lse_ref, merge_q = half
+        blocks = chunk.shape[0]
+        span = slice(start * HEAD, start * HEAD + width)
+        g_ref[...] = dot(merge_q[span, :], grad_branch[...], 1, 1).astype(BF16)
+
+        def head(index, carry):
+            to = pl.ds(pl.multiple_of(index * HEAD, HEAD), HEAD)
+            at = pl.ds(pl.multiple_of((index + start) * HEAD, HEAD), HEAD)
+            q, k, v, g = q_ref[at, :], k_ref[at, :], v_ref[at, :], g_ref[to, :]
+            scores = dot(k, q, 0, 0) + bias_ref[...]
+            prob = jnp.exp(scores - lse_ref[pl.ds(index + start, 1), :])
+            grad_prob = dot(v, g, 0, 0)
+            inner = jnp.sum(g.astype(F32) * c_ref[at, :].astype(F32), axis=0, keepdims=True)
+            grad_score = (prob * (grad_prob - inner)).astype(BF16)
+            d_ref[2, to, :] = dot(g, prob.astype(BF16), 1, 1).astype(BF16)
+            d_ref[0, to, :] = (dot(k, grad_score, 1, 0) * 0.125).astype(BF16)
+            d_ref[1, to, :] = dot(q, grad_score, 1, 1).astype(BF16)
+            return carry
+
+        lax.fori_loop(0, count, head, 0)
+        rows = x_t.shape[0] // blocks
+        for part in range(3):
+            grad = dot(x_t[...], d_ref[part], 1, 1)
+            for block in range(blocks):
+                piece = grad[block * rows : (block + 1) * rows, :]
+                chunk[block ^ rel, part * rows : (part + 1) * rows, :] = piece.astype(BF16)
+        qv_row[:, 0:width] = dot(ones, d_ref[0], 1, 1)
+        qv_row[:, width : 2 * width] = dot(ones, d_ref[2], 1, 1)
+        grad = dot(c_ref[span, :], grad_branch[...], 1, 0)
+        step = width // blocks
         for block in range(blocks):
-            piece = grad[block * rows : (block + 1) * rows, :]
-            chunk[block ^ rel, part * rows : (part + 1) * rows, :] = piece.astype(BF16)
-    ones = jnp.ones((8, xq.shape[0]), BF16)
-    qv_row[:, 0:LANES] = dot(ones, d_ref[0], 1, 1)
-    qv_row[:, LANES : 2 * LANES] = dot(ones, d_ref[2], 1, 1)
-    grad = dot(c_ref[...], grad_branch[...], 1, 0)
-    step = width // blocks
-    for block in range(blocks):
-        piece = grad[block * step : (block + 1) * step, :]
-        piece = jnp.concatenate([piece[:, :LANES], piece[:, LANES:]], axis=0)
-        chunk[block ^ rel, base : base + 2 * step, :] = piece.astype(BF16)
+            piece = grad[block * step : (block + 1) * step, :]
+            pieces = [piece[:, i * width : (i + 1) * width] for i in range(piece.shape[1] // width)]
+            piece = jnp.concatenate(pieces, axis=0)
+            chunk[block ^ rel, 3 * rows : 3 * rows + piece.shape[0], :] = piece.astype(BF16)
+
+
+def backward_heads(heads, which, *refs):
+    ids, lengths, xq, grad_branch = refs[:4]
+    backward_heads_body(heads, which, ids, lengths, xq, grad_branch, refs[4:10], refs[10:16], *refs[16:])
 
 
 ERF_P = 0.3275911 * 0.7071067811865476
@@ -337,8 +403,8 @@
     sums[6:8, :] = jnp.zeros((2, sums.shape[1]), F32)
 
 
-def down_grad_body(ids, which, active, grad_feed, chunk):
-    rel = ids[which[0]]
+def down_grad_body(which, ids, active, grad_feed, chunk):
+    rel = ids[which]
     blocks = chunk.shape[0]
     rows = active.shape[1] // blocks
     per = blocks // 4
@@ -357,9 +423,9 @@
 
 
 def up_grad_body(
-    ids, which, grad_feed, down, up, factor, normed_q, before, chunk, bias_row, grad_normed, g_ref
+    which, ids, grad_feed, down, up, factor, normed_q, before, chunk, bias_row, grad_normed, g_ref
 ):
-    rel = ids[which[0]]
+    rel = ids[which]
     blocks = chunk.shape[0]
     span = 512
 
@@ -393,10 +459,10 @@
 
 
 def up_grad_first_body(
-    ids, which, grad_feed, down, up, factor, normed_q, chunk, bias_row, grad_normed, g_ref
+    which, ids, grad_feed, down, up, factor, normed_q, chunk, bias_row, grad_normed, g_ref
 ):
     up_grad_body(
-        ids, which, grad_feed, down, up, factor, normed_q, None, chunk, bias_row, grad_normed, g_ref
+        which, ids, grad_feed, down, up, factor, normed_q, None, chunk, bias_row, grad_normed, g_ref
     )
 
 
@@ -451,12 +517,15 @@
         pack[12:15, :] = sums[3:6, :]
 
 
-def input_grad_body(clips, inputs, d_own, d_other, w_own, w_other, grad_first, out):
+def input_grad_body(spans, clips, inputs, grad_first, w_own, w_other, *refs):
+    out = refs[-1]
     total = None
-    for d_ref, weight in ((d_own, w_own), (d_other, w_other)):
-        for part in range(3):
-            term = dot(d_ref[part], weight[part], 0, 1)
-            total = term if total is None else total + term
+    for (start, count), d_own, d_other in zip(spans, refs[0:-1:2], refs[1:-1:2]):
+        span = slice(start * HEAD, (start + count) * HEAD)
+        for d_ref, weight in ((d_own, w_own), (d_other, w_other)):
+            for part in range(3):
+                term = dot(d_ref[part], weight[part, :, span], 0, 1)
+                total = term if total is None else total + term
     bent = jnp.tanh(inputs[...].astype(F32) / clips[0])
     out[...] = total * (1.0 - bent * bent) + grad_first[...]
 
@@ -466,86 +535,208 @@
     return 1.0 - bent * bent
 
 
-def down_final_body(ids, own, other, chunk, weight, out):
-    rows = weight.shape[0]
-    value = chunk[0].astype(F32)
-    slope = slope_of(weight[...], scale_row(own, other, 5, weight.shape[1]))
-    out[:, :LANES] = value[:rows] * slope[:, :LANES]
-    out[:, LANES:] = value[rows:] * slope[:, LANES:]
-
-
-def up_final_body(ids, own, other, chunk, weight, out):
-    rows = weight.shape[0]
-    value = chunk[0].astype(F32)
-    slope = slope_of(weight[...], scale_row(own, other, 4, weight.shape[1]))
-    for part in range(weight.shape[1] // LANES):
-        cols = slice(part * LANES, (part + 1) * LANES)
-        out[:, cols] = value[part * rows : (part + 1) * rows] * slope[:, cols]
-
-
-def rest_final_body(ids, own, other, chunk, project, merge, project_out, merge_out):
-    rows = project.shape[1]
-    step = merge.shape[1]
-    value = chunk[0].astype(F32)
-    for part in range(3):
-        slope = slope_of(project[part], scale_row(own, other, part, LANES))
-        project_out[part] = value[part * rows : (part + 1) * rows] * slope
-    slope = slope_of(merge[0], scale_row(own, other, 3, merge.shape[2]))
-    base = 3 * rows
-    merge_out[0, :, :LANES] = value[base : base + step] * slope[:, :LANES]
-    merge_out[0, :, LANES:] = value[base + step : base + 2 * step] * slope[:, LANES:]
+def pieces_of(rel, lows, highs, per, body):
+    step = pl.program_id(0)
+    half = lows[0].shape[0]
+
+    def block(index, carry):
+        at = (step * per + index) ^ rel
+        low = jnp.minimum(at, half - 1)
+        high = jnp.maximum(at - half, 0)
+        first = at < half
+        values = []
+        for lo, hi in zip(lows, highs):
+            values.append(jnp.where(first, lo[low].astype(F32), hi[high].astype(F32)))
+        body(index, values)
+        return carry
+
+    lax.fori_loop(0, per, block, 0)
+
+
+def down_final_body(per, which, ids, own, other, *refs):
+    weight, out = refs[-2:]
+    rows = weight.shape[0] // per
+    scale = scale_row(own, other, 5, weight.shape[1])
+
+    def block(index, values):
+        at = pl.ds(pl.multiple_of(index * rows, 16), rows)
+        slope = slope_of(weight[at, :], scale)
+        value = jnp.concatenate(values, axis=0)
+        out[at, :LANES] = value[:rows] * slope[:, :LANES]
+        out[at, LANES:] = value[rows:] * slope[:, LANES:]
+
+    pieces_of(ids[which], refs[0:-2:2], refs[1:-2:2], per, block)
+
+
+def up_final_body(per, which, ids, own, other, *refs):
+    weight, out = refs[-2:]
+    rows = weight.shape[0] // per
+    scale = scale_row(own, other, 4, weight.shape[1])
+
+    def block(index, values):
+        at = pl.ds(pl.multiple_of(index * rows, 16), rows)
+        slope = slope_of(weight[at, :], scale)
+        value = jnp.concatenate(values, axis=0)
+        for part in range(weight.shape[1] // LANES):
+            cols = slice(part * LANES, (part + 1) * LANES)
+            out[at, cols] = value[part * rows : (part + 1) * rows] * slope[:, cols]
+
+    pieces_of(ids[which], refs[0:-2:2], refs[1:-2:2], per, block)
+
+
+def rest_final_body(per, spans, which, ids, own, other, *refs):
+    groups = len(spans)
+    lows, highs = refs[0 : 2 * groups : 2], refs[1 : 2 * groups : 2]
+    project = refs[2 * groups]
+    merges = refs[2 * groups + 1 : 3 * groups + 1]
+    project_out = refs[3 * groups + 1]
+    merge_outs = refs[3 * groups + 2 :]
+    rows = project.shape[1] // per
+    project_scales = [scale_row(own, other, part, LANES) for part in range(3)]
+    merge_scale = scale_row(own, other, 3, merges[0].shape[2])
+
+    def block(index, values):
+        at = pl.ds(pl.multiple_of(index * rows, 16), rows)
+        slopes = [slope_of(project[part, at, :], project_scales[part]) for part in range(3)]
+        for (start, count), value, merge, merge_out in zip(spans, values, merges, merge_outs):
+            cols = slice(start * HEAD, (start + count) * HEAD)
+            for part in range(3):
+                piece = value[part * rows : (part + 1) * rows]
+                project_out[part, at, cols] = piece * slopes[part][:, cols]
+            slope = slope_of(merge[index], merge_scale)
+            step, width = merge.shape[1], count * HEAD
+            for part in range(merge.shape[2] // width):
+                piece = value[3 * rows + part * step : 3 * rows + (part + 1) * step]
+                across = slice(part * width, (part + 1) * width)
+                merge_out[index, :, across] = piece * slope[:, across]
+
+    pieces_of(ids[which], lows, highs, per, block)
 
 
 class Exchange:
-    def __init__(self, size):
+    def __init__(self, size, first):
         self.bits = size.bit_length() - 1
-        assert 1 << self.bits == size
+        assert 1 << self.bits == size and self.bits >= 4
         self.size = size
-        order = list(range(self.bits))
-        turned = order[:]
-        if self.bits > 1:
-            turned[0], turned[1] = 1, 0
-        self.orders = (order, turned)
-        self.halvings = min(self.bits, 4)
-        self.blocks = 1 << self.halvings
+        self.orders = [list(order) + list(range(4, self.bits)) for order in first]
+        self.blocks = 16
 
     def relative(self, position, core):
         total = 0
-        for stage in range(self.halvings):
+        for stage in range(4):
             bit = (position >> self.orders[core][stage]) & 1
-            total = total + (bit << (self.halvings - 1 - stage))
+            total = total + (bit << (3 - stage))
         return total
 
-    def swap(self, value, stage, same=False):
+    def swap(self, value, stage):
         pairs = []
         for index in range(self.size):
             for core in range(2):
-                to = index ^ (1 << self.orders[0 if same else core][stage])
+                to = index ^ (1 << self.orders[core][stage])
                 pairs.append((2 * index + core, 2 * to + core))
         return lax.ppermute(value, ("dp", "tensor"), pairs)
 
     def core_swap(self, value):
         return lax.ppermute(value, "tensor", [(0, 1), (1, 0)])
 
-    def reduce(self, mine, received):
-        terms = [mine, received]
-        count = self.blocks
-
-        def add(lo, hi):
-            total = terms[0][lo:hi].astype(F32)
-            for term in terms[1:]:
-                total = total + term[lo:hi].astype(F32)
-            return total.astype(BF16)
-
-        for stage in range(self.halvings):
+
+class Task:
+    def __init__(self, body, deps):
+        self.body, self.deps, self.sends = body, list(deps), []
+
+
+class Plan:
+    def __init__(self):
+        self.tasks = {}
+        self.values = {}
+        self.source = {}
+
+    def given(self, name, value):
+        self.values[name] = value
+        return name
+
+    def core(self, name, body, deps):
+        self.tasks[name] = Task(body, deps)
+        return name
+
+    def send(self, name, source, body):
+        self.tasks[source].sends.append((name, body))
+        self.source[name] = source
+        return name
+
+    def run(self):
+        values, last = dict(self.values), None
+
+        def take(name):
+            nonlocal last
+            if name in values:
+                return
+            if name in self.source:
+                take(self.source[name])
+                return
+            task = self.tasks[name]
+            for dep in task.deps:
+                take(dep)
+            inputs = [values[dep] for dep in task.deps]
+            if last is not None:
+                inputs, last = lax.optimization_barrier((inputs, last))
+            with jax.named_scope(name.replace(".", "_")):
+                result = task.body(*inputs)
+            values[name] = result
+            last = jax.tree.leaves(result)[0]
+            for sent, body in task.sends:
+                with jax.named_scope(sent.replace(".", "_")):
+                    values[sent] = body(result)
+
+        for name in ORDER:
+            if name in self.tasks:
+                take(name)
+        for name in self.tasks:
+            take(name)
+        return values
+
+    def reduce(self, name, way, mine, theirs, pick_mine, pick_theirs):
+        half = way.blocks // 2
+        high = self.send(name + ".high", theirs, lambda v: way.core_swap(pick_theirs(v)[half:]))
+        low = self.send(name + ".low", theirs, lambda v: way.core_swap(pick_theirs(v)[:half]))
+
+        def total(values):
+            out = values[0].astype(F32)
+            for value in values[1:]:
+                out = out + value.astype(F32)
+            return out.astype(BF16)
+
+        def cut(lo, hi):
+            def body(mine, *others):
+                return total([pick_mine(mine)[lo:hi]] + [other[lo:hi] for other in others])
+
+            return body
+
+        def first(mine, high):
+            return total([pick_mine(mine)[half:], high])
+
+        def join(value, other):
+            return jnp.concatenate([value, other], axis=0)
+
+        def swap(stage):
+            return lambda value: way.swap(value, stage)
+
+        terms, count = [mine, low], half
+        value = self.core(f"{name}.add0", first, [mine, high])
+        for stage in range(4):
+            if stage > 0:
+                value = self.core(f"{name}.add{stage}", cut(count, 2 * count), terms)
+            terms.append(self.send(f"{name}.in{stage}", value, swap(stage)))
             count //= 2
-            terms.append(self.swap(add(count, 2 * count), stage))
-        value = add(0, 1)
-        for stage in range(self.halvings, self.bits):
-            value = (value.astype(F32) + self.swap(value, stage).astype(F32)).astype(BF16)
-        for stage in reversed(range(self.halvings)):
-            value = jnp.concatenate([value, self.swap(value, stage)], axis=0)
-        return value
+        value = self.core(f"{name}.sum", cut(0, 1), terms)
+        for stage in range(4, way.bits):
+            sent = self.send(f"{name}.in{stage}", value, swap(stage))
+            value = self.core(f"{name}.sum{stage}", lambda a, b: total([a, b]), [value, sent])
+        for stage in reversed(range(4)):
+            sent = self.send(f"{name}.out{stage}", value, swap(stage))
+            if stage > 0:
+                value = self.core(f"{name}.join{stage}", join, [value, sent])
+        return [value, sent]
 
 
 def local(
@@ -564,7 +755,9 @@
     clip_scales,
     cotangent,
 ):
-    exchange = Exchange(lax.axis_size("dp"))
+    size = lax.axis_size("dp")
+    exchange = Exchange(size, ((0, 1, 2, 3), (1, 0, 2, 3)))
+    same_way = Exchange(size, ((0, 1, 2, 3), (0, 1, 2, 3)))
     blocks = exchange.blocks
     member = lax.axis_index("tensor")
     place = lax.axis_index("dp")
@@ -572,8 +765,6 @@
     own_rel = jnp.where(member == 0, rel0, rel1)
     other_rel = jnp.where(member == 0, rel1, rel0)
     ids = jnp.stack([own_rel, other_rel, member * (LONG // SHORT)]).astype(jnp.int32)
-    own_id = jnp.zeros((1,), jnp.int32)
-    other_id = jnp.ones((1,), jnp.int32)
     total, width = inputs.shape
     hidden = up_weight.shape[1]
     project = jnp.transpose(project_weight, (1, 0, 2))
@@ -592,6 +783,7 @@
         ],
         out_specs=pl.BlockSpec((16, hidden), lambda i: (0, 0)),
         out_shape=shaped((16, hidden), F32),
+        compiler_params=pltpu.CompilerParams(vmem_limit_bytes=16 << 20),
     )(project, merge_weight, up_weight, down_weight, query_value_bias, up_bias[None])
     other_pack = exchange.core_swap(own_pack)
     pack_spec = pl.BlockSpec((16, hidden), lambda i: (0, 0))
@@ -602,6 +794,7 @@
         in_specs=[pack_spec, pack_spec, project_block],
         out_specs=project_block,
         out_shape=shaped(project.shape, BF16),
+        compiler_params=pltpu.CompilerParams(vmem_limit_bytes=16 << 20),
     )(own_pack, other_pack, project)
     project_other = exchange.core_swap(project_own)
     rest_blocks = [
@@ -615,6 +808,7 @@
         in_specs=[pack_spec, pack_spec] + rest_blocks,
         out_specs=rest_blocks,
         out_shape=[shaped(a.shape, BF16) for a in (merge_weight, up_weight, down_weight)],
+        compiler_params=pltpu.CompilerParams(vmem_limit_bytes=20 << 20),
     )(own_pack, other_pack, merge_weight, up_weight, down_weight)
     merge_other = exchange.core_swap(merge_own)
     up_other = exchange.core_swap(up_own)
@@ -632,6 +826,7 @@
         [mask_scratch],
         in_specs=[SMEM] * 3 + [VMEM] * 3,
         out_specs=[VMEM] * 6,
+        limit=16 << 20,
     )
     other_heads = call(
         forward_second_body,
@@ -641,6 +836,7 @@
         [mask_scratch],
         in_specs=[SMEM] * 2 + [VMEM] * 3,
         out_specs=[VMEM] * 5,
+        limit=16 << 20,
     )
 
     vectors = jnp.concatenate([merge_bias[None], down_bias[None], norm_gains, norm_shifts], axis=0)
@@ -699,151 +895,237 @@
         ],
         in_specs=[SMEM] + [VMEM] * 13,
         out_specs=[VMEM] * 11,
-    )
-
-    chunk_shape = shaped((blocks, 2 * hidden // blocks, LANES), BF16)
-
-    def down_half(which, active):
+        limit=40 << 20,
+    )
+
+    plan = Plan()
+    chunk_shape = (blocks, 2 * hidden // blocks, LANES)
+    chunk = shaped(chunk_shape, BF16)
+
+    def down_half(which, active, grad):
         return call(
-            down_grad_body,
-            chunk_shape,
-            (ids, which, active, grad_feed),
+            partial(down_grad_body, which),
+            chunk,
+            (ids, active, grad),
             2 * total * width * hidden,
-            in_specs=[SMEM] * 2 + [VMEM] * 2,
+            in_specs=[SMEM] + [VMEM] * 2,
             out_specs=VMEM,
         )
 
-    down_got = exchange.core_swap(down_half(other_id, active_other))
-    down_rel = exchange.reduce(down_half(own_id, active_own), down_got)
-
-    def up_half(body, which, down, up, factor, *before):
+    feed = plan.given("feed", grad_feed)
+    down_theirs = plan.core(
+        "down.theirs",
+        lambda grad: down_half(1, active_other, grad),
+        [feed],
+    )
+    down_mine = plan.core(
+        "down.mine", lambda grad: down_half(0, active_own, grad), [feed]
+    )
+
+    def same(value):
+        return value
+
+    def take(index):
+        return lambda values: values[index]
+
+    down_out = plan.reduce("down", exchange, down_mine, down_theirs, same, same)
+
+    def up_half(body, which, grad, down, up, factor, *before):
         return call(
-            body,
-            [chunk_shape, shaped((1, hidden), F32), rows_f32],
-            (ids, which, grad_feed, down, up, factor, normed_q) + before,
+            partial(body, which),
+            [chunk, shaped((1, hidden), F32), rows_f32],
+            (ids, grad, down, up, factor, normed_q) + before,
             2 * total * width * hidden * 3,
             [pltpu.VMEM((total, hidden), BF16)],
-            in_specs=[SMEM] * 2 + [VMEM] * (5 + len(before)),
+            in_specs=[SMEM] + [VMEM] * (5 + len(before)),
             out_specs=[VMEM] * 3,
+            limit=22 << 20,
         )
 
-    up_theirs, bias_other, partial_normed = up_half(
-        up_grad_first_body, other_id, down_other, up_other, factor_other
-    )
-    up_got = exchange.core_swap(up_theirs)
-    up_mine, bias_own, grad_normed = up_half(
-        up_grad_body, own_id, down_own, up_own, factor_own, partial_normed
-    )
-    up_rel = exchange.reduce(up_mine, up_got)
+    up_theirs = plan.core(
+        "up.theirs",
+        lambda grad: up_half(
+            up_grad_first_body, 1, grad, down_other, up_other, factor_other
+        ),
+        [feed],
+    )
+    up_mine = plan.core(
+        "up.mine",
+        lambda grad, before: up_half(
+            up_grad_body, 0, grad, down_own, up_own, factor_own, before[2]
+        ),
+        [feed, up_theirs],
+    )
+    up_out = plan.reduce("up", exchange, up_mine, up_theirs, take(0), take(0))
 
     small = shaped((16, width), F32)
-    grad_first, grad_branch, small_theirs, small_mine = call(
-        first_norm_back_body,
-        [rows_f32, rows_bf16, small, small],
-        (clip_scales, grad_normed, grad_sum, unit, inverse, vectors, sums, bias_other, bias_own),
-        2 * total * width * 1000,
-        [pltpu.VMEM((3, 8, width), F32)],
-        in_specs=[SMEM] + [VMEM] * 8,
-        out_specs=[VMEM] * 4,
-    )
-
-    def heads_half(which, heads, merge_q):
+
+    def norm_back(theirs, mine):
+        ins = (clip_scales, mine[2], grad_sum, unit, inverse, vectors, sums, theirs[1], mine[1])
         return call(
-            backward_heads_body,
-            [
-                chunk_shape,
-                shaped((3, LANES, total), BF16),
-                shaped((8, 2 * LANES), F32),
-            ],
-            (ids, row_lengths, which, xq) + tuple(heads) + (merge_q, grad_branch),
-            heads_flops * 2,
-            [
-                mask_scratch,
-                pltpu.VMEM((LANES, total), BF16),
-                pltpu.VMEM((width, total), BF16),
-            ],
-            in_specs=[SMEM] * 3 + [VMEM] * 8,
-            out_specs=[VMEM] * 3,
+            first_norm_back_body,
+            [rows_f32, rows_bf16, small, small],
+            ins,
+            2 * total * width * 1000,
+            [pltpu.VMEM((3, 8, width), F32)],
+            in_specs=[SMEM] + [VMEM] * 8,
+            out_specs=[VMEM] * 4,
         )
 
-    rest_theirs, d_other, qv_other = heads_half(other_id, other_heads, merge_other)
-    rest_got = exchange.core_swap(rest_theirs)
-    rest_mine, d_own, qv_own = heads_half(own_id, own_heads, merge_own)
-    rest_rel = exchange.reduce(rest_mine, rest_got)
-    input_grad = call(
-        input_grad_body,
-        rows_f32,
-        (clip_scales, inputs, d_own, d_other, project_own, project_other, grad_first),
-        2 * total * width * 6 * LANES,
-        in_specs=[SMEM] + [VMEM] * 6,
-        out_specs=VMEM,
-    )
-
-    def joined(sums_part, qv_row):
-        return jnp.concatenate([sums_part[:8], qv_row[:1], sums_part[12:15]], axis=0)
-
-    row = lax.broadcasted_iota(jnp.int32, (12, width), 0)
+    first_back = plan.core("norm", norm_back, [up_theirs, up_mine])
+
+    spans = SPANS
+    groups = []
+    for group, (start, count) in enumerate(spans):
+        span_width = count * HEAD
+        group_shape = (blocks, 3 * width // blocks + LANES * 2 // blocks, span_width)
+
+        def heads_back(back, heads=(start, count), group_shape=group_shape):
+            grads = shaped((3, group_shape[2], total), BF16)
+            row = shaped((8, 2 * group_shape[2]), F32)
+            travel = shaped(group_shape, BF16)
+            halves = tuple(other_heads) + (merge_other,) + tuple(own_heads) + (merge_own,)
+            return call(
+                partial(backward_heads, heads, (0, 1)),
+                [travel, travel, grads, grads, row, row],
+                (ids, row_lengths, xq, back[1]) + halves,
+                heads_flops * 4,
+                [
+                    mask_scratch,
+                    pltpu.VMEM((group_shape[2], total), BF16),
+                    pltpu.VMEM((width, total), BF16),
+                ],
+                in_specs=[SMEM] * 2 + [VMEM] * 14,
+                out_specs=[VMEM] * 6,
+                limit=24 << 20,
+            )
+
+        heads_task = plan.core(f"heads{group}", heads_back, [first_back])
+        groups.append(heads_task)
+    outs = []
+    for group, task in enumerate(groups):
+        outs += plan.reduce(f"rest{group}", exchange, task, task, take(1), take(0))
+
+    def input_part(back, *results):
+        pairs = []
+        for result in results:
+            pairs += [result[3], result[2]]
+        return call(
+            partial(input_grad_body, spans),
+            rows_f32,
+            (clip_scales, inputs, back[0], project_own, project_other) + tuple(pairs),
+            2 * total * width * 6 * LANES,
+            in_specs=[SMEM] + [VMEM] * (4 + len(pairs)),
+            out_specs=VMEM,
+            limit=20 << 20,
+        )
+
+    input_task = plan.core("input", input_part, [first_back] + groups)
+
+    def joined(sums_part, rows):
+        qv = [row[0:1, : row.shape[1] // 2] for row in rows]
+        qv += [row[0:1, row.shape[1] // 2 :] for row in rows]
+        return jnp.concatenate(
+            [sums_part[:8], jnp.concatenate(qv, axis=1), sums_part[12:15]], axis=0
+        )
+
+    small_row = lax.broadcasted_iota(jnp.int32, (12, width), 0)
 
     def merge_small(a, b):
-        return jnp.where(row < 9, a + b, jnp.maximum(a, b))
-
-    small_all = joined(small_mine, qv_own)
-    small_all = merge_small(small_all, exchange.core_swap(joined(small_theirs, qv_other)))
+        return jnp.where(small_row < 9, a + b, jnp.maximum(a, b))
+
+    theirs_small = plan.core(
+        "small.theirs",
+        lambda back, *results: joined(back[2], [result[4] for result in results]),
+        [first_back] + groups,
+    )
+    small_got = plan.send("small.got", theirs_small, exchange.core_swap)
+    small_value = plan.core(
+        "small.mine",
+        lambda got, back, *results: merge_small(
+            joined(back[3], [result[5] for result in results]), got
+        ),
+        [small_got, first_back] + groups,
+    )
     for stage in range(exchange.bits):
-        small_all = merge_small(small_all, exchange.swap(small_all, stage, same=True))
-
-    def final(body, rel, weights, weight_specs, out_shapes, out_specs):
+        swap = partial(same_way.swap, stage=stage)
+        small_in = plan.send(f"small.in{stage}", small_value, swap)
+        small_value = plan.core(f"small.sum{stage}", merge_small, [small_value, small_in])
+
+    final_steps = 4
+    per = blocks // final_steps
+
+    def final(body, parts, weights, weight_specs, out_shapes, out_specs):
+        part_specs = [pl.BlockSpec(part.shape, lambda i, s: (0, 0, 0)) for part in parts]
         spec = pltpu.PrefetchScalarGridSpec(
             num_scalar_prefetch=1,
-            grid=(blocks,),
-            in_specs=[
-                pl.BlockSpec((16, hidden), lambda i, s: (0, 0)),
-                pl.BlockSpec((16, hidden), lambda i, s: (0, 0)),
-                pl.BlockSpec((1,) + rel.shape[1:], lambda i, s: (i ^ s[0], 0, 0)),
-            ]
+            grid=(final_steps,),
+            in_specs=[pl.BlockSpec((16, hidden), lambda i, s: (0, 0))] * 2
+            + part_specs
             + weight_specs,
             out_specs=out_specs,
         )
-        return call(
-            body,
-            out_shapes,
-            (ids, own_pack, other_pack, rel) + weights,
-            1,
-            grid_spec=spec,
+        ins = (ids, own_pack, other_pack) + tuple(parts) + weights
+        return call(body, out_shapes, ins, 1, grid_spec=spec, limit=16 << 20)
+
+    down_spec = pl.BlockSpec((hidden // final_steps, width), lambda i, s: (i, 0))
+
+    def down_final(*parts):
+        return final(
+            partial(down_final_body, per, 0),
+            parts,
+            (down_weight,),
+            [down_spec],
+            shaped(down_weight.shape, F32),
+            down_spec,
         )
 
-    down_spec = pl.BlockSpec((hidden // blocks, width), lambda i, s: (i, 0))
-    down_grad = final(
-        down_final_body,
-        down_rel,
-        (down_weight,),
-        [down_spec],
-        shaped(down_weight.shape, F32),
-        down_spec,
-    )
-    up_spec = pl.BlockSpec((width // blocks, hidden), lambda i, s: (i, 0))
-    up_grad = final(
-        up_final_body, up_rel, (up_weight,), [up_spec], shaped(up_weight.shape, F32), up_spec
-    )
-    project_spec = pl.BlockSpec((3, width // blocks, LANES), lambda i, s: (0, i, 0))
-    merge_spec = pl.BlockSpec((1, LANES // blocks, width), lambda i, s: (i, 0, 0))
-    merge_parts = merge_weight.reshape(blocks, LANES // blocks, width)
-    project_grad, merge_grad = final(
-        rest_final_body,
-        rest_rel,
-        (project, merge_parts),
-        [project_spec, merge_spec],
-        [shaped(project.shape, F32), shaped(merge_parts.shape, F32)],
-        [project_spec, merge_spec],
-    )
+    up_spec = pl.BlockSpec((width // final_steps, hidden), lambda i, s: (i, 0))
+
+    def up_final(*parts):
+        return final(
+            partial(up_final_body, per, 0),
+            parts,
+            (up_weight,),
+            [up_spec],
+            shaped(up_weight.shape, F32),
+            up_spec,
+        )
+
+    project_spec = pl.BlockSpec((3, width // final_steps, LANES), lambda i, s: (0, i, 0))
+    merges, merge_specs = [], []
+    for start, count in spans:
+        part = merge_weight[start * HEAD : (start + count) * HEAD]
+        merges.append(part.reshape(blocks, count * HEAD // blocks, width))
+        merge_specs.append(
+            pl.BlockSpec((per, count * HEAD // blocks, width), lambda i, s: (i, 0, 0))
+        )
+
+    def rest_final(*parts):
+        return final(
+            partial(rest_final_body, per, spans, 0),
+            parts,
+            (project,) + tuple(merges),
+            [project_spec] + merge_specs,
+            [shaped(project.shape, F32)] + [shaped(part.shape, F32) for part in merges],
+            [project_spec] + merge_specs,
+        )
+
+    plan.core("down.final", down_final, down_out)
+    plan.core("up.final", up_final, up_out)
+    plan.core("rest.final", rest_final, outs)
+    values = plan.run()
+    small_all = values[small_value]
+    project_grad, *merge_grads = values["rest.final"]
+    merge_grads = [part.reshape(-1, width) for part in merge_grads]
     peaks = small_all[9:12, 0]
     return (
         output,
-        input_grad,
+        values[input_task],
         jnp.transpose(project_grad, (1, 0, 2)),
-        merge_grad.reshape(merge_weight.shape),
-        up_grad,
-        down_grad,
+        jnp.concatenate(merge_grads, axis=0),
+        values["up.final"],
+        values["down.final"],
         small_all[8].reshape(2, LANES),
         small_all[4],
         small_all[6:8].reshape(hidden),

time: 343 us -> 233 us (0.68)
  Pallas kernels: 160 us -> 106 us
  waiting for transfers between devices: 83.7 us -> 50.8 us
  other arithmetic: 32 us -> 4.94 us
  local copies, waits for them, and re-layouts: 13.4 us -> 19.4 us
    ppermute x28 -> x36, waiting for transfers between devices: 82.2 us -> 49.4 us  [swap(): return lax.ppermute(value, ('dp', 'tensor'), pairs)]
    pallas_call x11, Pallas kernels: 111 us -> 84.8 us  [call(): pl.pallas_call(body, in_specs=in_specs, out_specs=out_specs, scratch_shap...]
    pallas_call x3, Pallas kernels: 35.2 us -> 14.4 us  [call(): return pl.pallas_call(body, grid_spec=grid_spec, **params)(*ins)]
    convert_element_type x12 -> x20, other arithmetic: 16.9 us -> 2.73 us  [total(): return out.astype(BF16)]
    ppermute x28 -> x36, starting transfers between devices: 48.1 us -> 38.7 us  [swap(): return lax.ppermute(value, ('dp', 'tensor'), pairs)]
    ppermute x9 -> x14, starting transfers between devices: 2.23 us -> 8.65 us  [core_swap(): return lax.ppermute(value, 'tensor', [(0, 1), (1, 0)])]
    concatenate x10 -> x2, other arithmetic: 6.87 us -> 1.1 us  [the longest x1 1.09 us: local(): jnp.concatenate(merge_grads, axis=0)]
    unnamed x53 -> x60, local copies, waits for them, and re-layouts: 6.24 us -> 11.9 us
  transfers between devices with their start and end apart: 37 -> 50, of which waited for: 13 -> 14; matrix products, arithmetic and copies ran while one was open for 11% -> 5% of each run, Pallas kernels for 21% -> 30%
where the time goes in v2:
time: 233 us; the launch traced here: 230 us
  Pallas kernels  106 us (45%)
  waiting for transfers between devices  50.8 us (22%)
  starting transfers between devices  47.4 us (20%)
  local copies, waits for them, and re-layouts  19.4 us (8%)
  other arithmetic  4.94 us (2%)
    pallas_call x11, Pallas kernels, call(): pl.pallas_call(body, in_specs=in_specs, out_specs=out_specs, scratch_shap...  84.8 us
    ppermute x36, waiting for transfers between devices, swap(): return lax.ppermute(value, ('dp', 'tensor'), pairs)  49.4 us
    ppermute x36, starting transfers between devices, swap(): return lax.ppermute(value, ('dp', 'tensor'), pairs)  38.7 us
    pallas_call x3, Pallas kernels, call(): return pl.pallas_call(body, grid_spec=grid_spec, **params)(*ins)  14.4 us
    unnamed x60, local copies, waits for them, and re-layouts  11.9 us
    ppermute x14, starting transfers between devices, core_swap(): return lax.ppermute(value, 'tensor', [(0, 1), (1, 0)])  8.65 us
  transfers between devices with their start and end apart: 50, of which 14 were waited for; matrix products, arithmetic and copies ran while one was open for 5% of the time, Pallas kernels for 30%

profile of v2, /device:TPU:1, one launch (start us, length us, event | category | flops | bytes accessed | tf_op | source)
XLA Modules:
  0.0 229.6 jit_solution(475594438020109871)
XLA Ops:
  1.3 1.7 copy-done
  3.0 1.7 copy-done.2
  4.7 1.5 copy-done.5
  7.9 1.4 shard_map.237.own.pack.pack_own
  9.4 1.2 collective-permute-done.other.pack.pack_other
  10.7 2.8 %shard_map.241 = (bf16[384,768]{1,0:T(8,128)(2,1)S(1)}, bf16[768,1536]{1,0:T(8,128)(2,1)}, bf16[1536,768]{1,0:T(8,128)(2,1)}) custom-call(f32[16,1536]{1,0:T(8,128)S(1)} %shard_map.237.own.pack.pack_own, f32[16,1536]{1,0:T(8,128)S(1)} %collective-permute-done.other.pack.pack_other, bf16[384,768]{1,0:T(8,128)(2,1)S(1)} %copy-done.9, ...), custom_call_target="tpu_custom_call" | custom-call | tf_op jit(solution)/shard_map/pallas_call | solution.py:805
  14.1 2.1 shard_map.238.weight.w_own
  18.1 7.0 %shard_map.239 = (bf16[512,768]{1,0:T(8,128)(2,1)S(1)}, bf16[384,512]{1,0:T(8,128)(2,1)S(1)}, bf16[384,512]{1,0:T(8,128)(2,1)S(1)}, bf16[384,512]{1,0:T(8,128)(2...) custom-call(s32[3]{0:T(128)S(1)} %pad_add_fusion.ids.refs_0_, s32[8]{0:T(128)S(1)} %copy-done.19, ...), custom_call_target="tpu_custom_call" | custom-call | flops 3623878656 | bytes 5029944 | tf_op jit(solution)/shard_map/pallas_call | solution.py:95
  25.2 7.2 %shard_map.240 = (bf16[384,512]{1,0:T(8,128)(2,1)S(1)}, bf16[384,512]{1,0:T(8,128)(2,1)S(1)}, bf16[384,512]{1,0:T(8,128)(2,1)S(1)}, bf16[384,512]{1,0:T(8,128)(2,1)S(1)}, f32[8,512]{1,0:T(8,128)S(1)}) custom-call(s32[3]{0:T(128)S(1)} %pad_add_fusion.ids.refs_0_, s32[8]{0:T(128)S(1)} %copy-done.19, bf16[512,768]{1,0:T(8,128)(2,1)S(1)} %get-tuple-element.205.xq.refs_2_, ...), custom_call_target="tpu_custom_call" | custom-call | flops 3623878656 | bytes 4243500 | tf_op jit(solution)/shard_map/pallas_call | solution.py:95
  32.4 25.4 %shard_map.242 = (f32[512,768]{1,0:T(8,128)S(1)}, f32[512,128]{1,0:T(8,128)S(1)}, bf16[512,768]{1,0:T(8,128)(2,1)S(1)}, bf16[512,1536]{1,0:T(8,128)(2,1)S(1)}, b...) custom-call(f32[3]{0:T(128)S(1)} %copy-done.15, ...), custom_call_target="tpu_custom_call" | custom-call | flops 14495514624 | bytes 25274380 | tf_op jit(solution)/shard_map/pallas_call | solution.py:95
  57.8 2.6 %down_theirs.1 = bf16[16,192,384]{2,1,0:T(8,128)(2,1)S(1)} custom-call(s32[3]{0:T(128)S(1)} %pad_add_fusion.ids.refs_0_, bf16[512,1536]{1,0:T(8,128)(2,1)S(1)} %get-tuple-element.213.active, bf16[512,768]{1,0:T(8,128)(2,1)S(1)} %get-tuple-element.223.grad_feed), custom_call_target="tpu_custom_call" | custom-call | flops 1207959552 | bytes 4718604 | tf_op jit(solution)/shard_map/down_theirs/pallas_call | solution.py:95
  60.5 1.3 fusion.2
  62.2 2.6 %down_mine.1 = bf16[16,192,384]{2,1,0:T(8,128)(2,1)S(1)} custom-call(s32[3]{0:T(128)S(1)} %pad_add_fusion.ids.refs_0_, bf16[512,1536]{1,0:T(8,128)(2,1)S(1)} %get-tuple-element.212.active, bf16[512,768]{1,0:T(8,128)(2,1)S(1)} %get-tuple-element.223.grad_feed), custom_call_target="tpu_custom_call" | custom-call | flops 1207959552 | bytes 4718604 | tf_op jit(solution)/shard_map/down_mine/pallas_call | solution.py:95
  65.2 2.4 %collective-permute-start.8 = (bf16[8,192,384]{2,1,0:T(8,128)(2,1)S(1)}, bf16[8,192,384]{2,1,0:T(8,128)(2,1)S(1)}, u32[]{:S(2)}, u32[]{:S(2)}) collective-permute-start(bf16[8,192,384]{2,1,0:T(8,128)(2,1)S(1)} %add_convert_fusion.1), channel_id=1, source_target_pairs={{0,2},{1,5},{2,0},{3,7},{4,6},{5,1},{6,4},{7,3},{8,10},{9,13},{10,... | collective-permute-start | bytes 3538952 | tf_op jit(solution)/shard_map/down_in0/ppermute | solution.py:637
  67.7 7.6 %up_theirs.1 = (bf16[16,192,384]{2,1,0:T(8,128)(2,1)S(1)}, f32[1,1536]{1,0:T(1,128)S(1)}, f32[512,768]{1,0:T(8,128)S(1)}) custom-call(s32[3]{0:T(128)S(1)} %pad_add_fusion.ids.refs_0_, bf16[512,768]{1,0:T(8,128)(2,1)S(1)} %get-tuple-element.223.grad_feed, bf16[1536,768]{1,0:T(8,128)(2,1)} %collective-permute-done.4.down_other.down, ...), custom_call_target="tpu_custom_call" | custom-call | flops 3623878656 | bytes 11802636 | tf_op jit(solution)/shard_map/up_theirs/pallas_call | solution.py:95
  76.9 7.4 %up_mine.1 = (bf16[16,192,384]{2,1,0:T(8,128)(2,1)S(1)}, f32[1,1536]{1,0:T(1,128)S(1)}, f32[512,768]{1,0:T(8,128)S(1)}) custom-call(s32[3]{0:T(128)S(1)} %pad_add_fusion.ids.refs_0_, bf16[512,768]{1,0:T(8,128)(2,1)S(1)} %get-tuple-element.223.grad_feed, bf16[1536,768]{1,0:T(8,128)(2,1)} %get-tuple-element.209.down_own.down, ...), custom_call_target="tpu_custom_call" | custom-call | flops 3623878656 | bytes 13375500 | tf_op jit(solution)/shard_map/up_mine/pallas_call | solution.py:95
  87.1 2.3 norm.1
  89.4 10.2 %heads0.1 = (bf16[16,192,256]{2,1,0:T(8,128)(2,1)S(1)}, bf16[16,192,256]{2,1,0:T(8,128)(2,1)S(1)}, bf16[3,256,512]{2,1,0:T(8,128)(2,1)S(1)}, bf16[3,256,512]{2,1...) custom-call(s32[3]{0:T(128)S(1)} %pad_add_fusion.ids.refs_0_, s32[8]{0:T(128)S(1)} %copy-done.19, ...), custom_call_target="tpu_custom_call" | custom-call | flops 14495514624 | bytes 10682412 | tf_op jit(solution)/shard_map/heads0/pallas_call | solution.py:95
  100.9 1.4 collective-permute-start.10
  102.3 6.6 %heads1.1 = (bf16[16,192,128]{2,1,0:T(8,128)(2,1)S(1)}, bf16[16,192,128]{2,1,0:T(8,128)(2,1)S(1)}, bf16[3,128,512]{2,1,0:T(8,128)(2,1)S(1)}, bf16[3,128,512]{2,1...) custom-call(s32[3]{0:T(128)S(1)} %pad_add_fusion.ids.refs_0_, s32[8]{0:T(128)S(1)} %copy-done.19, ...), custom_call_target="tpu_custom_call" | custom-call | flops 14495514624 | bytes 8306732 | tf_op jit(solution)/shard_map/heads1/pallas_call | solution.py:95
  111.1 2.3 %collective-permute-start.13 = (bf16[1,192,384]{2,1,0:T(8,128)(2,1)S(1)}, bf16[1,192,384]{2,1,0:T(8,128)(2,1)S(1)}, u32[]{:S(2)}, u32[]{:S(2)}) collective-permute-start(bf16[1,192,384]{2,1,0:T(8,128)(2,1)S(1)} %add_convert_fusion.14), channel_id=1, source_target_pairs={{0,16},{1,17},{2,18},{3,19},{4,20},{5,21},{6,22},{7,23},{8,24},{9,... | collective-permute-start | bytes 442376 | tf_op jit(solution)/shard_map/down_in3/ppermute | solution.py:637
  113.6 1.4 collective-permute-start.24
  115.2 4.8 %collective-permute-done.14 = bf16[4,192,384]{2,1,0:T(8,128)(2,1)S(1)} collective-permute-done((bf16[4,192,384]{2,1,0:T(8,128)(2,1)S(1)}, bf16[4,192,384]{2,1,0:T(8,128)(2,1)S(1)}, u32[]{:S(2)}, u32[]{:S(2)}) %collective-permute-start.14) | collective-permute-done | bytes 589856 | tf_op jit(solution)/shard_map/up_in1/ppermute | solution.py:637
  120.0 2.2 collective-permute-start.18
  122.6 5.9 %input.1 = f32[512,768]{1,0:T(8,128)} custom-call(f32[3]{0:T(128)S(1)} %copy-done.15, bf16[512,768]{1,0:T(8,128)(2,1)S(1)} %copy-done.13, f32[512,768]{1,0:T(8,128)S(1)} %get-tuple-element.293.grad_first, bf16[3,768,384]{2,1,0:T(8,128)(2,1)} %shard_map.238.weight.w_own, bf16[3,768,384]{2,1,0:T(8,128)(2,1)} %collective-permute-done.1.weight.w_other, ...), custom_call_target="tpu_custom_call" | custom-call | flops 1811939328 | bytes 9830412 | tf_op jit(solution)/shard_map/input/pallas_call | solution.py:95
  128.5 5.8 %collective-permute-start.19 = (bf16[1,192,384]{2,1,0:T(8,128)(2,1)S(1)}, bf16[1,192,384]{2,1,0:T(8,128)(2,1)S(1)}, u32[]{:S(2)}, u32[]{:S(2)}) collective-permute-start(bf16[1,192,384]{2,1,0:T(8,128)(2,1)S(1)} %add_convert_fusion.13), channel_id=1, source_target_pairs={{0,16},{1,17},{2,18},{3,19},{4,20},{5,21},{6,22},{7,23},{8,24},{9,... | collective-permute-start | bytes 442376 | tf_op jit(solution)/shard_map/down_out3/ppermute | solution.py:637
  134.4 6.7 %collective-permute-done.19 = bf16[1,192,384]{2,1,0:T(8,128)(2,1)S(1)} collective-permute-done((bf16[1,192,384]{2,1,0:T(8,128)(2,1)S(1)}, bf16[1,192,384]{2,1,0:T(8,128)(2,1)S(1)}, u32[]{:S(2)}, u32[]{:S(2)}) %collective-permute-start.19) | collective-permute-done | bytes 147488 | tf_op jit(solution)/shard_map/down_out3/ppermute | solution.py:637
  142.2 1.5 collective-permute-start.28
  143.7 4.3 %collective-permute-start.27 = (f32[12,768]{1,0:T(8,128)S(1)}, f32[12,768]{1,0:T(8,128)S(1)}, u32[]{:S(2)}, u32[]{:S(2)}) collective-permute-start(f32[12,768]{1,0:T(8,128)S(1)} %pad_maximum_fusion.1), channel_id=1, source_target_pairs={{0,1},{1,0},{2,3},{3,2},{4,5},{5,4},{6,7},{7,6},{8,9},{9,8},{10,11... | collective-permute-start | bytes 110600 | tf_op jit(solution)/shard_map/small_got/ppermute | solution.py:640
  148.6 5.5 %collective-permute-done.29 = bf16[2,192,384]{2,1,0:T(8,128)(2,1)S(1)} collective-permute-done((bf16[2,192,384]{2,1,0:T(8,128)(2,1)S(1)}, bf16[2,192,384]{2,1,0:T(8,128)(2,1)S(1)}, u32[]{:S(2)}, u32[]{:S(2)}) %collective-permute-start.29) | collective-permute-done | bytes 294944 | tf_op jit(solution)/shard_map/down_out2/ppermute | solution.py:637
  154.5 1.4 collective-permute-start.31
  156.0 1.5 collective-permute-start.32
  157.7 2.0 collective-permute-done.25
  159.8 4.3 %collective-permute-done.33 = bf16[4,192,384]{2,1,0:T(8,128)(2,1)S(1)} collective-permute-done((bf16[4,192,384]{2,1,0:T(8,128)(2,1)S(1)}, bf16[4,192,384]{2,1,0:T(8,128)(2,1)S(1)}, u32[]{:S(2)}, u32[]{:S(2)}) %collective-permute-start.33) | collective-permute-done | bytes 589856 | tf_op jit(solution)/shard_map/down_out1/ppermute | solution.py:637
  164.7 1.2 collective-permute-start.35
  165.9 1.2 collective-permute-start.36
  167.2 2.7 %collective-permute-start.34 = (bf16[1,192,256]{2,1,0:T(8,128)(2,1)S(1)}, bf16[1,192,256]{2,1,0:T(8,128)(2,1)S(1)}, u32[]{:S(2)}, u32[]{:S(2)}) collective-permute-start(bf16[1,192,256]{2,1,0:T(8,128)(2,1)S(1)} %add_convert_fusion.15), channel_id=1, source_target_pairs={{0,16},{1,17},{2,18},{3,19},{4,20},{5,21},{6,22},{7,23},{8,24},{9,... | collective-permute-start | bytes 294920 | tf_op jit(solution)/shard_map/rest0_out3/ppermute | solution.py:637
  171.7 10.8 %collective-permute-done.35 = f32[12,768]{1,0:T(8,128)S(1)} collective-permute-done((f32[12,768]{1,0:T(8,128)S(1)}, f32[12,768]{1,0:T(8,128)S(1)}, u32[]{:S(2)}, u32[]{:S(2)}) %collective-permute-start.35) | collective-permute-done | bytes 36896 | tf_op jit(solution)/shard_map/small_in1/ppermute | solution.py:637
  182.5 1.8 collective-permute-start.40
  184.4 2.2 collective-permute-done.40
  188.3 2.9 %collective-permute-done.38 = bf16[2,192,256]{2,1,0:T(8,128)(2,1)S(1)} collective-permute-done((bf16[2,192,256]{2,1,0:T(8,128)(2,1)S(1)}, bf16[2,192,256]{2,1,0:T(8,128)(2,1)S(1)}, u32[]{:S(2)}, u32[]{:S(2)}) %collective-permute-start.38) | collective-permute-done | bytes 196640 | tf_op jit(solution)/shard_map/rest0_out2/ppermute | solution.py:637
  191.3 2.0 collective-permute-start.41
  196.6 5.7 %collective-permute-done.41 = bf16[4,192,256]{2,1,0:T(8,128)(2,1)S(1)} collective-permute-done((bf16[4,192,256]{2,1,0:T(8,128)(2,1)S(1)}, bf16[4,192,256]{2,1,0:T(8,128)(2,1)S(1)}, u32[]{:S(2)}, u32[]{:S(2)}) %collective-permute-start.41) | collective-permute-done | bytes 393248 | tf_op jit(solution)/shard_map/rest0_out1/ppermute | solution.py:637
  205.5 3.8 %down_final.1 = f32[1536,768]{1,0:T(8,128)} custom-call(s32[3]{0:T(128)S(1)} %pad_add_fusion.ids.refs_0_, f32[16,1536]{1,0:T(8,128)S(1)} %shard_map.237.own.pack.pack_own, f32[16,1536]{1,0:T(8,128)S(1)} %collective-permute-done.other.pack.pack_other, bf16[8,192,384]{2,1,0:T(8,128)(2,1)S(1)} %constant_dynamic-update-slice_fusion.6.refs_0_, ...), custom_call_target="tpu_custom_call" | custom-call | flops 1 | bytes 9633804 | tf_op jit(solution)/shard_map/down_final/pallas_call | solution.py:94
  212.4 1.7 copy-done.4
  214.1 5.5 %up_final.1 = f32[768,1536]{1,0:T(8,128)} custom-call(s32[3]{0:T(128)S(1)} %pad_add_fusion.ids.refs_0_, f32[16,1536]{1,0:T(8,128)S(1)} %shard_map.237.own.pack.pack_own, f32[16,1536]{1,0:T(8,128)S(1)} %collective-permute-done.other.pack.pack_other, bf16[8,192,384]{2,1,0:T(8,128)(2,1)} %constant_dynamic-update-slice_fusion.16.refs_0_, ...), custom_call_target="tpu_custom_call" | custom-call | flops 1 | bytes 9633804 | tf_op jit(solution)/shard_map/up_final/pallas_call | solution.py:94
  219.5 3.8 %collective-permute-done.48.refs_3_ = bf16[8,192,128]{2,1,0:T(8,128)(2,1)S(1)} collective-permute-done((bf16[8,192,128]{2,1,0:T(8,128)(2,1)S(1)}, bf16[8,192,128]{2,1,0:T(8,128)(2,1)S(1)}, u32[]{:S(2)}, u32[]{:S(2)}) %collective-permute-start.48) | collective-permute-done | bytes 393248 | tf_op jit(solution)/shard_map/rest1_out0/ppermute | solution.py:637
  223.3 5.1 %rest_final.1 = (f32[3,768,384]{2,1,0:T(8,128)}, f32[16,16,768]{2,1,0:T(8,128)S(1)}, f32[16,8,768]{2,1,0:T(8,128)S(1)}) custom-call(s32[3]{0:T(128)S(1)} %pad_add_fusion.ids.refs_0_, f32[16,1536]{1,0:T(8,128)S(1)} %shard_map.237.own.pack.pack_own, f32[16,1536]{1,0:T(8,128)S(1)} %collective-permute-done.other.pack.pack_other, ...), custom_call_target="tpu_custom_call" | custom-call | flops 1 | bytes 9633804 | tf_op jit(solution)/shard_map/rest_final/pallas_call | solution.py:94
  (194 shorter events, 31.9 us)
Async XLA Ops:
  13.5 18.9 %collective-permute-start.3 = (bf16[768,1536]{1,0:T(8,128)(2,1)}, bf16[768,1536]{1,0:T(8,128)(2,1)}, u32[]{:S(2)}, u32[]{:S(2)}) collective-permute-start(bf16[768,1536]{1,0:T(8,128)(2,1)} %get-tuple-element.208.up_own.up), channel_id=1, source_target_pairs={{0,1},{1,0},{2,3},{3,2},{4,5},{5,4},{6,7},{7,6},{8,9},{9,8},{10,11... | collective-permute-start | bytes 7077896 | tf_op jit(solution)/shard_map/ppermute | solution.py:640
  13.7 18.7 %collective-permute-start.4 = (bf16[1536,768]{1,0:T(8,128)(2,1)}, bf16[1536,768]{1,0:T(8,128)(2,1)}, u32[]{:S(2)}, u32[]{:S(2)}) collective-permute-start(bf16[1536,768]{1,0:T(8,128)(2,1)} %get-tuple-element.209.down_own.down), channel_id=1, source_target_pairs={{0,1},{1,0},{2,3},{3,2},{4,5},{5,4},{6,7},{7,6},{8,9},{9,8},{10,11... | collective-permute-start | bytes 7077896 | tf_op jit(solution)/shard_map/ppermute | solution.py:640
  16.3 8.9 %collective-permute-start.1 = (bf16[3,768,384]{2,1,0:T(8,128)(2,1)}, bf16[3,768,384]{2,1,0:T(8,128)(2,1)}, u32[]{:S(2)}, u32[]{:S(2)}) collective-permute-start(bf16[3,768,384]{2,1,0:T(8,128)(2,1)} %shard_map.238.weight.w_own), channel_id=1, source_target_pairs={{0,1},{1,0},{2,3},{3,2},{4,5},{5,4},{6,7},{7,6},{8,9},{9,8},{10,11... | collective-permute-start | bytes 5308424 | tf_op jit(solution)/shard_map/ppermute | solution.py:640
  16.5 15.8 %collective-permute-start.2 = (bf16[384,768]{1,0:T(8,128)(2,1)}, bf16[384,768]{1,0:T(8,128)(2,1)S(1)}, u32[]{:S(2)}, u32[]{:S(2)}) collective-permute-start(bf16[384,768]{1,0:T(8,128)(2,1)} %copy-done.17), channel_id=1, source_target_pairs={{0,1},{1,0},{2,3},{3,2},{4,5},{5,4},{6,7},{7,6},{8,9},{9,8},{10,11... | collective-permute-start | bytes 1769480 | tf_op jit(solution)/shard_map/ppermute | solution.py:640
  61.7 3.2 %collective-permute-start.5 = (bf16[8,192,384]{2,1,0:T(8,128)(2,1)S(1)}, bf16[8,192,384]{2,1,0:T(8,128)(2,1)S(1)}, u32[]{:S(2)}, u32[]{:S(2)}) collective-permute-start(bf16[8,192,384]{2,1,0:T(8,128)(2,1)S(1)} %get-tuple-element.401), channel_id=1, source_target_pairs={{0,1},{1,0},{2,3},{3,2},{4,5},{5,4},{6,7},{7,6},{8,9},{9,8},{10,11... | collective-permute-start | bytes 3538952 | tf_op jit(solution)/shard_map/down_high/ppermute | solution.py:640
  61.9 22.4 %collective-permute-start.7 = (bf16[8,192,384]{2,1,0:T(8,128)(2,1)}, bf16[8,192,384]{2,1,0:T(8,128)(2,1)S(1)}, u32[]{:S(2)}, u32[]{:S(2)}) collective-permute-start(bf16[8,192,384]{2,1,0:T(8,128)(2,1)} %get-tuple-element.400), channel_id=1, source_target_pairs={{0,1},{1,0},{2,3},{3,2},{4,5},{5,4},{6,7},{7,6},{8,9},{9,8},{10,11... | collective-permute-start | bytes 3538952 | tf_op jit(solution)/shard_map/down_low/ppermute | solution.py:640
  65.2 19.1 %collective-permute-start.8 = (bf16[8,192,384]{2,1,0:T(8,128)(2,1)S(1)}, bf16[8,192,384]{2,1,0:T(8,128)(2,1)S(1)}, u32[]{:S(2)}, u32[]{:S(2)}) collective-permute-start(bf16[8,192,384]{2,1,0:T(8,128)(2,1)S(1)} %add_convert_fusion.1), channel_id=1, source_target_pairs={{0,2},{1,5},{2,0},{3,7},{4,6},{5,1},{6,4},{7,3},{8,10},{9,13},{10,... | collective-permute-start | bytes 3538952 | tf_op jit(solution)/shard_map/down_in0/ppermute | solution.py:637
  75.5 10.2 %collective-permute-start.6 = (bf16[8,192,384]{2,1,0:T(8,128)(2,1)S(1)}, bf16[8,192,384]{2,1,0:T(8,128)(2,1)S(1)}, u32[]{:S(2)}, u32[]{:S(2)}) collective-permute-start(bf16[8,192,384]{2,1,0:T(8,128)(2,1)S(1)} %get-tuple-element.399), channel_id=1, source_target_pairs={{0,1},{1,0},{2,3},{3,2},{4,5},{5,4},{6,7},{7,6},{8,9},{9,8},{10,11... | collective-permute-start | bytes 3538952 | tf_op jit(solution)/shard_map/up_high/ppermute | solution.py:640
  76.9 32.1 %collective-permute-start.11 = (bf16[8,192,384]{2,1,0:T(8,128)(2,1)S(1)}, bf16[8,192,384]{2,1,0:T(8,128)(2,1)S(1)}, u32[]{:S(2)}, u32[]{:S(2)}) collective-permute-start(bf16[8,192,384]{2,1,0:T(8,128)(2,1)S(1)} %get-tuple-element.398), channel_id=1, source_target_pairs={{0,1},{1,0},{2,3},{3,2},{4,5},{5,4},{6,7},{7,6},{8,9},{9,8},{10,11... | collective-permute-start | bytes 3538952 | tf_op jit(solution)/shard_map/up_low/ppermute | solution.py:640
  84.5 16.2 %collective-permute-start.9 = (bf16[4,192,384]{2,1,0:T(8,128)(2,1)S(1)}, bf16[4,192,384]{2,1,0:T(8,128)(2,1)S(1)}, u32[]{:S(2)}, u32[]{:S(2)}) collective-permute-start(bf16[4,192,384]{2,1,0:T(8,128)(2,1)S(1)} %add_convert_fusion.4), channel_id=1, source_target_pairs={{0,4},{1,3},{2,6},{3,1},{4,0},{5,7},{6,2},{7,5},{8,12},{9,11},{10,... | collective-permute-start | bytes 1769480 | tf_op jit(solution)/shard_map/down_in1/ppermute | solution.py:637
  86.0 23.8 %collective-permute-start.12 = (bf16[8,192,384]{2,1,0:T(8,128)(2,1)S(1)}, bf16[8,192,384]{2,1,0:T(8,128)(2,1)S(1)}, u32[]{:S(2)}, u32[]{:S(2)}) collective-permute-start(bf16[8,192,384]{2,1,0:T(8,128)(2,1)S(1)} %add_convert_fusion), channel_id=1, source_target_pairs={{0,2},{1,5},{2,0},{3,7},{4,6},{5,1},{6,4},{7,3},{8,10},{9,13},{10,... | collective-permute-start | bytes 3538952 | tf_op jit(solution)/shard_map/up_in0/ppermute | solution.py:637
  99.7 13.8 %collective-permute-start.15 = (bf16[8,192,256]{2,1,0:T(8,128)(2,1)S(1)}, bf16[8,192,256]{2,1,0:T(8,128)(2,1)S(1)}, u32[]{:S(2)}, u32[]{:S(2)}) collective-permute-start(bf16[8,192,256]{2,1,0:T(8,128)(2,1)S(1)} %get-tuple-element.403), channel_id=1, source_target_pairs={{0,1},{1,0},{2,3},{3,2},{4,5},{5,4},{6,7},{7,6},{8,9},{9,8},{10,11... | collective-permute-start | bytes 2359304 | tf_op jit(solution)/shard_map/rest0_high/ppermute | solution.py:640
  100.7 40.5 %collective-permute-start.17 = (bf16[8,192,256]{2,1,0:T(8,128)(2,1)S(1)}, bf16[8,192,256]{2,1,0:T(8,128)(2,1)S(1)}, u32[]{:S(2)}, u32[]{:S(2)}) collective-permute-start(bf16[8,192,256]{2,1,0:T(8,128)(2,1)S(1)} %get-tuple-element.402), channel_id=1, source_target_pairs={{0,1},{1,0},{2,3},{3,2},{4,5},{5,4},{6,7},{7,6},{8,9},{9,8},{10,11... | collective-permute-start | bytes 2359304 | tf_op jit(solution)/shard_map/rest0_low/ppermute | solution.py:640
  100.9 9.2 %collective-permute-start.10 = (bf16[2,192,384]{2,1,0:T(8,128)(2,1)S(1)}, bf16[2,192,384]{2,1,0:T(8,128)(2,1)S(1)}, u32[]{:S(2)}, u32[]{:S(2)}) collective-permute-start(bf16[2,192,384]{2,1,0:T(8,128)(2,1)S(1)} %add_convert_fusion.8), channel_id=1, source_target_pairs={{0,8},{1,9},{2,10},{3,11},{4,12},{5,13},{6,14},{7,15},{8,0},{9,1},... | collective-permute-start | bytes 884744 | tf_op jit(solution)/shard_map/down_in2/ppermute | solution.py:637
  109.8 31.6 %collective-permute-start.23 = (bf16[8,192,128]{2,1,0:T(8,128)(2,1)S(1)}, bf16[8,192,128]{2,1,0:T(8,128)(2,1)S(1)}, u32[]{:S(2)}, u32[]{:S(2)}) collective-permute-start(bf16[8,192,128]{2,1,0:T(8,128)(2,1)S(1)} %get-tuple-element.404), channel_id=1, source_target_pairs={{0,1},{1,0},{2,3},{3,2},{4,5},{5,4},{6,7},{7,6},{8,9},{9,8},{10,11... | collective-permute-start | bytes 1179656 | tf_op jit(solution)/shard_map/rest1_low/ppermute | solution.py:640
  110.1 9.9 %collective-permute-start.14 = (bf16[4,192,384]{2,1,0:T(8,128)(2,1)S(1)}, bf16[4,192,384]{2,1,0:T(8,128)(2,1)S(1)}, u32[]{:S(2)}, u32[]{:S(2)}) collective-permute-start(bf16[4,192,384]{2,1,0:T(8,128)(2,1)S(1)} %add_convert_fusion.3), channel_id=1, source_target_pairs={{0,4},{1,3},{2,6},{3,1},{4,0},{5,7},{6,2},{7,5},{8,12},{9,11},{10,... | collective-permute-start | bytes 1769480 | tf_op jit(solution)/shard_map/up_in1/ppermute | solution.py:637
  111.1 11.3 %collective-permute-start.13 = (bf16[1,192,384]{2,1,0:T(8,128)(2,1)S(1)}, bf16[1,192,384]{2,1,0:T(8,128)(2,1)S(1)}, u32[]{:S(2)}, u32[]{:S(2)}) collective-permute-start(bf16[1,192,384]{2,1,0:T(8,128)(2,1)S(1)} %add_convert_fusion.14), channel_id=1, source_target_pairs={{0,16},{1,17},{2,18},{3,19},{4,20},{5,21},{6,22},{7,23},{8,24},{9,... | collective-permute-start | bytes 442376 | tf_op jit(solution)/shard_map/down_in3/ppermute | solution.py:637
  113.6 27.8 %collective-permute-start.24 = (bf16[8,192,128]{2,1,0:T(8,128)(2,1)S(1)}, bf16[8,192,128]{2,1,0:T(8,128)(2,1)S(1)}, u32[]{:S(2)}, u32[]{:S(2)}) collective-permute-start(bf16[8,192,128]{2,1,0:T(8,128)(2,1)S(1)} %add_convert_fusion.6), channel_id=1, source_target_pairs={{0,2},{1,5},{2,0},{3,7},{4,6},{5,1},{6,4},{7,3},{8,10},{9,13},{10,... | collective-permute-start | bytes 1179656 | tf_op jit(solution)/shard_map/rest1_in0/ppermute | solution.py:637
  120.0 21.2 %collective-permute-start.18 = (bf16[8,192,256]{2,1,0:T(8,128)(2,1)S(1)}, bf16[8,192,256]{2,1,0:T(8,128)(2,1)S(1)}, u32[]{:S(2)}, u32[]{:S(2)}) collective-permute-start(bf16[8,192,256]{2,1,0:T(8,128)(2,1)S(1)} %add_convert_fusion.2), channel_id=1, source_target_pairs={{0,2},{1,5},{2,0},{3,7},{4,6},{5,1},{6,4},{7,3},{8,10},{9,13},{10,... | collective-permute-start | bytes 2359304 | tf_op jit(solution)/shard_map/rest0_in0/ppermute | solution.py:637
  122.4 6.2 %collective-permute-start.20 = (bf16[2,192,384]{2,1,0:T(8,128)(2,1)S(1)}, bf16[2,192,384]{2,1,0:T(8,128)(2,1)S(1)}, u32[]{:S(2)}, u32[]{:S(2)}) collective-permute-start(bf16[2,192,384]{2,1,0:T(8,128)(2,1)S(1)} %add_convert_fusion.7), channel_id=1, source_target_pairs={{0,8},{1,9},{2,10},{3,11},{4,12},{5,13},{6,14},{7,15},{8,0},{9,1},... | collective-permute-start | bytes 884744 | tf_op jit(solution)/shard_map/up_in2/ppermute | solution.py:637
  128.5 12.6 %collective-permute-start.19 = (bf16[1,192,384]{2,1,0:T(8,128)(2,1)S(1)}, bf16[1,192,384]{2,1,0:T(8,128)(2,1)S(1)}, u32[]{:S(2)}, u32[]{:S(2)}) collective-permute-start(bf16[1,192,384]{2,1,0:T(8,128)(2,1)S(1)} %add_convert_fusion.13), channel_id=1, source_target_pairs={{0,16},{1,17},{2,18},{3,19},{4,20},{5,21},{6,22},{7,23},{8,24},{9,... | collective-permute-start | bytes 442376 | tf_op jit(solution)/shard_map/down_out3/ppermute | solution.py:637
  141.5 6.5 %collective-permute-start.22 = (bf16[1,192,384]{2,1,0:T(8,128)(2,1)S(1)}, bf16[1,192,384]{2,1,0:T(8,128)(2,1)S(1)}, u32[]{:S(2)}, u32[]{:S(2)}) collective-permute-start(bf16[1,192,384]{2,1,0:T(8,128)(2,1)S(1)} %add_convert_fusion.12), channel_id=1, source_target_pairs={{0,16},{1,17},{2,18},{3,19},{4,20},{5,21},{6,22},{7,23},{8,24},{9,... | collective-permute-start | bytes 442376 | tf_op jit(solution)/shard_map/up_in3/ppermute | solution.py:637
  141.6 7.0 %collective-permute-start.21 = (bf16[4,192,256]{2,1,0:T(8,128)(2,1)S(1)}, bf16[4,192,256]{2,1,0:T(8,128)(2,1)S(1)}, u32[]{:S(2)}, u32[]{:S(2)}) collective-permute-start(bf16[4,192,256]{2,1,0:T(8,128)(2,1)S(1)} %add_convert_fusion.5), channel_id=1, source_target_pairs={{0,4},{1,3},{2,6},{3,1},{4,0},{5,7},{6,2},{7,5},{8,12},{9,11},{10,... | collective-permute-start | bytes 1179656 | tf_op jit(solution)/shard_map/rest0_in1/ppermute | solution.py:637
  141.6 12.5 %collective-permute-start.29 = (bf16[2,192,384]{2,1,0:T(8,128)(2,1)S(1)}, bf16[2,192,384]{2,1,0:T(8,128)(2,1)S(1)}, u32[]{:S(2)}, u32[]{:S(2)}) collective-permute-start(bf16[2,192,384]{2,1,0:T(8,128)(2,1)S(1)} %constant_dynamic-update-slice_fusion), channel_id=1, source_target_pairs={{0,8},{1,9},{2,10},{3,11},{4,12},{5,13},{6,14},{7,15},{8,0},{9,1},... | collective-permute-start | bytes 884744 | tf_op jit(solution)/shard_map/down_out2/ppermute | solution.py:637
  142.2 12.0 %collective-permute-start.28 = (bf16[4,192,128]{2,1,0:T(8,128)(2,1)S(1)}, bf16[4,192,128]{2,1,0:T(8,128)(2,1)S(1)}, u32[]{:S(2)}, u32[]{:S(2)}) collective-permute-start(bf16[4,192,128]{2,1,0:T(8,128)(2,1)S(1)} %add_convert_fusion.10), channel_id=1, source_target_pairs={{0,4},{1,3},{2,6},{3,1},{4,0},{5,7},{6,2},{7,5},{8,12},{9,11},{10,... | collective-permute-start | bytes 589832 | tf_op jit(solution)/shard_map/rest1_in1/ppermute | solution.py:637
  143.7 10.6 %collective-permute-start.27 = (f32[12,768]{1,0:T(8,128)S(1)}, f32[12,768]{1,0:T(8,128)S(1)}, u32[]{:S(2)}, u32[]{:S(2)}) collective-permute-start(f32[12,768]{1,0:T(8,128)S(1)} %pad_maximum_fusion.1), channel_id=1, source_target_pairs={{0,1},{1,0},{2,3},{3,2},{4,5},{5,4},{6,7},{7,6},{8,9},{9,8},{10,11... | collective-permute-start | bytes 110600 | tf_op jit(solution)/shard_map/small_got/ppermute | solution.py:640
  148.1 9.4 %collective-permute-start.26 = (bf16[1,192,384]{2,1,0:T(8,128)(2,1)S(1)}, bf16[1,192,384]{2,1,0:T(8,128)(2,1)S(1)}, u32[]{:S(2)}, u32[]{:S(2)}) collective-permute-start(bf16[1,192,384]{2,1,0:T(8,128)(2,1)S(1)} %add_convert_fusion.11), channel_id=1, source_target_pairs={{0,16},{1,17},{2,18},{3,19},{4,20},{5,21},{6,22},{7,23},{8,24},{9,... | collective-permute-start | bytes 442376 | tf_op jit(solution)/shard_map/up_out3/ppermute | solution.py:637
  154.4 5.3 %collective-permute-start.25 = (bf16[2,192,256]{2,1,0:T(8,128)(2,1)S(1)}, bf16[2,192,256]{2,1,0:T(8,128)(2,1)S(1)}, u32[]{:S(2)}, u32[]{:S(2)}) collective-permute-start(bf16[2,192,256]{2,1,0:T(8,128)(2,1)S(1)} %add_convert_fusion.9), channel_id=1, source_target_pairs={{0,8},{1,9},{2,10},{3,11},{4,12},{5,13},{6,14},{7,15},{8,0},{9,1},... | collective-permute-start | bytes 589832 | tf_op jit(solution)/shard_map/rest0_in2/ppermute | solution.py:637
  154.5 9.6 %collective-permute-start.33 = (bf16[4,192,384]{2,1,0:T(8,128)(2,1)S(1)}, bf16[4,192,384]{2,1,0:T(8,128)(2,1)S(1)}, u32[]{:S(2)}, u32[]{:S(2)}) collective-permute-start(bf16[4,192,384]{2,1,0:T(8,128)(2,1)S(1)} %constant_dynamic-update-slice_fusion.2), channel_id=1, source_target_pairs={{0,4},{1,3},{2,6},{3,1},{4,0},{5,7},{6,2},{7,5},{8,12},{9,11},{10,... | collective-permute-start | bytes 1769480 | tf_op jit(solution)/shard_map/down_out1/ppermute | solution.py:637
  154.5 11.3 %collective-permute-start.31 = (bf16[2,192,128]{2,1,0:T(8,128)(2,1)S(1)}, bf16[2,192,128]{2,1,0:T(8,128)(2,1)S(1)}, u32[]{:S(2)}, u32[]{:S(2)}) collective-permute-start(bf16[2,192,128]{2,1,0:T(8,128)(2,1)S(1)} %add_convert_fusion.17), channel_id=1, source_target_pairs={{0,8},{1,9},{2,10},{3,11},{4,12},{5,13},{6,14},{7,15},{8,0},{9,1},... | collective-permute-start | bytes 294920 | tf_op jit(solution)/shard_map/rest1_in2/ppermute | solution.py:637
  156.0 8.6 %collective-permute-start.32 = (f32[12,768]{1,0:T(8,128)S(1)}, f32[12,768]{1,0:T(8,128)S(1)}, u32[]{:S(2)}, u32[]{:S(2)}) collective-permute-start(f32[12,768]{1,0:T(8,128)S(1)} %maximum_select_fusion.4), channel_id=1, source_target_pairs={{0,2},{1,3},{2,0},{3,1},{4,6},{5,7},{6,4},{7,5},{8,10},{9,11},{10,... | collective-permute-start | bytes 110600 | tf_op jit(solution)/shard_map/small_in0/ppermute | solution.py:637
  157.5 12.4 %collective-permute-start.37 = (bf16[2,192,384]{2,1,0:T(8,128)(2,1)S(1)}, bf16[2,192,384]{2,1,0:T(8,128)(2,1)S(1)}, u32[]{:S(2)}, u32[]{:S(2)}) collective-permute-start(bf16[2,192,384]{2,1,0:T(8,128)(2,1)S(1)} %constant_dynamic-update-slice_fusion.4), channel_id=1, source_target_pairs={{0,8},{1,9},{2,10},{3,11},{4,12},{5,13},{6,14},{7,15},{8,0},{9,1},... | collective-permute-start | bytes 884744 | tf_op jit(solution)/shard_map/up_out2/ppermute | solution.py:637
  159.7 7.4 %collective-permute-start.30 = (bf16[1,192,256]{2,1,0:T(8,128)(2,1)S(1)}, bf16[1,192,256]{2,1,0:T(8,128)(2,1)S(1)}, u32[]{:S(2)}, u32[]{:S(2)}) collective-permute-start(bf16[1,192,256]{2,1,0:T(8,128)(2,1)S(1)} %add_convert_fusion.16), channel_id=1, source_target_pairs={{0,16},{1,17},{2,18},{3,19},{4,20},{5,21},{6,22},{7,23},{8,24},{9,... | collective-permute-start | bytes 294920 | tf_op jit(solution)/shard_map/rest0_in3/ppermute | solution.py:637
  164.2 41.3 %collective-permute-start.47 = (bf16[8,192,384]{2,1,0:T(8,128)(2,1)S(1)}, bf16[8,192,384]{2,1,0:T(8,128)(2,1)S(1)}, u32[]{:S(2)}, u32[]{:S(2)}) collective-permute-start(bf16[8,192,384]{2,1,0:T(8,128)(2,1)S(1)} %constant_dynamic-update-slice_fusion.6.refs_0_), channel_id=1, source_target_pairs={{0,2},{1,5},{2,0},{3,7},{4,6},{5,1},{6,4},{7,3},{8,10},{9,13},{10,... | collective-permute-start | bytes 3538952 | tf_op jit(solution)/shard_map/down_out0/ppermute | solution.py:637
  164.7 17.8 %collective-permute-start.35 = (f32[12,768]{1,0:T(8,128)S(1)}, f32[12,768]{1,0:T(8,128)S(1)}, u32[]{:S(2)}, u32[]{:S(2)}) collective-permute-start(f32[12,768]{1,0:T(8,128)S(1)} %maximum_select_fusion.3), channel_id=1, source_target_pairs={{0,4},{1,5},{2,6},{3,7},{4,0},{5,1},{6,2},{7,3},{8,12},{9,13},{10,... | collective-permute-start | bytes 110600 | tf_op jit(solution)/shard_map/small_in1/ppermute | solution.py:637
  165.9 5.0 %collective-permute-start.36 = (bf16[1,192,128]{2,1,0:T(8,128)(2,1)S(1)}, bf16[1,192,128]{2,1,0:T(8,128)(2,1)S(1)}, u32[]{:S(2)}, u32[]{:S(2)}) collective-permute-start(bf16[1,192,128]{2,1,0:T(8,128)(2,1)S(1)} %add_convert_fusion.19), channel_id=1, source_target_pairs={{0,16},{1,17},{2,18},{3,19},{4,20},{5,21},{6,22},{7,23},{8,24},{9,... | collective-permute-start | bytes 147464 | tf_op jit(solution)/shard_map/rest1_in3/ppermute | solution.py:637
  167.2 17.1 %collective-permute-start.34 = (bf16[1,192,256]{2,1,0:T(8,128)(2,1)S(1)}, bf16[1,192,256]{2,1,0:T(8,128)(2,1)S(1)}, u32[]{:S(2)}, u32[]{:S(2)}) collective-permute-start(bf16[1,192,256]{2,1,0:T(8,128)(2,1)S(1)} %add_convert_fusion.15), channel_id=1, source_target_pairs={{0,16},{1,17},{2,18},{3,19},{4,20},{5,21},{6,22},{7,23},{8,24},{9,... | collective-permute-start | bytes 294920 | tf_op jit(solution)/shard_map/rest0_out3/ppermute | solution.py:637
  170.1 23.3 %collective-permute-start.43 = (bf16[4,192,384]{2,1,0:T(8,128)(2,1)S(1)}, bf16[4,192,384]{2,1,0:T(8,128)(2,1)S(1)}, u32[]{:S(2)}, u32[]{:S(2)}) collective-permute-start(bf16[4,192,384]{2,1,0:T(8,128)(2,1)S(1)} %constant_dynamic-update-slice_fusion.8), channel_id=1, source_target_pairs={{0,4},{1,3},{2,6},{3,1},{4,0},{5,7},{6,2},{7,5},{8,12},{9,11},{10,... | collective-permute-start | bytes 1769480 | tf_op jit(solution)/shard_map/up_out1/ppermute | solution.py:637
  170.9 16.9 %collective-permute-start.39 = (bf16[1,192,128]{2,1,0:T(8,128)(2,1)S(1)}, bf16[1,192,128]{2,1,0:T(8,128)(2,1)S(1)}, u32[]{:S(2)}, u32[]{:S(2)}) collective-permute-start(bf16[1,192,128]{2,1,0:T(8,128)(2,1)S(1)} %add_convert_fusion.18), channel_id=1, source_target_pairs={{0,16},{1,17},{2,18},{3,19},{4,20},{5,21},{6,22},{7,23},{8,24},{9,... | collective-permute-start | bytes 147464 | tf_op jit(solution)/shard_map/rest1_out3/ppermute | solution.py:637
  182.5 4.1 %collective-permute-start.40 = (f32[12,768]{1,0:T(8,128)S(1)}, f32[12,768]{1,0:T(8,128)S(1)}, u32[]{:S(2)}, u32[]{:S(2)}) collective-permute-start(f32[12,768]{1,0:T(8,128)S(1)} %maximum_select_fusion.2), channel_id=1, source_target_pairs={{0,8},{1,9},{2,10},{3,11},{4,12},{5,13},{6,14},{7,15},{8,0},{9,1},... | collective-permute-start | bytes 110600 | tf_op jit(solution)/shard_map/small_in2/ppermute | solution.py:637
  184.3 6.9 %collective-permute-start.38 = (bf16[2,192,256]{2,1,0:T(8,128)(2,1)S(1)}, bf16[2,192,256]{2,1,0:T(8,128)(2,1)S(1)}, u32[]{:S(2)}, u32[]{:S(2)}) collective-permute-start(bf16[2,192,256]{2,1,0:T(8,128)(2,1)S(1)} %constant_dynamic-update-slice_fusion.10), channel_id=1, source_target_pairs={{0,8},{1,9},{2,10},{3,11},{4,12},{5,13},{6,14},{7,15},{8,0},{9,1},... | collective-permute-start | bytes 589832 | tf_op jit(solution)/shard_map/rest0_out2/ppermute | solution.py:637
  186.7 6.6 %collective-permute-start.44 = (f32[12,768]{1,0:T(8,128)S(1)}, f32[12,768]{1,0:T(8,128)S(1)}, u32[]{:S(2)}, u32[]{:S(2)}) collective-permute-start(f32[12,768]{1,0:T(8,128)S(1)} %maximum_select_fusion.1), channel_id=1, source_target_pairs={{0,16},{1,17},{2,18},{3,19},{4,20},{5,21},{6,22},{7,23},{8,24},{9,... | collective-permute-start | bytes 110600 | tf_op jit(solution)/shard_map/small_in3/ppermute | solution.py:637
  187.8 7.9 %collective-permute-start.42 = (bf16[2,192,128]{2,1,0:T(8,128)(2,1)S(1)}, bf16[2,192,128]{2,1,0:T(8,128)(2,1)S(1)}, u32[]{:S(2)}, u32[]{:S(2)}) collective-permute-start(bf16[2,192,128]{2,1,0:T(8,128)(2,1)S(1)} %constant_dynamic-update-slice_fusion.12), channel_id=1, source_target_pairs={{0,8},{1,9},{2,10},{3,11},{4,12},{5,13},{6,14},{7,15},{8,0},{9,1},... | collective-permute-start | bytes 294920 | tf_op jit(solution)/shard_map/rest1_out2/ppermute | solution.py:637
  191.3 11.0 %collective-permute-start.41 = (bf16[4,192,256]{2,1,0:T(8,128)(2,1)S(1)}, bf16[4,192,256]{2,1,0:T(8,128)(2,1)S(1)}, u32[]{:S(2)}, u32[]{:S(2)}) collective-permute-start(bf16[4,192,256]{2,1,0:T(8,128)(2,1)S(1)} %constant_dynamic-update-slice_fusion.14), channel_id=1, source_target_pairs={{0,4},{1,3},{2,6},{3,1},{4,0},{5,7},{6,2},{7,5},{8,12},{9,11},{10,... | collective-permute-start | bytes 1179656 | tf_op jit(solution)/shard_map/rest0_out1/ppermute | solution.py:637
  195.1 17.2 %collective-permute-start.49 = (bf16[8,192,384]{2,1,0:T(8,128)(2,1)}, bf16[8,192,384]{2,1,0:T(8,128)(2,1)}, u32[]{:S(2)}, u32[]{:S(2)}) collective-permute-start(bf16[8,192,384]{2,1,0:T(8,128)(2,1)} %constant_dynamic-update-slice_fusion.16.refs_0_), channel_id=1, source_target_pairs={{0,2},{1,5},{2,0},{3,7},{4,6},{5,1},{6,4},{7,3},{8,10},{9,13},{10,... | collective-permute-start | bytes 3538952 | tf_op jit(solution)/shard_map/up_out0/ppermute | solution.py:637
  195.7 13.6 %collective-permute-start.46 = (bf16[4,192,128]{2,1,0:T(8,128)(2,1)S(1)}, bf16[4,192,128]{2,1,0:T(8,128)(2,1)S(1)}, u32[]{:S(2)}, u32[]{:S(2)}) collective-permute-start(bf16[4,192,128]{2,1,0:T(8,128)(2,1)S(1)} %constant_dynamic-update-slice_fusion.18), channel_id=1, source_target_pairs={{0,4},{1,3},{2,6},{3,1},{4,0},{5,7},{6,2},{7,5},{8,12},{9,11},{10,... | collective-permute-start | bytes 589832 | tf_op jit(solution)/shard_map/rest1_out1/ppermute | solution.py:637
  203.9 15.6 %collective-permute-start.45 = (bf16[8,192,256]{2,1,0:T(8,128)(2,1)}, bf16[8,192,256]{2,1,0:T(8,128)(2,1)}, u32[]{:S(2)}, u32[]{:S(2)}) collective-permute-start(bf16[8,192,256]{2,1,0:T(8,128)(2,1)} %constant_dynamic-update-slice_fusion.20.refs_0_), channel_id=1, source_target_pairs={{0,2},{1,5},{2,0},{3,7},{4,6},{5,1},{6,4},{7,3},{8,10},{9,13},{10,... | collective-permute-start | bytes 2359304 | tf_op jit(solution)/shard_map/rest0_out0/ppermute | solution.py:637
  209.4 13.9 %collective-permute-start.48 = (bf16[8,192,128]{2,1,0:T(8,128)(2,1)S(1)}, bf16[8,192,128]{2,1,0:T(8,128)(2,1)S(1)}, u32[]{:S(2)}, u32[]{:S(2)}) collective-permute-start(bf16[8,192,128]{2,1,0:T(8,128)(2,1)S(1)} %constant_dynamic-update-slice_fusion.22.refs_2_), channel_id=1, source_target_pairs={{0,2},{1,5},{2,0},{3,7},{4,6},{5,1},{6,4},{7,3},{8,10},{9,13},{10,... | collective-permute-start | bytes 1179656 | tf_op jit(solution)/shard_map/rest1_out0/ppermute | solution.py:637
  (26 other events, 86.9 us)

commit v3 on v2

v3 whole, which is shorter than its diff:
```python
from functools import partial

import jax
import jax.numpy as jnp
from jax import lax
from jax.experimental import pallas as pl
from jax.experimental.pallas import tpu as pltpu
from jax.sharding import PartitionSpec as P

HEAD = 64
LONG = 512
SHORT = 128
EPSILON = 1e-12
DECAY = 0.9
F32 = jnp.float32
BF16 = jnp.bfloat16
VMEM = pl.BlockSpec(memory_space=pltpu.VMEM)
SMEM = pl.BlockSpec(memory_space=pltpu.SMEM)
ORDER = (
    "down.theirshigh",
    "down.minehigh",
    "down.add0",
    "down.theirslow",
    "down.minelow",
    "up.theirs",
    "up.mine",
    "down.add1",
    "up.add0",
    "norm",
    "heads.theirs",
    "heads.mine",
    "rest.add0",
    "down.add2",
    "up.add1",
    "small.theirs",
    "input",
    "down.add3",
    "down.sum",
    "up.add2",
    "rest.add1",
    "down.join3",
    "up.add3",
    "rest.add2",
    "small.mine",
    "down.join2",
    "up.sum",
    "rest.add3",
    "small.sum0",
    "down.join1",
    "up.join3",
    "small.sum1",
    "rest.sum",
    "up.join2",
    "rest.join3",
    "small.sum2",
    "down.final",
    "rest.join2",
    "up.join1",
    "small.sum3",
    "rest.join1",
    "up.final",
    "rest.final",
)
COST = 1
LANES = 384
TILE = 64


def dot(a, b, ca, cb):
    return lax.dot_general(a, b, (((ca,), (cb,)), ((), ())), preferred_element_type=F32)


def shaped(shape, dtype):
    return jax.ShapeDtypeStruct(shape, dtype)


def call(
    body, out_shape, ins, scratch=(), in_specs=None, out_specs=None, limit=None
):
    nbytes = sum(a.size * a.dtype.itemsize for a in ins)
    nbytes += sum(o.size * o.dtype.itemsize for o in jax.tree.leaves(out_shape))
    params = dict(
        out_shape=out_shape,
        compiler_params=pltpu.CompilerParams(vmem_limit_bytes=limit or (nbytes + (6 << 20))),
        cost_estimate=pl.CostEstimate(flops=1, bytes_accessed=COST, transcendentals=0),
    )
    return pl.pallas_call(
        body, in_specs=in_specs, out_specs=out_specs, scratch_shapes=list(scratch), **params
    )(*ins)


def peak(value):
    top = jnp.max(jnp.abs(value.astype(F32)), axis=0, keepdims=True)
    return jnp.max(top, axis=1, keepdims=True)


def raise_peaks(pack, tiles):
    for row, tile in enumerate(tiles):
        at = slice(8 + row, 9 + row)
        pack[at, :] = jnp.maximum(pack[at, :], peak(tile))


def project_peaks_body(project, qv_bias, pack):
    @pl.when(pl.program_id(0) == 0)
    def _():
        pack[...] = jnp.zeros_like(pack)
        pack[0:2, :] = qv_bias[...]

    raise_peaks(pack, [project[0], project[1], project[2]])


def rest_peaks_body(merge, up, down, up_bias, pack):
    @pl.when(pl.program_id(0) == 0)
    def _():
        pack[...] = jnp.zeros_like(pack)
        pack[0:1, :] = up_bias[...]

    raise_peaks(pack, [merge[...], up[...], down[...]])


def scale_row(own, other, row, width):
    at = slice(8 + row, 9 + row)
    return 0.5 * jnp.maximum(own[at, 0:width], other[at, 0:width])


def clip_tile(value, scale):
    return (scale * jnp.tanh(value.astype(F32) * (1.0 / scale))).astype(BF16)


def clip_project_body(own, other, project, out):
    for part in range(3):
        out[part] = clip_tile(project[part], scale_row(own, other, part, LANES))


def clip_rest_body(own, other, merge, up, down, merge_q, up_q, down_q):
    for row, (src, dst) in enumerate(((merge, merge_q), (up, up_q), (down, down_q))):
        dst[...] = clip_tile(src[...], scale_row(own, other, row, src.shape[1]))


def key_bias(lengths, first):
    key = lax.broadcasted_iota(jnp.int32, (LONG, 1), 0)
    query = lax.broadcasted_iota(jnp.int32, (1, LONG), 1)
    single = lengths[first] > SHORT
    limit = jnp.full((LONG, 1), lengths[first], jnp.int32)
    for slot in range(1, LONG // SHORT):
        own = jnp.where(single, lengths[first], slot * SHORT + lengths[first + slot])
        limit = jnp.where(key >= slot * SHORT, own, limit)
    key_row = jnp.where(single, 0, key // SHORT)
    query_row = jnp.where(single, 0, query // SHORT)
    key_row = jnp.where(key < limit, key_row, -1)
    return jnp.where(key_row == query_row, 0.0, -1e30).astype(F32)


def qkv_into(xq, weight, bias_pack, q_ref, k_ref, v_ref):
    for part, ref in enumerate((q_ref, k_ref, v_ref)):
        value = dot(xq, weight[part], 1, 0)
        if part == 0:
            value = value + bias_pack[0:1, :]
        if part == 2:
            value = value + bias_pack[1:2, :]
        value = value.astype(BF16)
        if part == 0:
            value = value * jnp.asarray(0.125, BF16)
        ref[...] = value.T


def attend(lengths, first, q_ref, k_ref, v_ref, c_ref, lse_ref, bias_ref):
    bias_ref[...] = key_bias(lengths, first)

    def head(index, carry):
        at = pl.ds(pl.multiple_of(index * HEAD, HEAD), HEAD)
        scores = dot(k_ref[at, :], q_ref[at, :], 0, 0) + bias_ref[...]
        top = jnp.max(scores, axis=0, keepdims=True)
        prob = jnp.exp(scores - top)
        total = jnp.sum(prob, axis=0, keepdims=True)
        mixed = dot(v_ref[at, :], prob.astype(BF16), 1, 0)
        c_ref[at, :] = (mixed * (1.0 / total)).astype(BF16)
        lse_ref[pl.ds(index, 1), :] = top + jnp.log(total)
        return carry

    lax.fori_loop(0, q_ref.shape[0] // HEAD, head, 0)


def forward_first_body(
    ids, lengths, clips, inputs, weight, pack, xq, q_ref, k_ref, v_ref, c_ref, lse_ref, bias_ref
):
    scale = clips[0]
    xq[...] = clip_tile(inputs[...], scale)
    qkv_into(xq[...], weight, pack, q_ref, k_ref, v_ref)
    attend(lengths, ids[2], q_ref, k_ref, v_ref, c_ref, lse_ref, bias_ref)


def forward_second_body(
    ids, lengths, xq, weight, pack, q_ref, k_ref, v_ref, c_ref, lse_ref, bias_ref
):
    qkv_into(xq[...], weight, pack, q_ref, k_ref, v_ref)
    attend(lengths, ids[2], q_ref, k_ref, v_ref, c_ref, lse_ref, bias_ref)


def backward_heads_body(
    which,
    ids,
    lengths,
    xq,
    grad_branch,
    q_ref,
    k_ref,
    v_ref,
    c_ref,
    lse_ref,
    merge_q,
    *refs,
):
    *outs, d_ref, qv_row, bias_ref, g_ref, x_t = refs
    bias_ref[...] = key_bias(lengths, ids[2])
    x_t[...] = xq[...].T
    count, rel = outs[0].shape[0], ids[which]
    width = q_ref.shape[0]
    g_ref[...] = dot(merge_q[...], grad_branch[...], 1, 1).astype(BF16)

    def head(index, carry):
        at = pl.ds(pl.multiple_of(index * HEAD, HEAD), HEAD)
        q, k, v, g = q_ref[at, :], k_ref[at, :], v_ref[at, :], g_ref[at, :]
        scores = dot(k, q, 0, 0) + bias_ref[...]
        prob = jnp.exp(scores - lse_ref[pl.ds(index, 1), :])
        grad_prob = dot(v, g, 0, 0)
        inner = jnp.sum(g.astype(F32) * c_ref[at, :].astype(F32), axis=0, keepdims=True)
        grad_score = (prob * (grad_prob - inner)).astype(BF16)
        d_ref[2, at, :] = dot(g, prob.astype(BF16), 1, 1).astype(BF16)
        d_ref[0, at, :] = (dot(k, grad_score, 1, 0) * 0.125).astype(BF16)
        d_ref[1, at, :] = dot(q, grad_score, 1, 1).astype(BF16)
        return carry

    lax.fori_loop(0, width // HEAD, head, 0)
    rows, step = x_t.shape[0] // (2 * count), width // (2 * count)
    if len(outs) == 2:
        outs = [out.at[:, at * rows : (at + 1) * rows, :] for out in outs for at in range(4)]
    for half, parts in ((1, outs[:4]), (0, outs[4:])):
        base = half_base(rel, half, 2 * count)
        at = pl.ds(pl.multiple_of(base * rows, count * rows), count * rows)
        for part in range(3):
            grad = dot(x_t[at, :], d_ref[part], 1, 1).astype(BF16)
            for block in range(count):
                to = ((base + block) ^ rel) % count
                piece = grad[block * rows : (block + 1) * rows, :]
                parts[part][to] = piece
        at = pl.ds(pl.multiple_of(base * step, count * step), count * step)
        grad = dot(c_ref[at, :], grad_branch[...], 1, 0)
        for block in range(count):
            to = ((base + block) ^ rel) % count
            piece = grad[block * step : (block + 1) * step, :]
            piece = jnp.concatenate([piece[:, :width], piece[:, width:]], axis=0)
            parts[3][to] = piece.astype(BF16)
    ones = jnp.ones((8, xq.shape[0]), BF16)
    qv_row[:, 0:width] = dot(ones, d_ref[0], 1, 1)
    qv_row[:, width : 2 * width] = dot(ones, d_ref[2], 1, 1)


def gelu_parts(hidden, scale):
    area = 0.5 + 0.5 * lax.erf(hidden * 0.7071067811865476)
    bell = jnp.exp(-0.5 * hidden * hidden)
    active = hidden * area
    slope = area + hidden * bell * 0.3989422804014327
    bent = jnp.tanh(active * (1.0 / scale))
    return (scale * bent).astype(BF16), ((1.0 - bent * bent) * slope).astype(BF16), active


def fold(value, op):
    rows, lanes = value.shape
    return op(value.reshape(rows // 8, 8, lanes), axis=0)


def middle_body(
    clips,
    c_own,
    c_other,
    merge_own,
    merge_other,
    inputs,
    up_own,
    up_other,
    down_own,
    down_other,
    pack_own,
    pack_other,
    vectors,
    cotangent,
    unit_out,
    inverse_out,
    normed_q,
    active_own,
    active_other,
    factor_own,
    factor_other,
    output,
    grad_sum,
    grad_feed,
    sums,
    work,
    hidden_ref,
    tops,
    sum_ref,
):
    total = inputs.shape[0]
    work[...] = dot(c_own[...], merge_own[...], 0, 0) + dot(c_other[...], merge_other[...], 0, 0)
    tops[...] = jnp.zeros_like(tops)
    sum_ref[...] = jnp.zeros_like(sum_ref)
    clip_first, clip_second = clips[1], clips[2]

    def first_norm(index, carry):
        at = pl.ds(pl.multiple_of(index * TILE, TILE), TILE)
        rows = inputs[at, :].astype(F32)
        value = rows + work[at, :] + vectors[0:1, :]
        mean = jnp.mean(value, axis=-1, keepdims=True)
        centred = value - mean
        inverse = lax.rsqrt(jnp.mean(centred * centred, axis=-1, keepdims=True) + EPSILON)
        unit = centred * inverse
        normed = unit * vectors[2:3, :] + vectors[4:5, :]
        unit_out[at, :] = unit
        inverse_out[at, :] = jnp.broadcast_to(inverse, (TILE, 128))
        normed_q[at, :] = clip_tile(normed, clip_first)
        tops[0] = jnp.maximum(tops[0], fold(jnp.abs(rows), jnp.max))
        tops[1] = jnp.maximum(tops[1], fold(jnp.abs(normed), jnp.max))
        work[at, :] = normed
        return carry

    lax.fori_loop(0, total // TILE, first_norm, 0)
    span = hidden_ref.shape[1]
    for weight, pack, active_ref, factor_ref in (
        (up_own, pack_own, active_own, factor_own),
        (up_other, pack_other, active_other, factor_other),
    ):

        def columns(index, carry):
            cols = pl.ds(pl.multiple_of(index * span, span), span)
            hidden_ref[...] = dot(normed_q[...], weight[:, cols], 1, 0)
            bias = pack[0:1, cols]

            def rows(row, carry):
                at = pl.ds(pl.multiple_of(row * TILE, TILE), TILE)
                clipped, factor, active = gelu_parts(hidden_ref[at, :] + bias, clip_second)
                active_ref[at, cols] = clipped
                factor_ref[at, cols] = factor
                tops[2, :, 0:span] = jnp.maximum(tops[2, :, 0:span], fold(jnp.abs(active), jnp.max))
                return carry

            lax.fori_loop(0, total // TILE, rows, 0)
            return carry

        lax.fori_loop(0, weight.shape[1] // span, columns, 0)
    work[...] += dot(active_own[...], down_own[...], 1, 0) + dot(
        active_other[...], down_other[...], 1, 0
    )

    def second_norm(index, carry):
        at = pl.ds(pl.multiple_of(index * TILE, TILE), TILE)
        value = work[at, :] + vectors[1:2, :]
        mean = jnp.mean(value, axis=-1, keepdims=True)
        centred = value - mean
        inverse = lax.rsqrt(jnp.mean(centred * centred, axis=-1, keepdims=True) + EPSILON)
        unit = centred * inverse
        output[at, :] = (unit * vectors[3:4, :] + vectors[5:6, :]).astype(BF16)
        upstream = cotangent[at, :].astype(F32)
        scaled = upstream * vectors[3:4, :]
        grad = inverse * (
            scaled
            - jnp.mean(scaled, axis=-1, keepdims=True)
            - unit * jnp.mean(scaled * unit, axis=-1, keepdims=True)
        )
        grad_sum[at, :] = grad
        grad_feed[at, :] = grad.astype(BF16)
        sum_ref[0] += fold(upstream * unit, jnp.sum)
        sum_ref[1] += fold(upstream, jnp.sum)
        sum_ref[2] += fold(grad, jnp.sum)
        return carry

    lax.fori_loop(0, total // TILE, second_norm, 0)
    for row in range(3):
        sums[row : row + 1, :] = jnp.sum(sum_ref[row], axis=0, keepdims=True)
    for row in range(3):
        top = jnp.max(jnp.max(tops[row], axis=0, keepdims=True), axis=1, keepdims=True)
        sums[3 + row : 4 + row, :] = jnp.broadcast_to(top, (1, sums.shape[1]))
    sums[6:8, :] = jnp.zeros((2, sums.shape[1]), F32)


def half_base(rel, half, blocks):
    return (half ^ (rel // (blocks // 2))) * (blocks // 2)


def down_grad_body(which, half, ids, active, grad_feed, chunk):
    rel = ids[which]
    count = chunk.shape[0]
    rows = active.shape[1] // (2 * count)
    base = half_base(rel, half, 2 * count)
    per = count // 2
    for tile in range(2):
        first = base + tile * per
        cols = pl.ds(pl.multiple_of(first * rows, per * rows), per * rows)
        grad = dot(active[:, cols], grad_feed[...], 0, 0)
        for block in range(per):
            piece = grad[block * rows : (block + 1) * rows, :].astype(BF16)
            to = ((first + block) ^ rel) % count
            chunk[to, 0:rows, :] = piece[:, :LANES]
            chunk[to, rows : 2 * rows, :] = piece[:, LANES:]


def up_grad_body(
    which, ids, grad_feed, down, up, factor, normed_q, before, high, low, bias_row, grad_normed, g_ref
):
    rel = ids[which]
    count = high.shape[0]
    span = 512

    def columns(index, carry):
        cols = pl.ds(pl.multiple_of(index * span, span), span)
        grad = dot(grad_feed[...], down[cols, :], 1, 1) * factor[:, cols].astype(F32)
        grad = grad.astype(BF16)
        g_ref[:, cols] = grad
        bias_row[0:1, cols] = jnp.sum(grad.astype(F32), axis=0, keepdims=True)
        return carry

    lax.fori_loop(0, g_ref.shape[1] // span, columns, 0)
    rows = normed_q.shape[1] // (2 * count)
    for half, chunk in ((1, high), (0, low)):
        base = half_base(rel, half, 2 * count)
        cols = pl.ds(pl.multiple_of(base * rows, count * rows), count * rows)
        grad = dot(normed_q[:, cols], g_ref[...], 0, 0)
        for block in range(count):
            to = ((base + block) ^ rel) % count
            for part in range(grad.shape[1] // LANES):
                piece = grad[block * rows : (block + 1) * rows, part * LANES : (part + 1) * LANES]
                chunk[to, part * rows : (part + 1) * rows, :] = piece.astype(BF16)
    result = dot(g_ref[...], up[...], 1, 1)
    if before is not None:
        result = result + before[...]
    grad_normed[...] = result


def up_grad_first_body(which, ids, grad_feed, down, up, factor, normed_q, *outs):
    up_grad_body(which, ids, grad_feed, down, up, factor, normed_q, None, *outs)


def first_norm_back_body(
    clips,
    grad_normed,
    grad_sum,
    unit_ref,
    inverse_ref,
    vectors,
    sums,
    bias_other,
    bias_own,
    grad_first,
    grad_branch,
    pack_other,
    pack_own,
    sum_ref,
):
    clip_first = clips[1]
    sum_ref[...] = jnp.zeros_like(sum_ref)

    def rows(index, carry):
        at = pl.ds(pl.multiple_of(index * TILE, TILE), TILE)
        unit = unit_ref[at, :]
        bent = jnp.tanh((unit * vectors[2:3, :] + vectors[4:5, :]) * (1.0 / clip_first))
        grad = grad_normed[at, :] * (1.0 - bent * bent) + grad_sum[at, :]
        scaled = grad * vectors[2:3, :]
        back = inverse_ref[at, 0:1] * (
            scaled
            - jnp.mean(scaled, axis=-1, keepdims=True)
            - unit * jnp.mean(scaled * unit, axis=-1, keepdims=True)
        )
        grad_first[at, :] = back
        grad_branch[at, :] = back.astype(BF16)
        sum_ref[0] += fold(grad * unit, jnp.sum)
        sum_ref[1] += fold(grad, jnp.sum)
        sum_ref[2] += fold(back, jnp.sum)
        return carry

    lax.fori_loop(0, unit_ref.shape[0] // TILE, rows, 0)
    width = unit_ref.shape[1]
    for pack, bias in ((pack_other, bias_other), (pack_own, bias_own)):
        pack[...] = jnp.zeros_like(pack)
        for row, source in ((0, 0), (2, 1), (4, 2)):
            pack[row : row + 1, :] = jnp.sum(sum_ref[source], axis=0, keepdims=True)
        pack[1:2, :] = sums[0:1, :]
        pack[3:4, :] = sums[1:2, :]
        pack[5:6, :] = sums[2:3, :]
        pack[6:7, :] = bias[0:1, 0:width]
        pack[7:8, :] = bias[0:1, width : 2 * width]
        pack[12:15, :] = sums[3:6, :]


def input_grad_body(clips, inputs, grad_first, w_own, w_other, d_own, d_other, out):
    terms = []
    for d_ref, weight in ((d_own, w_own), (d_other, w_other)):
        for part in range(3):
            terms.append(dot(d_ref[part], weight[part], 0, 1))
    bent = jnp.tanh(inputs[...].astype(F32) * (1.0 / clips[0]))
    out[...] = sum(terms[1:], terms[0]) * (1.0 - bent * bent) + grad_first[...]


def slope_of(weight, scale):
    bent = jnp.tanh(weight.astype(F32) * (1.0 / scale))
    return 1.0 - bent * bent


def block_value(rel, low, high, at):
    half = low.shape[0]
    at = at ^ rel
    first = low[jnp.minimum(at, half - 1)].astype(F32)
    return jnp.where(at < half, first, high[jnp.maximum(at - half, 0)].astype(F32))


def down_final_body(per, ids, own, other, low, high, weight, out):
    rows = weight.shape[0] // per
    slope = slope_of(weight[...], scale_row(own, other, 2, weight.shape[1]))
    for index in range(per):
        value = block_value(ids[0], low, high, pl.program_id(0) * per + index)
        at = slice(index * rows, (index + 1) * rows)
        out[at, :LANES] = value[:rows] * slope[at, :LANES]
        out[at, LANES:] = value[rows:] * slope[at, LANES:]


def up_final_body(per, ids, own, other, low, high, weight, out):
    rows = weight.shape[0] // per
    slope = slope_of(weight[...], scale_row(own, other, 1, weight.shape[1]))
    for index in range(per):
        value = block_value(ids[0], low, high, pl.program_id(0) * per + index)
        at = slice(index * rows, (index + 1) * rows)
        for part in range(weight.shape[1] // LANES):
            cols = slice(part * LANES, (part + 1) * LANES)
            out[at, cols] = value[part * rows : (part + 1) * rows] * slope[at, cols]


def rest_final_body(
    per, ids, own, other, low, high, p_own, p_other, project, merge, project_out, merge_out
):
    rows = project.shape[1] // per
    slopes = []
    for part in range(3):
        slopes.append(slope_of(project[part], scale_row(p_own, p_other, part, LANES)))
    scale = scale_row(own, other, 0, merge.shape[1])
    values = []
    for index in range(per):
        value = block_value(ids[0], low, high, pl.program_id(0) * per + index)
        values.append(value[3 * rows :])
        at = slice(index * rows, (index + 1) * rows)
        for part in range(3):
            project_out[part, at, :] = value[part * rows : (part + 1) * rows] * slopes[part][at]
    step = merge.shape[0] // per
    slope = slope_of(merge[...], scale)
    for part in range(2):
        across = slice(part * LANES, (part + 1) * LANES)
        piece = jnp.concatenate([v[part * step : (part + 1) * step] for v in values], axis=0)
        merge_out[:, across] = piece * slope[:, across]


class Exchange:
    def __init__(self, size, first):
        self.bits = size.bit_length() - 1
        assert 1 << self.bits == size and self.bits >= 4
        self.size = size
        self.orders = [list(order) + list(range(4, self.bits)) for order in first]
        self.blocks = 16

    def relative(self, position, core):
        total = 0
        for stage in range(4):
            bit = (position >> self.orders[core][stage]) & 1
            total = total + (bit << (3 - stage))
        return total

    def swap(self, value, stage):
        pairs = []
        for index in range(self.size):
            for core in range(2):
                to = index ^ (1 << self.orders[core][stage])
                pairs.append((2 * index + core, 2 * to + core))
        return lax.ppermute(value, ("dp", "tensor"), pairs)

    def core_swap(self, value):
        return lax.ppermute(value, "tensor", [(0, 1), (1, 0)])


class Task:
    def __init__(self, body, deps):
        self.body, self.deps, self.sends = body, list(deps), []


class Plan:
    def __init__(self):
        self.tasks = {}
        self.values = {}
        self.source = {}

    def given(self, name, value):
        self.values[name] = value
        return name

    def core(self, name, body, deps):
        self.tasks[name] = Task(body, deps)
        return name

    def send(self, name, source, body):
        self.tasks[source].sends.append((name, body))
        self.source[name] = source
        return name

    def run(self):
        values, last = dict(self.values), None

        def take(name):
            nonlocal last
            if name in values:
                return
            if name in self.source:
                take(self.source[name])
                return
            task = self.tasks[name]
            for dep in task.deps:
                take(dep)
            inputs = [values[dep] for dep in task.deps]
            if last is not None:
                inputs, last = lax.optimization_barrier((inputs, last))
            with jax.named_scope(name.replace(".", "_")):
                result = task.body(*inputs)
            values[name] = result
            last = jax.tree.leaves(result)[0]
            for sent, body in task.sends:
                with jax.named_scope(sent.replace(".", "_")):
                    values[sent] = body(result)

        for name in ORDER:
            if name in self.tasks:
                take(name)
        for name in self.tasks:
            take(name)
        return values

    def swap(self, name, source, way, stage, pick=lambda value: value):
        return self.send(name, source, lambda value: way.swap(pick(value), stage))

    def reduce(self, name, way, mine, theirs, pick):
        def swapped(index):
            return lambda v: [way.core_swap(value) for value in pick(v, index)]

        def whole(values):
            return values[0] if len(values) == 1 else jnp.concatenate(values, axis=1)

        high = self.send(name + ".high", theirs[0], swapped(0))
        low = self.send(name + ".low", theirs[1], swapped(1))
        value = self.core(
            f"{name}.add0",
            lambda mine, high: total([whole(pick(mine, 0)), whole(high)]),
            [mine[0], high],
        )
        got = self.swap(f"{name}.in0", value, way, 0)

        def second(mine, low, got):
            return split_in_two([whole(pick(mine, 1)), whole(low), got])

        def more(kept, got):
            return split_in_two([kept[0], got])

        value = self.core(f"{name}.add1", second, [mine[1], low, got])
        for stage in (1, 2, 3):
            got = self.swap(f"{name}.in{stage}", value, way, stage, second_of)
            if stage < 3:
                value = self.core(f"{name}.add{stage + 1}", more, [value, got])
        value = self.core(f"{name}.sum", lambda kept, got: total([kept[0], got]), [value, got])
        for stage in range(4, way.bits):
            sent = self.swap(f"{name}.in{stage}", value, way, stage)
            value = self.core(f"{name}.sum{stage}", lambda a, b: total([a, b]), [value, sent])
        for stage in reversed(range(4)):
            sent = self.swap(f"{name}.out{stage}", value, way, stage)
            if stage > 0:
                value = self.core(
                    f"{name}.join{stage}",
                    lambda a, b: jnp.concatenate([a, b], axis=0),
                    [value, sent],
                )
        return [value, sent]


def total(values):
    out = values[0].astype(F32)
    for value in values[1:]:
        out = out + value.astype(F32)
    return out.astype(BF16)


def split_in_two(values):
    half = values[0].shape[0] // 2
    return total([value[:half] for value in values]), total([value[half:] for value in values])


def second_of(value):
    return value[1]


def local(
    inputs,
    row_lengths,
    project_weight,
    merge_weight,
    up_weight,
    down_weight,
    query_value_bias,
    merge_bias,
    up_bias,
    down_bias,
    norm_gains,
    norm_shifts,
    clip_scales,
    cotangent,
):
    size = lax.axis_size("dp")
    exchange = Exchange(size, ((0, 1, 2, 3), (1, 0, 2, 3)))
    same_way = Exchange(size, ((0, 1, 2, 3), (0, 1, 2, 3)))
    blocks = exchange.blocks
    member = lax.axis_index("tensor")
    place = lax.axis_index("dp")
    rel0, rel1 = exchange.relative(place, 0), exchange.relative(place, 1)
    own_rel = jnp.where(member == 0, rel0, rel1)
    other_rel = jnp.where(member == 0, rel1, rel0)
    ids = jnp.stack([own_rel, other_rel, member * (LONG // SHORT)]).astype(jnp.int32)
    total, width = inputs.shape
    hidden = up_weight.shape[1]
    project = jnp.transpose(project_weight, (1, 0, 2))

    steps = 4
    small_grid = pltpu.CompilerParams(vmem_limit_bytes=12 << 20)
    project_block = pl.BlockSpec((3, width // steps, LANES), lambda i: (0, i, 0))
    rest_blocks = [
        pl.BlockSpec((LANES // steps, width), lambda i: (i, 0)),
        pl.BlockSpec((width // steps, hidden), lambda i: (i, 0)),
        pl.BlockSpec((hidden // steps, width), lambda i: (i, 0)),
    ]
    project_pack_spec = pl.BlockSpec((16, LANES), lambda i: (0, 0))
    pack_spec = pl.BlockSpec((16, hidden), lambda i: (0, 0))
    rest_weights = (merge_weight, up_weight, down_weight)

    def project_peaks():
        return pl.pallas_call(
            project_peaks_body,
            grid=(steps,),
            in_specs=[project_block, pl.BlockSpec((2, LANES), lambda i: (0, 0))],
            out_specs=project_pack_spec,
            out_shape=shaped((16, LANES), F32),
            compiler_params=small_grid,
        )(project, query_value_bias)

    def rest_peaks(weights):
        return pl.pallas_call(
            rest_peaks_body,
            grid=(steps,),
            in_specs=rest_blocks + [pl.BlockSpec((1, hidden), lambda i: (0, 0))],
            out_specs=pack_spec,
            out_shape=shaped((16, hidden), F32),
            compiler_params=small_grid,
        )(*weights, up_bias[None])

    def clip_project(own, other):
        return pl.pallas_call(
            clip_project_body,
            grid=(steps,),
            in_specs=[project_pack_spec, project_pack_spec, project_block],
            out_specs=project_block,
            out_shape=shaped(project.shape, BF16),
            compiler_params=small_grid,
        )(own, other, project)

    def clip_rest(own, other):
        return pl.pallas_call(
            clip_rest_body,
            grid=(steps,),
            in_specs=[pack_spec, pack_spec] + rest_blocks,
            out_specs=rest_blocks,
            out_shape=[shaped(a.shape, BF16) for a in rest_weights],
            compiler_params=small_grid,
        )(own, other, *rest_weights)

    project_own_pack = project_peaks()
    project_other_pack = exchange.core_swap(project_own_pack)
    project_own = clip_project(project_own_pack, project_other_pack)
    project_other = exchange.core_swap(project_own)
    tied, project_own = lax.optimization_barrier((rest_weights, project_own))
    own_pack = rest_peaks(tied)
    other_pack = exchange.core_swap(own_pack)
    other_pack, project_other = lax.optimization_barrier((other_pack, project_other))
    merge_own, up_own, down_own = clip_rest(own_pack, other_pack)
    merge_other = exchange.core_swap(merge_own)
    up_other = exchange.core_swap(up_own)
    down_other = exchange.core_swap(down_own)
    project_own, merge_own = lax.optimization_barrier((project_own, merge_own))

    head_shape = shaped((LANES, total), BF16)
    heads_out = [head_shape] * 4 + [shaped((8, total), F32)]
    mask_scratch = pltpu.VMEM((LONG, LONG), F32)
    xq, *own_heads = call(
        forward_first_body,
        [shaped((total, width), BF16)] + heads_out,
        (ids, row_lengths, clip_scales, inputs, project_own, project_own_pack),
        [mask_scratch],
        in_specs=[SMEM] * 3 + [VMEM] * 3,
        out_specs=[VMEM] * 6,
        limit=16 << 20,
    )
    other_heads = call(
        forward_second_body,
        heads_out,
        (ids, row_lengths, xq, project_other, project_other_pack),
        [mask_scratch],
        in_specs=[SMEM] * 2 + [VMEM] * 3,
        out_specs=[VMEM] * 5,
        limit=16 << 20,
    )

    vectors = jnp.concatenate([merge_bias[None], down_bias[None], norm_gains, norm_shifts], axis=0)
    rows_f32 = shaped((total, width), F32)
    rows_bf16 = shaped((total, width), BF16)
    wide = shaped((total, hidden), BF16)
    (
        unit,
        inverse,
        normed_q,
        active_own,
        active_other,
        factor_own,
        factor_other,
        output,
        grad_sum,
        grad_feed,
        sums,
    ) = call(
        middle_body,
        [
            rows_f32,
            shaped((total, 128), F32),
            rows_bf16,
            wide,
            wide,
            wide,
            wide,
            rows_bf16,
            rows_f32,
            rows_bf16,
            shaped((8, width), F32),
        ],
        (
            clip_scales,
            own_heads[3],
            other_heads[3],
            merge_own,
            merge_other,
            inputs,
            up_own,
            up_other,
            down_own,
            down_other,
            own_pack,
            other_pack,
            vectors,
            cotangent,
        ),
        [
            pltpu.VMEM((total, width), F32),
            pltpu.VMEM((total, 256), F32),
            pltpu.VMEM((3, 8, width), F32),
            pltpu.VMEM((3, 8, width), F32),
        ],
        in_specs=[SMEM] + [VMEM] * 13,
        out_specs=[VMEM] * 11,
        limit=32 << 20,
    )

    plan = Plan()
    chunk = shaped((blocks // 2, 2 * hidden // blocks, LANES), BF16)

    def down_half(which, half, active, grad):
        return call(
            partial(down_grad_body, which, half),
            chunk,
            (ids, active, grad),
            in_specs=[SMEM] + [VMEM] * 2,
            out_specs=VMEM,
            limit=9 << 20,
        )

    feed = plan.given("feed", grad_feed)
    down_tasks = {}
    for half, word in ((1, "high"), (0, "low")):
        for which, active in ((1, active_other), (0, active_own)):
            down_tasks[which, half] = plan.core(
                ("down.mine", "down.theirs")[which] + word,
                lambda grad, which=which, half=half, active=active: down_half(
                    which, half, active, grad
                ),
                [feed],
            )

    def take(index):
        return lambda values: values[index]

    def part(values, index):
        return values[index]

    def one(values, index):
        return [values[index]]

    down_out = plan.reduce(
        "down",
        exchange,
        (down_tasks[0, 1], down_tasks[0, 0]),
        (down_tasks[1, 1], down_tasks[1, 0]),
        lambda value, index: [value],
    )

    def up_half(body, which, grad, down, up, factor, *before):
        return call(
            partial(body, which),
            [chunk, chunk, shaped((1, hidden), F32), rows_f32],
            (ids, grad, down, up, factor, normed_q) + before,
            [pltpu.VMEM((total, hidden), BF16)],
            in_specs=[SMEM] + [VMEM] * (5 + len(before)),
            out_specs=[VMEM] * 4,
            limit=20 << 20,
        )

    up_theirs = plan.core(
        "up.theirs",
        lambda grad: up_half(
            up_grad_first_body, 1, grad, down_other, up_other, factor_other
        ),
        [feed],
    )
    up_mine = plan.core(
        "up.mine",
        lambda grad, before: up_half(
            up_grad_body, 0, grad, down_own, up_own, factor_own, before[3]
        ),
        [feed, up_theirs],
    )
    up_out = plan.reduce("up", exchange, (up_mine, up_mine), (up_theirs, up_theirs), one)

    small = shaped((16, width), F32)

    def norm_back(theirs, mine):
        ins = (clip_scales, mine[3], grad_sum, unit, inverse, vectors, sums, theirs[2], mine[2])
        return call(
            first_norm_back_body,
            [rows_f32, rows_bf16, small, small],
            ins,
            [pltpu.VMEM((3, 8, width), F32)],
            in_specs=[SMEM] + [VMEM] * 8,
            out_specs=[VMEM] * 4,
        )

    first_back = plan.core("norm", norm_back, [up_theirs, up_mine])

    def heads_back(which, back, heads, merge_q):
        count = (1, 4)[which]
        parts = [shaped((chunk.shape[0], chunk.shape[1] // count, LANES), BF16)] * count
        *outs, grads, row = call(
            partial(backward_heads_body, which),
            parts + parts + [shaped((3, LANES, total), BF16), shaped((8, 2 * LANES), F32)],
            (ids, row_lengths, xq, back[1]) + tuple(heads) + (merge_q,),
            [
                mask_scratch,
                pltpu.VMEM((LANES, total), BF16),
                pltpu.VMEM((width, total), BF16),
            ],
            in_specs=[SMEM] * 2 + [VMEM] * 8,
            out_specs=[VMEM] * (2 * count + 2),
            limit=18 << 20,
        )
        return outs[:count], outs[count:], grads, row

    heads_theirs = plan.core(
        "heads.theirs", lambda back: heads_back(1, back, other_heads, merge_other), [first_back]
    )
    heads_mine = plan.core(
        "heads.mine", lambda back: heads_back(0, back, own_heads, merge_own), [first_back]
    )
    rest_out = plan.reduce(
        "rest", exchange, (heads_mine, heads_mine), (heads_theirs, heads_theirs), part
    )

    def input_part(back, theirs, mine):
        return call(
            input_grad_body,
            rows_f32,
            (clip_scales, inputs, back[0], project_own, project_other, mine[2], theirs[2]),
            in_specs=[SMEM] + [VMEM] * 6,
            out_specs=VMEM,
            limit=16 << 20,
        )

    input_task = plan.core("input", input_part, [first_back, heads_theirs, heads_mine])

    def joined(sums_part, row):
        return jnp.concatenate([sums_part[:8], row[0:1], sums_part[12:15]], axis=0)

    small_row = lax.broadcasted_iota(jnp.int32, (12, width), 0)

    def merge_small(a, b):
        return jnp.where(small_row < 9, a + b, jnp.maximum(a, b))

    theirs_small = plan.core(
        "small.theirs", lambda back, heads: joined(back[2], heads[3]), [first_back, heads_theirs]
    )
    small_got = plan.send("small.got", theirs_small, exchange.core_swap)
    small_value = plan.core(
        "small.mine",
        lambda got, back, heads: merge_small(joined(back[3], heads[3]), got),
        [small_got, first_back, heads_mine],
    )
    for stage in range(exchange.bits):
        swap = partial(same_way.swap, stage=stage)
        small_in = plan.send(f"small.in{stage}", small_value, swap)
        small_value = plan.core(f"small.sum{stage}", merge_small, [small_value, small_in])

    final_steps = 4
    per = blocks // final_steps

    def final(body, parts, weights, specs, packs=()):
        part_specs = [pl.BlockSpec(part.shape, lambda i, s: (0, 0, 0)) for part in parts]
        pack = pl.BlockSpec((16, hidden), lambda i, s: (0, 0))
        ins = (ids, own_pack, other_pack) + tuple(parts) + tuple(packs) + weights
        return pl.pallas_call(
            partial(body, per),
            grid_spec=pltpu.PrefetchScalarGridSpec(
                num_scalar_prefetch=1,
                grid=(final_steps,),
                in_specs=[pack, pack]
                + part_specs
                + [pl.BlockSpec((16, LANES), lambda i, s: (0, 0))] * len(packs)
                + specs,
                out_specs=specs,
            ),
            out_shape=[shaped(weight.shape, F32) for weight in weights],
            compiler_params=pltpu.CompilerParams(vmem_limit_bytes=10 << 20),
            cost_estimate=pl.CostEstimate(flops=1, bytes_accessed=1, transcendentals=0),
        )(*ins)

    down_spec = pl.BlockSpec((hidden // final_steps, width), lambda i, s: (i, 0))
    plan.core(
        "down.final",
        lambda *parts: final(down_final_body, parts, (down_weight,), [down_spec])[0],
        down_out,
    )
    up_spec = pl.BlockSpec((width // final_steps, hidden), lambda i, s: (i, 0))
    plan.core(
        "up.final",
        lambda *parts: final(up_final_body, parts, (up_weight,), [up_spec])[0],
        up_out,
    )
    project_spec = pl.BlockSpec((3, width // final_steps, LANES), lambda i, s: (0, i, 0))
    merge_spec = pl.BlockSpec((LANES // final_steps, width), lambda i, s: (i, 0))
    plan.core(
        "rest.final",
        lambda *parts: final(
            rest_final_body,
            parts,
            (project, merge_weight),
            [project_spec, merge_spec],
            (project_own_pack, project_other_pack),
        ),
        rest_out,
    )
    values = plan.run()
    small_all = values[small_value]
    project_grad, merge_grad = values["rest.final"]
    peaks = small_all[9:12, 0]
    return (
        output,
        values[input_task],
        jnp.transpose(project_grad, (1, 0, 2)),
        merge_grad,
        values["up.final"],
        values["down.final"],
        small_all[8].reshape(2, LANES),
        small_all[4],
        small_all[6:8].reshape(hidden),
        small_all[5],
        small_all[0:2],
        small_all[2:4],
        DECAY * clip_scales + (1.0 - DECAY) * peaks,
    )


def solution(mesh):
    return jax.shard_map(
        local,
        mesh=mesh,
        in_specs=(
            P(("dp", "tensor"), None),
            P("dp"),
            P(None, None, "tensor"),
            P("tensor", None),
            P(None, "tensor"),
            P("tensor", None),
            P(None, "tensor"),
            P(),
            P("tensor"),
            P(),
            P(),
            P(),
            P(),
            P(("dp", "tensor"), None),
        ),
        out_specs=(
            P(("dp", "tensor"), None),
            P(("dp", "tensor"), None),
            P(None, None, "tensor"),
            P("tensor", None),
            P(None, "tensor"),
            P("tensor", None),
            P(None, "tensor"),
            P(),
            P("tensor"),
            P(),
            P(),
            P(),
            P(),
        ),
        check_vma=False,
    )
```

time: 233 us -> 229 us (0.983); the launches traced: 230 us -> 228 us
  waiting for transfers between devices: 50.8 us -> 69 us
  local copies, waits for them, and re-layouts: 19.4 us -> 12.3 us
  Pallas kernels: 106 us -> 99.5 us
  starting transfers between devices: 47.4 us -> 41.6 us
    ppermute x36 -> x28, waiting for transfers between devices: 49.4 us -> 63.6 us  [swap(): return lax.ppermute(value, ('dp', 'tensor'), pairs)]
    ppermute x36 -> x28, starting transfers between devices: 38.7 us -> 32.9 us  [swap(): return lax.ppermute(value, ('dp', 'tensor'), pairs)]
    pallas_call x11 -> x13, Pallas kernels: 84.8 us -> 79.4 us  [call(): pl.pallas_call(body, in_specs=in_specs, out_specs=out_specs, scratch_shap...]
    unnamed x60 -> x68, local copies, waits for them, and re-layouts: 11.9 us -> 7.77 us
    ppermute x14 -> x19, waiting for transfers between devices: 1.43 us -> 5.36 us  [core_swap(): return lax.ppermute(value, 'tensor', [(0, 1), (1, 0)])]
    pallas_call x6 -> x7, Pallas kernels: 20.8 us -> 20.1 us  [the longest x3 14.4 us: final(): pl.pallas_call(partial(body, per), grid_spec=pltpu.PrefetchScalarGridSpec...]
    ppermute x14 -> x19, starting transfers between devices: 8.65 us -> 8.69 us  [core_swap(): return lax.ppermute(value, 'tensor', [(0, 1), (1, 0)])]
  transfers between devices with their start and end apart: 50 -> 47, of which waited for: 14 -> 19; matrix products, arithmetic and copies ran while one was open for 5% -> 5% of each run, Pallas kernels for 30% -> 28%
where the time goes in v3:
time: 229 us; the launch traced here: 228 us
  Pallas kernels  99.5 us (43%)
  waiting for transfers between devices  69 us (30%)
  starting transfers between devices  41.6 us (18%)
  local copies, waits for them, and re-layouts  12.3 us (5%)
  other arithmetic  4.42 us (2%)
    pallas_call x13, Pallas kernels, call(): pl.pallas_call(body, in_specs=in_specs, out_specs=out_specs, scratch_shap...  79.4 us
    ppermute x28, waiting for transfers between devices, swap(): return lax.ppermute(value, ('dp', 'tensor'), pairs)  63.6 us
    ppermute x28, starting transfers between devices, swap(): return lax.ppermute(value, ('dp', 'tensor'), pairs)  32.9 us
    pallas_call x3, Pallas kernels, final(): pl.pallas_call(partial(body, per), grid_spec=pltpu.PrefetchScalarGridSpec...  14.4 us
    ppermute x19, starting transfers between devices, core_swap(): return lax.ppermute(value, 'tensor', [(0, 1), (1, 0)])  8.69 us
    unnamed x68, local copies, waits for them, and re-layouts  7.77 us
    ppermute x19, waiting for transfers between devices, core_swap(): return lax.ppermute(value, 'tensor', [(0, 1), (1, 0)])  5.36 us
  transfers between devices with their start and end apart: 47, of which 19 were waited for; matrix products, arithmetic and copies ran while one was open for 5% of the time, Pallas kernels for 28%

profile of v3, /device:TPU:1, one launch (start us, length us, event | category | flops | bytes accessed | tf_op | source)
XLA Modules:
  0.0 228.2 jit_solution(5848863678311067972)
XLA Ops:
  0.7 1.5 copy-done.3
  7.6 2.2 collective-permute-done.1.other.pack_other
  9.7 1.2 copy-done.8
  11.0 3.0 %shard_map.240 = (bf16[384,768]{1,0:T(8,128)(2,1)}, bf16[768,1536]{1,0:T(8,128)(2,1)}, bf16[1536,768]{1,0:T(8,128)(2,1)}) custom-call(f32[16,1536]{1,0:T(8,128)S(1)} %shard_map.239.own.pack_own, f32[16,1536]{1,0:T(8,128)S(1)} %collective-permute-done.1.other.pack_other, bf16[384,768]{1,0:T(8,128)(2,1)S(1)} %copy-done.11, bf16[768,1536]{1,0:T(8,128)(2,1)S(1)} %copy-done.1, ...), custom_call_target="tpu_custom_call" | custom-call | tf_op jit(solution)/shard_map/pallas_call | solution.py:775
  14.8 1.5 copy-done.6
  16.3 6.1 %shard_map.241 = (bf16[512,768]{1,0:T(8,128)(2,1)S(1)}, bf16[384,512]{1,0:T(8,128)(2,1)S(1)}, bf16[384,512]{1,0:T(8,128)(2,1)S(1)}, bf16[384,512]{1,0:T(8,128)(2...) custom-call(s32[3]{0:T(128)S(1)} %pad_add_fusion.ids, s32[8]{0:T(128)S(1)} %copy-done.20, f32[3]{0:T(128)S(1)} %copy-done.21, ...), custom_call_target="tpu_custom_call" | custom-call | flops 1 | bytes 1 | tf_op jit(solution)/shard_map/pallas_call | solution.py:87
  22.4 6.1 %shard_map.242 = (bf16[384,512]{1,0:T(8,128)(2,1)S(1)}, bf16[384,512]{1,0:T(8,128)(2,1)S(1)}, bf16[384,512]{1,0:T(8,128)(2,1)S(1)}, bf16[384,512]{1,0:T(8,128)(2,1)S(1)}, f32[8,512]{1,0:T(8,128)S(1)}) custom-call(s32[3]{0:T(128)S(1)} %pad_add_fusion.ids, s32[8]{0:T(128)S(1)} %copy-done.20, bf16[512,768]{1,0:T(8,128)(2,1)S(1)} %get-tuple-element.172.xq, ...), custom_call_target="tpu_custom_call" | custom-call | flops 1 | bytes 1 | tf_op jit(solution)/shard_map/pallas_call | solution.py:87
  29.3 23.4 %shard_map.243 = (f32[512,768]{1,0:T(8,128)S(1)}, f32[512,128]{1,0:T(8,128)S(1)}, bf16[512,768]{1,0:T(8,128)(2,1)S(1)}, bf16[512,1536]{1,0:T(8,128)(2,1)S(1)}, b...) custom-call(f32[3]{0:T(128)S(1)} %copy-done.21, ...), custom_call_target="tpu_custom_call" | custom-call | flops 1 | bytes 1 | tf_op jit(solution)/shard_map/pallas_call | solution.py:87
  52.8 1.4 down_theirshigh.1
  54.5 1.4 down_minehigh.1
  57.4 1.4 down_theirslow.1
  59.2 2.4 %collective-permute-start.9 = (bf16[8,192,384]{2,1,0:T(8,128)(2,1)S(1)}, bf16[8,192,384]{2,1,0:T(8,128)(2,1)S(1)}, u32[]{:S(2)}, u32[]{:S(2)}) collective-permute-start(bf16[8,192,384]{2,1,0:T(8,128)(2,1)S(1)} %add_convert_fusion.2), channel_id=1, source_target_pairs={{0,2},{1,5},{2,0},{3,7},{4,6},{5,1},{6,4},{7,3},{8,10},{9,13},{10,... | collective-permute-start | bytes 3538952 | tf_op jit(solution)/shard_map/down_in0/ppermute | solution.py:580
  61.6 1.4 down_minelow.1
  62.9 7.2 %up_theirs.1 = (bf16[8,192,384]{2,1,0:T(8,128)(2,1)S(1)}, bf16[8,192,384]{2,1,0:T(8,128)(2,1)S(1)}, f32[1,1536]{1,0:T(1,128)S(1)}, f32[512,768]{1,0:T(8,128)S(1)}) custom-call(s32[3]{0:T(128)S(1)} %pad_add_fusion.ids, bf16[512,768]{1,0:T(8,128)(2,1)S(1)} %get-tuple-element.194.grad_feed, bf16[1536,768]{1,0:T(8,128)(2,1)} %collective-permute-done.5.down_other.down, ...), custom_call_target="tpu_custom_call" | custom-call | flops 1 | bytes 1 | tf_op jit(solution)/shard_map/up_theirs/pallas_call | solution.py:87
  70.9 7.0 %up_mine.1 = (bf16[8,192,384]{2,1,0:T(8,128)(2,1)S(1)}, bf16[8,192,384]{2,1,0:T(8,128)(2,1)S(1)}, f32[1,1536]{1,0:T(1,128)S(1)}, f32[512,768]{1,0:T(8,128)S(1)}) custom-call(s32[3]{0:T(128)S(1)} %pad_add_fusion.ids, bf16[512,768]{1,0:T(8,128)(2,1)S(1)} %get-tuple-element.194.grad_feed, bf16[1536,768]{1,0:T(8,128)(2,1)} %get-tuple-element.177.down_own.down, ...), custom_call_target="tpu_custom_call" | custom-call | flops 1 | bytes 1 | tf_op jit(solution)/shard_map/up_mine/pallas_call | solution.py:87
  78.8 1.3 collective-permute-start.11
  80.1 2.4 %norm.1 = (f32[512,768]{1,0:T(8,128)S(1)}, bf16[512,768]{1,0:T(8,128)(2,1)S(1)}, f32[16,768]{1,0:T(8,128)S(1)}, f32[16,768]{1,0:T(8,128)S(1)}) custom-call(f32[3]{0:T(128)S(1)} %copy-done.21, f32[512,768]{1,0:T(8,128)S(1)} %get-tuple-element.206.grad_normed, f32[512,768]{1,0:T(8,128)S(1)} %get-tuple-element.207.grad_sum, ...), custom_call_target="tpu_custom_call" | custom-call | flops 1 | bytes 1 | tf_op jit(solution)/shard_map/norm/pallas_call | solution.py:87
  82.5 8.5 %heads_theirs.1 = (bf16[8,48,384]{2,1,0:T(8,128)(2,1)S(1)}, bf16[8,48,384]{2,1,0:T(8,128)(2,1)S(1)}, bf16[8,48,384]{2,1,0:T(8,128)(2,1)S(1)}, bf16[8,48,384]{2,1...) custom-call(s32[3]{0:T(128)S(1)} %pad_add_fusion.ids, ...), custom_call_target="tpu_custom_call" | custom-call | flops 1 | bytes 1 | tf_op jit(solution)/shard_map/heads_theirs/pallas_call | solution.py:87
  93.2 8.7 %heads_mine.1 = (bf16[8,192,384]{2,1,0:T(8,128)(2,1)S(1)}, bf16[8,192,384]{2,1,0:T(8,128)(2,1)S(1)}, bf16[3,384,512]{2,1,0:T(8,128)(2,1)S(1)}, f32[8,768]{1,0:T(8,128)S(1)}) custom-call(s32[3]{0:T(128)S(1)} %pad_add_fusion.ids, s32[8]{0:T(128)S(1)} %copy-done.20, bf16[512,768]{1,0:T(8,128)(2,1)S(1)} %get-tuple-element.172.xq, ...), custom_call_target="tpu_custom_call" | custom-call | flops 1 | bytes 1 | tf_op jit(solution)/shard_map/heads_mine/pallas_call | solution.py:87
  103.3 1.4 collective-permute-start.23
  105.1 1.3 collective-permute-start.22
  106.5 4.5 %input.1 = f32[512,768]{1,0:T(8,128)} custom-call(f32[3]{0:T(128)S(1)} %copy-done.21, bf16[512,768]{1,0:T(8,128)(2,1)S(1)} %copy-done.10, f32[512,768]{1,0:T(8,128)S(1)} %get-tuple-element.253.grad_first, bf16[3,768,384]{2,1,0:T(8,128)(2,1)S(1)} %copy-done.7, bf16[3,768,384]{2,1,0:T(8,128)(2,1)S(1)} %copy-done.9, ...), custom_call_target="tpu_custom_call" | custom-call | flops 1 | bytes 1 | tf_op jit(solution)/shard_map/input/pallas_call | solution.py:87
  111.1 2.4 %collective-permute-start.24 = (bf16[1,192,384]{2,1,0:T(8,128)(2,1)S(1)}, bf16[1,192,384]{2,1,0:T(8,128)(2,1)S(1)}, u32[]{:S(2)}, u32[]{:S(2)}) collective-permute-start(bf16[1,192,384]{2,1,0:T(8,128)(2,1)S(1)} %get-tuple-element.334), channel_id=1, source_target_pairs={{0,16},{1,17},{2,18},{3,19},{4,20},{5,21},{6,22},{7,23},{8,24},{9,... | collective-permute-start | bytes 442376 | tf_op jit(solution)/shard_map/down_in3/ppermute | solution.py:580
  113.5 2.0 collective-permute-start.17
  115.5 4.5 %collective-permute-done.24 = bf16[1,192,384]{2,1,0:T(8,128)(2,1)S(1)} collective-permute-done((bf16[1,192,384]{2,1,0:T(8,128)(2,1)S(1)}, bf16[1,192,384]{2,1,0:T(8,128)(2,1)S(1)}, u32[]{:S(2)}, u32[]{:S(2)}) %collective-permute-start.24) | collective-permute-done | bytes 147488 | tf_op jit(solution)/shard_map/down_in3/ppermute | solution.py:580
  120.0 1.6 collective-permute-start.19
  122.8 2.4 %collective-permute-start.27 = (bf16[1,192,384]{2,1,0:T(8,128)(2,1)S(1)}, bf16[1,192,384]{2,1,0:T(8,128)(2,1)S(1)}, u32[]{:S(2)}, u32[]{:S(2)}) collective-permute-start(bf16[1,192,384]{2,1,0:T(8,128)(2,1)S(1)} %add_convert_fusion.21), channel_id=1, source_target_pairs={{0,16},{1,17},{2,18},{3,19},{4,20},{5,21},{6,22},{7,23},{8,24},{9,... | collective-permute-start | bytes 442376 | tf_op jit(solution)/shard_map/down_out3/ppermute | solution.py:580
  126.4 1.7 collective-permute-start.26
  128.4 4.2 %collective-permute-done.27 = bf16[1,192,384]{2,1,0:T(8,128)(2,1)S(1)} collective-permute-done((bf16[1,192,384]{2,1,0:T(8,128)(2,1)S(1)}, bf16[1,192,384]{2,1,0:T(8,128)(2,1)S(1)}, u32[]{:S(2)}, u32[]{:S(2)}) %collective-permute-start.27) | collective-permute-done | bytes 147488 | tf_op jit(solution)/shard_map/down_out3/ppermute | solution.py:580
  132.8 5.7 %collective-permute-done.26 = bf16[2,192,384]{2,1,0:T(8,128)(2,1)S(1)} collective-permute-done((bf16[2,192,384]{2,1,0:T(8,128)(2,1)S(1)}, bf16[2,192,384]{2,1,0:T(8,128)(2,1)S(1)}, u32[]{:S(2)}, u32[]{:S(2)}) %collective-permute-start.26) | collective-permute-done | bytes 294944 | tf_op jit(solution)/shard_map/up_in2/ppermute | solution.py:580
  139.0 7.0 %collective-permute-done.30 = bf16[2,192,384]{2,1,0:T(8,128)(2,1)S(1)} collective-permute-done((bf16[2,192,384]{2,1,0:T(8,128)(2,1)S(1)}, bf16[2,192,384]{2,1,0:T(8,128)(2,1)S(1)}, u32[]{:S(2)}, u32[]{:S(2)}) %collective-permute-start.30) | collective-permute-done | bytes 294944 | tf_op jit(solution)/shard_map/down_out2/ppermute | solution.py:580
  146.2 1.4 collective-permute-done.29
  148.8 8.3 %collective-permute-done.28 = bf16[2,192,384]{2,1,0:T(8,128)(2,1)S(1)} collective-permute-done((bf16[2,192,384]{2,1,0:T(8,128)(2,1)S(1)}, bf16[2,192,384]{2,1,0:T(8,128)(2,1)S(1)}, u32[]{:S(2)}, u32[]{:S(2)}) %collective-permute-start.28) | collective-permute-done | bytes 294944 | tf_op jit(solution)/shard_map/rest_in2/ppermute | solution.py:580
  157.6 1.4 collective-permute-start.40
  159.1 1.2 collective-permute-start.38
  160.4 4.8 %collective-permute-done.32 = bf16[1,192,384]{2,1,0:T(8,128)(2,1)S(1)} collective-permute-done((bf16[1,192,384]{2,1,0:T(8,128)(2,1)S(1)}, bf16[1,192,384]{2,1,0:T(8,128)(2,1)S(1)}, u32[]{:S(2)}, u32[]{:S(2)}) %collective-permute-start.32) | collective-permute-done | bytes 147488 | tf_op jit(solution)/shard_map/rest_in3/ppermute | solution.py:580
  165.3 5.6 %collective-permute-done.38 = bf16[2,192,384]{2,1,0:T(8,128)(2,1)S(1)} collective-permute-done((bf16[2,192,384]{2,1,0:T(8,128)(2,1)S(1)}, bf16[2,192,384]{2,1,0:T(8,128)(2,1)S(1)}, u32[]{:S(2)}, u32[]{:S(2)}) %collective-permute-start.38) | collective-permute-done | bytes 294944 | tf_op jit(solution)/shard_map/up_out2/ppermute | solution.py:580
  171.0 1.2 collective-permute-done.37
  172.3 1.5 collective-permute-start.41
  173.8 4.6 %collective-permute-done.41 = f32[12,768]{1,0:T(8,128)S(1)} collective-permute-done((f32[12,768]{1,0:T(8,128)S(1)}, f32[12,768]{1,0:T(8,128)S(1)}, u32[]{:S(2)}, u32[]{:S(2)}) %collective-permute-start.41) | collective-permute-done | bytes 36896 | tf_op jit(solution)/shard_map/small_in2/ppermute | solution.py:580
  178.5 3.7 %down_final.1 = f32[1536,768]{1,0:T(8,128)} custom-call(s32[3]{0:T(128)S(1)} %pad_add_fusion.ids, f32[16,1536]{1,0:T(8,128)S(1)} %shard_map.239.own.pack_own, f32[16,1536]{1,0:T(8,128)S(1)} %collective-permute-done.1.other.pack_other, bf16[8,192,384]{2,1,0:T(8,128)(2,1)S(1)} %constant_dynamic-update-slice_fusion.8.low, ...), custom_call_target="tpu_custom_call" | custom-call | flops 1 | bytes 1 | tf_op jit(solution)/shard_map/down_final/pallas_call | solution.py:1031
  182.3 1.5 collective-permute-start.43
  185.6 5.0 %collective-permute-start.46 = (bf16[8,192,384]{2,1,0:T(8,128)(2,1)}, bf16[8,192,384]{2,1,0:T(8,128)(2,1)}, u32[]{:S(2)}, u32[]{:S(2)}) collective-permute-start(bf16[8,192,384]{2,1,0:T(8,128)(2,1)} %constant_dynamic-update-slice_fusion.18.low), channel_id=1, source_target_pairs={{0,2},{1,5},{2,0},{3,7},{4,6},{5,1},{6,4},{7,3},{8,10},{9,13},{10,... | collective-permute-start | bytes 3538952 | tf_op jit(solution)/shard_map/up_out0/ppermute | solution.py:580
  192.8 5.9 %collective-permute-start.45 = (bf16[8,192,384]{2,1,0:T(8,128)(2,1)}, bf16[8,192,384]{2,1,0:T(8,128)(2,1)}, u32[]{:S(2)}, u32[]{:S(2)}) collective-permute-start(bf16[8,192,384]{2,1,0:T(8,128)(2,1)} %constant_dynamic-update-slice_fusion.20.low), channel_id=1, source_target_pairs={{0,2},{1,5},{2,0},{3,7},{4,6},{5,1},{6,4},{7,3},{8,10},{9,13},{10,... | collective-permute-start | bytes 3538952 | tf_op jit(solution)/shard_map/rest_out0/ppermute | solution.py:580
  201.7 8.7 %collective-permute-done.46.high = bf16[8,192,384]{2,1,0:T(8,128)(2,1)} collective-permute-done((bf16[8,192,384]{2,1,0:T(8,128)(2,1)}, bf16[8,192,384]{2,1,0:T(8,128)(2,1)}, u32[]{:S(2)}, u32[]{:S(2)}) %collective-permute-start.46) | collective-permute-done | bytes 1179680 | tf_op jit(solution)/shard_map/up_out0/ppermute | solution.py:580
  210.5 5.3 %up_final.1 = f32[768,1536]{1,0:T(8,128)} custom-call(s32[3]{0:T(128)S(1)} %pad_add_fusion.ids, f32[16,1536]{1,0:T(8,128)S(1)} %shard_map.239.own.pack_own, f32[16,1536]{1,0:T(8,128)S(1)} %collective-permute-done.1.other.pack_other, bf16[8,192,384]{2,1,0:T(8,128)(2,1)} %constant_dynamic-update-slice_fusion.18.low, ...), custom_call_target="tpu_custom_call" | custom-call | flops 1 | bytes 1 | tf_op jit(solution)/shard_map/up_final/pallas_call | solution.py:1031
  215.8 7.0 %collective-permute-done.45.high = bf16[8,192,384]{2,1,0:T(8,128)(2,1)} collective-permute-done((bf16[8,192,384]{2,1,0:T(8,128)(2,1)}, bf16[8,192,384]{2,1,0:T(8,128)(2,1)}, u32[]{:S(2)}, u32[]{:S(2)}) %collective-permute-start.45) | collective-permute-done | bytes 1179680 | tf_op jit(solution)/shard_map/rest_out0/ppermute | solution.py:580
  222.8 5.4 %rest_final.1 = (f32[3,768,384]{2,1,0:T(8,128)}, f32[384,768]{1,0:T(8,128)}) custom-call(s32[3]{0:T(128)S(1)} %pad_add_fusion.ids, f32[16,1536]{1,0:T(8,128)S(1)} %shard_map.239.own.pack_own, f32[16,1536]{1,0:T(8,128)S(1)} %collective-permute-done.1.other.pack_other, bf16[8,192,384]{2,1,0:T(8,128)(2,1)} %constant_dynamic-update-slice_fusion.20.low, ...), custom_call_target="tpu_custom_call" | custom-call | flops 1 | bytes 1 | tf_op jit(solution)/shard_map/rest_final/pallas_call | solution.py:1031
  (183 shorter events, 27.7 us)
Async XLA Ops:
  3.6 1.3 collective-permute-start
  5.8 3.9 %collective-permute-start.2 = (bf16[3,768,384]{2,1,0:T(8,128)(2,1)S(1)}, bf16[3,768,384]{2,1,0:T(8,128)(2,1)S(1)}, u32[]{:S(2)}, u32[]{:S(2)}) collective-permute-start(bf16[3,768,384]{2,1,0:T(8,128)(2,1)S(1)} %shard_map.238.weight.w_own), channel_id=1, source_target_pairs={{0,1},{1,0},{2,3},{3,2},{4,5},{5,4},{6,7},{7,6},{8,9},{9,8},{10,11... | collective-permute-start | bytes 5308424 | tf_op jit(solution)/shard_map/ppermute | solution.py:583
  7.1 2.6 %collective-permute-start.1 = (f32[16,1536]{1,0:T(8,128)S(1)}, f32[16,1536]{1,0:T(8,128)S(1)}, u32[]{:S(2)}, u32[]{:S(2)}) collective-permute-start(f32[16,1536]{1,0:T(8,128)S(1)} %shard_map.239.own.pack_own), channel_id=1, source_target_pairs={{0,1},{1,0},{2,3},{3,2},{4,5},{5,4},{6,7},{7,6},{8,9},{9,8},{10,11... | collective-permute-start | bytes 294920 | tf_op jit(solution)/shard_map/ppermute | solution.py:583
  13.9 15.4 %collective-permute-start.4 = (bf16[768,1536]{1,0:T(8,128)(2,1)}, bf16[768,1536]{1,0:T(8,128)(2,1)}, u32[]{:S(2)}, u32[]{:S(2)}) collective-permute-start(bf16[768,1536]{1,0:T(8,128)(2,1)} %get-tuple-element.176.up_own.up), channel_id=1, source_target_pairs={{0,1},{1,0},{2,3},{3,2},{4,5},{5,4},{6,7},{7,6},{8,9},{9,8},{10,11... | collective-permute-start | bytes 7077896 | tf_op jit(solution)/shard_map/ppermute | solution.py:583
  14.1 15.2 %collective-permute-start.5 = (bf16[1536,768]{1,0:T(8,128)(2,1)}, bf16[1536,768]{1,0:T(8,128)(2,1)}, u32[]{:S(2)}, u32[]{:S(2)}) collective-permute-start(bf16[1536,768]{1,0:T(8,128)(2,1)} %get-tuple-element.177.down_own.down), channel_id=1, source_target_pairs={{0,1},{1,0},{2,3},{3,2},{4,5},{5,4},{6,7},{7,6},{8,9},{9,8},{10,11... | collective-permute-start | bytes 7077896 | tf_op jit(solution)/shard_map/ppermute | solution.py:583
  14.4 14.9 %collective-permute-start.3 = (bf16[384,768]{1,0:T(8,128)(2,1)}, bf16[384,768]{1,0:T(8,128)(2,1)}, u32[]{:S(2)}, u32[]{:S(2)}) collective-permute-start(bf16[384,768]{1,0:T(8,128)(2,1)} %get-tuple-element.175.merge_own.merge_q), channel_id=1, source_target_pairs={{0,1},{1,0},{2,3},{3,2},{4,5},{5,4},{6,7},{7,6},{8,9},{9,8},{10,11... | collective-permute-start | bytes 1769480 | tf_op jit(solution)/shard_map/ppermute | solution.py:583
  29.3 23.5 %copy-start.18 = (bf16[384,512]{1,0:T(8,128)(2,1)}, bf16[384,512]{1,0:T(8,128)(2,1)S(1)}, u32[]{:S(2)}) copy-start(bf16[384,512]{1,0:T(8,128)(2,1)S(1)} %get-tuple-element.220.v_ref) | copy-start | bytes 1179652
  54.1 2.9 %collective-permute-start.6 = (bf16[8,192,384]{2,1,0:T(8,128)(2,1)S(1)}, bf16[8,192,384]{2,1,0:T(8,128)(2,1)S(1)}, u32[]{:S(2)}, u32[]{:S(2)}) collective-permute-start(bf16[8,192,384]{2,1,0:T(8,128)(2,1)S(1)} %down_theirshigh.1), channel_id=1, source_target_pairs={{0,1},{1,0},{2,3},{3,2},{4,5},{5,4},{6,7},{7,6},{8,9},{9,8},{10,11... | collective-permute-start | bytes 3538952 | tf_op jit(solution)/shard_map/down_high/ppermute | solution.py:583
  58.8 19.2 %collective-permute-start.8 = (bf16[8,192,384]{2,1,0:T(8,128)(2,1)S(1)}, bf16[8,192,384]{2,1,0:T(8,128)(2,1)S(1)}, u32[]{:S(2)}, u32[]{:S(2)}) collective-permute-start(bf16[8,192,384]{2,1,0:T(8,128)(2,1)S(1)} %down_theirslow.1), channel_id=1, source_target_pairs={{0,1},{1,0},{2,3},{3,2},{4,5},{5,4},{6,7},{7,6},{8,9},{9,8},{10,11... | collective-permute-start | bytes 3538952 | tf_op jit(solution)/shard_map/down_low/ppermute | solution.py:583
  59.2 18.8 %collective-permute-start.9 = (bf16[8,192,384]{2,1,0:T(8,128)(2,1)S(1)}, bf16[8,192,384]{2,1,0:T(8,128)(2,1)S(1)}, u32[]{:S(2)}, u32[]{:S(2)}) collective-permute-start(bf16[8,192,384]{2,1,0:T(8,128)(2,1)S(1)} %add_convert_fusion.2), channel_id=1, source_target_pairs={{0,2},{1,5},{2,0},{3,7},{4,6},{5,1},{6,4},{7,3},{8,10},{9,13},{10,... | collective-permute-start | bytes 3538952 | tf_op jit(solution)/shard_map/down_in0/ppermute | solution.py:580
  70.1 8.3 %collective-permute-start.7 = (bf16[8,192,384]{2,1,0:T(8,128)(2,1)S(1)}, bf16[8,192,384]{2,1,0:T(8,128)(2,1)S(1)}, u32[]{:S(2)}, u32[]{:S(2)}) collective-permute-start(bf16[8,192,384]{2,1,0:T(8,128)(2,1)S(1)} %get-tuple-element.190), channel_id=1, source_target_pairs={{0,1},{1,0},{2,3},{3,2},{4,5},{5,4},{6,7},{7,6},{8,9},{9,8},{10,11... | collective-permute-start | bytes 3538952 | tf_op jit(solution)/shard_map/up_high/ppermute | solution.py:583
  70.8 33.8 %collective-permute-start.10 = (bf16[8,192,384]{2,1,0:T(8,128)(2,1)S(1)}, bf16[8,192,384]{2,1,0:T(8,128)(2,1)S(1)}, u32[]{:S(2)}, u32[]{:S(2)}) collective-permute-start(bf16[8,192,384]{2,1,0:T(8,128)(2,1)S(1)} %get-tuple-element.191), channel_id=1, source_target_pairs={{0,1},{1,0},{2,3},{3,2},{4,5},{5,4},{6,7},{7,6},{8,9},{9,8},{10,11... | collective-permute-start | bytes 3538952 | tf_op jit(solution)/shard_map/up_low/ppermute | solution.py:583
  78.8 25.8 %collective-permute-start.11 = (bf16[8,192,384]{2,1,0:T(8,128)(2,1)S(1)}, bf16[8,192,384]{2,1,0:T(8,128)(2,1)S(1)}, u32[]{:S(2)}, u32[]{:S(2)}) collective-permute-start(bf16[8,192,384]{2,1,0:T(8,128)(2,1)S(1)} %add_convert_fusion.1), channel_id=1, source_target_pairs={{0,2},{1,5},{2,0},{3,7},{4,6},{5,1},{6,4},{7,3},{8,10},{9,13},{10,... | collective-permute-start | bytes 3538952 | tf_op jit(solution)/shard_map/up_in0/ppermute | solution.py:580
  91.0 1.6 collective-permute-start.13
  91.2 1.8 collective-permute-start.14
  91.6 11.5 %collective-permute-start.12 = (bf16[4,192,384]{2,1,0:T(8,128)(2,1)S(1)}, bf16[4,192,384]{2,1,0:T(8,128)(2,1)S(1)}, u32[]{:S(2)}, u32[]{:S(2)}) collective-permute-start(bf16[4,192,384]{2,1,0:T(8,128)(2,1)S(1)} %get-tuple-element.322), channel_id=1, source_target_pairs={{0,4},{1,3},{2,6},{3,1},{4,0},{5,7},{6,2},{7,5},{8,12},{9,11},{10,... | collective-permute-start | bytes 1769480 | tf_op jit(solution)/shard_map/down_in1/ppermute | solution.py:580
  92.6 9.3 %collective-permute-start.15 = (bf16[8,48,384]{2,1,0:T(8,128)(2,1)S(1)}, bf16[8,48,384]{2,1,0:T(8,128)(2,1)S(1)}, u32[]{:S(2)}, u32[]{:S(2)}) collective-permute-start(bf16[8,48,384]{2,1,0:T(8,128)(2,1)S(1)} %get-tuple-element.224), channel_id=1, source_target_pairs={{0,1},{1,0},{2,3},{3,2},{4,5},{5,4},{6,7},{7,6},{8,9},{9,8},{10,11... | collective-permute-start | bytes 884744 | tf_op jit(solution)/shard_map/rest_high/ppermute | solution.py:583
  93.1 8.9 %collective-permute-start.16 = (bf16[8,48,384]{2,1,0:T(8,128)(2,1)S(1)}, bf16[8,48,384]{2,1,0:T(8,128)(2,1)S(1)}, u32[]{:S(2)}, u32[]{:S(2)}) collective-permute-start(bf16[8,48,384]{2,1,0:T(8,128)(2,1)S(1)} %get-tuple-element.225), channel_id=1, source_target_pairs={{0,1},{1,0},{2,3},{3,2},{4,5},{5,4},{6,7},{7,6},{8,9},{9,8},{10,11... | collective-permute-start | bytes 884744 | tf_op jit(solution)/shard_map/rest_high/ppermute | solution.py:583
  102.2 22.9 %collective-permute-start.21 = (bf16[8,192,384]{2,1,0:T(8,128)(2,1)S(1)}, bf16[8,192,384]{2,1,0:T(8,128)(2,1)S(1)}, u32[]{:S(2)}, u32[]{:S(2)}) collective-permute-start(bf16[8,192,384]{2,1,0:T(8,128)(2,1)S(1)} %add_convert_fusion), channel_id=1, source_target_pairs={{0,2},{1,5},{2,0},{3,7},{4,6},{5,1},{6,4},{7,3},{8,10},{9,13},{10,... | collective-permute-start | bytes 3538952 | tf_op jit(solution)/shard_map/rest_in0/ppermute | solution.py:580
  103.3 7.8 %collective-permute-start.23 = (bf16[2,192,384]{2,1,0:T(8,128)(2,1)S(1)}, bf16[2,192,384]{2,1,0:T(8,128)(2,1)S(1)}, u32[]{:S(2)}, u32[]{:S(2)}) collective-permute-start(bf16[2,192,384]{2,1,0:T(8,128)(2,1)S(1)} %get-tuple-element.328), channel_id=1, source_target_pairs={{0,8},{1,9},{2,10},{3,11},{4,12},{5,13},{6,14},{7,15},{8,0},{9,1},... | collective-permute-start | bytes 884744 | tf_op jit(solution)/shard_map/down_in2/ppermute | solution.py:580
  105.1 16.4 %collective-permute-start.22 = (bf16[4,192,384]{2,1,0:T(8,128)(2,1)S(1)}, bf16[4,192,384]{2,1,0:T(8,128)(2,1)S(1)}, u32[]{:S(2)}, u32[]{:S(2)}) collective-permute-start(bf16[4,192,384]{2,1,0:T(8,128)(2,1)S(1)} %get-tuple-element.320), channel_id=1, source_target_pairs={{0,4},{1,3},{2,6},{3,1},{4,0},{5,7},{6,2},{7,5},{8,12},{9,11},{10,... | collective-permute-start | bytes 1769480 | tf_op jit(solution)/shard_map/up_in1/ppermute | solution.py:580
  111.1 8.8 %collective-permute-start.24 = (bf16[1,192,384]{2,1,0:T(8,128)(2,1)S(1)}, bf16[1,192,384]{2,1,0:T(8,128)(2,1)S(1)}, u32[]{:S(2)}, u32[]{:S(2)}) collective-permute-start(bf16[1,192,384]{2,1,0:T(8,128)(2,1)S(1)} %get-tuple-element.334), channel_id=1, source_target_pairs={{0,16},{1,17},{2,18},{3,19},{4,20},{5,21},{6,22},{7,23},{8,24},{9,... | collective-permute-start | bytes 442376 | tf_op jit(solution)/shard_map/down_in3/ppermute | solution.py:580
  113.5 9.3 %collective-permute-start.17 = (bf16[8,48,384]{2,1,0:T(8,128)(2,1)S(1)}, bf16[8,48,384]{2,1,0:T(8,128)(2,1)S(1)}, u32[]{:S(2)}, u32[]{:S(2)}) collective-permute-start(bf16[8,48,384]{2,1,0:T(8,128)(2,1)S(1)} %get-tuple-element.226), channel_id=1, source_target_pairs={{0,1},{1,0},{2,3},{3,2},{4,5},{5,4},{6,7},{7,6},{8,9},{9,8},{10,11... | collective-permute-start | bytes 884744 | tf_op jit(solution)/shard_map/rest_low/ppermute | solution.py:583
  115.5 9.7 %collective-permute-start.18 = (bf16[8,48,384]{2,1,0:T(8,128)(2,1)S(1)}, bf16[8,48,384]{2,1,0:T(8,128)(2,1)S(1)}, u32[]{:S(2)}, u32[]{:S(2)}) collective-permute-start(bf16[8,48,384]{2,1,0:T(8,128)(2,1)S(1)} %get-tuple-element.227), channel_id=1, source_target_pairs={{0,1},{1,0},{2,3},{3,2},{4,5},{5,4},{6,7},{7,6},{8,9},{9,8},{10,11... | collective-permute-start | bytes 884744 | tf_op jit(solution)/shard_map/rest_low/ppermute | solution.py:583
  120.0 5.2 %collective-permute-start.19 = (bf16[8,48,384]{2,1,0:T(8,128)(2,1)S(1)}, bf16[8,48,384]{2,1,0:T(8,128)(2,1)S(1)}, u32[]{:S(2)}, u32[]{:S(2)}) collective-permute-start(bf16[8,48,384]{2,1,0:T(8,128)(2,1)S(1)} %get-tuple-element.228), channel_id=1, source_target_pairs={{0,1},{1,0},{2,3},{3,2},{4,5},{5,4},{6,7},{7,6},{8,9},{9,8},{10,11... | collective-permute-start | bytes 884744 | tf_op jit(solution)/shard_map/rest_low/ppermute | solution.py:583
  121.5 3.6 %collective-permute-start.20 = (bf16[8,48,384]{2,1,0:T(8,128)(2,1)S(1)}, bf16[8,48,384]{2,1,0:T(8,128)(2,1)S(1)}, u32[]{:S(2)}, u32[]{:S(2)}) collective-permute-start(bf16[8,48,384]{2,1,0:T(8,128)(2,1)S(1)} %get-tuple-element.229), channel_id=1, source_target_pairs={{0,1},{1,0},{2,3},{3,2},{4,5},{5,4},{6,7},{7,6},{8,9},{9,8},{10,11... | collective-permute-start | bytes 884744 | tf_op jit(solution)/shard_map/rest_low/ppermute | solution.py:583
  122.8 9.9 %collective-permute-start.27 = (bf16[1,192,384]{2,1,0:T(8,128)(2,1)S(1)}, bf16[1,192,384]{2,1,0:T(8,128)(2,1)S(1)}, u32[]{:S(2)}, u32[]{:S(2)}) collective-permute-start(bf16[1,192,384]{2,1,0:T(8,128)(2,1)S(1)} %add_convert_fusion.21), channel_id=1, source_target_pairs={{0,16},{1,17},{2,18},{3,19},{4,20},{5,21},{6,22},{7,23},{8,24},{9,... | collective-permute-start | bytes 442376 | tf_op jit(solution)/shard_map/down_out3/ppermute | solution.py:580
  125.9 12.8 %collective-permute-start.25 = (bf16[4,192,384]{2,1,0:T(8,128)(2,1)S(1)}, bf16[4,192,384]{2,1,0:T(8,128)(2,1)S(1)}, u32[]{:S(2)}, u32[]{:S(2)}) collective-permute-start(bf16[4,192,384]{2,1,0:T(8,128)(2,1)S(1)} %get-tuple-element.318), channel_id=1, source_target_pairs={{0,4},{1,3},{2,6},{3,1},{4,0},{5,7},{6,2},{7,5},{8,12},{9,11},{10,... | collective-permute-start | bytes 1769480 | tf_op jit(solution)/shard_map/rest_in1/ppermute | solution.py:580
  126.4 12.1 %collective-permute-start.26 = (bf16[2,192,384]{2,1,0:T(8,128)(2,1)S(1)}, bf16[2,192,384]{2,1,0:T(8,128)(2,1)S(1)}, u32[]{:S(2)}, u32[]{:S(2)}) collective-permute-start(bf16[2,192,384]{2,1,0:T(8,128)(2,1)S(1)} %get-tuple-element.326), channel_id=1, source_target_pairs={{0,8},{1,9},{2,10},{3,11},{4,12},{5,13},{6,14},{7,15},{8,0},{9,1},... | collective-permute-start | bytes 884744 | tf_op jit(solution)/shard_map/up_in2/ppermute | solution.py:580
  128.2 10.7 %collective-permute-start.31 = (f32[12,768]{1,0:T(8,128)S(1)}, f32[12,768]{1,0:T(8,128)S(1)}, u32[]{:S(2)}, u32[]{:S(2)}) collective-permute-start(f32[12,768]{1,0:T(8,128)S(1)} %pad_maximum_fusion), channel_id=1, source_target_pairs={{0,1},{1,0},{2,3},{3,2},{4,5},{5,4},{6,7},{7,6},{8,9},{9,8},{10,11... | collective-permute-start | bytes 110600 | tf_op jit(solution)/shard_map/small_got/ppermute | solution.py:583
  132.7 13.3 %collective-permute-start.30 = (bf16[2,192,384]{2,1,0:T(8,128)(2,1)S(1)}, bf16[2,192,384]{2,1,0:T(8,128)(2,1)S(1)}, u32[]{:S(2)}, u32[]{:S(2)}) collective-permute-start(bf16[2,192,384]{2,1,0:T(8,128)(2,1)S(1)} %constant_dynamic-update-slice_fusion.4), channel_id=1, source_target_pairs={{0,8},{1,9},{2,10},{3,11},{4,12},{5,13},{6,14},{7,15},{8,0},{9,1},... | collective-permute-start | bytes 884744 | tf_op jit(solution)/shard_map/down_out2/ppermute | solution.py:580
  138.6 9.0 %collective-permute-start.29 = (bf16[1,192,384]{2,1,0:T(8,128)(2,1)S(1)}, bf16[1,192,384]{2,1,0:T(8,128)(2,1)S(1)}, u32[]{:S(2)}, u32[]{:S(2)}) collective-permute-start(bf16[1,192,384]{2,1,0:T(8,128)(2,1)S(1)} %get-tuple-element.332), channel_id=1, source_target_pairs={{0,16},{1,17},{2,18},{3,19},{4,20},{5,21},{6,22},{7,23},{8,24},{9,... | collective-permute-start | bytes 442376 | tf_op jit(solution)/shard_map/up_in3/ppermute | solution.py:580
  139.0 18.2 %collective-permute-start.33 = (f32[12,768]{1,0:T(8,128)S(1)}, f32[12,768]{1,0:T(8,128)S(1)}, u32[]{:S(2)}, u32[]{:S(2)}) collective-permute-start(f32[12,768]{1,0:T(8,128)S(1)} %maximum_select_fusion.4), channel_id=1, source_target_pairs={{0,2},{1,3},{2,0},{3,1},{4,6},{5,7},{6,4},{7,5},{8,10},{9,11},{10,... | collective-permute-start | bytes 110600 | tf_op jit(solution)/shard_map/small_in0/ppermute | solution.py:580
  146.0 11.1 %collective-permute-start.28 = (bf16[2,192,384]{2,1,0:T(8,128)(2,1)S(1)}, bf16[2,192,384]{2,1,0:T(8,128)(2,1)S(1)}, u32[]{:S(2)}, u32[]{:S(2)}) collective-permute-start(bf16[2,192,384]{2,1,0:T(8,128)(2,1)S(1)} %get-tuple-element.324), channel_id=1, source_target_pairs={{0,8},{1,9},{2,10},{3,11},{4,12},{5,13},{6,14},{7,15},{8,0},{9,1},... | collective-permute-start | bytes 884744 | tf_op jit(solution)/shard_map/rest_in2/ppermute | solution.py:580
  146.1 11.2 %collective-permute-start.36 = (bf16[4,192,384]{2,1,0:T(8,128)(2,1)S(1)}, bf16[4,192,384]{2,1,0:T(8,128)(2,1)S(1)}, u32[]{:S(2)}, u32[]{:S(2)}) collective-permute-start(bf16[4,192,384]{2,1,0:T(8,128)(2,1)S(1)} %constant_dynamic-update-slice_fusion.6), channel_id=1, source_target_pairs={{0,4},{1,3},{2,6},{3,1},{4,0},{5,7},{6,2},{7,5},{8,12},{9,11},{10,... | collective-permute-start | bytes 1769480 | tf_op jit(solution)/shard_map/down_out1/ppermute | solution.py:580
  147.7 11.3 %collective-permute-start.35 = (bf16[1,192,384]{2,1,0:T(8,128)(2,1)S(1)}, bf16[1,192,384]{2,1,0:T(8,128)(2,1)S(1)}, u32[]{:S(2)}, u32[]{:S(2)}) collective-permute-start(bf16[1,192,384]{2,1,0:T(8,128)(2,1)S(1)} %add_convert_fusion.18), channel_id=1, source_target_pairs={{0,16},{1,17},{2,18},{3,19},{4,20},{5,21},{6,22},{7,23},{8,24},{9,... | collective-permute-start | bytes 442376 | tf_op jit(solution)/shard_map/up_out3/ppermute | solution.py:580
  157.3 3.0 %collective-permute-start.34 = (f32[12,768]{1,0:T(8,128)S(1)}, f32[12,768]{1,0:T(8,128)S(1)}, u32[]{:S(2)}, u32[]{:S(2)}) collective-permute-start(f32[12,768]{1,0:T(8,128)S(1)} %maximum_select_fusion.3), channel_id=1, source_target_pairs={{0,4},{1,5},{2,6},{3,7},{4,0},{5,1},{6,2},{7,3},{8,12},{9,13},{10,... | collective-permute-start | bytes 110600 | tf_op jit(solution)/shard_map/small_in1/ppermute | solution.py:580
  157.3 7.9 %collective-permute-start.32 = (bf16[1,192,384]{2,1,0:T(8,128)(2,1)S(1)}, bf16[1,192,384]{2,1,0:T(8,128)(2,1)S(1)}, u32[]{:S(2)}, u32[]{:S(2)}) collective-permute-start(bf16[1,192,384]{2,1,0:T(8,128)(2,1)S(1)} %get-tuple-element.330), channel_id=1, source_target_pairs={{0,16},{1,17},{2,18},{3,19},{4,20},{5,21},{6,22},{7,23},{8,24},{9,... | collective-permute-start | bytes 442376 | tf_op jit(solution)/shard_map/rest_in3/ppermute | solution.py:580
  157.6 20.9 %collective-permute-start.40 = (bf16[8,192,384]{2,1,0:T(8,128)(2,1)S(1)}, bf16[8,192,384]{2,1,0:T(8,128)(2,1)S(1)}, u32[]{:S(2)}, u32[]{:S(2)}) collective-permute-start(bf16[8,192,384]{2,1,0:T(8,128)(2,1)S(1)} %constant_dynamic-update-slice_fusion.8.low), channel_id=1, source_target_pairs={{0,2},{1,5},{2,0},{3,7},{4,6},{5,1},{6,4},{7,3},{8,10},{9,13},{10,... | collective-permute-start | bytes 3538952 | tf_op jit(solution)/shard_map/down_out0/ppermute | solution.py:580
  159.1 11.8 %collective-permute-start.38 = (bf16[2,192,384]{2,1,0:T(8,128)(2,1)S(1)}, bf16[2,192,384]{2,1,0:T(8,128)(2,1)S(1)}, u32[]{:S(2)}, u32[]{:S(2)}) collective-permute-start(bf16[2,192,384]{2,1,0:T(8,128)(2,1)S(1)} %constant_dynamic-update-slice_fusion.10), channel_id=1, source_target_pairs={{0,8},{1,9},{2,10},{3,11},{4,12},{5,13},{6,14},{7,15},{8,0},{9,1},... | collective-permute-start | bytes 884744 | tf_op jit(solution)/shard_map/up_out2/ppermute | solution.py:580
  165.2 7.0 %collective-permute-start.37 = (bf16[1,192,384]{2,1,0:T(8,128)(2,1)S(1)}, bf16[1,192,384]{2,1,0:T(8,128)(2,1)S(1)}, u32[]{:S(2)}, u32[]{:S(2)}) collective-permute-start(bf16[1,192,384]{2,1,0:T(8,128)(2,1)S(1)} %add_convert_fusion.15), channel_id=1, source_target_pairs={{0,16},{1,17},{2,18},{3,19},{4,20},{5,21},{6,22},{7,23},{8,24},{9,... | collective-permute-start | bytes 442376 | tf_op jit(solution)/shard_map/rest_out3/ppermute | solution.py:580
  172.2 9.9 %collective-permute-start.39 = (bf16[2,192,384]{2,1,0:T(8,128)(2,1)S(1)}, bf16[2,192,384]{2,1,0:T(8,128)(2,1)S(1)}, u32[]{:S(2)}, u32[]{:S(2)}) collective-permute-start(bf16[2,192,384]{2,1,0:T(8,128)(2,1)S(1)} %constant_dynamic-update-slice_fusion.14), channel_id=1, source_target_pairs={{0,8},{1,9},{2,10},{3,11},{4,12},{5,13},{6,14},{7,15},{8,0},{9,1},... | collective-permute-start | bytes 884744 | tf_op jit(solution)/shard_map/rest_out2/ppermute | solution.py:580
  172.3 6.1 %collective-permute-start.41 = (f32[12,768]{1,0:T(8,128)S(1)}, f32[12,768]{1,0:T(8,128)S(1)}, u32[]{:S(2)}, u32[]{:S(2)}) collective-permute-start(f32[12,768]{1,0:T(8,128)S(1)} %maximum_select_fusion.2), channel_id=1, source_target_pairs={{0,8},{1,9},{2,10},{3,11},{4,12},{5,13},{6,14},{7,15},{8,0},{9,1},... | collective-permute-start | bytes 110600 | tf_op jit(solution)/shard_map/small_in2/ppermute | solution.py:580
  173.8 10.1 %collective-permute-start.44 = (bf16[4,192,384]{2,1,0:T(8,128)(2,1)S(1)}, bf16[4,192,384]{2,1,0:T(8,128)(2,1)S(1)}, u32[]{:S(2)}, u32[]{:S(2)}) collective-permute-start(bf16[4,192,384]{2,1,0:T(8,128)(2,1)S(1)} %constant_dynamic-update-slice_fusion.12), channel_id=1, source_target_pairs={{0,4},{1,3},{2,6},{3,1},{4,0},{5,7},{6,2},{7,5},{8,12},{9,11},{10,... | collective-permute-start | bytes 1769480 | tf_op jit(solution)/shard_map/up_out1/ppermute | solution.py:580
  182.3 8.8 %collective-permute-start.42 = (bf16[4,192,384]{2,1,0:T(8,128)(2,1)S(1)}, bf16[4,192,384]{2,1,0:T(8,128)(2,1)S(1)}, u32[]{:S(2)}, u32[]{:S(2)}) collective-permute-start(bf16[4,192,384]{2,1,0:T(8,128)(2,1)S(1)} %constant_dynamic-update-slice_fusion.16), channel_id=1, source_target_pairs={{0,4},{1,3},{2,6},{3,1},{4,0},{5,7},{6,2},{7,5},{8,12},{9,11},{10,... | collective-permute-start | bytes 1769480 | tf_op jit(solution)/shard_map/rest_out1/ppermute | solution.py:580
  182.3 8.3 %collective-permute-start.43 = (f32[12,768]{1,0:T(8,128)S(1)}, f32[12,768]{1,0:T(8,128)S(1)}, u32[]{:S(2)}, u32[]{:S(2)}) collective-permute-start(f32[12,768]{1,0:T(8,128)S(1)} %maximum_select_fusion.1), channel_id=1, source_target_pairs={{0,16},{1,17},{2,18},{3,19},{4,20},{5,21},{6,22},{7,23},{8,24},{9,... | collective-permute-start | bytes 110600 | tf_op jit(solution)/shard_map/small_in3/ppermute | solution.py:580
  185.6 24.9 %collective-permute-start.46 = (bf16[8,192,384]{2,1,0:T(8,128)(2,1)}, bf16[8,192,384]{2,1,0:T(8,128)(2,1)}, u32[]{:S(2)}, u32[]{:S(2)}) collective-permute-start(bf16[8,192,384]{2,1,0:T(8,128)(2,1)} %constant_dynamic-update-slice_fusion.18.low), channel_id=1, source_target_pairs={{0,2},{1,5},{2,0},{3,7},{4,6},{5,1},{6,4},{7,3},{8,10},{9,13},{10,... | collective-permute-start | bytes 3538952 | tf_op jit(solution)/shard_map/up_out0/ppermute | solution.py:580
  192.8 30.0 %collective-permute-start.45 = (bf16[8,192,384]{2,1,0:T(8,128)(2,1)}, bf16[8,192,384]{2,1,0:T(8,128)(2,1)}, u32[]{:S(2)}, u32[]{:S(2)}) collective-permute-start(bf16[8,192,384]{2,1,0:T(8,128)(2,1)} %constant_dynamic-update-slice_fusion.20.low), channel_id=1, source_target_pairs={{0,2},{1,5},{2,0},{3,7},{4,6},{5,1},{6,4},{7,3},{8,10},{9,13},{10,... | collective-permute-start | bytes 3538952 | tf_op jit(solution)/shard_map/rest_out0/ppermute | solution.py:580
  (27 other events, 169.6 us)

commit v4 on v3

--- a/solution.py
+++ b/solution.py
@@ -19,8 +19,8 @@
 ORDER = (
     "down.theirshigh",
     "down.minehigh",
+    "down.theirslow",
     "down.add0",
-    "down.theirslow",
     "down.minelow",
     "up.theirs",
     "up.mine",
@@ -29,19 +29,19 @@
     "norm",
     "heads.theirs",
     "heads.mine",
-    "rest.add0",
     "down.add2",
     "up.add1",
-    "small.theirs",
+    "rest.add0",
     "input",
     "down.add3",
+    "small.theirs",
     "down.sum",
     "up.add2",
     "rest.add1",
+    "small.mine",
     "down.join3",
     "up.add3",
     "rest.add2",
-    "small.mine",
     "down.join2",
     "up.sum",
     "rest.add3",
@@ -50,9 +50,9 @@
     "up.join3",
     "small.sum1",
     "rest.sum",
+    "small.sum2",
     "up.join2",
     "rest.join3",
-    "small.sum2",
     "down.final",
     "rest.join2",
     "up.join1",
@@ -63,7 +63,8 @@
 )
 COST = 1
 LANES = 384
-TILE = 64
+TILE = 128
+GELU_TILE = 32
 
 
 def dot(a, b, ca, cb):
@@ -178,7 +179,7 @@
         lse_ref[pl.ds(index, 1), :] = top + jnp.log(total)
         return carry
 
-    lax.fori_loop(0, q_ref.shape[0] // HEAD, head, 0)
+    lax.fori_loop(0, q_ref.shape[0] // HEAD, head, 0, unroll=2)
 
 
 def forward_first_body(
@@ -231,7 +232,7 @@
         d_ref[1, at, :] = dot(q, grad_score, 1, 1).astype(BF16)
         return carry
 
-    lax.fori_loop(0, width // HEAD, head, 0)
+    lax.fori_loop(0, width // HEAD, head, 0, unroll=2)
     rows, step = x_t.shape[0] // (2 * count), width // (2 * count)
     if len(outs) == 2:
         outs = [out.at[:, at * rows : (at + 1) * rows, :] for out in outs for at in range(4)]
@@ -298,6 +299,7 @@
     sums,
     work,
     hidden_ref,
+    second_ref,
     tops,
     sum_ref,
 ):
@@ -331,23 +333,33 @@
         (up_other, pack_other, active_other, factor_other),
     ):
 
-        def columns(index, carry):
+        def gelu_chunk(source, index):
             cols = pl.ds(pl.multiple_of(index * span, span), span)
-            hidden_ref[...] = dot(normed_q[...], weight[:, cols], 1, 0)
             bias = pack[0:1, cols]
-
-            def rows(row, carry):
-                at = pl.ds(pl.multiple_of(row * TILE, TILE), TILE)
-                clipped, factor, active = gelu_parts(hidden_ref[at, :] + bias, clip_second)
+            top = tops[2, :, 0:span]
+            for row in range(total // GELU_TILE):
+                at = slice(row * GELU_TILE, (row + 1) * GELU_TILE)
+                clipped, factor, active = gelu_parts(source[at, :] + bias, clip_second)
                 active_ref[at, cols] = clipped
                 factor_ref[at, cols] = factor
-                tops[2, :, 0:span] = jnp.maximum(tops[2, :, 0:span], fold(jnp.abs(active), jnp.max))
-                return carry
-
-            lax.fori_loop(0, total // TILE, rows, 0)
+                top = jnp.maximum(top, fold(jnp.abs(active), jnp.max))
+            tops[2, :, 0:span] = top
+
+        def multiply(target, index):
+            cols = pl.ds(pl.multiple_of(index * span, span), span)
+            target[...] = dot(normed_q[...], weight[:, cols], 1, 0)
+
+        chunks = weight.shape[1] // span
+        multiply(hidden_ref, 0)
+
+        def pair(index, carry):
+            multiply(second_ref, 2 * index + 1)
+            gelu_chunk(hidden_ref, 2 * index)
+            multiply(hidden_ref, jnp.minimum(2 * index + 2, chunks - 1))
+            gelu_chunk(second_ref, 2 * index + 1)
             return carry
 
-        lax.fori_loop(0, weight.shape[1] // span, columns, 0)
+        lax.fori_loop(0, chunks // 2, pair, 0)
     work[...] += dot(active_own[...], down_own[...], 1, 0) + dot(
         active_other[...], down_other[...], 1, 0
     )
@@ -419,7 +431,7 @@
         bias_row[0:1, cols] = jnp.sum(grad.astype(F32), axis=0, keepdims=True)
         return carry
 
-    lax.fori_loop(0, g_ref.shape[1] // span, columns, 0)
+    lax.fori_loop(0, g_ref.shape[1] // span, columns, 0, unroll=True)
     rows = normed_q.shape[1] // (2 * count)
     for half, chunk in ((1, high), (0, low)):
         base = half_base(rel, half, 2 * count)
@@ -634,6 +646,9 @@
         for name in ORDER:
             if name in self.tasks:
                 take(name)
+            elif name[1:] in self.source:
+                take(name[1:])
+                values[name[1:]], last = lax.optimization_barrier((values[name[1:]], last))
         for name in self.tasks:
             take(name)
         return values
@@ -867,6 +882,7 @@
         [
             pltpu.VMEM((total, width), F32),
             pltpu.VMEM((total, 256), F32),
+            pltpu.VMEM((total, 256), F32),
             pltpu.VMEM((3, 8, width), F32),
             pltpu.VMEM((3, 8, width), F32),
         ],

time: 229 us -> 227 us (level); the launches traced: 228 us -> 223 us
  starting transfers between devices: 41.6 us -> 33 us
  Pallas kernels: 99.5 us -> 102 us
    ppermute x28, starting transfers between devices: 32.9 us -> 23.8 us  [swap(): return lax.ppermute(value, ('dp', 'tensor'), pairs)]
    ppermute x28, waiting for transfers between devices: 63.6 us -> 66.5 us  [swap(): return lax.ppermute(value, ('dp', 'tensor'), pairs)]
  transfers between devices with their start and end apart: 47 -> 47, of which waited for: 19 -> 16; matrix products, arithmetic and copies ran while one was open for 5% -> 5% of each run, Pallas kernels for 28% -> 32%
where the time goes in v4:
time: 227 us; the launch traced here: 223 us
  Pallas kernels  102 us (45%)
  waiting for transfers between devices  69.8 us (31%)
  starting transfers between devices  33 us (15%)
  local copies, waits for them, and re-layouts  12.9 us (6%)
  other arithmetic  4.4 us (2%)
    pallas_call x13, Pallas kernels, call(): pl.pallas_call(body, in_specs=in_specs, out_specs=out_specs, scratch_shap...  81.5 us
    ppermute x28, waiting for transfers between devices, swap(): return lax.ppermute(value, ('dp', 'tensor'), pairs)  66.5 us
    ppermute x28, starting transfers between devices, swap(): return lax.ppermute(value, ('dp', 'tensor'), pairs)  23.8 us
    pallas_call x3, Pallas kernels, final(): pl.pallas_call(partial(body, per), grid_spec=pltpu.PrefetchScalarGridSpec...  14.4 us
    ppermute x19, starting transfers between devices, core_swap(): return lax.ppermute(value, 'tensor', [(0, 1), (1, 0)])  9.23 us
    unnamed x68, local copies, waits for them, and re-layouts  8.31 us
  transfers between devices with their start and end apart: 47, of which 16 were waited for; matrix products, arithmetic and copies ran while one was open for 5% of the time, Pallas kernels for 32%

profile of v4, /device:TPU:1, one launch (start us, length us, event | category | flops | bytes accessed | tf_op | source)
XLA Modules:
  0.0 223.3 jit_solution(18098716332159000034)
XLA Ops:
  0.7 1.5 copy-done.3
  3.7 1.1 collective-permute-done.other.pack.p_other
  7.6 2.2 collective-permute-done.1.other.pack_other
  9.7 1.2 copy-done.8
  11.0 3.0 %shard_map.240 = (bf16[384,768]{1,0:T(8,128)(2,1)}, bf16[768,1536]{1,0:T(8,128)(2,1)}, bf16[1536,768]{1,0:T(8,128)(2,1)}) custom-call(f32[16,1536]{1,0:T(8,128)S(1)} %shard_map.239.own.pack_own, f32[16,1536]{1,0:T(8,128)S(1)} %collective-permute-done.1.other.pack_other, bf16[384,768]{1,0:T(8,128)(2,1)S(1)} %copy-done.11, bf16[768,1536]{1,0:T(8,128)(2,1)S(1)} %copy-done.1, ...), custom_call_target="tpu_custom_call" | custom-call | tf_op jit(solution)/shard_map/pallas_call | solution.py:790
  14.8 1.5 copy-done.6
  16.3 5.7 %shard_map.241 = (bf16[512,768]{1,0:T(8,128)(2,1)S(1)}, bf16[384,512]{1,0:T(8,128)(2,1)S(1)}, bf16[384,512]{1,0:T(8,128)(2,1)S(1)}, bf16[384,512]{1,0:T(8,128)(2...) custom-call(s32[3]{0:T(128)S(1)} %pad_add_fusion.ids, s32[8]{0:T(128)S(1)} %copy-done.20, f32[3]{0:T(128)S(1)} %copy-done.21, ...), custom_call_target="tpu_custom_call" | custom-call | flops 1 | bytes 1 | tf_op jit(solution)/shard_map/pallas_call | solution.py:88
  22.0 5.6 %shard_map.242 = (bf16[384,512]{1,0:T(8,128)(2,1)S(1)}, bf16[384,512]{1,0:T(8,128)(2,1)S(1)}, bf16[384,512]{1,0:T(8,128)(2,1)S(1)}, bf16[384,512]{1,0:T(8,128)(2,1)S(1)}, f32[8,512]{1,0:T(8,128)S(1)}) custom-call(s32[3]{0:T(128)S(1)} %pad_add_fusion.ids, s32[8]{0:T(128)S(1)} %copy-done.20, bf16[512,768]{1,0:T(8,128)(2,1)S(1)} %get-tuple-element.172.xq, ...), custom_call_target="tpu_custom_call" | custom-call | flops 1 | bytes 1 | tf_op jit(solution)/shard_map/pallas_call | solution.py:88
  28.4 19.2 %shard_map.243 = (f32[512,768]{1,0:T(8,128)S(1)}, f32[512,128]{1,0:T(8,128)S(1)}, bf16[512,768]{1,0:T(8,128)(2,1)S(1)}, bf16[512,1536]{1,0:T(8,128)(2,1)S(1)}, b...) custom-call(f32[3]{0:T(128)S(1)} %copy-done.21, ...), custom_call_target="tpu_custom_call" | custom-call | flops 1 | bytes 1 | tf_op jit(solution)/shard_map/pallas_call | solution.py:88
  47.5 1.4 down_theirshigh.1
  49.3 1.4 down_minehigh.1
  50.7 1.4 down_theirslow.1
  52.7 2.6 %collective-permute-start.9 = (bf16[8,192,384]{2,1,0:T(8,128)(2,1)S(1)}, bf16[8,192,384]{2,1,0:T(8,128)(2,1)S(1)}, u32[]{:S(2)}, u32[]{:S(2)}) collective-permute-start(bf16[8,192,384]{2,1,0:T(8,128)(2,1)S(1)} %add_convert_fusion.2), channel_id=1, source_target_pairs={{0,2},{1,5},{2,0},{3,7},{4,6},{5,1},{6,4},{7,3},{8,10},{9,13},{10,... | collective-permute-start | bytes 3538952 | tf_op jit(solution)/shard_map/down_in0/ppermute | solution.py:592
  55.3 1.4 down_minelow.1
  56.7 6.4 %up_theirs.1 = (bf16[8,192,384]{2,1,0:T(8,128)(2,1)S(1)}, bf16[8,192,384]{2,1,0:T(8,128)(2,1)S(1)}, f32[1,1536]{1,0:T(1,128)S(1)}, f32[512,768]{1,0:T(8,128)S(1)}) custom-call(s32[3]{0:T(128)S(1)} %pad_add_fusion.ids, bf16[512,768]{1,0:T(8,128)(2,1)S(1)} %get-tuple-element.194.grad_feed, bf16[1536,768]{1,0:T(8,128)(2,1)} %collective-permute-done.5.down_other.down, ...), custom_call_target="tpu_custom_call" | custom-call | flops 1 | bytes 1 | tf_op jit(solution)/shard_map/up_theirs/pallas_call | solution.py:88
  63.6 6.4 %up_mine.1 = (bf16[8,192,384]{2,1,0:T(8,128)(2,1)S(1)}, bf16[8,192,384]{2,1,0:T(8,128)(2,1)S(1)}, f32[1,1536]{1,0:T(1,128)S(1)}, f32[512,768]{1,0:T(8,128)S(1)}) custom-call(s32[3]{0:T(128)S(1)} %pad_add_fusion.ids, bf16[512,768]{1,0:T(8,128)(2,1)S(1)} %get-tuple-element.194.grad_feed, bf16[1536,768]{1,0:T(8,128)(2,1)} %get-tuple-element.177.down_own.down, ...), custom_call_target="tpu_custom_call" | custom-call | flops 1 | bytes 1 | tf_op jit(solution)/shard_map/up_mine/pallas_call | solution.py:88
  70.9 1.3 collective-permute-start.15
  72.8 2.2 %norm.1 = (f32[512,768]{1,0:T(8,128)S(1)}, bf16[512,768]{1,0:T(8,128)(2,1)S(1)}, f32[16,768]{1,0:T(8,128)S(1)}, f32[16,768]{1,0:T(8,128)S(1)}) custom-call(f32[3]{0:T(128)S(1)} %copy-done.21, f32[512,768]{1,0:T(8,128)S(1)} %get-tuple-element.206.grad_normed, f32[512,768]{1,0:T(8,128)S(1)} %get-tuple-element.207.grad_sum, ...), custom_call_target="tpu_custom_call" | custom-call | flops 1 | bytes 1 | tf_op jit(solution)/shard_map/norm/pallas_call | solution.py:88
  75.1 18.1 %heads_theirs.1 = (bf16[8,48,384]{2,1,0:T(8,128)(2,1)S(1)}, bf16[8,48,384]{2,1,0:T(8,128)(2,1)S(1)}, bf16[8,48,384]{2,1,0:T(8,128)(2,1)S(1)}, bf16[8,48,384]{2,1...) custom-call(s32[3]{0:T(128)S(1)} %pad_add_fusion.ids, ...), custom_call_target="tpu_custom_call" | custom-call | flops 1 | bytes 1 | tf_op jit(solution)/shard_map/heads_theirs/pallas_call | solution.py:88
  93.2 1.6 collective-permute-start.10
  94.8 8.0 %heads_mine.1 = (bf16[8,192,384]{2,1,0:T(8,128)(2,1)S(1)}, bf16[8,192,384]{2,1,0:T(8,128)(2,1)S(1)}, bf16[3,384,512]{2,1,0:T(8,128)(2,1)S(1)}, f32[8,768]{1,0:T(8,128)S(1)}) custom-call(s32[3]{0:T(128)S(1)} %pad_add_fusion.ids, s32[8]{0:T(128)S(1)} %copy-done.20, bf16[512,768]{1,0:T(8,128)(2,1)S(1)} %get-tuple-element.172.xq, ...), custom_call_target="tpu_custom_call" | custom-call | flops 1 | bytes 1 | tf_op jit(solution)/shard_map/heads_mine/pallas_call | solution.py:88
  103.5 1.4 collective-permute-start.23
  106.9 4.5 %input.1 = f32[512,768]{1,0:T(8,128)} custom-call(f32[3]{0:T(128)S(1)} %copy-done.21, bf16[512,768]{1,0:T(8,128)(2,1)S(1)} %copy-done.10, f32[512,768]{1,0:T(8,128)S(1)} %get-tuple-element.251.grad_first, bf16[3,768,384]{2,1,0:T(8,128)(2,1)S(1)} %copy-done.7, bf16[3,768,384]{2,1,0:T(8,128)(2,1)S(1)} %copy-done.9, ...), custom_call_target="tpu_custom_call" | custom-call | flops 1 | bytes 1 | tf_op jit(solution)/shard_map/input/pallas_call | solution.py:88
  111.8 2.4 %collective-permute-start.24 = (bf16[1,192,384]{2,1,0:T(8,128)(2,1)S(1)}, bf16[1,192,384]{2,1,0:T(8,128)(2,1)S(1)}, u32[]{:S(2)}, u32[]{:S(2)}) collective-permute-start(bf16[1,192,384]{2,1,0:T(8,128)(2,1)S(1)} %get-tuple-element.334), channel_id=1, source_target_pairs={{0,16},{1,17},{2,18},{3,19},{4,20},{5,21},{6,22},{7,23},{8,24},{9,... | collective-permute-start | bytes 442376 | tf_op jit(solution)/shard_map/down_in3/ppermute | solution.py:592
  114.2 1.5 collective-permute-start.17
  115.8 4.8 %collective-permute-done.24 = bf16[1,192,384]{2,1,0:T(8,128)(2,1)S(1)} collective-permute-done((bf16[1,192,384]{2,1,0:T(8,128)(2,1)S(1)}, bf16[1,192,384]{2,1,0:T(8,128)(2,1)S(1)}, u32[]{:S(2)}, u32[]{:S(2)}) %collective-permute-start.24) | collective-permute-done | bytes 147488 | tf_op jit(solution)/shard_map/down_in3/ppermute | solution.py:592
  120.7 1.6 collective-permute-start.19
  122.2 1.2 collective-permute-start.20
  123.7 2.4 %collective-permute-start.27 = (bf16[1,192,384]{2,1,0:T(8,128)(2,1)S(1)}, bf16[1,192,384]{2,1,0:T(8,128)(2,1)S(1)}, u32[]{:S(2)}, u32[]{:S(2)}) collective-permute-start(bf16[1,192,384]{2,1,0:T(8,128)(2,1)S(1)} %add_convert_fusion.21), channel_id=1, source_target_pairs={{0,16},{1,17},{2,18},{3,19},{4,20},{5,21},{6,22},{7,23},{8,24},{9,... | collective-permute-start | bytes 442376 | tf_op jit(solution)/shard_map/down_out3/ppermute | solution.py:592
  128.7 1.2 collective-permute-start.33
  129.9 3.6 %collective-permute-done.27 = bf16[1,192,384]{2,1,0:T(8,128)(2,1)S(1)} collective-permute-done((bf16[1,192,384]{2,1,0:T(8,128)(2,1)S(1)}, bf16[1,192,384]{2,1,0:T(8,128)(2,1)S(1)}, u32[]{:S(2)}, u32[]{:S(2)}) %collective-permute-start.27) | collective-permute-done | bytes 147488 | tf_op jit(solution)/shard_map/down_out3/ppermute | solution.py:592
  133.6 3.2 %collective-permute-done.26 = bf16[2,192,384]{2,1,0:T(8,128)(2,1)S(1)} collective-permute-done((bf16[2,192,384]{2,1,0:T(8,128)(2,1)S(1)}, bf16[2,192,384]{2,1,0:T(8,128)(2,1)S(1)}, u32[]{:S(2)}, u32[]{:S(2)}) %collective-permute-start.26) | collective-permute-done | bytes 294944 | tf_op jit(solution)/shard_map/up_in2/ppermute | solution.py:592
  138.0 7.2 %collective-permute-done.31 = bf16[2,192,384]{2,1,0:T(8,128)(2,1)S(1)} collective-permute-done((bf16[2,192,384]{2,1,0:T(8,128)(2,1)S(1)}, bf16[2,192,384]{2,1,0:T(8,128)(2,1)S(1)}, u32[]{:S(2)}, u32[]{:S(2)}) %collective-permute-start.31) | collective-permute-done | bytes 294944 | tf_op jit(solution)/shard_map/down_out2/ppermute | solution.py:592
  145.4 1.2 collective-permute-start.36
  146.7 1.6 collective-permute-start.35
  148.3 7.1 %collective-permute-done.29 = bf16[2,192,384]{2,1,0:T(8,128)(2,1)S(1)} collective-permute-done((bf16[2,192,384]{2,1,0:T(8,128)(2,1)S(1)}, bf16[2,192,384]{2,1,0:T(8,128)(2,1)S(1)}, u32[]{:S(2)}, u32[]{:S(2)}) %collective-permute-start.29) | collective-permute-done | bytes 294944 | tf_op jit(solution)/shard_map/rest_in2/ppermute | solution.py:592
  156.1 1.5 collective-permute-start.41
  157.6 2.3 %collective-permute-start.38 = (bf16[2,192,384]{2,1,0:T(8,128)(2,1)S(1)}, bf16[2,192,384]{2,1,0:T(8,128)(2,1)S(1)}, u32[]{:S(2)}, u32[]{:S(2)}) collective-permute-start(bf16[2,192,384]{2,1,0:T(8,128)(2,1)S(1)} %constant_dynamic-update-slice_fusion.10), channel_id=1, source_target_pairs={{0,8},{1,9},{2,10},{3,11},{4,12},{5,13},{6,14},{7,15},{8,0},{9,1},... | collective-permute-start | bytes 884744 | tf_op jit(solution)/shard_map/up_out2/ppermute | solution.py:592
  160.0 2.3 %collective-permute-done.32 = bf16[1,192,384]{2,1,0:T(8,128)(2,1)S(1)} collective-permute-done((bf16[1,192,384]{2,1,0:T(8,128)(2,1)S(1)}, bf16[1,192,384]{2,1,0:T(8,128)(2,1)S(1)}, u32[]{:S(2)}, u32[]{:S(2)}) %collective-permute-start.32) | collective-permute-done | bytes 147488 | tf_op jit(solution)/shard_map/rest_in3/ppermute | solution.py:592
  162.5 10.7 %collective-permute-done.39 = f32[12,768]{1,0:T(8,128)S(1)} collective-permute-done((f32[12,768]{1,0:T(8,128)S(1)}, f32[12,768]{1,0:T(8,128)S(1)}, u32[]{:S(2)}, u32[]{:S(2)}) %collective-permute-start.39) | collective-permute-done | bytes 36896 | tf_op jit(solution)/shard_map/small_in2/ppermute | solution.py:592
  174.1 3.7 %down_final.1 = f32[1536,768]{1,0:T(8,128)} custom-call(s32[3]{0:T(128)S(1)} %pad_add_fusion.ids, f32[16,1536]{1,0:T(8,128)S(1)} %shard_map.239.own.pack_own, f32[16,1536]{1,0:T(8,128)S(1)} %collective-permute-done.1.other.pack_other, bf16[8,192,384]{2,1,0:T(8,128)(2,1)S(1)} %constant_dynamic-update-slice_fusion.8.low, ...), custom_call_target="tpu_custom_call" | custom-call | flops 1 | bytes 1 | tf_op jit(solution)/shard_map/down_final/pallas_call | solution.py:1047
  177.8 2.6 %collective-permute-done.40 = bf16[2,192,384]{2,1,0:T(8,128)(2,1)S(1)} collective-permute-done((bf16[2,192,384]{2,1,0:T(8,128)(2,1)S(1)}, bf16[2,192,384]{2,1,0:T(8,128)(2,1)S(1)}, u32[]{:S(2)}, u32[]{:S(2)}) %collective-permute-start.40) | collective-permute-done | bytes 294944 | tf_op jit(solution)/shard_map/rest_out2/ppermute | solution.py:592
  180.9 2.3 %collective-permute-start.43 = (f32[12,768]{1,0:T(8,128)S(1)}, f32[12,768]{1,0:T(8,128)S(1)}, u32[]{:S(2)}, u32[]{:S(2)}) collective-permute-start(f32[12,768]{1,0:T(8,128)S(1)} %maximum_select_fusion.1), channel_id=1, source_target_pairs={{0,16},{1,17},{2,18},{3,19},{4,20},{5,21},{6,22},{7,23},{8,24},{9,... | collective-permute-start | bytes 110600 | tf_op jit(solution)/shard_map/small_in3/ppermute | solution.py:592
  185.0 4.6 %collective-permute-done.42 = bf16[4,192,384]{2,1,0:T(8,128)(2,1)S(1)} collective-permute-done((bf16[4,192,384]{2,1,0:T(8,128)(2,1)S(1)}, bf16[4,192,384]{2,1,0:T(8,128)(2,1)S(1)}, u32[]{:S(2)}, u32[]{:S(2)}) %collective-permute-start.42) | collective-permute-done | bytes 589856 | tf_op jit(solution)/shard_map/rest_out1/ppermute | solution.py:592
  194.4 10.9 %collective-permute-done.46.high = bf16[8,192,384]{2,1,0:T(8,128)(2,1)} collective-permute-done((bf16[8,192,384]{2,1,0:T(8,128)(2,1)}, bf16[8,192,384]{2,1,0:T(8,128)(2,1)}, u32[]{:S(2)}, u32[]{:S(2)}) %collective-permute-start.46) | collective-permute-done | bytes 1179680 | tf_op jit(solution)/shard_map/up_out0/ppermute | solution.py:592
  205.3 5.3 %up_final.1 = f32[768,1536]{1,0:T(8,128)} custom-call(s32[3]{0:T(128)S(1)} %pad_add_fusion.ids, f32[16,1536]{1,0:T(8,128)S(1)} %shard_map.239.own.pack_own, f32[16,1536]{1,0:T(8,128)S(1)} %collective-permute-done.1.other.pack_other, bf16[8,192,384]{2,1,0:T(8,128)(2,1)} %constant_dynamic-update-slice_fusion.18.low, ...), custom_call_target="tpu_custom_call" | custom-call | flops 1 | bytes 1 | tf_op jit(solution)/shard_map/up_final/pallas_call | solution.py:1047
  210.6 7.0 %collective-permute-done.45.high = bf16[8,192,384]{2,1,0:T(8,128)(2,1)} collective-permute-done((bf16[8,192,384]{2,1,0:T(8,128)(2,1)}, bf16[8,192,384]{2,1,0:T(8,128)(2,1)}, u32[]{:S(2)}, u32[]{:S(2)}) %collective-permute-start.45) | collective-permute-done | bytes 1179680 | tf_op jit(solution)/shard_map/rest_out0/ppermute | solution.py:592
  217.7 5.4 %rest_final.1 = (f32[3,768,384]{2,1,0:T(8,128)}, f32[384,768]{1,0:T(8,128)}) custom-call(s32[3]{0:T(128)S(1)} %pad_add_fusion.ids, f32[16,1536]{1,0:T(8,128)S(1)} %shard_map.239.own.pack_own, f32[16,1536]{1,0:T(8,128)S(1)} %collective-permute-done.1.other.pack_other, bf16[8,192,384]{2,1,0:T(8,128)(2,1)} %constant_dynamic-update-slice_fusion.20.low, ...), custom_call_target="tpu_custom_call" | custom-call | flops 1 | bytes 1 | tf_op jit(solution)/shard_map/rest_final/pallas_call | solution.py:1047
  (183 shorter events, 25.2 us)
Async XLA Ops:
  3.6 1.3 collective-permute-start
  5.8 3.9 %collective-permute-start.2 = (bf16[3,768,384]{2,1,0:T(8,128)(2,1)S(1)}, bf16[3,768,384]{2,1,0:T(8,128)(2,1)S(1)}, u32[]{:S(2)}, u32[]{:S(2)}) collective-permute-start(bf16[3,768,384]{2,1,0:T(8,128)(2,1)S(1)} %shard_map.238.weight.w_own), channel_id=1, source_target_pairs={{0,1},{1,0},{2,3},{3,2},{4,5},{5,4},{6,7},{7,6},{8,9},{9,8},{10,11... | collective-permute-start | bytes 5308424 | tf_op jit(solution)/shard_map/ppermute | solution.py:595
  7.1 2.6 %collective-permute-start.1 = (f32[16,1536]{1,0:T(8,128)S(1)}, f32[16,1536]{1,0:T(8,128)S(1)}, u32[]{:S(2)}, u32[]{:S(2)}) collective-permute-start(f32[16,1536]{1,0:T(8,128)S(1)} %shard_map.239.own.pack_own), channel_id=1, source_target_pairs={{0,1},{1,0},{2,3},{3,2},{4,5},{5,4},{6,7},{7,6},{8,9},{9,8},{10,11... | collective-permute-start | bytes 294920 | tf_op jit(solution)/shard_map/ppermute | solution.py:595
  13.9 14.4 %collective-permute-start.4 = (bf16[768,1536]{1,0:T(8,128)(2,1)}, bf16[768,1536]{1,0:T(8,128)(2,1)}, u32[]{:S(2)}, u32[]{:S(2)}) collective-permute-start(bf16[768,1536]{1,0:T(8,128)(2,1)} %get-tuple-element.176.up_own.up), channel_id=1, source_target_pairs={{0,1},{1,0},{2,3},{3,2},{4,5},{5,4},{6,7},{7,6},{8,9},{9,8},{10,11... | collective-permute-start | bytes 7077896 | tf_op jit(solution)/shard_map/ppermute | solution.py:595
  14.1 14.2 %collective-permute-start.5 = (bf16[1536,768]{1,0:T(8,128)(2,1)}, bf16[1536,768]{1,0:T(8,128)(2,1)}, u32[]{:S(2)}, u32[]{:S(2)}) collective-permute-start(bf16[1536,768]{1,0:T(8,128)(2,1)} %get-tuple-element.177.down_own.down), channel_id=1, source_target_pairs={{0,1},{1,0},{2,3},{3,2},{4,5},{5,4},{6,7},{7,6},{8,9},{9,8},{10,11... | collective-permute-start | bytes 7077896 | tf_op jit(solution)/shard_map/ppermute | solution.py:595
  14.4 13.9 %collective-permute-start.3 = (bf16[384,768]{1,0:T(8,128)(2,1)}, bf16[384,768]{1,0:T(8,128)(2,1)}, u32[]{:S(2)}, u32[]{:S(2)}) collective-permute-start(bf16[384,768]{1,0:T(8,128)(2,1)} %get-tuple-element.175.merge_own.merge_q), channel_id=1, source_target_pairs={{0,1},{1,0},{2,3},{3,2},{4,5},{5,4},{6,7},{7,6},{8,9},{9,8},{10,11... | collective-permute-start | bytes 1769480 | tf_op jit(solution)/shard_map/ppermute | solution.py:595
  48.9 3.4 %collective-permute-start.6 = (bf16[8,192,384]{2,1,0:T(8,128)(2,1)S(1)}, bf16[8,192,384]{2,1,0:T(8,128)(2,1)S(1)}, u32[]{:S(2)}, u32[]{:S(2)}) collective-permute-start(bf16[8,192,384]{2,1,0:T(8,128)(2,1)S(1)} %down_theirshigh.1), channel_id=1, source_target_pairs={{0,1},{1,0},{2,3},{3,2},{4,5},{5,4},{6,7},{7,6},{8,9},{9,8},{10,11... | collective-permute-start | bytes 3538952 | tf_op jit(solution)/shard_map/down_high/ppermute | solution.py:595
  52.1 17.9 %collective-permute-start.8 = (bf16[8,192,384]{2,1,0:T(8,128)(2,1)S(1)}, bf16[8,192,384]{2,1,0:T(8,128)(2,1)S(1)}, u32[]{:S(2)}, u32[]{:S(2)}) collective-permute-start(bf16[8,192,384]{2,1,0:T(8,128)(2,1)S(1)} %down_theirslow.1), channel_id=1, source_target_pairs={{0,1},{1,0},{2,3},{3,2},{4,5},{5,4},{6,7},{7,6},{8,9},{9,8},{10,11... | collective-permute-start | bytes 3538952 | tf_op jit(solution)/shard_map/down_low/ppermute | solution.py:595
  52.7 17.4 %collective-permute-start.9 = (bf16[8,192,384]{2,1,0:T(8,128)(2,1)S(1)}, bf16[8,192,384]{2,1,0:T(8,128)(2,1)S(1)}, u32[]{:S(2)}, u32[]{:S(2)}) collective-permute-start(bf16[8,192,384]{2,1,0:T(8,128)(2,1)S(1)} %add_convert_fusion.2), channel_id=1, source_target_pairs={{0,2},{1,5},{2,0},{3,7},{4,6},{5,1},{6,4},{7,3},{8,10},{9,13},{10,... | collective-permute-start | bytes 3538952 | tf_op jit(solution)/shard_map/down_in0/ppermute | solution.py:592
  63.0 7.5 %collective-permute-start.7 = (bf16[8,192,384]{2,1,0:T(8,128)(2,1)S(1)}, bf16[8,192,384]{2,1,0:T(8,128)(2,1)S(1)}, u32[]{:S(2)}, u32[]{:S(2)}) collective-permute-start(bf16[8,192,384]{2,1,0:T(8,128)(2,1)S(1)} %get-tuple-element.190), channel_id=1, source_target_pairs={{0,1},{1,0},{2,3},{3,2},{4,5},{5,4},{6,7},{7,6},{8,9},{9,8},{10,11... | collective-permute-start | bytes 3538952 | tf_op jit(solution)/shard_map/up_high/ppermute | solution.py:595
  63.5 39.9 %collective-permute-start.14 = (bf16[8,192,384]{2,1,0:T(8,128)(2,1)S(1)}, bf16[8,192,384]{2,1,0:T(8,128)(2,1)S(1)}, u32[]{:S(2)}, u32[]{:S(2)}) collective-permute-start(bf16[8,192,384]{2,1,0:T(8,128)(2,1)S(1)} %get-tuple-element.191), channel_id=1, source_target_pairs={{0,1},{1,0},{2,3},{3,2},{4,5},{5,4},{6,7},{7,6},{8,9},{9,8},{10,11... | collective-permute-start | bytes 3538952 | tf_op jit(solution)/shard_map/up_low/ppermute | solution.py:595
  70.9 32.7 %collective-permute-start.15 = (bf16[8,192,384]{2,1,0:T(8,128)(2,1)S(1)}, bf16[8,192,384]{2,1,0:T(8,128)(2,1)S(1)}, u32[]{:S(2)}, u32[]{:S(2)}) collective-permute-start(bf16[8,192,384]{2,1,0:T(8,128)(2,1)S(1)} %add_convert_fusion.1), channel_id=1, source_target_pairs={{0,2},{1,5},{2,0},{3,7},{4,6},{5,1},{6,4},{7,3},{8,10},{9,13},{10,... | collective-permute-start | bytes 3538952 | tf_op jit(solution)/shard_map/up_in0/ppermute | solution.py:592
  72.2 30.6 %collective-permute-start.16 = (bf16[4,192,384]{2,1,0:T(8,128)(2,1)S(1)}, bf16[4,192,384]{2,1,0:T(8,128)(2,1)S(1)}, u32[]{:S(2)}, u32[]{:S(2)}) collective-permute-start(bf16[4,192,384]{2,1,0:T(8,128)(2,1)S(1)} %get-tuple-element.322), channel_id=1, source_target_pairs={{0,4},{1,3},{2,6},{3,1},{4,0},{5,7},{6,2},{7,5},{8,12},{9,11},{10,... | collective-permute-start | bytes 1769480 | tf_op jit(solution)/shard_map/down_in1/ppermute | solution.py:592
  93.2 12.3 %collective-permute-start.10 = (bf16[8,48,384]{2,1,0:T(8,128)(2,1)S(1)}, bf16[8,48,384]{2,1,0:T(8,128)(2,1)S(1)}, u32[]{:S(2)}, u32[]{:S(2)}) collective-permute-start(bf16[8,48,384]{2,1,0:T(8,128)(2,1)S(1)} %get-tuple-element.222), channel_id=1, source_target_pairs={{0,1},{1,0},{2,3},{3,2},{4,5},{5,4},{6,7},{7,6},{8,9},{9,8},{10,11... | collective-permute-start | bytes 884744 | tf_op jit(solution)/shard_map/rest_high/ppermute | solution.py:595
  94.8 10.7 %collective-permute-start.11 = (bf16[8,48,384]{2,1,0:T(8,128)(2,1)S(1)}, bf16[8,48,384]{2,1,0:T(8,128)(2,1)S(1)}, u32[]{:S(2)}, u32[]{:S(2)}) collective-permute-start(bf16[8,48,384]{2,1,0:T(8,128)(2,1)S(1)} %get-tuple-element.223), channel_id=1, source_target_pairs={{0,1},{1,0},{2,3},{3,2},{4,5},{5,4},{6,7},{7,6},{8,9},{9,8},{10,11... | collective-permute-start | bytes 884744 | tf_op jit(solution)/shard_map/rest_high/ppermute | solution.py:595
  102.8 2.7 %collective-permute-start.12 = (bf16[8,48,384]{2,1,0:T(8,128)(2,1)S(1)}, bf16[8,48,384]{2,1,0:T(8,128)(2,1)S(1)}, u32[]{:S(2)}, u32[]{:S(2)}) collective-permute-start(bf16[8,48,384]{2,1,0:T(8,128)(2,1)S(1)} %get-tuple-element.224), channel_id=1, source_target_pairs={{0,1},{1,0},{2,3},{3,2},{4,5},{5,4},{6,7},{7,6},{8,9},{9,8},{10,11... | collective-permute-start | bytes 884744 | tf_op jit(solution)/shard_map/rest_high/ppermute | solution.py:595
  103.5 2.0 collective-permute-start.13
  103.5 8.2 %collective-permute-start.23 = (bf16[2,192,384]{2,1,0:T(8,128)(2,1)S(1)}, bf16[2,192,384]{2,1,0:T(8,128)(2,1)S(1)}, u32[]{:S(2)}, u32[]{:S(2)}) collective-permute-start(bf16[2,192,384]{2,1,0:T(8,128)(2,1)S(1)} %get-tuple-element.328), channel_id=1, source_target_pairs={{0,8},{1,9},{2,10},{3,11},{4,12},{5,13},{6,14},{7,15},{8,0},{9,1},... | collective-permute-start | bytes 884744 | tf_op jit(solution)/shard_map/down_in2/ppermute | solution.py:592
  105.8 21.7 %collective-permute-start.21 = (bf16[8,192,384]{2,1,0:T(8,128)(2,1)S(1)}, bf16[8,192,384]{2,1,0:T(8,128)(2,1)S(1)}, u32[]{:S(2)}, u32[]{:S(2)}) collective-permute-start(bf16[8,192,384]{2,1,0:T(8,128)(2,1)S(1)} %add_convert_fusion), channel_id=1, source_target_pairs={{0,2},{1,5},{2,0},{3,7},{4,6},{5,1},{6,4},{7,3},{8,10},{9,13},{10,... | collective-permute-start | bytes 3538952 | tf_op jit(solution)/shard_map/rest_in0/ppermute | solution.py:592
  106.1 16.1 %collective-permute-start.22 = (bf16[4,192,384]{2,1,0:T(8,128)(2,1)S(1)}, bf16[4,192,384]{2,1,0:T(8,128)(2,1)S(1)}, u32[]{:S(2)}, u32[]{:S(2)}) collective-permute-start(bf16[4,192,384]{2,1,0:T(8,128)(2,1)S(1)} %get-tuple-element.320), channel_id=1, source_target_pairs={{0,4},{1,3},{2,6},{3,1},{4,0},{5,7},{6,2},{7,5},{8,12},{9,11},{10,... | collective-permute-start | bytes 1769480 | tf_op jit(solution)/shard_map/up_in1/ppermute | solution.py:592
  111.8 8.8 %collective-permute-start.24 = (bf16[1,192,384]{2,1,0:T(8,128)(2,1)S(1)}, bf16[1,192,384]{2,1,0:T(8,128)(2,1)S(1)}, u32[]{:S(2)}, u32[]{:S(2)}) collective-permute-start(bf16[1,192,384]{2,1,0:T(8,128)(2,1)S(1)} %get-tuple-element.334), channel_id=1, source_target_pairs={{0,16},{1,17},{2,18},{3,19},{4,20},{5,21},{6,22},{7,23},{8,24},{9,... | collective-permute-start | bytes 442376 | tf_op jit(solution)/shard_map/down_in3/ppermute | solution.py:592
  114.2 9.4 %collective-permute-start.17 = (bf16[8,48,384]{2,1,0:T(8,128)(2,1)S(1)}, bf16[8,48,384]{2,1,0:T(8,128)(2,1)S(1)}, u32[]{:S(2)}, u32[]{:S(2)}) collective-permute-start(bf16[8,48,384]{2,1,0:T(8,128)(2,1)S(1)} %get-tuple-element.226), channel_id=1, source_target_pairs={{0,1},{1,0},{2,3},{3,2},{4,5},{5,4},{6,7},{7,6},{8,9},{9,8},{10,11... | collective-permute-start | bytes 884744 | tf_op jit(solution)/shard_map/rest_low/ppermute | solution.py:595
  115.8 7.9 %collective-permute-start.18 = (bf16[8,48,384]{2,1,0:T(8,128)(2,1)S(1)}, bf16[8,48,384]{2,1,0:T(8,128)(2,1)S(1)}, u32[]{:S(2)}, u32[]{:S(2)}) collective-permute-start(bf16[8,48,384]{2,1,0:T(8,128)(2,1)S(1)} %get-tuple-element.227), channel_id=1, source_target_pairs={{0,1},{1,0},{2,3},{3,2},{4,5},{5,4},{6,7},{7,6},{8,9},{9,8},{10,11... | collective-permute-start | bytes 884744 | tf_op jit(solution)/shard_map/rest_low/ppermute | solution.py:595
  120.7 5.4 %collective-permute-start.19 = (bf16[8,48,384]{2,1,0:T(8,128)(2,1)S(1)}, bf16[8,48,384]{2,1,0:T(8,128)(2,1)S(1)}, u32[]{:S(2)}, u32[]{:S(2)}) collective-permute-start(bf16[8,48,384]{2,1,0:T(8,128)(2,1)S(1)} %get-tuple-element.228), channel_id=1, source_target_pairs={{0,1},{1,0},{2,3},{3,2},{4,5},{5,4},{6,7},{7,6},{8,9},{9,8},{10,11... | collective-permute-start | bytes 884744 | tf_op jit(solution)/shard_map/rest_low/ppermute | solution.py:595
  122.2 4.3 %collective-permute-start.20 = (bf16[8,48,384]{2,1,0:T(8,128)(2,1)S(1)}, bf16[8,48,384]{2,1,0:T(8,128)(2,1)S(1)}, u32[]{:S(2)}, u32[]{:S(2)}) collective-permute-start(bf16[8,48,384]{2,1,0:T(8,128)(2,1)S(1)} %get-tuple-element.229), channel_id=1, source_target_pairs={{0,1},{1,0},{2,3},{3,2},{4,5},{5,4},{6,7},{7,6},{8,9},{9,8},{10,11... | collective-permute-start | bytes 884744 | tf_op jit(solution)/shard_map/rest_low/ppermute | solution.py:595
  123.6 4.6 %collective-permute-start.28 = (f32[12,768]{1,0:T(8,128)S(1)}, f32[12,768]{1,0:T(8,128)S(1)}, u32[]{:S(2)}, u32[]{:S(2)}) collective-permute-start(f32[12,768]{1,0:T(8,128)S(1)} %pad_maximum_fusion), channel_id=1, source_target_pairs={{0,1},{1,0},{2,3},{3,2},{4,5},{5,4},{6,7},{7,6},{8,9},{9,8},{10,11... | collective-permute-start | bytes 110600 | tf_op jit(solution)/shard_map/small_got/ppermute | solution.py:595
  123.7 9.8 %collective-permute-start.27 = (bf16[1,192,384]{2,1,0:T(8,128)(2,1)S(1)}, bf16[1,192,384]{2,1,0:T(8,128)(2,1)S(1)}, u32[]{:S(2)}, u32[]{:S(2)}) collective-permute-start(bf16[1,192,384]{2,1,0:T(8,128)(2,1)S(1)} %add_convert_fusion.21), channel_id=1, source_target_pairs={{0,16},{1,17},{2,18},{3,19},{4,20},{5,21},{6,22},{7,23},{8,24},{9,... | collective-permute-start | bytes 442376 | tf_op jit(solution)/shard_map/down_out3/ppermute | solution.py:592
  126.1 10.8 %collective-permute-start.26 = (bf16[2,192,384]{2,1,0:T(8,128)(2,1)S(1)}, bf16[2,192,384]{2,1,0:T(8,128)(2,1)S(1)}, u32[]{:S(2)}, u32[]{:S(2)}) collective-permute-start(bf16[2,192,384]{2,1,0:T(8,128)(2,1)S(1)} %get-tuple-element.326), channel_id=1, source_target_pairs={{0,8},{1,9},{2,10},{3,11},{4,12},{5,13},{6,14},{7,15},{8,0},{9,1},... | collective-permute-start | bytes 884744 | tf_op jit(solution)/shard_map/up_in2/ppermute | solution.py:592
  128.3 9.6 %collective-permute-start.25 = (bf16[4,192,384]{2,1,0:T(8,128)(2,1)S(1)}, bf16[4,192,384]{2,1,0:T(8,128)(2,1)S(1)}, u32[]{:S(2)}, u32[]{:S(2)}) collective-permute-start(bf16[4,192,384]{2,1,0:T(8,128)(2,1)S(1)} %get-tuple-element.318), channel_id=1, source_target_pairs={{0,4},{1,3},{2,6},{3,1},{4,0},{5,7},{6,2},{7,5},{8,12},{9,11},{10,... | collective-permute-start | bytes 1769480 | tf_op jit(solution)/shard_map/rest_in1/ppermute | solution.py:592
  128.7 26.8 %collective-permute-start.33 = (f32[12,768]{1,0:T(8,128)S(1)}, f32[12,768]{1,0:T(8,128)S(1)}, u32[]{:S(2)}, u32[]{:S(2)}) collective-permute-start(f32[12,768]{1,0:T(8,128)S(1)} %maximum_select_fusion.4), channel_id=1, source_target_pairs={{0,2},{1,3},{2,0},{3,1},{4,6},{5,7},{6,4},{7,5},{8,10},{9,11},{10,... | collective-permute-start | bytes 110600 | tf_op jit(solution)/shard_map/small_in0/ppermute | solution.py:592
  133.6 11.7 %collective-permute-start.31 = (bf16[2,192,384]{2,1,0:T(8,128)(2,1)S(1)}, bf16[2,192,384]{2,1,0:T(8,128)(2,1)S(1)}, u32[]{:S(2)}, u32[]{:S(2)}) collective-permute-start(bf16[2,192,384]{2,1,0:T(8,128)(2,1)S(1)} %constant_dynamic-update-slice_fusion.4), channel_id=1, source_target_pairs={{0,8},{1,9},{2,10},{3,11},{4,12},{5,13},{6,14},{7,15},{8,0},{9,1},... | collective-permute-start | bytes 884744 | tf_op jit(solution)/shard_map/down_out2/ppermute | solution.py:592
  136.9 9.7 %collective-permute-start.30 = (bf16[1,192,384]{2,1,0:T(8,128)(2,1)S(1)}, bf16[1,192,384]{2,1,0:T(8,128)(2,1)S(1)}, u32[]{:S(2)}, u32[]{:S(2)}) collective-permute-start(bf16[1,192,384]{2,1,0:T(8,128)(2,1)S(1)} %get-tuple-element.332), channel_id=1, source_target_pairs={{0,16},{1,17},{2,18},{3,19},{4,20},{5,21},{6,22},{7,23},{8,24},{9,... | collective-permute-start | bytes 442376 | tf_op jit(solution)/shard_map/up_in3/ppermute | solution.py:592
  145.3 10.1 %collective-permute-start.29 = (bf16[2,192,384]{2,1,0:T(8,128)(2,1)S(1)}, bf16[2,192,384]{2,1,0:T(8,128)(2,1)S(1)}, u32[]{:S(2)}, u32[]{:S(2)}) collective-permute-start(bf16[2,192,384]{2,1,0:T(8,128)(2,1)S(1)} %get-tuple-element.324), channel_id=1, source_target_pairs={{0,8},{1,9},{2,10},{3,11},{4,12},{5,13},{6,14},{7,15},{8,0},{9,1},... | collective-permute-start | bytes 884744 | tf_op jit(solution)/shard_map/rest_in2/ppermute | solution.py:592
  145.4 10.5 %collective-permute-start.36 = (bf16[4,192,384]{2,1,0:T(8,128)(2,1)S(1)}, bf16[4,192,384]{2,1,0:T(8,128)(2,1)S(1)}, u32[]{:S(2)}, u32[]{:S(2)}) collective-permute-start(bf16[4,192,384]{2,1,0:T(8,128)(2,1)S(1)} %constant_dynamic-update-slice_fusion.6), channel_id=1, source_target_pairs={{0,4},{1,3},{2,6},{3,1},{4,0},{5,7},{6,2},{7,5},{8,12},{9,11},{10,... | collective-permute-start | bytes 1769480 | tf_op jit(solution)/shard_map/down_out1/ppermute | solution.py:592
  146.7 10.9 %collective-permute-start.35 = (bf16[1,192,384]{2,1,0:T(8,128)(2,1)S(1)}, bf16[1,192,384]{2,1,0:T(8,128)(2,1)S(1)}, u32[]{:S(2)}, u32[]{:S(2)}) collective-permute-start(bf16[1,192,384]{2,1,0:T(8,128)(2,1)S(1)} %add_convert_fusion.18), channel_id=1, source_target_pairs={{0,16},{1,17},{2,18},{3,19},{4,20},{5,21},{6,22},{7,23},{8,24},{9,... | collective-permute-start | bytes 442376 | tf_op jit(solution)/shard_map/up_out3/ppermute | solution.py:592
  155.6 4.3 %collective-permute-start.34 = (f32[12,768]{1,0:T(8,128)S(1)}, f32[12,768]{1,0:T(8,128)S(1)}, u32[]{:S(2)}, u32[]{:S(2)}) collective-permute-start(f32[12,768]{1,0:T(8,128)S(1)} %maximum_select_fusion.3), channel_id=1, source_target_pairs={{0,4},{1,5},{2,6},{3,7},{4,0},{5,1},{6,2},{7,3},{8,12},{9,13},{10,... | collective-permute-start | bytes 110600 | tf_op jit(solution)/shard_map/small_in1/ppermute | solution.py:592
  155.7 6.7 %collective-permute-start.32 = (bf16[1,192,384]{2,1,0:T(8,128)(2,1)S(1)}, bf16[1,192,384]{2,1,0:T(8,128)(2,1)S(1)}, u32[]{:S(2)}, u32[]{:S(2)}) collective-permute-start(bf16[1,192,384]{2,1,0:T(8,128)(2,1)S(1)} %get-tuple-element.330), channel_id=1, source_target_pairs={{0,16},{1,17},{2,18},{3,19},{4,20},{5,21},{6,22},{7,23},{8,24},{9,... | collective-permute-start | bytes 442376 | tf_op jit(solution)/shard_map/rest_in3/ppermute | solution.py:592
  156.1 18.0 %collective-permute-start.41 = (bf16[8,192,384]{2,1,0:T(8,128)(2,1)S(1)}, bf16[8,192,384]{2,1,0:T(8,128)(2,1)S(1)}, u32[]{:S(2)}, u32[]{:S(2)}) collective-permute-start(bf16[8,192,384]{2,1,0:T(8,128)(2,1)S(1)} %constant_dynamic-update-slice_fusion.8.low), channel_id=1, source_target_pairs={{0,2},{1,5},{2,0},{3,7},{4,6},{5,1},{6,4},{7,3},{8,10},{9,13},{10,... | collective-permute-start | bytes 3538952 | tf_op jit(solution)/shard_map/down_out0/ppermute | solution.py:592
  157.6 15.6 %collective-permute-start.38 = (bf16[2,192,384]{2,1,0:T(8,128)(2,1)S(1)}, bf16[2,192,384]{2,1,0:T(8,128)(2,1)S(1)}, u32[]{:S(2)}, u32[]{:S(2)}) collective-permute-start(bf16[2,192,384]{2,1,0:T(8,128)(2,1)S(1)} %constant_dynamic-update-slice_fusion.10), channel_id=1, source_target_pairs={{0,8},{1,9},{2,10},{3,11},{4,12},{5,13},{6,14},{7,15},{8,0},{9,1},... | collective-permute-start | bytes 884744 | tf_op jit(solution)/shard_map/up_out2/ppermute | solution.py:592
  160.0 13.2 %collective-permute-start.39 = (f32[12,768]{1,0:T(8,128)S(1)}, f32[12,768]{1,0:T(8,128)S(1)}, u32[]{:S(2)}, u32[]{:S(2)}) collective-permute-start(f32[12,768]{1,0:T(8,128)S(1)} %maximum_select_fusion.2), channel_id=1, source_target_pairs={{0,8},{1,9},{2,10},{3,11},{4,12},{5,13},{6,14},{7,15},{8,0},{9,1},... | collective-permute-start | bytes 110600 | tf_op jit(solution)/shard_map/small_in2/ppermute | solution.py:592
  162.4 11.0 %collective-permute-start.37 = (bf16[1,192,384]{2,1,0:T(8,128)(2,1)S(1)}, bf16[1,192,384]{2,1,0:T(8,128)(2,1)S(1)}, u32[]{:S(2)}, u32[]{:S(2)}) collective-permute-start(bf16[1,192,384]{2,1,0:T(8,128)(2,1)S(1)} %add_convert_fusion.15), channel_id=1, source_target_pairs={{0,16},{1,17},{2,18},{3,19},{4,20},{5,21},{6,22},{7,23},{8,24},{9,... | collective-permute-start | bytes 442376 | tf_op jit(solution)/shard_map/rest_out3/ppermute | solution.py:592
  173.4 7.0 %collective-permute-start.40 = (bf16[2,192,384]{2,1,0:T(8,128)(2,1)S(1)}, bf16[2,192,384]{2,1,0:T(8,128)(2,1)S(1)}, u32[]{:S(2)}, u32[]{:S(2)}) collective-permute-start(bf16[2,192,384]{2,1,0:T(8,128)(2,1)S(1)} %constant_dynamic-update-slice_fusion.14), channel_id=1, source_target_pairs={{0,8},{1,9},{2,10},{3,11},{4,12},{5,13},{6,14},{7,15},{8,0},{9,1},... | collective-permute-start | bytes 884744 | tf_op jit(solution)/shard_map/rest_out2/ppermute | solution.py:592
  173.5 9.7 %collective-permute-start.44 = (bf16[4,192,384]{2,1,0:T(8,128)(2,1)S(1)}, bf16[4,192,384]{2,1,0:T(8,128)(2,1)S(1)}, u32[]{:S(2)}, u32[]{:S(2)}) collective-permute-start(bf16[4,192,384]{2,1,0:T(8,128)(2,1)S(1)} %constant_dynamic-update-slice_fusion.12), channel_id=1, source_target_pairs={{0,4},{1,3},{2,6},{3,1},{4,0},{5,7},{6,2},{7,5},{8,12},{9,11},{10,... | collective-permute-start | bytes 1769480 | tf_op jit(solution)/shard_map/up_out1/ppermute | solution.py:592
  180.5 9.1 %collective-permute-start.42 = (bf16[4,192,384]{2,1,0:T(8,128)(2,1)S(1)}, bf16[4,192,384]{2,1,0:T(8,128)(2,1)S(1)}, u32[]{:S(2)}, u32[]{:S(2)}) collective-permute-start(bf16[4,192,384]{2,1,0:T(8,128)(2,1)S(1)} %constant_dynamic-update-slice_fusion.16), channel_id=1, source_target_pairs={{0,4},{1,3},{2,6},{3,1},{4,0},{5,7},{6,2},{7,5},{8,12},{9,11},{10,... | collective-permute-start | bytes 1769480 | tf_op jit(solution)/shard_map/rest_out1/ppermute | solution.py:592
  180.9 4.1 %collective-permute-start.43 = (f32[12,768]{1,0:T(8,128)S(1)}, f32[12,768]{1,0:T(8,128)S(1)}, u32[]{:S(2)}, u32[]{:S(2)}) collective-permute-start(f32[12,768]{1,0:T(8,128)S(1)} %maximum_select_fusion.1), channel_id=1, source_target_pairs={{0,16},{1,17},{2,18},{3,19},{4,20},{5,21},{6,22},{7,23},{8,24},{9,... | collective-permute-start | bytes 110600 | tf_op jit(solution)/shard_map/small_in3/ppermute | solution.py:592
  184.9 20.4 %collective-permute-start.46 = (bf16[8,192,384]{2,1,0:T(8,128)(2,1)}, bf16[8,192,384]{2,1,0:T(8,128)(2,1)}, u32[]{:S(2)}, u32[]{:S(2)}) collective-permute-start(bf16[8,192,384]{2,1,0:T(8,128)(2,1)} %constant_dynamic-update-slice_fusion.18.low), channel_id=1, source_target_pairs={{0,2},{1,5},{2,0},{3,7},{4,6},{5,1},{6,4},{7,3},{8,10},{9,13},{10,... | collective-permute-start | bytes 3538952 | tf_op jit(solution)/shard_map/up_out0/ppermute | solution.py:592
  191.3 26.3 %collective-permute-start.45 = (bf16[8,192,384]{2,1,0:T(8,128)(2,1)}, bf16[8,192,384]{2,1,0:T(8,128)(2,1)}, u32[]{:S(2)}, u32[]{:S(2)}) collective-permute-start(bf16[8,192,384]{2,1,0:T(8,128)(2,1)} %constant_dynamic-update-slice_fusion.20.low), channel_id=1, source_target_pairs={{0,2},{1,5},{2,0},{3,7},{4,6},{5,1},{6,4},{7,3},{8,10},{9,13},{10,... | collective-permute-start | bytes 3538952 | tf_op jit(solution)/shard_map/rest_out0/ppermute | solution.py:592
  194.4 23.3 %copy-start.12 = (bf16[384,768]{1,0:T(8,128)(2,1)S(1)}, bf16[384,768]{1,0:T(8,128)(2,1)}, u32[]{:S(2)}) copy-start(bf16[384,768]{1,0:T(8,128)(2,1)} %merge.4) | copy-start | bytes 1769476
  (27 other events, 162.4 us)

commit v5 on v4

--- a/solution.py
+++ b/solution.py
@@ -179,7 +179,7 @@
         lse_ref[pl.ds(index, 1), :] = top + jnp.log(total)
         return carry
 
-    lax.fori_loop(0, q_ref.shape[0] // HEAD, head, 0, unroll=2)
+    lax.fori_loop(0, q_ref.shape[0] // HEAD, head, 0)
 
 
 def forward_first_body(
@@ -232,7 +232,7 @@
         d_ref[1, at, :] = dot(q, grad_score, 1, 1).astype(BF16)
         return carry
 
-    lax.fori_loop(0, width // HEAD, head, 0, unroll=2)
+    lax.fori_loop(0, width // HEAD, head, 0)
     rows, step = x_t.shape[0] // (2 * count), width // (2 * count)
     if len(outs) == 2:
         outs = [out.at[:, at * rows : (at + 1) * rows, :] for out in outs for at in range(4)]
@@ -431,7 +431,7 @@
         bias_row[0:1, cols] = jnp.sum(grad.astype(F32), axis=0, keepdims=True)
         return carry
 
-    lax.fori_loop(0, g_ref.shape[1] // span, columns, 0, unroll=True)
+    lax.fori_loop(0, g_ref.shape[1] // span, columns, 0)
     rows = normed_q.shape[1] // (2 * count)
     for half, chunk in ((1, high), (0, low)):
         base = half_base(rel, half, 2 * count)

time: 227 us -> 216 us (0.952); the launches traced: 223 us -> 215 us
  Pallas kernels: 102 us -> 95 us
  waiting for transfers between devices: 69.8 us -> 66.3 us
  starting transfers between devices: 33 us -> 35.8 us
    pallas_call x13, Pallas kernels: 81.5 us -> 74.9 us  [call(): pl.pallas_call(body, in_specs=in_specs, out_specs=out_specs, scratch_shap...]
    ppermute x28, waiting for transfers between devices: 66.5 us -> 62.9 us  [swap(): return lax.ppermute(value, ('dp', 'tensor'), pairs)]
    ppermute x28, starting transfers between devices: 23.8 us -> 26.2 us  [swap(): return lax.ppermute(value, ('dp', 'tensor'), pairs)]
  transfers between devices with their start and end apart: 47 -> 47, of which waited for: 16 -> 16; matrix products, arithmetic and copies ran while one was open for 5% -> 5% of each run, Pallas kernels for 32% -> 30%
where the time goes in v5:
time: 216 us; the launch traced here: 215 us
  Pallas kernels  95 us (44%)
  waiting for transfers between devices  66.3 us (31%)
  starting transfers between devices  35.8 us (17%)
  local copies, waits for them, and re-layouts  12.3 us (6%)
  other arithmetic  4.41 us (2%)
    pallas_call x13, Pallas kernels, call(): pl.pallas_call(body, in_specs=in_specs, out_specs=out_specs, scratch_shap...  74.9 us
    ppermute x28, waiting for transfers between devices, swap(): return lax.ppermute(value, ('dp', 'tensor'), pairs)  62.9 us
    ppermute x28, starting transfers between devices, swap(): return lax.ppermute(value, ('dp', 'tensor'), pairs)  26.2 us
    pallas_call x3, Pallas kernels, final(): pl.pallas_call(partial(body, per), grid_spec=pltpu.PrefetchScalarGridSpec...  14.4 us
    ppermute x19, starting transfers between devices, core_swap(): return lax.ppermute(value, 'tensor', [(0, 1), (1, 0)])  9.56 us
    unnamed x68, local copies, waits for them, and re-layouts  7.77 us
  transfers between devices with their start and end apart: 47, of which 16 were waited for; matrix products, arithmetic and copies ran while one was open for 5% of the time, Pallas kernels for 30%

profile of v5, /device:TPU:1, one launch (start us, length us, event | category | flops | bytes accessed | tf_op | source)
XLA Modules:
  0.0 215.2 jit_solution(13936784492787097004)
XLA Ops:
  0.7 1.5 copy-done.3
  3.7 1.1 collective-permute-done.other.pack.p_other
  7.6 2.2 %collective-permute-done.1.other.pack_other = f32[16,1536]{1,0:T(8,128)S(1)} collective-permute-done((f32[16,1536]{1,0:T(8,128)S(1)}, f32[16,1536]{1,0:T(8,128)S(1)}, u32[]{:S(2)}, u32[]{:S(2)}) %collective-permute-start.1) | collective-permute-done | bytes 98336 | tf_op jit(solution)/shard_map/ppermute | solution.py:595
  9.7 1.2 copy-done.8
  11.0 3.0 %shard_map.240 = (bf16[384,768]{1,0:T(8,128)(2,1)}, bf16[768,1536]{1,0:T(8,128)(2,1)}, bf16[1536,768]{1,0:T(8,128)(2,1)}) custom-call(f32[16,1536]{1,0:T(8,128)S(1)} %shard_map.239.own.pack_own, f32[16,1536]{1,0:T(8,128)S(1)} %collective-permute-done.1.other.pack_other, bf16[384,768]{1,0:T(8,128)(2,1)S(1)} %copy-done.11, bf16[768,1536]{1,0:T(8,128)(2,1)S(1)} %copy-done.1, ...), custom_call_target="tpu_custom_call" | custom-call | tf_op jit(solution)/shard_map/pallas_call | solution.py:790
  14.8 1.5 copy-done.6
  16.3 6.1 %shard_map.241 = (bf16[512,768]{1,0:T(8,128)(2,1)S(1)}, bf16[384,512]{1,0:T(8,128)(2,1)S(1)}, bf16[384,512]{1,0:T(8,128)(2,1)S(1)}, bf16[384,512]{1,0:T(8,128)(2...) custom-call(s32[3]{0:T(128)S(1)} %pad_add_fusion.ids, s32[8]{0:T(128)S(1)} %copy-done.20, f32[3]{0:T(128)S(1)} %copy-done.21, ...), custom_call_target="tpu_custom_call" | custom-call | flops 1 | bytes 1 | tf_op jit(solution)/shard_map/pallas_call | solution.py:88
  22.4 6.1 %shard_map.242 = (bf16[384,512]{1,0:T(8,128)(2,1)S(1)}, bf16[384,512]{1,0:T(8,128)(2,1)S(1)}, bf16[384,512]{1,0:T(8,128)(2,1)S(1)}, bf16[384,512]{1,0:T(8,128)(2,1)S(1)}, f32[8,512]{1,0:T(8,128)S(1)}) custom-call(s32[3]{0:T(128)S(1)} %pad_add_fusion.ids, s32[8]{0:T(128)S(1)} %copy-done.20, bf16[512,768]{1,0:T(8,128)(2,1)S(1)} %get-tuple-element.172.xq, ...), custom_call_target="tpu_custom_call" | custom-call | flops 1 | bytes 1 | tf_op jit(solution)/shard_map/pallas_call | solution.py:88
  29.3 19.2 %shard_map.243 = (f32[512,768]{1,0:T(8,128)S(1)}, f32[512,128]{1,0:T(8,128)S(1)}, bf16[512,768]{1,0:T(8,128)(2,1)S(1)}, bf16[512,1536]{1,0:T(8,128)(2,1)S(1)}, b...) custom-call(f32[3]{0:T(128)S(1)} %copy-done.21, ...), custom_call_target="tpu_custom_call" | custom-call | flops 1 | bytes 1 | tf_op jit(solution)/shard_map/pallas_call | solution.py:88
  48.5 1.4 down_theirshigh.1
  50.3 1.4 down_minehigh.1
  51.7 1.4 down_theirslow.1
  53.6 2.6 %collective-permute-start.9 = (bf16[8,192,384]{2,1,0:T(8,128)(2,1)S(1)}, bf16[8,192,384]{2,1,0:T(8,128)(2,1)S(1)}, u32[]{:S(2)}, u32[]{:S(2)}) collective-permute-start(bf16[8,192,384]{2,1,0:T(8,128)(2,1)S(1)} %add_convert_fusion.2), channel_id=1, source_target_pairs={{0,2},{1,5},{2,0},{3,7},{4,6},{5,1},{6,4},{7,3},{8,10},{9,13},{10,... | collective-permute-start | bytes 3538952 | tf_op jit(solution)/shard_map/down_in0/ppermute | solution.py:592
  56.3 1.4 down_minelow.1
  57.6 7.0 %up_theirs.1 = (bf16[8,192,384]{2,1,0:T(8,128)(2,1)S(1)}, bf16[8,192,384]{2,1,0:T(8,128)(2,1)S(1)}, f32[1,1536]{1,0:T(1,128)S(1)}, f32[512,768]{1,0:T(8,128)S(1)}) custom-call(s32[3]{0:T(128)S(1)} %pad_add_fusion.ids, bf16[512,768]{1,0:T(8,128)(2,1)S(1)} %get-tuple-element.194.grad_feed, bf16[1536,768]{1,0:T(8,128)(2,1)} %collective-permute-done.5.down_other.down, ...), custom_call_target="tpu_custom_call" | custom-call | flops 1 | bytes 1 | tf_op jit(solution)/shard_map/up_theirs/pallas_call | solution.py:88
  65.3 7.0 %up_mine.1 = (bf16[8,192,384]{2,1,0:T(8,128)(2,1)S(1)}, bf16[8,192,384]{2,1,0:T(8,128)(2,1)S(1)}, f32[1,1536]{1,0:T(1,128)S(1)}, f32[512,768]{1,0:T(8,128)S(1)}) custom-call(s32[3]{0:T(128)S(1)} %pad_add_fusion.ids, bf16[512,768]{1,0:T(8,128)(2,1)S(1)} %get-tuple-element.194.grad_feed, bf16[1536,768]{1,0:T(8,128)(2,1)} %get-tuple-element.177.down_own.down, ...), custom_call_target="tpu_custom_call" | custom-call | flops 1 | bytes 1 | tf_op jit(solution)/shard_map/up_mine/pallas_call | solution.py:88
  73.2 1.3 collective-permute-start.15
  74.7 2.2 %norm.1 = (f32[512,768]{1,0:T(8,128)S(1)}, bf16[512,768]{1,0:T(8,128)(2,1)S(1)}, f32[16,768]{1,0:T(8,128)S(1)}, f32[16,768]{1,0:T(8,128)S(1)}) custom-call(f32[3]{0:T(128)S(1)} %copy-done.21, f32[512,768]{1,0:T(8,128)S(1)} %get-tuple-element.206.grad_normed, f32[512,768]{1,0:T(8,128)S(1)} %get-tuple-element.207.grad_sum, ...), custom_call_target="tpu_custom_call" | custom-call | flops 1 | bytes 1 | tf_op jit(solution)/shard_map/norm/pallas_call | solution.py:88
  77.0 8.7 %heads_theirs.1 = (bf16[8,48,384]{2,1,0:T(8,128)(2,1)S(1)}, bf16[8,48,384]{2,1,0:T(8,128)(2,1)S(1)}, bf16[8,48,384]{2,1,0:T(8,128)(2,1)S(1)}, bf16[8,48,384]{2,1...) custom-call(s32[3]{0:T(128)S(1)} %pad_add_fusion.ids, ...), custom_call_target="tpu_custom_call" | custom-call | flops 1 | bytes 1 | tf_op jit(solution)/shard_map/heads_theirs/pallas_call | solution.py:88
  85.7 1.0 collective-permute-start.10
  86.8 8.5 %heads_mine.1 = (bf16[8,192,384]{2,1,0:T(8,128)(2,1)S(1)}, bf16[8,192,384]{2,1,0:T(8,128)(2,1)S(1)}, bf16[3,384,512]{2,1,0:T(8,128)(2,1)S(1)}, f32[8,768]{1,0:T(8,128)S(1)}) custom-call(s32[3]{0:T(128)S(1)} %pad_add_fusion.ids, s32[8]{0:T(128)S(1)} %copy-done.20, bf16[512,768]{1,0:T(8,128)(2,1)S(1)} %get-tuple-element.172.xq, ...), custom_call_target="tpu_custom_call" | custom-call | flops 1 | bytes 1 | tf_op jit(solution)/shard_map/heads_mine/pallas_call | solution.py:88
  96.0 1.4 collective-permute-start.23
  99.7 4.5 %input.1 = f32[512,768]{1,0:T(8,128)} custom-call(f32[3]{0:T(128)S(1)} %copy-done.21, bf16[512,768]{1,0:T(8,128)(2,1)S(1)} %copy-done.10, f32[512,768]{1,0:T(8,128)S(1)} %get-tuple-element.251.grad_first, bf16[3,768,384]{2,1,0:T(8,128)(2,1)S(1)} %copy-done.7, bf16[3,768,384]{2,1,0:T(8,128)(2,1)S(1)} %copy-done.9, ...), custom_call_target="tpu_custom_call" | custom-call | flops 1 | bytes 1 | tf_op jit(solution)/shard_map/input/pallas_call | solution.py:88
  104.3 2.4 %collective-permute-start.24 = (bf16[1,192,384]{2,1,0:T(8,128)(2,1)S(1)}, bf16[1,192,384]{2,1,0:T(8,128)(2,1)S(1)}, u32[]{:S(2)}, u32[]{:S(2)}) collective-permute-start(bf16[1,192,384]{2,1,0:T(8,128)(2,1)S(1)} %get-tuple-element.334), channel_id=1, source_target_pairs={{0,16},{1,17},{2,18},{3,19},{4,20},{5,21},{6,22},{7,23},{8,24},{9,... | collective-permute-start | bytes 442376 | tf_op jit(solution)/shard_map/down_in3/ppermute | solution.py:592
  106.7 1.5 collective-permute-start.17
  108.3 4.8 %collective-permute-done.24 = bf16[1,192,384]{2,1,0:T(8,128)(2,1)S(1)} collective-permute-done((bf16[1,192,384]{2,1,0:T(8,128)(2,1)S(1)}, bf16[1,192,384]{2,1,0:T(8,128)(2,1)S(1)}, u32[]{:S(2)}, u32[]{:S(2)}) %collective-permute-start.24) | collective-permute-done | bytes 147488 | tf_op jit(solution)/shard_map/down_in3/ppermute | solution.py:592
  113.1 1.6 collective-permute-start.19
  114.7 2.1 collective-permute-start.20
  117.1 2.4 %collective-permute-start.27 = (bf16[1,192,384]{2,1,0:T(8,128)(2,1)S(1)}, bf16[1,192,384]{2,1,0:T(8,128)(2,1)S(1)}, u32[]{:S(2)}, u32[]{:S(2)}) collective-permute-start(bf16[1,192,384]{2,1,0:T(8,128)(2,1)S(1)} %add_convert_fusion.21), channel_id=1, source_target_pairs={{0,16},{1,17},{2,18},{3,19},{4,20},{5,21},{6,22},{7,23},{8,24},{9,... | collective-permute-start | bytes 442376 | tf_op jit(solution)/shard_map/down_out3/ppermute | solution.py:592
  120.7 1.2 collective-permute-start.25
  122.4 4.5 %collective-permute-done.27 = bf16[1,192,384]{2,1,0:T(8,128)(2,1)S(1)} collective-permute-done((bf16[1,192,384]{2,1,0:T(8,128)(2,1)S(1)}, bf16[1,192,384]{2,1,0:T(8,128)(2,1)S(1)}, u32[]{:S(2)}, u32[]{:S(2)}) %collective-permute-start.27) | collective-permute-done | bytes 147488 | tf_op jit(solution)/shard_map/down_out3/ppermute | solution.py:592
  127.0 3.2 %collective-permute-done.26 = bf16[2,192,384]{2,1,0:T(8,128)(2,1)S(1)} collective-permute-done((bf16[2,192,384]{2,1,0:T(8,128)(2,1)S(1)}, bf16[2,192,384]{2,1,0:T(8,128)(2,1)S(1)}, u32[]{:S(2)}, u32[]{:S(2)}) %collective-permute-start.26) | collective-permute-done | bytes 294944 | tf_op jit(solution)/shard_map/up_in2/ppermute | solution.py:592
  130.6 8.1 %collective-permute-done.31 = bf16[2,192,384]{2,1,0:T(8,128)(2,1)S(1)} collective-permute-done((bf16[2,192,384]{2,1,0:T(8,128)(2,1)S(1)}, bf16[2,192,384]{2,1,0:T(8,128)(2,1)S(1)}, u32[]{:S(2)}, u32[]{:S(2)}) %collective-permute-start.31) | collective-permute-done | bytes 294944 | tf_op jit(solution)/shard_map/down_out2/ppermute | solution.py:592
  139.2 2.2 %collective-permute-start.35 = (bf16[1,192,384]{2,1,0:T(8,128)(2,1)S(1)}, bf16[1,192,384]{2,1,0:T(8,128)(2,1)S(1)}, u32[]{:S(2)}, u32[]{:S(2)}) collective-permute-start(bf16[1,192,384]{2,1,0:T(8,128)(2,1)S(1)} %add_convert_fusion.18), channel_id=1, source_target_pairs={{0,16},{1,17},{2,18},{3,19},{4,20},{5,21},{6,22},{7,23},{8,24},{9,... | collective-permute-start | bytes 442376 | tf_op jit(solution)/shard_map/up_out3/ppermute | solution.py:592
  141.4 7.9 %collective-permute-done.29 = bf16[2,192,384]{2,1,0:T(8,128)(2,1)S(1)} collective-permute-done((bf16[2,192,384]{2,1,0:T(8,128)(2,1)S(1)}, bf16[2,192,384]{2,1,0:T(8,128)(2,1)S(1)}, u32[]{:S(2)}, u32[]{:S(2)}) %collective-permute-start.29) | collective-permute-done | bytes 294944 | tf_op jit(solution)/shard_map/rest_in2/ppermute | solution.py:592
  149.8 1.4 collective-permute-start.41
  152.9 4.9 %collective-permute-done.32 = bf16[1,192,384]{2,1,0:T(8,128)(2,1)S(1)} collective-permute-done((bf16[1,192,384]{2,1,0:T(8,128)(2,1)S(1)}, bf16[1,192,384]{2,1,0:T(8,128)(2,1)S(1)}, u32[]{:S(2)}, u32[]{:S(2)}) %collective-permute-start.32) | collective-permute-done | bytes 147488 | tf_op jit(solution)/shard_map/rest_in3/ppermute | solution.py:592
  157.9 6.7 %collective-permute-done.39 = f32[12,768]{1,0:T(8,128)S(1)} collective-permute-done((f32[12,768]{1,0:T(8,128)S(1)}, f32[12,768]{1,0:T(8,128)S(1)}, u32[]{:S(2)}, u32[]{:S(2)}) %collective-permute-start.39) | collective-permute-done | bytes 36896 | tf_op jit(solution)/shard_map/small_in2/ppermute | solution.py:592
  165.9 3.7 %down_final.1 = f32[1536,768]{1,0:T(8,128)} custom-call(s32[3]{0:T(128)S(1)} %pad_add_fusion.ids, f32[16,1536]{1,0:T(8,128)S(1)} %shard_map.239.own.pack_own, f32[16,1536]{1,0:T(8,128)S(1)} %collective-permute-done.1.other.pack_other, bf16[8,192,384]{2,1,0:T(8,128)(2,1)S(1)} %constant_dynamic-update-slice_fusion.8.low, ...), custom_call_target="tpu_custom_call" | custom-call | flops 1 | bytes 1 | tf_op jit(solution)/shard_map/down_final/pallas_call | solution.py:1047
  169.6 1.1 collective-permute-done.40
  171.5 3.0 %collective-permute-start.43 = (f32[12,768]{1,0:T(8,128)S(1)}, f32[12,768]{1,0:T(8,128)S(1)}, u32[]{:S(2)}, u32[]{:S(2)}) collective-permute-start(f32[12,768]{1,0:T(8,128)S(1)} %maximum_select_fusion.1), channel_id=1, source_target_pairs={{0,16},{1,17},{2,18},{3,19},{4,20},{5,21},{6,22},{7,23},{8,24},{9,... | collective-permute-start | bytes 110600 | tf_op jit(solution)/shard_map/small_in3/ppermute | solution.py:592
  176.3 1.0 collective-permute-start.46
  177.4 3.3 %collective-permute-done.42 = bf16[4,192,384]{2,1,0:T(8,128)(2,1)S(1)} collective-permute-done((bf16[4,192,384]{2,1,0:T(8,128)(2,1)S(1)}, bf16[4,192,384]{2,1,0:T(8,128)(2,1)S(1)}, u32[]{:S(2)}, u32[]{:S(2)}) %collective-permute-start.42) | collective-permute-done | bytes 589856 | tf_op jit(solution)/shard_map/rest_out1/ppermute | solution.py:592
  182.5 1.1 collective-permute-start.45
  186.7 10.7 %collective-permute-done.46.high = bf16[8,192,384]{2,1,0:T(8,128)(2,1)} collective-permute-done((bf16[8,192,384]{2,1,0:T(8,128)(2,1)}, bf16[8,192,384]{2,1,0:T(8,128)(2,1)}, u32[]{:S(2)}, u32[]{:S(2)}) %collective-permute-start.46) | collective-permute-done | bytes 1179680 | tf_op jit(solution)/shard_map/up_out0/ppermute | solution.py:592
  197.5 5.3 %up_final.1 = f32[768,1536]{1,0:T(8,128)} custom-call(s32[3]{0:T(128)S(1)} %pad_add_fusion.ids, f32[16,1536]{1,0:T(8,128)S(1)} %shard_map.239.own.pack_own, f32[16,1536]{1,0:T(8,128)S(1)} %collective-permute-done.1.other.pack_other, bf16[8,192,384]{2,1,0:T(8,128)(2,1)} %constant_dynamic-update-slice_fusion.18.low, ...), custom_call_target="tpu_custom_call" | custom-call | flops 1 | bytes 1 | tf_op jit(solution)/shard_map/up_final/pallas_call | solution.py:1047
  202.8 7.0 %collective-permute-done.45.high = bf16[8,192,384]{2,1,0:T(8,128)(2,1)} collective-permute-done((bf16[8,192,384]{2,1,0:T(8,128)(2,1)}, bf16[8,192,384]{2,1,0:T(8,128)(2,1)}, u32[]{:S(2)}, u32[]{:S(2)}) %collective-permute-start.45) | collective-permute-done | bytes 1179680 | tf_op jit(solution)/shard_map/rest_out0/ppermute | solution.py:592
  209.8 5.4 %rest_final.1 = (f32[3,768,384]{2,1,0:T(8,128)}, f32[384,768]{1,0:T(8,128)}) custom-call(s32[3]{0:T(128)S(1)} %pad_add_fusion.ids, f32[16,1536]{1,0:T(8,128)S(1)} %shard_map.239.own.pack_own, f32[16,1536]{1,0:T(8,128)S(1)} %collective-permute-done.1.other.pack_other, bf16[8,192,384]{2,1,0:T(8,128)(2,1)} %constant_dynamic-update-slice_fusion.20.low, ...), custom_call_target="tpu_custom_call" | custom-call | flops 1 | bytes 1 | tf_op jit(solution)/shard_map/rest_final/pallas_call | solution.py:1047
  (183 shorter events, 25.4 us)
Async XLA Ops:
  3.6 1.3 collective-permute-start
  5.8 3.9 %collective-permute-start.2 = (bf16[3,768,384]{2,1,0:T(8,128)(2,1)S(1)}, bf16[3,768,384]{2,1,0:T(8,128)(2,1)S(1)}, u32[]{:S(2)}, u32[]{:S(2)}) collective-permute-start(bf16[3,768,384]{2,1,0:T(8,128)(2,1)S(1)} %shard_map.238.weight.w_own), channel_id=1, source_target_pairs={{0,1},{1,0},{2,3},{3,2},{4,5},{5,4},{6,7},{7,6},{8,9},{9,8},{10,11... | collective-permute-start | bytes 5308424 | tf_op jit(solution)/shard_map/ppermute | solution.py:595
  7.1 2.6 %collective-permute-start.1 = (f32[16,1536]{1,0:T(8,128)S(1)}, f32[16,1536]{1,0:T(8,128)S(1)}, u32[]{:S(2)}, u32[]{:S(2)}) collective-permute-start(f32[16,1536]{1,0:T(8,128)S(1)} %shard_map.239.own.pack_own), channel_id=1, source_target_pairs={{0,1},{1,0},{2,3},{3,2},{4,5},{5,4},{6,7},{7,6},{8,9},{9,8},{10,11... | collective-permute-start | bytes 294920 | tf_op jit(solution)/shard_map/ppermute | solution.py:595
  13.9 15.4 %collective-permute-start.4 = (bf16[768,1536]{1,0:T(8,128)(2,1)}, bf16[768,1536]{1,0:T(8,128)(2,1)}, u32[]{:S(2)}, u32[]{:S(2)}) collective-permute-start(bf16[768,1536]{1,0:T(8,128)(2,1)} %get-tuple-element.176.up_own.up), channel_id=1, source_target_pairs={{0,1},{1,0},{2,3},{3,2},{4,5},{5,4},{6,7},{7,6},{8,9},{9,8},{10,11... | collective-permute-start | bytes 7077896 | tf_op jit(solution)/shard_map/ppermute | solution.py:595
  14.1 15.2 %collective-permute-start.5 = (bf16[1536,768]{1,0:T(8,128)(2,1)}, bf16[1536,768]{1,0:T(8,128)(2,1)}, u32[]{:S(2)}, u32[]{:S(2)}) collective-permute-start(bf16[1536,768]{1,0:T(8,128)(2,1)} %get-tuple-element.177.down_own.down), channel_id=1, source_target_pairs={{0,1},{1,0},{2,3},{3,2},{4,5},{5,4},{6,7},{7,6},{8,9},{9,8},{10,11... | collective-permute-start | bytes 7077896 | tf_op jit(solution)/shard_map/ppermute | solution.py:595
  14.4 14.9 %collective-permute-start.3 = (bf16[384,768]{1,0:T(8,128)(2,1)}, bf16[384,768]{1,0:T(8,128)(2,1)}, u32[]{:S(2)}, u32[]{:S(2)}) collective-permute-start(bf16[384,768]{1,0:T(8,128)(2,1)} %get-tuple-element.175.merge_own.merge_q), channel_id=1, source_target_pairs={{0,1},{1,0},{2,3},{3,2},{4,5},{5,4},{6,7},{7,6},{8,9},{9,8},{10,11... | collective-permute-start | bytes 1769480 | tf_op jit(solution)/shard_map/ppermute | solution.py:595
  49.9 3.4 %collective-permute-start.6 = (bf16[8,192,384]{2,1,0:T(8,128)(2,1)S(1)}, bf16[8,192,384]{2,1,0:T(8,128)(2,1)S(1)}, u32[]{:S(2)}, u32[]{:S(2)}) collective-permute-start(bf16[8,192,384]{2,1,0:T(8,128)(2,1)S(1)} %down_theirshigh.1), channel_id=1, source_target_pairs={{0,1},{1,0},{2,3},{3,2},{4,5},{5,4},{6,7},{7,6},{8,9},{9,8},{10,11... | collective-permute-start | bytes 3538952 | tf_op jit(solution)/shard_map/down_high/ppermute | solution.py:595
  53.1 19.2 %collective-permute-start.8 = (bf16[8,192,384]{2,1,0:T(8,128)(2,1)S(1)}, bf16[8,192,384]{2,1,0:T(8,128)(2,1)S(1)}, u32[]{:S(2)}, u32[]{:S(2)}) collective-permute-start(bf16[8,192,384]{2,1,0:T(8,128)(2,1)S(1)} %down_theirslow.1), channel_id=1, source_target_pairs={{0,1},{1,0},{2,3},{3,2},{4,5},{5,4},{6,7},{7,6},{8,9},{9,8},{10,11... | collective-permute-start | bytes 3538952 | tf_op jit(solution)/shard_map/down_low/ppermute | solution.py:595
  53.6 18.7 %collective-permute-start.9 = (bf16[8,192,384]{2,1,0:T(8,128)(2,1)S(1)}, bf16[8,192,384]{2,1,0:T(8,128)(2,1)S(1)}, u32[]{:S(2)}, u32[]{:S(2)}) collective-permute-start(bf16[8,192,384]{2,1,0:T(8,128)(2,1)S(1)} %add_convert_fusion.2), channel_id=1, source_target_pairs={{0,2},{1,5},{2,0},{3,7},{4,6},{5,1},{6,4},{7,3},{8,10},{9,13},{10,... | collective-permute-start | bytes 3538952 | tf_op jit(solution)/shard_map/down_in0/ppermute | solution.py:592
  64.7 8.1 %collective-permute-start.7 = (bf16[8,192,384]{2,1,0:T(8,128)(2,1)S(1)}, bf16[8,192,384]{2,1,0:T(8,128)(2,1)S(1)}, u32[]{:S(2)}, u32[]{:S(2)}) collective-permute-start(bf16[8,192,384]{2,1,0:T(8,128)(2,1)S(1)} %get-tuple-element.190), channel_id=1, source_target_pairs={{0,1},{1,0},{2,3},{3,2},{4,5},{5,4},{6,7},{7,6},{8,9},{9,8},{10,11... | collective-permute-start | bytes 3538952 | tf_op jit(solution)/shard_map/up_high/ppermute | solution.py:595
  65.1 30.8 %collective-permute-start.14 = (bf16[8,192,384]{2,1,0:T(8,128)(2,1)S(1)}, bf16[8,192,384]{2,1,0:T(8,128)(2,1)S(1)}, u32[]{:S(2)}, u32[]{:S(2)}) collective-permute-start(bf16[8,192,384]{2,1,0:T(8,128)(2,1)S(1)} %get-tuple-element.191), channel_id=1, source_target_pairs={{0,1},{1,0},{2,3},{3,2},{4,5},{5,4},{6,7},{7,6},{8,9},{9,8},{10,11... | collective-permute-start | bytes 3538952 | tf_op jit(solution)/shard_map/up_low/ppermute | solution.py:595
  73.2 22.8 %collective-permute-start.15 = (bf16[8,192,384]{2,1,0:T(8,128)(2,1)S(1)}, bf16[8,192,384]{2,1,0:T(8,128)(2,1)S(1)}, u32[]{:S(2)}, u32[]{:S(2)}) collective-permute-start(bf16[8,192,384]{2,1,0:T(8,128)(2,1)S(1)} %add_convert_fusion.1), channel_id=1, source_target_pairs={{0,2},{1,5},{2,0},{3,7},{4,6},{5,1},{6,4},{7,3},{8,10},{9,13},{10,... | collective-permute-start | bytes 3538952 | tf_op jit(solution)/shard_map/up_in0/ppermute | solution.py:592
  74.4 20.8 %collective-permute-start.16 = (bf16[4,192,384]{2,1,0:T(8,128)(2,1)S(1)}, bf16[4,192,384]{2,1,0:T(8,128)(2,1)S(1)}, u32[]{:S(2)}, u32[]{:S(2)}) collective-permute-start(bf16[4,192,384]{2,1,0:T(8,128)(2,1)S(1)} %get-tuple-element.322), channel_id=1, source_target_pairs={{0,4},{1,3},{2,6},{3,1},{4,0},{5,7},{6,2},{7,5},{8,12},{9,11},{10,... | collective-permute-start | bytes 1769480 | tf_op jit(solution)/shard_map/down_in1/ppermute | solution.py:592
  85.7 12.2 %collective-permute-start.10 = (bf16[8,48,384]{2,1,0:T(8,128)(2,1)S(1)}, bf16[8,48,384]{2,1,0:T(8,128)(2,1)S(1)}, u32[]{:S(2)}, u32[]{:S(2)}) collective-permute-start(bf16[8,48,384]{2,1,0:T(8,128)(2,1)S(1)} %get-tuple-element.222), channel_id=1, source_target_pairs={{0,1},{1,0},{2,3},{3,2},{4,5},{5,4},{6,7},{7,6},{8,9},{9,8},{10,11... | collective-permute-start | bytes 884744 | tf_op jit(solution)/shard_map/rest_high/ppermute | solution.py:595
  86.7 11.2 %collective-permute-start.11 = (bf16[8,48,384]{2,1,0:T(8,128)(2,1)S(1)}, bf16[8,48,384]{2,1,0:T(8,128)(2,1)S(1)}, u32[]{:S(2)}, u32[]{:S(2)}) collective-permute-start(bf16[8,48,384]{2,1,0:T(8,128)(2,1)S(1)} %get-tuple-element.223), channel_id=1, source_target_pairs={{0,1},{1,0},{2,3},{3,2},{4,5},{5,4},{6,7},{7,6},{8,9},{9,8},{10,11... | collective-permute-start | bytes 884744 | tf_op jit(solution)/shard_map/rest_high/ppermute | solution.py:595
  95.2 2.7 %collective-permute-start.12 = (bf16[8,48,384]{2,1,0:T(8,128)(2,1)S(1)}, bf16[8,48,384]{2,1,0:T(8,128)(2,1)S(1)}, u32[]{:S(2)}, u32[]{:S(2)}) collective-permute-start(bf16[8,48,384]{2,1,0:T(8,128)(2,1)S(1)} %get-tuple-element.224), channel_id=1, source_target_pairs={{0,1},{1,0},{2,3},{3,2},{4,5},{5,4},{6,7},{7,6},{8,9},{9,8},{10,11... | collective-permute-start | bytes 884744 | tf_op jit(solution)/shard_map/rest_high/ppermute | solution.py:595
  95.9 2.0 collective-permute-start.13
  96.0 8.2 %collective-permute-start.23 = (bf16[2,192,384]{2,1,0:T(8,128)(2,1)S(1)}, bf16[2,192,384]{2,1,0:T(8,128)(2,1)S(1)}, u32[]{:S(2)}, u32[]{:S(2)}) collective-permute-start(bf16[2,192,384]{2,1,0:T(8,128)(2,1)S(1)} %get-tuple-element.328), channel_id=1, source_target_pairs={{0,8},{1,9},{2,10},{3,11},{4,12},{5,13},{6,14},{7,15},{8,0},{9,1},... | collective-permute-start | bytes 884744 | tf_op jit(solution)/shard_map/down_in2/ppermute | solution.py:592
  98.3 21.7 %collective-permute-start.21 = (bf16[8,192,384]{2,1,0:T(8,128)(2,1)S(1)}, bf16[8,192,384]{2,1,0:T(8,128)(2,1)S(1)}, u32[]{:S(2)}, u32[]{:S(2)}) collective-permute-start(bf16[8,192,384]{2,1,0:T(8,128)(2,1)S(1)} %add_convert_fusion), channel_id=1, source_target_pairs={{0,2},{1,5},{2,0},{3,7},{4,6},{5,1},{6,4},{7,3},{8,10},{9,13},{10,... | collective-permute-start | bytes 3538952 | tf_op jit(solution)/shard_map/rest_in0/ppermute | solution.py:592
  99.2 15.5 %collective-permute-start.22 = (bf16[4,192,384]{2,1,0:T(8,128)(2,1)S(1)}, bf16[4,192,384]{2,1,0:T(8,128)(2,1)S(1)}, u32[]{:S(2)}, u32[]{:S(2)}) collective-permute-start(bf16[4,192,384]{2,1,0:T(8,128)(2,1)S(1)} %get-tuple-element.320), channel_id=1, source_target_pairs={{0,4},{1,3},{2,6},{3,1},{4,0},{5,7},{6,2},{7,5},{8,12},{9,11},{10,... | collective-permute-start | bytes 1769480 | tf_op jit(solution)/shard_map/up_in1/ppermute | solution.py:592
  104.3 8.8 %collective-permute-start.24 = (bf16[1,192,384]{2,1,0:T(8,128)(2,1)S(1)}, bf16[1,192,384]{2,1,0:T(8,128)(2,1)S(1)}, u32[]{:S(2)}, u32[]{:S(2)}) collective-permute-start(bf16[1,192,384]{2,1,0:T(8,128)(2,1)S(1)} %get-tuple-element.334), channel_id=1, source_target_pairs={{0,16},{1,17},{2,18},{3,19},{4,20},{5,21},{6,22},{7,23},{8,24},{9,... | collective-permute-start | bytes 442376 | tf_op jit(solution)/shard_map/down_in3/ppermute | solution.py:592
  106.7 10.3 %collective-permute-start.17 = (bf16[8,48,384]{2,1,0:T(8,128)(2,1)S(1)}, bf16[8,48,384]{2,1,0:T(8,128)(2,1)S(1)}, u32[]{:S(2)}, u32[]{:S(2)}) collective-permute-start(bf16[8,48,384]{2,1,0:T(8,128)(2,1)S(1)} %get-tuple-element.226), channel_id=1, source_target_pairs={{0,1},{1,0},{2,3},{3,2},{4,5},{5,4},{6,7},{7,6},{8,9},{9,8},{10,11... | collective-permute-start | bytes 884744 | tf_op jit(solution)/shard_map/rest_low/ppermute | solution.py:595
  108.3 8.8 %collective-permute-start.18 = (bf16[8,48,384]{2,1,0:T(8,128)(2,1)S(1)}, bf16[8,48,384]{2,1,0:T(8,128)(2,1)S(1)}, u32[]{:S(2)}, u32[]{:S(2)}) collective-permute-start(bf16[8,48,384]{2,1,0:T(8,128)(2,1)S(1)} %get-tuple-element.227), channel_id=1, source_target_pairs={{0,1},{1,0},{2,3},{3,2},{4,5},{5,4},{6,7},{7,6},{8,9},{9,8},{10,11... | collective-permute-start | bytes 884744 | tf_op jit(solution)/shard_map/rest_low/ppermute | solution.py:595
  113.1 6.3 %collective-permute-start.19 = (bf16[8,48,384]{2,1,0:T(8,128)(2,1)S(1)}, bf16[8,48,384]{2,1,0:T(8,128)(2,1)S(1)}, u32[]{:S(2)}, u32[]{:S(2)}) collective-permute-start(bf16[8,48,384]{2,1,0:T(8,128)(2,1)S(1)} %get-tuple-element.228), channel_id=1, source_target_pairs={{0,1},{1,0},{2,3},{3,2},{4,5},{5,4},{6,7},{7,6},{8,9},{9,8},{10,11... | collective-permute-start | bytes 884744 | tf_op jit(solution)/shard_map/rest_low/ppermute | solution.py:595
  114.7 5.2 %collective-permute-start.20 = (bf16[8,48,384]{2,1,0:T(8,128)(2,1)S(1)}, bf16[8,48,384]{2,1,0:T(8,128)(2,1)S(1)}, u32[]{:S(2)}, u32[]{:S(2)}) collective-permute-start(bf16[8,48,384]{2,1,0:T(8,128)(2,1)S(1)} %get-tuple-element.229), channel_id=1, source_target_pairs={{0,1},{1,0},{2,3},{3,2},{4,5},{5,4},{6,7},{7,6},{8,9},{9,8},{10,11... | collective-permute-start | bytes 884744 | tf_op jit(solution)/shard_map/rest_low/ppermute | solution.py:595
  117.0 3.7 %collective-permute-start.28 = (f32[12,768]{1,0:T(8,128)S(1)}, f32[12,768]{1,0:T(8,128)S(1)}, u32[]{:S(2)}, u32[]{:S(2)}) collective-permute-start(f32[12,768]{1,0:T(8,128)S(1)} %pad_maximum_fusion), channel_id=1, source_target_pairs={{0,1},{1,0},{2,3},{3,2},{4,5},{5,4},{6,7},{7,6},{8,9},{9,8},{10,11... | collective-permute-start | bytes 110600 | tf_op jit(solution)/shard_map/small_got/ppermute | solution.py:595
  117.1 9.8 %collective-permute-start.27 = (bf16[1,192,384]{2,1,0:T(8,128)(2,1)S(1)}, bf16[1,192,384]{2,1,0:T(8,128)(2,1)S(1)}, u32[]{:S(2)}, u32[]{:S(2)}) collective-permute-start(bf16[1,192,384]{2,1,0:T(8,128)(2,1)S(1)} %add_convert_fusion.21), channel_id=1, source_target_pairs={{0,16},{1,17},{2,18},{3,19},{4,20},{5,21},{6,22},{7,23},{8,24},{9,... | collective-permute-start | bytes 442376 | tf_op jit(solution)/shard_map/down_out3/ppermute | solution.py:592
  119.5 10.8 %collective-permute-start.26 = (bf16[2,192,384]{2,1,0:T(8,128)(2,1)S(1)}, bf16[2,192,384]{2,1,0:T(8,128)(2,1)S(1)}, u32[]{:S(2)}, u32[]{:S(2)}) collective-permute-start(bf16[2,192,384]{2,1,0:T(8,128)(2,1)S(1)} %get-tuple-element.326), channel_id=1, source_target_pairs={{0,8},{1,9},{2,10},{3,11},{4,12},{5,13},{6,14},{7,15},{8,0},{9,1},... | collective-permute-start | bytes 884744 | tf_op jit(solution)/shard_map/up_in2/ppermute | solution.py:592
  120.7 9.7 %collective-permute-start.25 = (bf16[4,192,384]{2,1,0:T(8,128)(2,1)S(1)}, bf16[4,192,384]{2,1,0:T(8,128)(2,1)S(1)}, u32[]{:S(2)}, u32[]{:S(2)}) collective-permute-start(bf16[4,192,384]{2,1,0:T(8,128)(2,1)S(1)} %get-tuple-element.318), channel_id=1, source_target_pairs={{0,4},{1,3},{2,6},{3,1},{4,0},{5,7},{6,2},{7,5},{8,12},{9,11},{10,... | collective-permute-start | bytes 1769480 | tf_op jit(solution)/shard_map/rest_in1/ppermute | solution.py:592
  122.1 27.3 %collective-permute-start.33 = (f32[12,768]{1,0:T(8,128)S(1)}, f32[12,768]{1,0:T(8,128)S(1)}, u32[]{:S(2)}, u32[]{:S(2)}) collective-permute-start(f32[12,768]{1,0:T(8,128)S(1)} %maximum_select_fusion.4), channel_id=1, source_target_pairs={{0,2},{1,3},{2,0},{3,1},{4,6},{5,7},{6,4},{7,5},{8,10},{9,11},{10,... | collective-permute-start | bytes 110600 | tf_op jit(solution)/shard_map/small_in0/ppermute | solution.py:592
  126.9 11.7 %collective-permute-start.31 = (bf16[2,192,384]{2,1,0:T(8,128)(2,1)S(1)}, bf16[2,192,384]{2,1,0:T(8,128)(2,1)S(1)}, u32[]{:S(2)}, u32[]{:S(2)}) collective-permute-start(bf16[2,192,384]{2,1,0:T(8,128)(2,1)S(1)} %constant_dynamic-update-slice_fusion.4), channel_id=1, source_target_pairs={{0,8},{1,9},{2,10},{3,11},{4,12},{5,13},{6,14},{7,15},{8,0},{9,1},... | collective-permute-start | bytes 884744 | tf_op jit(solution)/shard_map/down_out2/ppermute | solution.py:592
  130.3 8.8 %collective-permute-start.30 = (bf16[1,192,384]{2,1,0:T(8,128)(2,1)S(1)}, bf16[1,192,384]{2,1,0:T(8,128)(2,1)S(1)}, u32[]{:S(2)}, u32[]{:S(2)}) collective-permute-start(bf16[1,192,384]{2,1,0:T(8,128)(2,1)S(1)} %get-tuple-element.332), channel_id=1, source_target_pairs={{0,16},{1,17},{2,18},{3,19},{4,20},{5,21},{6,22},{7,23},{8,24},{9,... | collective-permute-start | bytes 442376 | tf_op jit(solution)/shard_map/up_in3/ppermute | solution.py:592
  138.7 10.6 %collective-permute-start.29 = (bf16[2,192,384]{2,1,0:T(8,128)(2,1)S(1)}, bf16[2,192,384]{2,1,0:T(8,128)(2,1)S(1)}, u32[]{:S(2)}, u32[]{:S(2)}) collective-permute-start(bf16[2,192,384]{2,1,0:T(8,128)(2,1)S(1)} %get-tuple-element.324), channel_id=1, source_target_pairs={{0,8},{1,9},{2,10},{3,11},{4,12},{5,13},{6,14},{7,15},{8,0},{9,1},... | collective-permute-start | bytes 884744 | tf_op jit(solution)/shard_map/rest_in2/ppermute | solution.py:592
  138.8 10.8 %collective-permute-start.36 = (bf16[4,192,384]{2,1,0:T(8,128)(2,1)S(1)}, bf16[4,192,384]{2,1,0:T(8,128)(2,1)S(1)}, u32[]{:S(2)}, u32[]{:S(2)}) collective-permute-start(bf16[4,192,384]{2,1,0:T(8,128)(2,1)S(1)} %constant_dynamic-update-slice_fusion.6), channel_id=1, source_target_pairs={{0,4},{1,3},{2,6},{3,1},{4,0},{5,7},{6,2},{7,5},{8,12},{9,11},{10,... | collective-permute-start | bytes 1769480 | tf_op jit(solution)/shard_map/down_out1/ppermute | solution.py:592
  139.2 12.0 %collective-permute-start.35 = (bf16[1,192,384]{2,1,0:T(8,128)(2,1)S(1)}, bf16[1,192,384]{2,1,0:T(8,128)(2,1)S(1)}, u32[]{:S(2)}, u32[]{:S(2)}) collective-permute-start(bf16[1,192,384]{2,1,0:T(8,128)(2,1)S(1)} %add_convert_fusion.18), channel_id=1, source_target_pairs={{0,16},{1,17},{2,18},{3,19},{4,20},{5,21},{6,22},{7,23},{8,24},{9,... | collective-permute-start | bytes 442376 | tf_op jit(solution)/shard_map/up_out3/ppermute | solution.py:592
  149.5 2.9 %collective-permute-start.34 = (f32[12,768]{1,0:T(8,128)S(1)}, f32[12,768]{1,0:T(8,128)S(1)}, u32[]{:S(2)}, u32[]{:S(2)}) collective-permute-start(f32[12,768]{1,0:T(8,128)S(1)} %maximum_select_fusion.3), channel_id=1, source_target_pairs={{0,4},{1,5},{2,6},{3,7},{4,0},{5,1},{6,2},{7,3},{8,12},{9,13},{10,... | collective-permute-start | bytes 110600 | tf_op jit(solution)/shard_map/small_in1/ppermute | solution.py:592
  149.5 8.3 %collective-permute-start.32 = (bf16[1,192,384]{2,1,0:T(8,128)(2,1)S(1)}, bf16[1,192,384]{2,1,0:T(8,128)(2,1)S(1)}, u32[]{:S(2)}, u32[]{:S(2)}) collective-permute-start(bf16[1,192,384]{2,1,0:T(8,128)(2,1)S(1)} %get-tuple-element.330), channel_id=1, source_target_pairs={{0,16},{1,17},{2,18},{3,19},{4,20},{5,21},{6,22},{7,23},{8,24},{9,... | collective-permute-start | bytes 442376 | tf_op jit(solution)/shard_map/rest_in3/ppermute | solution.py:592
  149.8 16.2 %collective-permute-start.41 = (bf16[8,192,384]{2,1,0:T(8,128)(2,1)S(1)}, bf16[8,192,384]{2,1,0:T(8,128)(2,1)S(1)}, u32[]{:S(2)}, u32[]{:S(2)}) collective-permute-start(bf16[8,192,384]{2,1,0:T(8,128)(2,1)S(1)} %constant_dynamic-update-slice_fusion.8.low), channel_id=1, source_target_pairs={{0,2},{1,5},{2,0},{3,7},{4,6},{5,1},{6,4},{7,3},{8,10},{9,13},{10,... | collective-permute-start | bytes 3538952 | tf_op jit(solution)/shard_map/down_out0/ppermute | solution.py:592
  151.2 13.4 %collective-permute-start.38 = (bf16[2,192,384]{2,1,0:T(8,128)(2,1)S(1)}, bf16[2,192,384]{2,1,0:T(8,128)(2,1)S(1)}, u32[]{:S(2)}, u32[]{:S(2)}) collective-permute-start(bf16[2,192,384]{2,1,0:T(8,128)(2,1)S(1)} %constant_dynamic-update-slice_fusion.10), channel_id=1, source_target_pairs={{0,8},{1,9},{2,10},{3,11},{4,12},{5,13},{6,14},{7,15},{8,0},{9,1},... | collective-permute-start | bytes 884744 | tf_op jit(solution)/shard_map/up_out2/ppermute | solution.py:592
  152.5 12.1 %collective-permute-start.39 = (f32[12,768]{1,0:T(8,128)S(1)}, f32[12,768]{1,0:T(8,128)S(1)}, u32[]{:S(2)}, u32[]{:S(2)}) collective-permute-start(f32[12,768]{1,0:T(8,128)S(1)} %maximum_select_fusion.2), channel_id=1, source_target_pairs={{0,8},{1,9},{2,10},{3,11},{4,12},{5,13},{6,14},{7,15},{8,0},{9,1},... | collective-permute-start | bytes 110600 | tf_op jit(solution)/shard_map/small_in2/ppermute | solution.py:592
  157.8 7.2 %collective-permute-start.37 = (bf16[1,192,384]{2,1,0:T(8,128)(2,1)S(1)}, bf16[1,192,384]{2,1,0:T(8,128)(2,1)S(1)}, u32[]{:S(2)}, u32[]{:S(2)}) collective-permute-start(bf16[1,192,384]{2,1,0:T(8,128)(2,1)S(1)} %add_convert_fusion.15), channel_id=1, source_target_pairs={{0,16},{1,17},{2,18},{3,19},{4,20},{5,21},{6,22},{7,23},{8,24},{9,... | collective-permute-start | bytes 442376 | tf_op jit(solution)/shard_map/rest_out3/ppermute | solution.py:592
  165.0 5.6 %collective-permute-start.40 = (bf16[2,192,384]{2,1,0:T(8,128)(2,1)S(1)}, bf16[2,192,384]{2,1,0:T(8,128)(2,1)S(1)}, u32[]{:S(2)}, u32[]{:S(2)}) collective-permute-start(bf16[2,192,384]{2,1,0:T(8,128)(2,1)S(1)} %constant_dynamic-update-slice_fusion.14), channel_id=1, source_target_pairs={{0,8},{1,9},{2,10},{3,11},{4,12},{5,13},{6,14},{7,15},{8,0},{9,1},... | collective-permute-start | bytes 884744 | tf_op jit(solution)/shard_map/rest_out2/ppermute | solution.py:592
  165.1 9.4 %collective-permute-start.44 = (bf16[4,192,384]{2,1,0:T(8,128)(2,1)S(1)}, bf16[4,192,384]{2,1,0:T(8,128)(2,1)S(1)}, u32[]{:S(2)}, u32[]{:S(2)}) collective-permute-start(bf16[4,192,384]{2,1,0:T(8,128)(2,1)S(1)} %constant_dynamic-update-slice_fusion.12), channel_id=1, source_target_pairs={{0,4},{1,3},{2,6},{3,1},{4,0},{5,7},{6,2},{7,5},{8,12},{9,11},{10,... | collective-permute-start | bytes 1769480 | tf_op jit(solution)/shard_map/up_out1/ppermute | solution.py:592
  170.8 10.0 %collective-permute-start.42 = (bf16[4,192,384]{2,1,0:T(8,128)(2,1)S(1)}, bf16[4,192,384]{2,1,0:T(8,128)(2,1)S(1)}, u32[]{:S(2)}, u32[]{:S(2)}) collective-permute-start(bf16[4,192,384]{2,1,0:T(8,128)(2,1)S(1)} %constant_dynamic-update-slice_fusion.16), channel_id=1, source_target_pairs={{0,4},{1,3},{2,6},{3,1},{4,0},{5,7},{6,2},{7,5},{8,12},{9,11},{10,... | collective-permute-start | bytes 1769480 | tf_op jit(solution)/shard_map/rest_out1/ppermute | solution.py:592
  171.5 5.8 %collective-permute-start.43 = (f32[12,768]{1,0:T(8,128)S(1)}, f32[12,768]{1,0:T(8,128)S(1)}, u32[]{:S(2)}, u32[]{:S(2)}) collective-permute-start(f32[12,768]{1,0:T(8,128)S(1)} %maximum_select_fusion.1), channel_id=1, source_target_pairs={{0,16},{1,17},{2,18},{3,19},{4,20},{5,21},{6,22},{7,23},{8,24},{9,... | collective-permute-start | bytes 110600 | tf_op jit(solution)/shard_map/small_in3/ppermute | solution.py:592
  176.3 21.1 %collective-permute-start.46 = (bf16[8,192,384]{2,1,0:T(8,128)(2,1)}, bf16[8,192,384]{2,1,0:T(8,128)(2,1)}, u32[]{:S(2)}, u32[]{:S(2)}) collective-permute-start(bf16[8,192,384]{2,1,0:T(8,128)(2,1)} %constant_dynamic-update-slice_fusion.18.low), channel_id=1, source_target_pairs={{0,2},{1,5},{2,0},{3,7},{4,6},{5,1},{6,4},{7,3},{8,10},{9,13},{10,... | collective-permute-start | bytes 3538952 | tf_op jit(solution)/shard_map/up_out0/ppermute | solution.py:592
  182.5 27.3 %collective-permute-start.45 = (bf16[8,192,384]{2,1,0:T(8,128)(2,1)}, bf16[8,192,384]{2,1,0:T(8,128)(2,1)}, u32[]{:S(2)}, u32[]{:S(2)}) collective-permute-start(bf16[8,192,384]{2,1,0:T(8,128)(2,1)} %constant_dynamic-update-slice_fusion.20.low), channel_id=1, source_target_pairs={{0,2},{1,5},{2,0},{3,7},{4,6},{5,1},{6,4},{7,3},{8,10},{9,13},{10,... | collective-permute-start | bytes 3538952 | tf_op jit(solution)/shard_map/rest_out0/ppermute | solution.py:592
  186.7 23.1 %copy-start.12 = (bf16[384,768]{1,0:T(8,128)(2,1)S(1)}, bf16[384,768]{1,0:T(8,128)(2,1)}, u32[]{:S(2)}) copy-start(bf16[384,768]{1,0:T(8,128)(2,1)} %merge.4) | copy-start | bytes 1769476
  (27 other events, 163.5 us)
